TPU v7x, 32 devices: a whole 2x2x4 slice. The times are simulated.
32 devices in a mesh: rep: 2 (over y), tensor: 4 (over z), req: 4 (over x, core).
Axes of the slice: x: 2, y: 2, z: 4, core: 2. Of those that a mesh axis runs over, the one named last changes fastest.
Arguments:
- hidden: bfloat16 [1024, 29568], P(('rep', 'req'), 'tensor'), parts along dimension 0, may hold values from -6 to 6
- down_projection_weight: bfloat16 [29568, 8192], P('tensor', 'req'), may hold values from -0.03125 to 0.03125
- adapter_shrink_weight: bfloat16 [29568, 8, 64], P('tensor'), may hold values from -0.03125 to 0.03125
- adapter_expand_weight: bfloat16 [8, 64, 8192], P(None, None, 'req'), may hold values from -0.75 to 0.75
- adapter_index_per_row: int32 [1024], P(('rep', 'req')), parts along dimension 0, may hold values from 0 to 7, as said below
Outputs:
- projected: bfloat16 [1024, 8192], P(('rep', 'tensor'), 'req'), parts along dimension 0
There are 2 independent parts, one for each index of `rep`. A program takes and returns all parts, laid end to end along the dimension named above; an argument that names none is the same for every part. Nothing has to cross between parts.
Inputs may be any that keep to these rules, and one draw needn't show every extreme that they name: `adapter_index_per_row`: within each aligned block of 128 rows the ids never fall; some row names 0 and some row names 7.
All inputs are finite; a program needn't handle non-finite values.
Results may differ from a plain program's by a relative error of at most 0.012.
Values may be sent and summed in bfloat16 or wider, within the bound.
No kernel may reach another device: no remote copies, remote signals or barrier semaphores. Data moves between devices by JAX's collectives and lax.ppermute only.
A program may use at most 128 MiB of HBM per device.

v0:
```python
import jax
import jax.numpy as jnp
from jax import lax
from jax.sharding import PartitionSpec as P


def on_device(
    hidden,
    down_projection_weight,
    adapter_shrink_weight,
    adapter_expand_weight,
    adapter_index_per_row,
):
    local_rows = hidden.shape[0]
    local_hidden_units = hidden.shape[1]
    adapter_table = adapter_shrink_weight.shape[1]
    adapter_rank_size = adapter_shrink_weight.shape[2]
    block_width = down_projection_weight.shape[1]
    columns = jnp.arange(adapter_table, dtype=jnp.int32)[None, :]
    onehot = (adapter_index_per_row[:, None] == columns).astype(jnp.float32)
    every = jnp.dot(
        hidden,
        adapter_shrink_weight.reshape(local_hidden_units, adapter_table * adapter_rank_size),
        preferred_element_type=jnp.float32,
    )
    shrink_part = jnp.sum(
        every.reshape(local_rows, adapter_table, adapter_rank_size) * onehot[:, :, None], axis=1
    )
    all_ids = lax.all_gather(adapter_index_per_row, "req", axis=0, tiled=True)
    partial_base = jnp.dot(
        lax.all_gather(hidden, "req", axis=0, tiled=True),
        down_projection_weight,
        preferred_element_type=jnp.float32,
    )
    local_base_output = lax.psum_scatter(
        partial_base.astype(jnp.bfloat16), "tensor", scatter_dimension=0, tiled=True
    ).astype(jnp.float32)
    shrink_full = lax.psum(shrink_part.astype(jnp.bfloat16), "tensor")
    shrink_every = lax.all_gather(shrink_full, "req", axis=0, tiled=True)
    own_rows = local_base_output.shape[0]
    first = lax.axis_index("tensor") * own_rows
    shrink_mine = lax.dynamic_slice_in_dim(shrink_every, first, own_rows, 0)
    ids_mine = lax.dynamic_slice_in_dim(all_ids, first, own_rows, 0)
    mask_mine = (ids_mine[:, None] == columns).astype(jnp.bfloat16)
    placed_rows = (shrink_mine[:, None, :] * mask_mine[:, :, None]).reshape(
        own_rows, adapter_table * adapter_rank_size
    )
    adapter_output = jnp.dot(
        placed_rows,
        adapter_expand_weight.reshape(adapter_table * adapter_rank_size, block_width),
        preferred_element_type=jnp.float32,
    )
    return (local_base_output + adapter_output).astype(jnp.bfloat16)


def solution(mesh):
    placed = (
        P(("rep", "req"), "tensor"),
        P("tensor", "req"),
        P("tensor", None, None),
        P(None, None, "req"),
        P(("rep", "req")),
    )
    return jax.shard_map(
        on_device,
        mesh=mesh,
        in_specs=placed,
        out_specs=P(("rep", "tensor"), "req"),
        check_vma=False,
    )
```

profile of v0, /device:TPU:0, one launch (start us, length us, event | category | flops | bytes accessed | tf_op | source)
XLA Modules:
  0.0 142.6 jit_solution(9706747871687297820)
XLA Ops:
  6.5 0.0 copy-start
  6.5 0.0 all-gather.3.cloned.1.call-start
  6.5 0.7 all-gather.3.cloned.1.call-update
  7.3 0.0 copy-start.1
  7.3 0.0 reduce-scatter.2.cloned.1.call-start
  7.3 59.0 %all-gather.3.cloned.1.call-done = bf16[512,7392]{0,1:T(8,128)(2,1)} async-done(((bf16[128,7392]{0,1:T(8,128)(2,1)}), bf16[512,7392]{0,1:T(8,128)(2,1)}) %all-gather.3.cloned.1.call-update) | async-done | bytes 7569424 | tf_op jit(solution)/shard_map/all_gather | solution.py:31
  66.3 22.6 %convolution_convert_fusion = bf16[512,2048]{1,0:T(8,128)(2,1)} fusion(bf16[512,7392]{0,1:T(8,128)(2,1)} %all-gather.3.cloned.1.call-done, bf16[7392,2048]{1,0:T(8,128)(2,1)} %param.6), kind=kOutput, calls=%fused_computation.2 | convolution fusion | flops 15503196160 | bytes 39944192 | tf_op jit(solution)/shard_map/dot_general | solution.py:30
  88.9 0.0 reduce-scatter.2.cloned.1.call-update
  88.9 0.0 copy-done.1
  88.9 5.0 %all-gather = s32[4,1,128]{2,1,0:T(1,128)S(1)} all-gather(s32[1,1,128]{2,1,0:T(1,128)S(1)} %bitcast.29), channel_id=1, replica_groups=mesh['rep'=2,'tensor'=4,'req'=4] {'req'}, dimensions={0}, use_global_device_ids=true | all-gather | bytes 2560 | tf_op jit(solution)/shard_map/all_gather | solution.py:29
  94.0 0.1 dynamic_slice.7
  94.1 6.2 %fusion.10 = bf16[128,64]{0,1:T(8,128)(2,1)S(1)} fusion(bf16[7392,8,64]{0,2,1:T(8,128)(2,1)} %param.7, bf16[128,7392]{0,1:T(8,128)(2,1)} %param.5, f32[128,8]{0,1:T(8,128)S(1)} %fusion.18), kind=kOutput, calls=%fused_computation.8 | convolution fusion | flops 969007104 | bytes 9482240 | tf_op jit(solution)/shard_map/dot_general | solution.py:21
  100.3 20.0 %psum.7 = bf16[128,64]{0,1:T(8,128)(2,1)S(1)} all-reduce(bf16[128,64]{0,1:T(8,128)(2,1)S(1)} %fusion.10), channel_id=1, replica_groups=mesh['rep'=2,'tensor'=4,'req'=4] {'tensor'}, use_global_device_ids=true, to_apply=%region_2.0 | all-reduce | flops 8192 | bytes 32768 | tf_op jit(solution)/shard_map/psum | solution.py:38
  120.3 5.3 %all_gather.10 = bf16[512,64]{0,1:T(8,128)(2,1)S(1)} all-gather(bf16[128,64]{0,1:T(8,128)(2,1)S(1)} %psum.7), channel_id=1, replica_groups=mesh['rep'=2,'tensor'=4,'req'=4] {'req'}, dimensions={0}, use_global_device_ids=true | all-gather | bytes 81920 | tf_op jit(solution)/shard_map/all_gather | solution.py:39
  125.5 7.9 %reduce-scatter.2.cloned.1.call-done = bf16[128,2048]{1,0:T(8,128)(2,1)} async-done(((bf16[512,2048]{1,0:T(8,128)(2,1)}), bf16[128,2048]{1,0:T(8,128)(2,1)}) %reduce-scatter.2.cloned.1.call-update) | async-done | bytes 524304 | tf_op jit(solution)/shard_map/reduce_scatter | solution.py:35
  133.5 0.0 copy-done
  133.5 2.3 %fusion.3 = bf16[128,2048]{1,0:T(8,128)(2,1)} fusion(bf16[8,64,2048]{2,1,0:T(8,128)(2,1)S(1)} %copy-done, bf16[128,2048]{1,0:T(8,128)(2,1)} %reduce-scatter.2.cloned.1.call-done, bf16[128,8]{0,1:T(8,128)(2,1)S(1)} %fusion.19, bf16[128,64]{0,1:T(8,128)(2,1)S(1)} %constant_dynamic-slice_fusion), kind=kOutput, calls=%fused_computation.5 | convolution fusion | flops 269287424 | bytes 3164160 | tf_op jit(solution)/shard_map/dot_general | solution.py:48
  (3 shorter events, 0.0 us)
Async XLA Ops:
  6.5 126.9 %copy-start = (bf16[8,64,2048]{2,1,0:T(8,128)(2,1)S(1)}, bf16[8,64,2048]{2,1,0:T(8,128)(2,1)}, u32[]{:S(2)}) copy-start(bf16[8,64,2048]{2,1,0:T(8,128)(2,1)} %param.8) | copy-start | bytes 6291460
  6.5 59.7 %all-gather.3.cloned.1.call-start = ((), (), s32[]{:S(2)}) async-start(), calls=%async_computation.1 | async-start | bytes 9461760 | tf_op jit(solution)/shard_map/all_gather | solution.py:31
  7.3 81.7 %copy-start.1 = (s32[128]{0:T(128)S(1)}, s32[128]{0:T(128)}, u32[]{:S(2)}) copy-start(s32[128]{0:T(128)} %param.9) | copy-start | bytes 1540
  7.3 126.2 %reduce-scatter.2.cloned.1.call-start = ((), (), s32[]{:S(2)}) async-start(), calls=%async_computation.2 | async-start | bytes 2621440 | tf_op jit(solution)/shard_map/reduce_scatter | solution.py:35
Sparse Core Ops, SparseCore 0:
  8.9 57.3 all-gather.2
  89.0 44.3 reduce-scatter.1
where the time goes:
time: 143 us
  waiting for transfers between devices  67.6 us (47%)
  matrix products  31.1 us (22%)
  blocking collectives  30.3 us (21%)
  between operations  13.4 us (9%)
    all_gather x1, waiting for transfers between devices, on_device(): lax.all_gather(hidden, 'req', axis=0, tiled=True)  59 us
    dot_general x1, matrix products, on_device(): jnp.dot(lax.all_gather(hidden, 'req', axis=0, tiled=True), down_projectio...  22.6 us
    psum x1, blocking collectives, on_device(): shrink_full = lax.psum(shrink_part.astype(jnp.bfloat16), 'tensor')  20 us
    reduce_scatter x1, waiting for transfers between devices, on_device(): lax.psum_scatter(partial_base.astype(jnp.bfloat16), 'tensor', scatter_dim...  7.95 us
    dot_general x1, matrix products, on_device(): jnp.dot(hidden, adapter_shrink_weight.reshape(local_hidden_units, adapter...  6.23 us
    all_gather x1, blocking collectives, on_device(): shrink_every = lax.all_gather(shrink_full, 'req', axis=0, tiled=True)  5.25 us
    all_gather x1, blocking collectives, on_device(): all_ids = lax.all_gather(adapter_index_per_row, 'req', axis=0, tiled=True)  5.04 us
  transfers between devices with their start and end apart: 2, of which 2 were waited for; matrix products, arithmetic and copies ran while one was open for 4% of the time, Pallas kernels for 0%

commit v1 on v0

v1 whole, which is shorter than its diff:
```python
import functools

import jax
import jax.numpy as jnp
from jax import lax
from jax.experimental import pallas as pl
from jax.experimental.pallas import tpu as pltpu
from jax.sharding import PartitionSpec as P

LANES = 128
DEPTH = 1024
SLOTS = 3
MIB = 1 << 20


def in_vmem():
    return pl.BlockSpec(memory_space=pltpu.VMEM)


def in_hbm():
    return pl.BlockSpec(memory_space=pl.ANY)


def padded(units):
    return (units // LANES + 1) * LANES


def turn_kernel(starts, hidden_ref, ids_ref, whole_ref, *chunk_refs):
    units, rows = hidden_ref.shape
    full = units // LANES
    for block in range(full + 1):
        if block < full:
            tile = hidden_ref[block * LANES : (block + 1) * LANES, :]
        else:
            ids = jnp.broadcast_to(
                ids_ref[...].astype(jnp.float32).astype(jnp.bfloat16),
                ((full + 1) * LANES - units, rows),
            )
            tile = jnp.concatenate([hidden_ref[full * LANES :, :], ids], axis=0)
        turned = tile.T
        at = slice(block * LANES, (block + 1) * LANES)
        whole_ref[:, at] = turned
        for (first, count), chunk_ref in zip(starts, chunk_refs):
            chunk_ref[:, at] = turned[first : first + count]


def emit(acc_ref, ids, keep_first, send_ref, keep_ref, width, adapters):
    rows = send_ref.shape[0]
    wide = acc_ref.shape[1] - width
    rank = wide // adapters
    column = lax.broadcasted_iota(jnp.int32, (2 * rows, wide), 1) // rank
    picked = jnp.where(column.astype(jnp.float32) == ids, acc_ref[:, width:], 0.0)
    tile = picked[:, :LANES]
    for at in range(LANES, wide, LANES):
        tile = tile + picked[:, at : at + LANES]
    tile = tile + pltpu.roll(tile, rank, 1)
    lane = lax.broadcasted_iota(jnp.int32, tile.shape, 1)
    tile = jnp.where(lane < rank, tile, ids).astype(jnp.bfloat16)
    first, second = tile[:rows], tile[rows:]
    send_ref[:, width:] = jnp.where(keep_first, second, first)
    keep_ref[:, width:] = jnp.where(keep_first, first, second)
    for at in range(0, width, 512):
        cols = slice(at, at + 512)
        first = acc_ref[:rows, cols].astype(jnp.bfloat16)
        second = acc_ref[rows:, cols].astype(jnp.bfloat16)
        send_ref[:, cols] = jnp.where(keep_first, second, first)
        keep_ref[:, cols] = jnp.where(keep_first, first, second)


def keeps_first():
    return lax.rem(lax.axis_index("req"), 2) == lax.rem(lax.axis_index("tensor"), 2)


def row_ids(refs, units):
    ids = jnp.concatenate([ref[:, units : units + 1] for ref in refs], axis=0)
    return ids.astype(jnp.float32)


def add_depth(refs, at, count, both_ref, acc_ref):
    rows = jnp.concatenate([ref[:, pl.ds(at, count)] for ref in refs], axis=0)
    acc_ref[...] += jnp.dot(
        rows, both_ref[pl.ds(at, count), :], preferred_element_type=jnp.float32
    )


def first_kernel(
    adapters,
    own_ref,
    other_ref,
    w_hbm,
    s_hbm,
    send_ref,
    keep_ref,
    both_ref,
    acc_ref,
    s_ref,
    s_tail,
    w_sems,
    s_sems,
):
    units, width = w_hbm.shape
    steps = units // DEPTH
    tail = units - steps * DEPTH
    slots = s_ref.shape[0]
    refs = (own_ref, other_ref)

    def w_copy(step, count=DEPTH):
        rows = pl.ds(step * DEPTH, count)
        return pltpu.make_async_copy(
            w_hbm.at[rows], both_ref.at[rows, pl.ds(0, width)], w_sems.at[step]
        )

    def s_copy(step):
        slot = lax.rem(step, slots)
        return pltpu.make_async_copy(
            s_hbm.at[:, pl.ds(step * DEPTH, DEPTH)], s_ref.at[slot], s_sems.at[slot]
        )

    s_tail_copy = pltpu.make_async_copy(
        s_hbm.at[:, pl.ds(steps * DEPTH, tail)], s_tail, s_sems.at[slots]
    )
    for step in range(steps):
        w_copy(step).start()
        if step < slots:
            s_copy(step).start()
    w_copy(steps, tail).start()
    s_tail_copy.start()
    acc_ref[...] = jnp.zeros_like(acc_ref)

    def take(step, carry):
        at = pl.multiple_of(step * DEPTH, DEPTH)
        s_copy(step).wait()
        both_ref[pl.ds(at, DEPTH), width:] = s_ref[lax.rem(step, slots)].T

        @pl.when(step + slots < steps)
        def _():
            s_copy(step + slots).start()

        w_copy(step).wait()
        add_depth(refs, at, DEPTH, both_ref, acc_ref)
        return carry

    lax.fori_loop(0, steps, take, 0)
    s_tail_copy.wait()
    both_ref[pl.ds(steps * DEPTH, tail), width:] = s_tail[...].T
    w_copy(steps, tail).wait()
    add_depth(refs, steps * DEPTH, tail, both_ref, acc_ref)
    emit(acc_ref, row_ids(refs, units), keeps_first(), send_ref, keep_ref, width, adapters)


def later_kernel(adapters, width, own_ref, other_ref, both_ref, send_ref, keep_ref, acc_ref):
    units = both_ref.shape[0]
    steps = units // DEPTH
    tail = units - steps * DEPTH
    refs = (own_ref, other_ref)
    acc_ref[...] = jnp.zeros_like(acc_ref)

    def step_of(step, carry):
        add_depth(refs, pl.multiple_of(step * DEPTH, DEPTH), DEPTH, both_ref, acc_ref)
        return carry

    lax.fori_loop(0, steps, step_of, 0)
    if tail:
        add_depth(refs, steps * DEPTH, tail, both_ref, acc_ref)
    emit(acc_ref, row_ids(refs, units), keeps_first(), send_ref, keep_ref, width, adapters)


def last_kernel(n_tensor, adapters, far, expand_ref, *refs):
    out_ref = refs[-1]
    near_sum, near_got = refs[0], refs[1]
    far_sums, far_gots = refs[2 : 2 + far], refs[2 + far : 2 + 2 * far]
    wide, width = expand_ref.shape
    rank = wide // adapters
    is_near = lax.axis_index("tensor") // 2 == lax.axis_index("req") // 2

    def total(first, count, far_at, cols):
        rows = slice(first, first + count)
        near = near_sum[rows, cols].astype(jnp.float32) + near_got[rows, cols].astype(jnp.float32)
        away = far_sums[far_at][:, cols].astype(jnp.float32) + far_gots[far_at][:, cols].astype(
            jnp.float32
        )
        return jnp.where(is_near, near, away)

    def whole(cols):
        parts, first = [], 0
        for at, ref in enumerate(far_sums):
            parts.append(total(first, ref.shape[0], at, cols))
            first += ref.shape[0]
        return jnp.concatenate(parts, axis=0)

    small = whole(slice(width, width + LANES))
    ids = small[:, rank : rank + 1] * (1.0 / n_tensor)
    lane = lax.broadcasted_iota(jnp.int32, small.shape, 1)
    shrink = jnp.where(lane < rank, small, 0.0)
    shrink = shrink + pltpu.roll(shrink, rank, 1)
    spread = jnp.concatenate([shrink] * (wide // LANES), axis=1)
    column = lax.broadcasted_iota(jnp.int32, spread.shape, 1) // rank
    placed = jnp.where(column.astype(jnp.float32) == ids, spread, 0.0).astype(jnp.bfloat16)
    for at in range(0, width, 512):
        cols = slice(at, at + 512)
        adapter = jnp.dot(placed, expand_ref[:, cols], preferred_element_type=jnp.float32)
        out_ref[:, cols] = (whole(cols) + adapter).astype(out_ref.dtype)


def paired(n_tensor, n_req, parts, hidden, weight, shrink, expand, ids):
    rows, units = hidden.shape
    width = weight.shape[1]
    adapters, rank = shrink.shape[1:]
    wide = adapters * rank
    room = padded(units)
    payload = width + LANES
    chunk = rows // parts
    bf16 = jnp.bfloat16

    def params(mib):
        return pltpu.CompilerParams(vmem_limit_bytes=mib * MIB)

    quick = pl.CostEstimate(flops=1, bytes_accessed=1, transcendentals=0)

    starts = [(at * chunk, chunk) for at in range(parts)]
    turned = pl.pallas_call(
        functools.partial(turn_kernel, starts),
        out_shape=[jax.ShapeDtypeStruct((rows, room), bf16)]
        + [jax.ShapeDtypeStruct((chunk, room), bf16)] * parts,
        in_specs=[in_vmem(), in_vmem()],
        out_specs=[in_vmem()] * (1 + parts),
        compiler_params=params(2),
        name="turn",
    )(hidden.T, ids.reshape(1, rows))
    own, chunks = turned[0], turned[1:]

    def left(array):
        return pltpu.with_memory_space_constraint(array, pltpu.HBM)

    across = [(i, i ^ 2) for i in range(n_req)]
    beside = [(i, i ^ 1) for i in range(n_req)]
    next_z = [(i, i ^ 1) for i in range(n_tensor)]
    to_near, to_far = [], []
    for t in range(n_tensor):
        for r in range(n_req):
            hop = (t * n_req + r, (t ^ 2) * n_req + r)
            (to_far if t // 2 == r // 2 else to_near).append(hop)

    direct = [lax.ppermute(part, "req", across) for part in chunks]
    other = lax.ppermute(own, "req", beside)

    shrink_rows = shrink.transpose(1, 2, 0).reshape(wide, units)
    near_send, near_keep, both = pl.pallas_call(
        functools.partial(first_kernel, adapters),
        out_shape=[
            jax.ShapeDtypeStruct((rows, payload), bf16),
            jax.ShapeDtypeStruct((rows, payload), bf16),
            pltpu.VMEM((units, width + wide), bf16),
        ],
        in_specs=[in_vmem(), in_vmem(), in_hbm(), in_hbm()],
        out_specs=[in_vmem()] * 3,
        scratch_shapes=[
            pltpu.VMEM((2 * rows, width + wide), jnp.float32),
            pltpu.VMEM((SLOTS, wide, DEPTH), bf16),
            pltpu.VMEM((wide, units % DEPTH), bf16),
            pltpu.SemaphoreType.DMA((units // DEPTH + 1,)),
            pltpu.SemaphoreType.DMA((SLOTS + 1,)),
        ],
        compiler_params=params(8),
        cost_estimate=quick,
        name="first",
    )(own, other, left(weight), left(shrink_rows))

    def halve(send, keep, hops):
        got = lax.ppermute(send, "tensor", next_z)
        total = (keep.astype(jnp.float32) + got.astype(jnp.float32)).astype(bf16)
        return total, lax.ppermute(total, ("tensor", "req"), hops)

    direct[0], near_send = lax.optimization_barrier((direct[0], near_send))
    near_sum, near_got = halve(near_send, near_keep, to_near)

    far_sums, far_gots = [], []
    for at in range(parts):
        part = direct[at]
        passed = lax.ppermute(part, "req", beside)
        send, keep = pl.pallas_call(
            functools.partial(later_kernel, adapters, width),
            out_shape=[jax.ShapeDtypeStruct((chunk, payload), bf16)] * 2,
            in_specs=[in_vmem()] * 3,
            out_specs=[in_vmem()] * 2,
            scratch_shapes=[pltpu.VMEM((2 * chunk, width + wide), jnp.float32)],
            compiler_params=params(3),
            cost_estimate=quick,
            name="later",
        )(part, passed, both)
        if at + 1 < parts:
            direct[at + 1], send = lax.optimization_barrier((direct[at + 1], send))
        total, got = halve(send, keep, to_far)
        far_sums.append(total)
        far_gots.append(got)

    return pl.pallas_call(
        functools.partial(last_kernel, n_tensor, adapters, parts),
        out_shape=jax.ShapeDtypeStruct((rows, width), bf16),
        in_specs=[in_vmem()] * (3 + 2 * parts),
        out_specs=in_vmem(),
        compiler_params=params(8),
        name="last",
    )(expand.reshape(wide, width), near_sum, near_got, *far_sums, *far_gots)


def gathered(hidden, weight, shrink, expand, ids):
    rows, units = hidden.shape
    adapters, rank = shrink.shape[1:]
    width = weight.shape[1]
    columns = jnp.arange(adapters, dtype=jnp.int32)[None, :]
    onehot = (ids[:, None] == columns).astype(jnp.float32)
    every = jnp.dot(
        hidden, shrink.reshape(units, adapters * rank), preferred_element_type=jnp.float32
    )
    part = jnp.sum(every.reshape(rows, adapters, rank) * onehot[:, :, None], axis=1)
    all_ids = lax.all_gather(ids, "req", axis=0, tiled=True)
    base = jnp.dot(
        lax.all_gather(hidden, "req", axis=0, tiled=True),
        weight,
        preferred_element_type=jnp.float32,
    )
    base = lax.psum_scatter(
        base.astype(jnp.bfloat16), "tensor", scatter_dimension=0, tiled=True
    ).astype(jnp.float32)
    shrunk = lax.all_gather(
        lax.psum(part.astype(jnp.bfloat16), "tensor"), "req", axis=0, tiled=True
    )
    mine = base.shape[0]
    first = lax.axis_index("tensor") * mine
    shrunk = lax.dynamic_slice_in_dim(shrunk, first, mine, 0)
    mask = lax.dynamic_slice_in_dim(all_ids, first, mine, 0)[:, None] == columns
    placed = (shrunk[:, None, :] * mask.astype(jnp.bfloat16)[:, :, None]).reshape(
        mine, adapters * rank
    )
    adapter = jnp.dot(
        placed, expand.reshape(adapters * rank, width), preferred_element_type=jnp.float32
    )
    return (base + adapter).astype(jnp.bfloat16)


def solution(mesh):
    n_tensor, n_req = mesh.shape["tensor"], mesh.shape["req"]
    if n_tensor == 4 and n_req == 4:
        on_device = functools.partial(paired, n_tensor, n_req, 4)
    else:
        on_device = gathered
    placed = (
        P(("rep", "req"), "tensor"),
        P("tensor", "req"),
        P("tensor", None, None),
        P(None, None, "req"),
        P(("rep", "req")),
    )
    return jax.shard_map(
        on_device,
        mesh=mesh,
        in_specs=placed,
        out_specs=P(("rep", "tensor"), "req"),
        check_vma=False,
    )
```

time: 143 us -> 152 us (1.063)
  the two profiles are of different devices: /device:TPU:0 before, /device:TPU:2 now
where the time goes in v1:
time: 152 us
  local copies, waits for them, and re-layouts  61.7 us (41%)
  Pallas kernels  52.1 us (34%)
  waiting for transfers between devices  19.3 us (13%)
  starting transfers between devices  18.3 us (12%)
    unnamed x16, local copies, waits for them, and re-layouts  61.7 us
    pallas_call x4, Pallas kernels, paired(): pl.pallas_call(functools.partial(later_kernel, adapters, width), out_shap...  30.2 us
    pallas_call x1, Pallas kernels, paired(): pl.pallas_call(functools.partial(first_kernel, adapters), out_shape=[jax....  19.8 us
    ppermute x5, waiting for transfers between devices, halve(): return (total, lax.ppermute(total, ('tensor', 'req'), hops))  11.7 us
    ppermute x5, starting transfers between devices, halve(): return (total, lax.ppermute(total, ('tensor', 'req'), hops))  9.99 us
    ppermute x5, starting transfers between devices, halve(): got = lax.ppermute(send, 'tensor', next_z)  5.6 us
    ppermute x1, waiting for transfers between devices, paired(): other = lax.ppermute(own, 'req', beside)  3.79 us
  transfers between devices with their start and end apart: 19, of which 6 were waited for; matrix products, arithmetic and copies ran while one was open for 0% of the time, Pallas kernels for 33%

profile of v1, /device:TPU:2, one launch (start us, length us, event | category | flops | bytes accessed | tf_op | source)
XLA Modules:
  0.0 151.9 jit_solution(16355209460419716034)
XLA Ops:
  0.0 1.5 copy-done.6
  2.9 3.8 %collective-permute-done.other_ref = bf16[128,7424]{1,0:T(8,128)(2,1)S(1)} collective-permute-done((bf16[128,7424]{1,0:T(8,128)(2,1)S(1)}, bf16[128,7424]{1,0:T(8,128)(2,1)S(1)}, u32[]{:S(2)}, u32[]{:S(2)}) %collective-permute-start) | collective-permute-done | bytes 1900576 | tf_op jit(solution)/shard_map/ppermute | solution.py:245
  6.7 19.8 %first.1 = (bf16[128,2176]{1,0:T(8,128)(2,1)S(1)}, bf16[128,2176]{1,0:T(8,128)(2,1)S(1)}, bf16[7392,2560]{1,0:T(8,128)(2,1)S(1)}) custom-call(bf16[128,7424]{1,0:T(8,128)(2,1)S(1)} %get-tuple-element.29.own_ref, bf16[128,7424]{1,0:T(8,128)(2,1)S(1)} %collective-permute-done.other_ref, bf16[7392,2048]{1,0:T(8,128)(2,1)} %w_hbm.1, bf16[512,7392]{1,0:T(8,128)(2,1)} %bitcast.9), custom_call_target="tpu_custom_call" | custom-call | flops 1 | bytes 1 | tf_op jit(solution)/shard_map/first/pallas_call | solution.py:248
  26.5 12.5 %copy-done = bf16[7392,2560]{1,0:T(8,128)(2,1)} copy-done((bf16[7392,2560]{1,0:T(8,128)(2,1)}, bf16[7392,2560]{1,0:T(8,128)(2,1)S(1)}, u32[]{:S(2)}) %copy-start) | copy-done | bytes 37847064
  39.0 1.6 %collective-permute-start.2 = (bf16[128,2176]{1,0:T(8,128)(2,1)S(1)}, bf16[128,2176]{1,0:T(8,128)(2,1)S(1)}, u32[]{:S(2)}, u32[]{:S(2)}) collective-permute-start(bf16[128,2176]{1,0:T(8,128)(2,1)S(1)} %get-tuple-element.33), channel_id=1, source_target_pairs={{0,4},{4,0},{8,12},{12,8},{1,5},{5,1},{9,13},{13,9},{2,6},{6,2},{1... | collective-permute-start | bytes 1671176 | tf_op jit(solution)/shard_map/ppermute | solution.py:270
  41.1 1.5 collective-permute-start.8
  43.1 11.8 %copy-done.1 = bf16[7392,2560]{1,0:T(8,128)(2,1)S(1)} copy-done((bf16[7392,2560]{1,0:T(8,128)(2,1)S(1)}, bf16[7392,2560]{1,0:T(8,128)(2,1)}, u32[]{:S(2)}) %copy-start.1) | copy-done | bytes 37847064
  54.9 7.6 %later.4 = (bf16[32,2176]{1,0:T(8,128)(2,1)S(1)}, bf16[32,2176]{1,0:T(8,128)(2,1)S(1)}) custom-call(bf16[32,7424]{1,0:T(8,128)(2,1)S(1)} %collective-permute-done.1.own_ref, bf16[32,7424]{1,0:T(8,128)(2,1)S(1)} %collective-permute-done.4.other_ref, bf16[7392,2560]{1,0:T(8,128)(2,1)S(1)} %copy-done.1), custom_call_target="tpu_custom_call" | custom-call | flops 1 | bytes 1 | tf_op jit(solution)/shard_map/later/pallas_call | solution.py:281
  62.8 4.8 %collective-permute-start.3 = (bf16[128,2176]{1,0:T(8,128)(2,1)S(1)}, bf16[128,2176]{1,0:T(8,128)(2,1)S(1)}, u32[]{:S(2)}, u32[]{:S(2)}) collective-permute-start(bf16[128,2176]{1,0:T(8,128)(2,1)S(1)} %add_convert_fusion.refs_0_), channel_id=1, source_target_pairs={{2,10},{3,11},{6,14},{7,15},{8,0},{9,1},{12,4},{13,5},{18,26},{19,... | collective-permute-start | bytes 1671176 | tf_op jit(solution)/shard_map/ppermute | solution.py:272
  67.7 11.8 %copy-done.2 = bf16[7392,2560]{1,0:T(8,128)(2,1)S(1)} copy-done((bf16[7392,2560]{1,0:T(8,128)(2,1)S(1)}, bf16[7392,2560]{1,0:T(8,128)(2,1)}, u32[]{:S(2)}) %copy-start.2) | copy-done | bytes 37847064
  79.5 7.6 %later.5 = (bf16[32,2176]{1,0:T(8,128)(2,1)S(1)}, bf16[32,2176]{1,0:T(8,128)(2,1)S(1)}) custom-call(bf16[32,7424]{1,0:T(8,128)(2,1)S(1)} %collective-permute-done.5.own_ref, bf16[32,7424]{1,0:T(8,128)(2,1)S(1)} %collective-permute-done.7.other_ref, bf16[7392,2560]{1,0:T(8,128)(2,1)S(1)} %copy-done.2), custom_call_target="tpu_custom_call" | custom-call | flops 1 | bytes 1 | tf_op jit(solution)/shard_map/later/pallas_call | solution.py:281
  87.0 1.6 %collective-permute-start.9 = (bf16[32,2176]{1,0:T(8,128)(2,1)S(1)}, bf16[32,2176]{1,0:T(8,128)(2,1)S(1)}, u32[]{:S(2)}, u32[]{:S(2)}) collective-permute-start(bf16[32,2176]{1,0:T(8,128)(2,1)S(1)} %get-tuple-element.44), channel_id=1, source_target_pairs={{0,4},{4,0},{8,12},{12,8},{1,5},{5,1},{9,13},{13,9},{2,6},{6,2},{1... | collective-permute-start | bytes 417800 | tf_op jit(solution)/shard_map/ppermute | solution.py:270
  88.7 1.3 collective-permute-start.15
  90.5 11.8 %copy-done.3 = bf16[7392,2560]{1,0:T(8,128)(2,1)S(1)} copy-done((bf16[7392,2560]{1,0:T(8,128)(2,1)S(1)}, bf16[7392,2560]{1,0:T(8,128)(2,1)}, u32[]{:S(2)}) %copy-start.3) | copy-done | bytes 37847064
  102.3 7.6 %later.6 = (bf16[32,2176]{1,0:T(8,128)(2,1)S(1)}, bf16[32,2176]{1,0:T(8,128)(2,1)S(1)}) custom-call(bf16[32,7424]{1,0:T(8,128)(2,1)S(1)} %collective-permute-done.8.own_ref, bf16[32,7424]{1,0:T(8,128)(2,1)S(1)} %collective-permute-done.10.other_ref, bf16[7392,2560]{1,0:T(8,128)(2,1)S(1)} %copy-done.3), custom_call_target="tpu_custom_call" | custom-call | flops 1 | bytes 1 | tf_op jit(solution)/shard_map/later/pallas_call | solution.py:281
  110.4 1.3 collective-permute-start.16
  112.2 11.8 %copy-done.4 = bf16[7392,2560]{1,0:T(8,128)(2,1)S(1)} copy-done((bf16[7392,2560]{1,0:T(8,128)(2,1)S(1)}, bf16[7392,2560]{1,0:T(8,128)(2,1)}, u32[]{:S(2)}) %copy-start.4) | copy-done | bytes 37847064
  124.0 7.6 %later.7 = (bf16[32,2176]{1,0:T(8,128)(2,1)S(1)}, bf16[32,2176]{1,0:T(8,128)(2,1)S(1)}) custom-call(bf16[32,7424]{1,0:T(8,128)(2,1)S(1)} %collective-permute-done.11.own_ref, bf16[32,7424]{1,0:T(8,128)(2,1)S(1)} %collective-permute-done.13.other_ref, bf16[7392,2560]{1,0:T(8,128)(2,1)S(1)} %copy-done.4), custom_call_target="tpu_custom_call" | custom-call | flops 1 | bytes 1 | tf_op jit(solution)/shard_map/later/pallas_call | solution.py:281
  131.6 1.6 %collective-permute-start.14 = (bf16[32,2176]{1,0:T(8,128)(2,1)S(1)}, bf16[32,2176]{1,0:T(8,128)(2,1)S(1)}, u32[]{:S(2)}, u32[]{:S(2)}) collective-permute-start(bf16[32,2176]{1,0:T(8,128)(2,1)S(1)} %get-tuple-element.52), channel_id=1, source_target_pairs={{0,4},{4,0},{8,12},{12,8},{1,5},{5,1},{9,13},{13,9},{2,6},{6,2},{1... | collective-permute-start | bytes 417800 | tf_op jit(solution)/shard_map/ppermute | solution.py:270
  134.5 2.8 %collective-permute-done.14 = bf16[32,2176]{1,0:T(8,128)(2,1)S(1)} collective-permute-done((bf16[32,2176]{1,0:T(8,128)(2,1)S(1)}, bf16[32,2176]{1,0:T(8,128)(2,1)S(1)}, u32[]{:S(2)}, u32[]{:S(2)}) %collective-permute-start.14) | collective-permute-done | bytes 139296 | tf_op jit(solution)/shard_map/ppermute | solution.py:270
  137.4 1.3 collective-permute-start.18
  138.7 9.7 %collective-permute-done.17.refs_8_ = bf16[32,2176]{1,0:T(8,128)(2,1)S(1)} collective-permute-done((bf16[32,2176]{1,0:T(8,128)(2,1)S(1)}, bf16[32,2176]{1,0:T(8,128)(2,1)S(1)}, u32[]{:S(2)}, u32[]{:S(2)}) %collective-permute-start.17) | collective-permute-done | bytes 139296 | tf_op jit(solution)/shard_map/ppermute | solution.py:272
  148.4 2.1 %collective-permute-done.18.refs_9_ = bf16[32,2176]{1,0:T(8,128)(2,1)S(1)} collective-permute-done((bf16[32,2176]{1,0:T(8,128)(2,1)S(1)}, bf16[32,2176]{1,0:T(8,128)(2,1)S(1)}, u32[]{:S(2)}, u32[]{:S(2)}) %collective-permute-start.18) | collective-permute-done | bytes 139296 | tf_op jit(solution)/shard_map/ppermute | solution.py:272
  150.4 1.4 last.1
  (42 shorter events, 5.7 us)
Async XLA Ops:
  2.7 3.9 %collective-permute-start = (bf16[128,7424]{1,0:T(8,128)(2,1)S(1)}, bf16[128,7424]{1,0:T(8,128)(2,1)S(1)}, u32[]{:S(2)}, u32[]{:S(2)}) collective-permute-start(bf16[128,7424]{1,0:T(8,128)(2,1)S(1)} %get-tuple-element.29.own_ref), channel_id=1, source_target_pairs={{0,1},{1,0},{2,3},{3,2},{4,5},{5,4},{6,7},{7,6},{8,9},{9,8},{10,11... | collective-permute-start | bytes 5701640 | tf_op jit(solution)/shard_map/ppermute | solution.py:245
  2.8 36.2 %collective-permute-start.1 = (bf16[32,7424]{1,0:T(8,128)(2,1)S(1)}, bf16[32,7424]{1,0:T(8,128)(2,1)S(1)}, u32[]{:S(2)}, u32[]{:S(2)}) collective-permute-start(bf16[32,7424]{1,0:T(8,128)(2,1)S(1)} %get-tuple-element.31), channel_id=1, source_target_pairs={{0,2},{1,3},{2,0},{3,1},{4,6},{5,7},{6,4},{7,5},{8,10},{9,11},{10,... | collective-permute-start | bytes 1425416 | tf_op jit(solution)/shard_map/ppermute | solution.py:244
  26.5 12.5 %copy-start = (bf16[7392,2560]{1,0:T(8,128)(2,1)}, bf16[7392,2560]{1,0:T(8,128)(2,1)S(1)}, u32[]{:S(2)}) copy-start(bf16[7392,2560]{1,0:T(8,128)(2,1)S(1)} %get-tuple-element.35.both_ref) | copy-start | bytes 113541120
  39.0 23.7 %collective-permute-start.2 = (bf16[128,2176]{1,0:T(8,128)(2,1)S(1)}, bf16[128,2176]{1,0:T(8,128)(2,1)S(1)}, u32[]{:S(2)}, u32[]{:S(2)}) collective-permute-start(bf16[128,2176]{1,0:T(8,128)(2,1)S(1)} %get-tuple-element.33), channel_id=1, source_target_pairs={{0,4},{4,0},{8,12},{12,8},{1,5},{5,1},{9,13},{13,9},{2,6},{6,2},{1... | collective-permute-start | bytes 1671176 | tf_op jit(solution)/shard_map/ppermute | solution.py:270
  40.6 2.6 %collective-permute-start.4 = (bf16[32,7424]{1,0:T(8,128)(2,1)S(1)}, bf16[32,7424]{1,0:T(8,128)(2,1)S(1)}, u32[]{:S(2)}, u32[]{:S(2)}) collective-permute-start(bf16[32,7424]{1,0:T(8,128)(2,1)S(1)} %collective-permute-done.1.own_ref), channel_id=1, source_target_pairs={{0,1},{1,0},{2,3},{3,2},{4,5},{5,4},{6,7},{7,6},{8,9},{9,8},{10,11... | collective-permute-start | bytes 1425416 | tf_op jit(solution)/shard_map/ppermute | solution.py:280
  40.6 21.9 %collective-permute-start.5 = (bf16[32,7424]{1,0:T(8,128)(2,1)S(1)}, bf16[32,7424]{1,0:T(8,128)(2,1)S(1)}, u32[]{:S(2)}, u32[]{:S(2)}) collective-permute-start(bf16[32,7424]{1,0:T(8,128)(2,1)S(1)} %get-tuple-element.37), channel_id=1, source_target_pairs={{0,2},{1,3},{2,0},{3,1},{4,6},{5,7},{6,4},{7,5},{8,10},{9,11},{10,... | collective-permute-start | bytes 1425416 | tf_op jit(solution)/shard_map/ppermute | solution.py:244
  41.1 45.9 %collective-permute-start.8 = (bf16[32,7424]{1,0:T(8,128)(2,1)S(1)}, bf16[32,7424]{1,0:T(8,128)(2,1)S(1)}, u32[]{:S(2)}, u32[]{:S(2)}) collective-permute-start(bf16[32,7424]{1,0:T(8,128)(2,1)S(1)} %get-tuple-element.42), channel_id=1, source_target_pairs={{0,2},{1,3},{2,0},{3,1},{4,6},{5,7},{6,4},{7,5},{8,10},{9,11},{10,... | collective-permute-start | bytes 1425416 | tf_op jit(solution)/shard_map/ppermute | solution.py:244
  42.6 67.2 %collective-permute-start.11 = (bf16[32,7424]{1,0:T(8,128)(2,1)S(1)}, bf16[32,7424]{1,0:T(8,128)(2,1)S(1)}, u32[]{:S(2)}, u32[]{:S(2)}) collective-permute-start(bf16[32,7424]{1,0:T(8,128)(2,1)S(1)} %get-tuple-element.47), channel_id=1, source_target_pairs={{0,2},{1,3},{2,0},{3,1},{4,6},{5,7},{6,4},{7,5},{8,10},{9,11},{10,... | collective-permute-start | bytes 1425416 | tf_op jit(solution)/shard_map/ppermute | solution.py:244
  43.1 11.8 %copy-start.1 = (bf16[7392,2560]{1,0:T(8,128)(2,1)S(1)}, bf16[7392,2560]{1,0:T(8,128)(2,1)}, u32[]{:S(2)}) copy-start(bf16[7392,2560]{1,0:T(8,128)(2,1)} %copy-done) | copy-start | bytes 113541120
  62.5 26.2 %collective-permute-start.6 = (bf16[32,2176]{1,0:T(8,128)(2,1)S(1)}, bf16[32,2176]{1,0:T(8,128)(2,1)S(1)}, u32[]{:S(2)}, u32[]{:S(2)}) collective-permute-start(bf16[32,2176]{1,0:T(8,128)(2,1)S(1)} %get-tuple-element.39), channel_id=1, source_target_pairs={{0,4},{4,0},{8,12},{12,8},{1,5},{5,1},{9,13},{13,9},{2,6},{6,2},{1... | collective-permute-start | bytes 417800 | tf_op jit(solution)/shard_map/ppermute | solution.py:270
  62.7 5.0 %collective-permute-start.7 = (bf16[32,7424]{1,0:T(8,128)(2,1)S(1)}, bf16[32,7424]{1,0:T(8,128)(2,1)S(1)}, u32[]{:S(2)}, u32[]{:S(2)}) collective-permute-start(bf16[32,7424]{1,0:T(8,128)(2,1)S(1)} %collective-permute-done.5.own_ref), channel_id=1, source_target_pairs={{0,1},{1,0},{2,3},{3,2},{4,5},{5,4},{6,7},{7,6},{8,9},{9,8},{10,11... | collective-permute-start | bytes 1425416 | tf_op jit(solution)/shard_map/ppermute | solution.py:280
  62.8 75.8 %collective-permute-start.3 = (bf16[128,2176]{1,0:T(8,128)(2,1)S(1)}, bf16[128,2176]{1,0:T(8,128)(2,1)S(1)}, u32[]{:S(2)}, u32[]{:S(2)}) collective-permute-start(bf16[128,2176]{1,0:T(8,128)(2,1)S(1)} %add_convert_fusion.refs_0_), channel_id=1, source_target_pairs={{2,10},{3,11},{6,14},{7,15},{8,0},{9,1},{12,4},{13,5},{18,26},{19,... | collective-permute-start | bytes 1671176 | tf_op jit(solution)/shard_map/ppermute | solution.py:272
  67.7 11.8 %copy-start.2 = (bf16[7392,2560]{1,0:T(8,128)(2,1)S(1)}, bf16[7392,2560]{1,0:T(8,128)(2,1)}, u32[]{:S(2)}) copy-start(bf16[7392,2560]{1,0:T(8,128)(2,1)} %copy-done) | copy-start | bytes 113541120
  87.0 23.3 %collective-permute-start.9 = (bf16[32,2176]{1,0:T(8,128)(2,1)S(1)}, bf16[32,2176]{1,0:T(8,128)(2,1)S(1)}, u32[]{:S(2)}, u32[]{:S(2)}) collective-permute-start(bf16[32,2176]{1,0:T(8,128)(2,1)S(1)} %get-tuple-element.44), channel_id=1, source_target_pairs={{0,4},{4,0},{8,12},{12,8},{1,5},{5,1},{9,13},{13,9},{2,6},{6,2},{1... | collective-permute-start | bytes 417800 | tf_op jit(solution)/shard_map/ppermute | solution.py:270
  88.7 1.8 %collective-permute-start.10 = (bf16[32,7424]{1,0:T(8,128)(2,1)S(1)}, bf16[32,7424]{1,0:T(8,128)(2,1)S(1)}, u32[]{:S(2)}, u32[]{:S(2)}) collective-permute-start(bf16[32,7424]{1,0:T(8,128)(2,1)S(1)} %collective-permute-done.8.own_ref), channel_id=1, source_target_pairs={{0,1},{1,0},{2,3},{3,2},{4,5},{5,4},{6,7},{7,6},{8,9},{9,8},{10,11... | collective-permute-start | bytes 1425416 | tf_op jit(solution)/shard_map/ppermute | solution.py:280
  88.7 50.0 %collective-permute-start.15 = (bf16[32,2176]{1,0:T(8,128)(2,1)S(1)}, bf16[32,2176]{1,0:T(8,128)(2,1)S(1)}, u32[]{:S(2)}, u32[]{:S(2)}) collective-permute-start(bf16[32,2176]{1,0:T(8,128)(2,1)S(1)} %add_convert_fusion.4.refs_2_), channel_id=1, source_target_pairs={{0,8},{1,9},{4,12},{5,13},{10,2},{11,3},{14,6},{15,7},{16,24},{17,... | collective-permute-start | bytes 417800 | tf_op jit(solution)/shard_map/ppermute | solution.py:272
  109.9 23.3 %collective-permute-start.12 = (bf16[32,2176]{1,0:T(8,128)(2,1)S(1)}, bf16[32,2176]{1,0:T(8,128)(2,1)S(1)}, u32[]{:S(2)}, u32[]{:S(2)}) collective-permute-start(bf16[32,2176]{1,0:T(8,128)(2,1)S(1)} %get-tuple-element.49), channel_id=1, source_target_pairs={{0,4},{4,0},{8,12},{12,8},{1,5},{5,1},{9,13},{13,9},{2,6},{6,2},{1... | collective-permute-start | bytes 417800 | tf_op jit(solution)/shard_map/ppermute | solution.py:270
  110.4 1.8 %collective-permute-start.13 = (bf16[32,7424]{1,0:T(8,128)(2,1)S(1)}, bf16[32,7424]{1,0:T(8,128)(2,1)S(1)}, u32[]{:S(2)}, u32[]{:S(2)}) collective-permute-start(bf16[32,7424]{1,0:T(8,128)(2,1)S(1)} %collective-permute-done.11.own_ref), channel_id=1, source_target_pairs={{0,1},{1,0},{2,3},{3,2},{4,5},{5,4},{6,7},{7,6},{8,9},{9,8},{10,11... | collective-permute-start | bytes 1425416 | tf_op jit(solution)/shard_map/ppermute | solution.py:280
  110.4 28.3 %collective-permute-start.16 = (bf16[32,2176]{1,0:T(8,128)(2,1)S(1)}, bf16[32,2176]{1,0:T(8,128)(2,1)S(1)}, u32[]{:S(2)}, u32[]{:S(2)}) collective-permute-start(bf16[32,2176]{1,0:T(8,128)(2,1)S(1)} %add_convert_fusion.3.refs_3_), channel_id=1, source_target_pairs={{0,8},{1,9},{4,12},{5,13},{10,2},{11,3},{14,6},{15,7},{16,24},{17,... | collective-permute-start | bytes 417800 | tf_op jit(solution)/shard_map/ppermute | solution.py:272
  112.2 11.8 %copy-start.4 = (bf16[7392,2560]{1,0:T(8,128)(2,1)S(1)}, bf16[7392,2560]{1,0:T(8,128)(2,1)}, u32[]{:S(2)}) copy-start(bf16[7392,2560]{1,0:T(8,128)(2,1)} %copy-done) | copy-start | bytes 113541120
  124.0 26.4 %copy-start.5 = (bf16[8,64,2048]{2,1,0:T(8,128)(2,1)S(1)}, bf16[8,64,2048]{2,1,0:T(8,128)(2,1)}, u32[]{:S(2)}) copy-start(bf16[8,64,2048]{2,1,0:T(8,128)(2,1)} %param.8) | copy-start | bytes 6291460
  131.6 5.8 %collective-permute-start.14 = (bf16[32,2176]{1,0:T(8,128)(2,1)S(1)}, bf16[32,2176]{1,0:T(8,128)(2,1)S(1)}, u32[]{:S(2)}, u32[]{:S(2)}) collective-permute-start(bf16[32,2176]{1,0:T(8,128)(2,1)S(1)} %get-tuple-element.52), channel_id=1, source_target_pairs={{0,4},{4,0},{8,12},{12,8},{1,5},{5,1},{9,13},{13,9},{2,6},{6,2},{1... | collective-permute-start | bytes 417800 | tf_op jit(solution)/shard_map/ppermute | solution.py:270
  133.2 15.1 %collective-permute-start.17 = (bf16[32,2176]{1,0:T(8,128)(2,1)S(1)}, bf16[32,2176]{1,0:T(8,128)(2,1)S(1)}, u32[]{:S(2)}, u32[]{:S(2)}) collective-permute-start(bf16[32,2176]{1,0:T(8,128)(2,1)S(1)} %add_convert_fusion.2.refs_4_), channel_id=1, source_target_pairs={{0,8},{1,9},{4,12},{5,13},{10,2},{11,3},{14,6},{15,7},{16,24},{17,... | collective-permute-start | bytes 417800 | tf_op jit(solution)/shard_map/ppermute | solution.py:272
  137.4 13.0 %collective-permute-start.18 = (bf16[32,2176]{1,0:T(8,128)(2,1)S(1)}, bf16[32,2176]{1,0:T(8,128)(2,1)S(1)}, u32[]{:S(2)}, u32[]{:S(2)}) collective-permute-start(bf16[32,2176]{1,0:T(8,128)(2,1)S(1)} %add_convert_fusion.1.refs_5_), channel_id=1, source_target_pairs={{0,8},{1,9},{4,12},{5,13},{10,2},{11,3},{14,6},{15,7},{16,24},{17,... | collective-permute-start | bytes 417800 | tf_op jit(solution)/shard_map/ppermute | solution.py:272
  (3 other events, 13.9 us)

commit v2 on v0

v2 whole, which is shorter than its diff:
```python
import functools

import jax
import jax.numpy as jnp
from jax import lax
from jax.experimental import pallas as pl
from jax.experimental.pallas import tpu as pltpu
from jax.sharding import PartitionSpec as P

LANES = 128
PANEL = 512
DEPTH = 1024
MIB = 1 << 20


def in_vmem():
    return pl.BlockSpec(memory_space=pltpu.VMEM)


def in_hbm():
    return pl.BlockSpec(memory_space=pltpu.HBM)


def left(array):
    return pltpu.with_memory_space_constraint(array, pltpu.HBM)


def turn_kernel(starts, hidden_ref, ids_ref, *chunk_refs):
    units, rows = hidden_ref.shape
    full = units // LANES
    for block in range(full + 1):
        if block < full:
            tile = hidden_ref[block * LANES : (block + 1) * LANES, :]
        else:
            ids = jnp.broadcast_to(
                ids_ref[...].astype(jnp.float32).astype(jnp.bfloat16),
                ((full + 1) * LANES - units, rows),
            )
            tile = jnp.concatenate([hidden_ref[full * LANES :, :], ids], axis=0)
        turned = tile.T
        at = slice(block * LANES, (block + 1) * LANES)
        for first, chunk_ref in zip(starts, chunk_refs):
            chunk_ref[:, at] = turned[first : first + chunk_ref.shape[0]]


def keeps_first():
    return lax.rem(lax.axis_index("req"), 2) == lax.rem(lax.axis_index("tensor"), 2)


def part_rows(value, keep_first, cols, send_ref, keep_ref):
    rows = send_ref.shape[0]
    value = value.astype(send_ref.dtype)
    first, second = value[:rows], value[rows:]
    send_ref[:, cols] = jnp.where(keep_first, second, first)
    keep_ref[:, cols] = jnp.where(keep_first, first, second)


def base_panel(panel, refs, panel_ref, send_ref, keep_ref):
    cols = slice(panel * PANEL, (panel + 1) * PANEL)
    rows = jnp.concatenate([ref[...] for ref in refs], axis=0)
    value = jnp.dot(rows, panel_ref[...], preferred_element_type=jnp.float32)
    part_rows(value, keeps_first(), cols, send_ref, keep_ref)


def shrink_panel(adapters, units, refs, panel_ref, send_ref, keep_ref):
    width = send_ref.shape[1] - LANES
    wide = panel_ref.shape[1]
    rank = wide // adapters
    rows = jnp.concatenate([ref[...] for ref in refs], axis=0)
    every = jnp.dot(rows, panel_ref[...], preferred_element_type=jnp.float32)
    ids = jnp.concatenate([ref[:, units : units + 1] for ref in refs], axis=0)
    ids = ids.astype(jnp.float32)
    column = lax.broadcasted_iota(jnp.int32, every.shape, 1) // rank
    picked = jnp.where(column.astype(jnp.float32) == ids, every, 0.0)
    tile = picked[:, :LANES]
    for at in range(LANES, wide, LANES):
        tile = tile + picked[:, at : at + LANES]
    tile = tile + pltpu.roll(tile, rank, 1)
    lane = lax.broadcasted_iota(jnp.int32, tile.shape, 1)
    tile = jnp.where(lane < rank, tile, ids)
    part_rows(tile, keeps_first(), slice(width, width + LANES), send_ref, keep_ref)


def first_kernel(adapters, own_ref, other_ref, w_hbm, s_hbm, send_ref, keep_ref, *refs):
    *panel_refs, spread_ref, s_ref, w_sems, s_sem = refs
    units = w_hbm.shape[0]
    rows = (own_ref, other_ref)
    copies = [
        pltpu.make_async_copy(
            w_hbm.at[:, pl.ds(panel * PANEL, PANEL)],
            panel_ref.at[pl.ds(0, units), :],
            w_sems.at[panel],
        )
        for panel, panel_ref in enumerate(panel_refs)
    ]
    s_copy = pltpu.make_async_copy(s_hbm, s_ref, s_sem)
    s_copy.start()
    for copy in copies:
        copy.start()
    for ref in (spread_ref, *panel_refs):
        ref[units:, :] = jnp.zeros_like(ref[units:, :])
    s_copy.wait()
    for at in range(0, units, DEPTH):
        to = min(at + DEPTH, units)
        spread_ref[at:to, :] = s_ref[:, at:to].T
    shrink_panel(adapters, units, rows, spread_ref, send_ref, keep_ref)
    for panel, panel_ref in enumerate(panel_refs):
        copies[panel].wait()
        base_panel(panel, rows, panel_ref, send_ref, keep_ref)


def later_kernel(adapters, units, own_ref, other_ref, *refs):
    *panel_refs, spread_ref, send_ref, keep_ref = refs
    rows = (own_ref, other_ref)
    shrink_panel(adapters, units, rows, spread_ref, send_ref, keep_ref)
    for panel, panel_ref in enumerate(panel_refs):
        base_panel(panel, rows, panel_ref, send_ref, keep_ref)


def add_kernel(first_ref, second_ref, out_ref):
    total = first_ref[...].astype(jnp.float32) + second_ref[...].astype(jnp.float32)
    out_ref[...] = total.astype(out_ref.dtype)


def last_kernel(n_tensor, adapters, near, far, expand_ref, *refs):
    out_ref = refs[-1]
    near_sums, near_gots = refs[:near], refs[near : 2 * near]
    far_sums, far_gots = refs[2 * near : 2 * near + far], refs[2 * near + far : -1]
    wide, width = expand_ref.shape
    rank = wide // adapters
    is_near = lax.axis_index("tensor") // 2 == lax.axis_index("req") // 2

    def total(sums, gots, cols):
        parts = [
            kept[:, cols].astype(jnp.float32) + got[:, cols].astype(jnp.float32)
            for kept, got in zip(sums, gots)
        ]
        return jnp.concatenate(parts, axis=0)

    def whole(cols):
        return jnp.where(
            is_near, total(near_sums, near_gots, cols), total(far_sums, far_gots, cols)
        )

    small = whole(slice(width, width + LANES))
    ids = small[:, rank : rank + 1] * (1.0 / n_tensor)
    lane = lax.broadcasted_iota(jnp.int32, small.shape, 1)
    shrink = jnp.where(lane < rank, small, 0.0)
    shrink = shrink + pltpu.roll(shrink, rank, 1)
    spread = jnp.concatenate([shrink] * (wide // LANES), axis=1)
    column = lax.broadcasted_iota(jnp.int32, spread.shape, 1) // rank
    placed = jnp.where(column.astype(jnp.float32) == ids, spread, 0.0).astype(jnp.bfloat16)
    for at in range(0, width, PANEL):
        cols = slice(at, at + PANEL)
        adapter = jnp.dot(placed, expand_ref[:, cols], preferred_element_type=jnp.float32)
        out_ref[:, cols] = (whole(cols) + adapter).astype(out_ref.dtype)


def paired(n_tensor, n_req, hidden, weight, shrink, expand, ids):
    rows, units = hidden.shape
    width = weight.shape[1]
    adapters, rank = shrink.shape[1:]
    wide = adapters * rank
    room = (units // LANES + 1) * LANES
    payload = width + LANES
    bf16 = jnp.bfloat16
    half, quarter = rows // 2, rows // 4
    quick = pl.CostEstimate(flops=1, bytes_accessed=1, transcendentals=0)

    def params(mib):
        return pltpu.CompilerParams(vmem_limit_bytes=mib * MIB)

    starts, counts = (0, half, half, half + quarter), (half, half, quarter, quarter)
    own_a, own_b, own_c, own_d = pl.pallas_call(
        functools.partial(turn_kernel, starts),
        out_shape=[jax.ShapeDtypeStruct((count, room), bf16) for count in counts],
        in_specs=[in_vmem(), in_vmem()],
        out_specs=[in_vmem()] * 4,
        compiler_params=params(2),
        name="turn",
    )(hidden.T, ids.reshape(1, rows))

    across = [(i, i ^ 2) for i in range(n_req)]
    beside = [(i, i ^ 1) for i in range(n_req)]
    next_z = [(i, i ^ 1) for i in range(n_tensor)]
    to_near, to_far = [], []
    for t in range(n_tensor):
        for r in range(n_req):
            hop = (t * n_req + r, (t ^ 2) * n_req + r)
            (to_far if t // 2 == r // 2 else to_near).append(hop)

    def over_x(part):
        return lax.ppermute(part, "req", across)

    def over_core(part):
        return lax.ppermute(part, "req", beside)

    def first_hop(send, keep):
        got = lax.ppermute(send, "tensor", next_z)
        return pl.pallas_call(
            add_kernel,
            out_shape=jax.ShapeDtypeStruct(keep.shape, bf16),
            in_specs=[in_vmem()] * 2,
            out_specs=in_vmem(),
            compiler_params=params(10),
            cost_estimate=quick,
            name="add",
        )(keep, got)

    def second_hop(total, hops):
        return lax.ppermute(total, ("tensor", "req"), hops)

    def product(own, other, both):
        count = own.shape[0]
        return pl.pallas_call(
            functools.partial(later_kernel, adapters, units),
            out_shape=[jax.ShapeDtypeStruct((count, payload), bf16)] * 2,
            in_specs=[in_vmem()] * (2 + len(both)),
            out_specs=[in_vmem()] * 2,
            compiler_params=params(10),
            cost_estimate=quick,
            name="later",
        )(own, other, *both)

    other_a = over_core(own_a)
    direct_a = over_x(own_a)
    other_b = over_core(own_b)

    shrink_rows = shrink.transpose(1, 2, 0).reshape(wide, units)
    send_a, keep_a, *both = pl.pallas_call(
        functools.partial(first_kernel, adapters),
        out_shape=[
            jax.ShapeDtypeStruct((half, payload), bf16),
            jax.ShapeDtypeStruct((half, payload), bf16),
            *[pltpu.VMEM((room, PANEL), bf16)] * (width // PANEL),
            pltpu.VMEM((room, wide), bf16),
        ],
        in_specs=[in_vmem(), in_vmem(), in_hbm(), in_hbm()],
        out_specs=[in_vmem()] * (3 + width // PANEL),
        scratch_shapes=[
            pltpu.VMEM((wide, units), bf16),
            pltpu.SemaphoreType.DMA((width // PANEL,)),
            pltpu.SemaphoreType.DMA,
        ],
        compiler_params=params(10),
        cost_estimate=quick,
        name="first",
    )(own_a, other_a, left(weight), left(shrink_rows))
    send_b, keep_b = product(own_b, other_b, both)

    direct_a, own_c, send_b = lax.optimization_barrier((direct_a, own_c, send_b))
    direct_c = over_x(own_c)
    sent_a, kept_a = product(direct_a, over_core(direct_a), both)

    near = [first_hop(send_a, keep_a), first_hop(send_b, keep_b)]
    direct_c, own_d, near, sent_a = lax.optimization_barrier((direct_c, own_d, near, sent_a))
    direct_d = over_x(own_d)
    passed_c = over_core(direct_c)
    far = [first_hop(sent_a, kept_a)]
    direct_c, far[0] = lax.optimization_barrier((direct_c, far[0]))
    sent_c, kept_c = product(direct_c, passed_c, both)

    direct_d, sent_c = lax.optimization_barrier((direct_d, sent_c))
    passed_d = over_core(direct_d)
    far.append(first_hop(sent_c, kept_c))
    direct_d, far[1] = lax.optimization_barrier((direct_d, far[1]))
    sent_d, kept_d = product(direct_d, passed_d, both)
    far.append(first_hop(sent_d, kept_d))

    near = [(total, second_hop(total, to_near)) for total in near]
    far = [(total, second_hop(total, to_far)) for total in far]
    pieces = [total for total, _ in near] + [got for _, got in near]
    pieces += [total for total, _ in far] + [got for _, got in far]
    return pl.pallas_call(
        functools.partial(last_kernel, n_tensor, adapters, len(near), len(far)),
        out_shape=jax.ShapeDtypeStruct((rows, width), bf16),
        in_specs=[in_vmem()] * (1 + len(pieces)),
        out_specs=in_vmem(),
        compiler_params=params(8),
        name="last",
    )(expand.reshape(wide, width), *pieces)


def gathered(hidden, weight, shrink, expand, ids):
    rows, units = hidden.shape
    adapters, rank = shrink.shape[1:]
    width = weight.shape[1]
    columns = jnp.arange(adapters, dtype=jnp.int32)[None, :]
    onehot = (ids[:, None] == columns).astype(jnp.float32)
    every = jnp.dot(
        hidden, shrink.reshape(units, adapters * rank), preferred_element_type=jnp.float32
    )
    part = jnp.sum(every.reshape(rows, adapters, rank) * onehot[:, :, None], axis=1)
    all_ids = lax.all_gather(ids, "req", axis=0, tiled=True)
    base = jnp.dot(
        lax.all_gather(hidden, "req", axis=0, tiled=True),
        weight,
        preferred_element_type=jnp.float32,
    )
    base = lax.psum_scatter(
        base.astype(jnp.bfloat16), "tensor", scatter_dimension=0, tiled=True
    ).astype(jnp.float32)
    shrunk = lax.all_gather(
        lax.psum(part.astype(jnp.bfloat16), "tensor"), "req", axis=0, tiled=True
    )
    mine = base.shape[0]
    first = lax.axis_index("tensor") * mine
    shrunk = lax.dynamic_slice_in_dim(shrunk, first, mine, 0)
    mask = lax.dynamic_slice_in_dim(all_ids, first, mine, 0)[:, None] == columns
    placed = (shrunk[:, None, :] * mask.astype(jnp.bfloat16)[:, :, None]).reshape(
        mine, adapters * rank
    )
    adapter = jnp.dot(
        placed, expand.reshape(adapters * rank, width), preferred_element_type=jnp.float32
    )
    return (base + adapter).astype(jnp.bfloat16)


def solution(mesh):
    n_tensor, n_req = mesh.shape["tensor"], mesh.shape["req"]
    if n_tensor == 4 and n_req == 4:
        on_device = functools.partial(paired, n_tensor, n_req)
    else:
        on_device = gathered
    placed = (
        P(("rep", "req"), "tensor"),
        P("tensor", "req"),
        P("tensor", None, None),
        P(None, None, "req"),
        P(("rep", "req")),
    )
    return jax.shard_map(
        on_device,
        mesh=mesh,
        in_specs=placed,
        out_specs=P(("rep", "tensor"), "req"),
        check_vma=False,
    )
```

time: 143 us -> 109 us (0.76)
  the two profiles are of different devices: /device:TPU:0 before, /device:TPU:2 now
where the time goes in v2:
time: 109 us
  waiting for transfers between devices  49.7 us (46%)
  Pallas kernels  38.9 us (36%)
  starting transfers between devices  18.2 us (17%)
  local copies, waits for them, and re-layouts  2.18 us (2%)
    ppermute x5, waiting for transfers between devices, first_hop(): got = lax.ppermute(send, 'tensor', next_z)  24 us
    pallas_call x4, Pallas kernels, product(): pl.pallas_call(functools.partial(later_kernel, adapters, units), out_shap...  23.6 us
    ppermute x5, waiting for transfers between devices, second_hop(): return lax.ppermute(total, ('tensor', 'req'), hops)  20.8 us
    pallas_call x1, Pallas kernels, paired(): pl.pallas_call(functools.partial(first_kernel, adapters), out_shape=[jax....  13 us
    ppermute x5, starting transfers between devices, second_hop(): return lax.ppermute(total, ('tensor', 'req'), hops)  9.67 us
    ppermute x5, starting transfers between devices, first_hop(): got = lax.ppermute(send, 'tensor', next_z)  5.76 us
    ppermute x3, waiting for transfers between devices, over_x(): return lax.ppermute(part, 'req', across)  2.91 us
    unnamed x6, local copies, waits for them, and re-layouts  2.18 us
  transfers between devices with their start and end apart: 18, of which 9 were waited for; matrix products, arithmetic and copies ran while one was open for 0% of the time, Pallas kernels for 34%

profile of v2, /device:TPU:2, one launch (start us, length us, event | category | flops | bytes accessed | tf_op | source)
XLA Modules:
  0.0 109.2 jit_solution(7337883215359492978)
XLA Ops:
  0.0 1.5 %copy-done.1 = bf16[128,7392]{0,1:T(8,128)(2,1)S(1)} copy-done((bf16[128,7392]{0,1:T(8,128)(2,1)S(1)}, bf16[128,7392]{0,1:T(8,128)(2,1)}, u32[]{:S(2)}) %copy-start.1) | copy-done | bytes 1892376
  3.3 2.0 %collective-permute-done.2.other_ref = bf16[64,7424]{1,0:T(8,128)(2,1)S(1)} collective-permute-done((bf16[64,7424]{1,0:T(8,128)(2,1)S(1)}, bf16[64,7424]{1,0:T(8,128)(2,1)S(1)}, u32[]{:S(2)}, u32[]{:S(2)}) %collective-permute-start.2) | collective-permute-done | bytes 950304 | tf_op jit(solution)/shard_map/ppermute | solution.py:196
  5.3 13.0 %first.1 = (bf16[64,2176]{1,0:T(8,128)(2,1)S(1)}, bf16[64,2176]{1,0:T(8,128)(2,1)S(1)}, bf16[7424,512]{1,0:T(8,128)(2,1)S(1)}, bf16[7424,512]{1,0:T(8,128)(2,1)S...) custom-call(bf16[64,7424]{1,0:T(8,128)(2,1)S(1)} %get-tuple-element.38.own_ref, ...), custom_call_target="tpu_custom_call" | custom-call | flops 1 | bytes 1 | tf_op jit(solution)/shard_map/first/pallas_call | solution.py:230
  18.3 5.1 %later.4 = (bf16[64,2176]{1,0:T(8,128)(2,1)S(1)}, bf16[64,2176]{1,0:T(8,128)(2,1)S(1)}) custom-call(bf16[64,7424]{1,0:T(8,128)(2,1)S(1)} %get-tuple-element.40.own_ref, bf16[64,7424]{1,0:T(8,128)(2,1)S(1)} %collective-permute-done.1.other_ref, bf16[7424,512]{1,0:T(8,128)(2,1)S(1)} %get-tuple-element.41.refs_0_, ...), custom_call_target="tpu_custom_call" | custom-call | flops 1 | bytes 1 | tf_op jit(solution)/shard_map/later/pallas_call | solution.py:215
  23.4 2.9 %collective-permute-done.own_ref = bf16[64,7424]{1,0:T(8,128)(2,1)S(1)} collective-permute-done((bf16[64,7424]{1,0:T(8,128)(2,1)S(1)}, bf16[64,7424]{1,0:T(8,128)(2,1)S(1)}, u32[]{:S(2)}, u32[]{:S(2)}) %collective-permute-start) | collective-permute-done | bytes 950304 | tf_op jit(solution)/shard_map/ppermute | solution.py:193
  26.6 1.8 %collective-permute-start.5 = (bf16[64,2176]{1,0:T(8,128)(2,1)S(1)}, bf16[64,2176]{1,0:T(8,128)(2,1)S(1)}, u32[]{:S(2)}, u32[]{:S(2)}) collective-permute-start(bf16[64,2176]{1,0:T(8,128)(2,1)S(1)} %get-tuple-element.52), channel_id=1, source_target_pairs={{0,4},{4,0},{8,12},{12,8},{1,5},{5,1},{9,13},{13,9},{2,6},{6,2},{1... | collective-permute-start | bytes 835592 | tf_op jit(solution)/shard_map/ppermute | solution.py:199
  28.7 7.5 %collective-permute-done.5.second_ref = bf16[64,2176]{1,0:T(8,128)(2,1)S(1)} collective-permute-done((bf16[64,2176]{1,0:T(8,128)(2,1)S(1)}, bf16[64,2176]{1,0:T(8,128)(2,1)S(1)}, u32[]{:S(2)}, u32[]{:S(2)}) %collective-permute-start.5) | collective-permute-done | bytes 278560 | tf_op jit(solution)/shard_map/ppermute | solution.py:199
  36.2 5.3 %collective-permute-done.4.second_ref = bf16[64,2176]{1,0:T(8,128)(2,1)S(1)} collective-permute-done((bf16[64,2176]{1,0:T(8,128)(2,1)S(1)}, bf16[64,2176]{1,0:T(8,128)(2,1)S(1)}, u32[]{:S(2)}, u32[]{:S(2)}) %collective-permute-start.4) | collective-permute-done | bytes 278560 | tf_op jit(solution)/shard_map/ppermute | solution.py:199
  41.5 5.3 %later.5 = (bf16[64,2176]{1,0:T(8,128)(2,1)S(1)}, bf16[64,2176]{1,0:T(8,128)(2,1)S(1)}) custom-call(bf16[64,7424]{1,0:T(8,128)(2,1)S(1)} %collective-permute-done.own_ref, bf16[64,7424]{1,0:T(8,128)(2,1)S(1)} %collective-permute-done.6.other_ref, bf16[7424,512]{1,0:T(8,128)(2,1)S(1)} %get-tuple-element.41.refs_0_, ...), custom_call_target="tpu_custom_call" | custom-call | flops 1 | bytes 1 | tf_op jit(solution)/shard_map/later/pallas_call | solution.py:215
  46.9 1.7 %collective-permute-start.10 = (bf16[32,7424]{1,0:T(8,128)(2,1)S(1)}, bf16[32,7424]{1,0:T(8,128)(2,1)S(1)}, u32[]{:S(2)}, u32[]{:S(2)}) collective-permute-start(bf16[32,7424]{1,0:T(8,128)(2,1)S(1)} %get-tuple-element.61), channel_id=1, source_target_pairs={{0,2},{1,3},{2,0},{3,1},{4,6},{5,7},{6,4},{7,5},{8,10},{9,11},{10,... | collective-permute-start | bytes 1425416 | tf_op jit(solution)/shard_map/ppermute | solution.py:193
  48.6 1.6 %collective-permute-start.9 = (bf16[64,2176]{1,0:T(8,128)(2,1)S(1)}, bf16[64,2176]{1,0:T(8,128)(2,1)S(1)}, u32[]{:S(2)}, u32[]{:S(2)}) collective-permute-start(bf16[64,2176]{1,0:T(8,128)(2,1)S(1)} %get-tuple-element.59), channel_id=1, source_target_pairs={{0,4},{4,0},{8,12},{12,8},{1,5},{5,1},{9,13},{13,9},{2,6},{6,2},{1... | collective-permute-start | bytes 835592 | tf_op jit(solution)/shard_map/ppermute | solution.py:199
  50.2 7.2 %collective-permute-done.9.second_ref = bf16[64,2176]{1,0:T(8,128)(2,1)S(1)} collective-permute-done((bf16[64,2176]{1,0:T(8,128)(2,1)S(1)}, bf16[64,2176]{1,0:T(8,128)(2,1)S(1)}, u32[]{:S(2)}, u32[]{:S(2)}) %collective-permute-start.9) | collective-permute-done | bytes 278560 | tf_op jit(solution)/shard_map/ppermute | solution.py:199
  57.5 6.6 %later.6 = (bf16[32,2176]{1,0:T(8,128)(2,1)S(1)}, bf16[32,2176]{1,0:T(8,128)(2,1)S(1)}) custom-call(bf16[32,7424]{1,0:T(8,128)(2,1)S(1)} %collective-permute-done.3.own_ref, bf16[32,7424]{1,0:T(8,128)(2,1)S(1)} %collective-permute-done.11.other_ref, bf16[7424,512]{1,0:T(8,128)(2,1)S(1)} %get-tuple-element.41.refs_0_, ...), custom_call_target="tpu_custom_call" | custom-call | flops 1 | bytes 1 | tf_op jit(solution)/shard_map/later/pallas_call | solution.py:215
  64.2 1.6 %collective-permute-start.12 = (bf16[32,2176]{1,0:T(8,128)(2,1)S(1)}, bf16[32,2176]{1,0:T(8,128)(2,1)S(1)}, u32[]{:S(2)}, u32[]{:S(2)}) collective-permute-start(bf16[32,2176]{1,0:T(8,128)(2,1)S(1)} %get-tuple-element.66), channel_id=1, source_target_pairs={{0,4},{4,0},{8,12},{12,8},{1,5},{5,1},{9,13},{13,9},{2,6},{6,2},{1... | collective-permute-start | bytes 417800 | tf_op jit(solution)/shard_map/ppermute | solution.py:199
  65.8 4.5 %collective-permute-start.7 = (bf16[64,2176]{1,0:T(8,128)(2,1)S(1)}, bf16[64,2176]{1,0:T(8,128)(2,1)S(1)}, u32[]{:S(2)}, u32[]{:S(2)}) collective-permute-start(bf16[64,2176]{1,0:T(8,128)(2,1)S(1)} %add.5.refs_0_), channel_id=1, source_target_pairs={{2,10},{3,11},{6,14},{7,15},{8,0},{9,1},{12,4},{13,5},{18,26},{19,... | collective-permute-start | bytes 835592 | tf_op jit(solution)/shard_map/ppermute | solution.py:211
  70.3 1.3 %collective-permute-start.8 = (bf16[64,2176]{1,0:T(8,128)(2,1)S(1)}, bf16[64,2176]{1,0:T(8,128)(2,1)S(1)}, u32[]{:S(2)}, u32[]{:S(2)}) collective-permute-start(bf16[64,2176]{1,0:T(8,128)(2,1)S(1)} %add.6.refs_1_), channel_id=1, source_target_pairs={{2,10},{3,11},{6,14},{7,15},{8,0},{9,1},{12,4},{13,5},{18,26},{19,... | collective-permute-start | bytes 835592 | tf_op jit(solution)/shard_map/ppermute | solution.py:211
  71.7 6.6 %later.7 = (bf16[32,2176]{1,0:T(8,128)(2,1)S(1)}, bf16[32,2176]{1,0:T(8,128)(2,1)S(1)}) custom-call(bf16[32,7424]{1,0:T(8,128)(2,1)S(1)} %collective-permute-done.10.own_ref, bf16[32,7424]{1,0:T(8,128)(2,1)S(1)} %collective-permute-done.13.other_ref, bf16[7424,512]{1,0:T(8,128)(2,1)S(1)} %get-tuple-element.41.refs_0_, ...), custom_call_target="tpu_custom_call" | custom-call | flops 1 | bytes 1 | tf_op jit(solution)/shard_map/later/pallas_call | solution.py:215
  80.2 1.3 %collective-permute-start.16 = (bf16[32,2176]{1,0:T(8,128)(2,1)S(1)}, bf16[32,2176]{1,0:T(8,128)(2,1)S(1)}, u32[]{:S(2)}, u32[]{:S(2)}) collective-permute-start(bf16[32,2176]{1,0:T(8,128)(2,1)S(1)} %add.8.refs_5_), channel_id=1, source_target_pairs={{0,8},{1,9},{4,12},{5,13},{10,2},{11,3},{14,6},{15,7},{16,24},{17,... | collective-permute-start | bytes 417800 | tf_op jit(solution)/shard_map/ppermute | solution.py:211
  81.5 4.1 %collective-permute-done.14.second_ref = bf16[32,2176]{1,0:T(8,128)(2,1)S(1)} collective-permute-done((bf16[32,2176]{1,0:T(8,128)(2,1)S(1)}, bf16[32,2176]{1,0:T(8,128)(2,1)S(1)}, u32[]{:S(2)}, u32[]{:S(2)}) %collective-permute-start.14) | collective-permute-done | bytes 139296 | tf_op jit(solution)/shard_map/ppermute | solution.py:199
  85.6 1.3 %collective-permute-start.17 = (bf16[32,2176]{1,0:T(8,128)(2,1)S(1)}, bf16[32,2176]{1,0:T(8,128)(2,1)S(1)}, u32[]{:S(2)}, u32[]{:S(2)}) collective-permute-start(bf16[32,2176]{1,0:T(8,128)(2,1)S(1)} %add.9.refs_6_), channel_id=1, source_target_pairs={{0,8},{1,9},{4,12},{5,13},{10,2},{11,3},{14,6},{15,7},{16,24},{17,... | collective-permute-start | bytes 417800 | tf_op jit(solution)/shard_map/ppermute | solution.py:211
  86.9 16.0 %collective-permute-done.15.refs_7_ = bf16[64,2176]{1,0:T(8,128)(2,1)S(1)} collective-permute-done((bf16[64,2176]{1,0:T(8,128)(2,1)S(1)}, bf16[64,2176]{1,0:T(8,128)(2,1)S(1)}, u32[]{:S(2)}, u32[]{:S(2)}) %collective-permute-start.15) | collective-permute-done | bytes 278560 | tf_op jit(solution)/shard_map/ppermute | solution.py:211
  102.9 3.0 %collective-permute-done.16.refs_8_ = bf16[32,2176]{1,0:T(8,128)(2,1)S(1)} collective-permute-done((bf16[32,2176]{1,0:T(8,128)(2,1)S(1)}, bf16[32,2176]{1,0:T(8,128)(2,1)S(1)}, u32[]{:S(2)}, u32[]{:S(2)}) %collective-permute-start.16) | collective-permute-done | bytes 139296 | tf_op jit(solution)/shard_map/ppermute | solution.py:211
  105.9 1.8 %collective-permute-done.17.refs_9_ = bf16[32,2176]{1,0:T(8,128)(2,1)S(1)} collective-permute-done((bf16[32,2176]{1,0:T(8,128)(2,1)S(1)}, bf16[32,2176]{1,0:T(8,128)(2,1)S(1)}, u32[]{:S(2)}, u32[]{:S(2)}) %collective-permute-start.17) | collective-permute-done | bytes 139296 | tf_op jit(solution)/shard_map/ppermute | solution.py:211
  107.7 1.4 %last.1 = bf16[128,2048]{1,0:T(8,128)(2,1)} custom-call(bf16[512,2048]{1,0:T(8,128)(2,1)S(1)} %bitcast.6, bf16[64,2176]{1,0:T(8,128)(2,1)S(1)} %add.5.refs_0_, bf16[64,2176]{1,0:T(8,128)(2,1)S(1)} %add.6.refs_1_, bf16[64,2176]{1,0:T(8,128)(2,1)S(1)} %collective-permute-done.7.refs_2_, bf16[64,2176]{1,0:T(8,128)(2,1)S(1)} %collective-permute-done.8.refs_3_, ...), custom_call_target="tpu_custom_call" | custom-call | tf_op jit(solution)/shard_map/last/pallas_call | solution.py:274
  (30 shorter events, 4.5 us)
Async XLA Ops:
  0.0 1.5 %copy-start.1 = (bf16[128,7392]{0,1:T(8,128)(2,1)S(1)}, bf16[128,7392]{0,1:T(8,128)(2,1)}, u32[]{:S(2)}) copy-start(bf16[128,7392]{0,1:T(8,128)(2,1)} %param.5) | copy-start | bytes 5677060
  1.5 0.7 copy-start.2
  2.7 2.6 %collective-permute-start.2 = (bf16[64,7424]{1,0:T(8,128)(2,1)S(1)}, bf16[64,7424]{1,0:T(8,128)(2,1)S(1)}, u32[]{:S(2)}, u32[]{:S(2)}) collective-permute-start(bf16[64,7424]{1,0:T(8,128)(2,1)S(1)} %get-tuple-element.38.own_ref), channel_id=1, source_target_pairs={{0,1},{1,0},{2,3},{3,2},{4,5},{5,4},{6,7},{7,6},{8,9},{9,8},{10,11... | collective-permute-start | bytes 2850824 | tf_op jit(solution)/shard_map/ppermute | solution.py:196
  2.8 15.5 %collective-permute-start.1 = (bf16[64,7424]{1,0:T(8,128)(2,1)S(1)}, bf16[64,7424]{1,0:T(8,128)(2,1)S(1)}, u32[]{:S(2)}, u32[]{:S(2)}) collective-permute-start(bf16[64,7424]{1,0:T(8,128)(2,1)S(1)} %get-tuple-element.40.own_ref), channel_id=1, source_target_pairs={{0,1},{1,0},{2,3},{3,2},{4,5},{5,4},{6,7},{7,6},{8,9},{9,8},{10,11... | collective-permute-start | bytes 2850824 | tf_op jit(solution)/shard_map/ppermute | solution.py:196
  3.3 23.0 %collective-permute-start = (bf16[64,7424]{1,0:T(8,128)(2,1)S(1)}, bf16[64,7424]{1,0:T(8,128)(2,1)S(1)}, u32[]{:S(2)}, u32[]{:S(2)}) collective-permute-start(bf16[64,7424]{1,0:T(8,128)(2,1)S(1)} %get-tuple-element.38.own_ref), channel_id=1, source_target_pairs={{0,2},{1,3},{2,0},{3,1},{4,6},{5,7},{6,4},{7,5},{8,10},{9,11},{10,... | collective-permute-start | bytes 2850824 | tf_op jit(solution)/shard_map/ppermute | solution.py:193
  26.3 15.2 %collective-permute-start.6 = (bf16[64,7424]{1,0:T(8,128)(2,1)S(1)}, bf16[64,7424]{1,0:T(8,128)(2,1)S(1)}, u32[]{:S(2)}, u32[]{:S(2)}) collective-permute-start(bf16[64,7424]{1,0:T(8,128)(2,1)S(1)} %collective-permute-done.own_ref), channel_id=1, source_target_pairs={{0,1},{1,0},{2,3},{3,2},{4,5},{5,4},{6,7},{7,6},{8,9},{9,8},{10,11... | collective-permute-start | bytes 2850824 | tf_op jit(solution)/shard_map/ppermute | solution.py:196
  26.3 20.5 %collective-permute-start.3 = (bf16[32,7424]{1,0:T(8,128)(2,1)S(1)}, bf16[32,7424]{1,0:T(8,128)(2,1)S(1)}, u32[]{:S(2)}, u32[]{:S(2)}) collective-permute-start(bf16[32,7424]{1,0:T(8,128)(2,1)S(1)} %get-tuple-element.47), channel_id=1, source_target_pairs={{0,2},{1,3},{2,0},{3,1},{4,6},{5,7},{6,4},{7,5},{8,10},{9,11},{10,... | collective-permute-start | bytes 1425416 | tf_op jit(solution)/shard_map/ppermute | solution.py:193
  26.6 9.5 %collective-permute-start.5 = (bf16[64,2176]{1,0:T(8,128)(2,1)S(1)}, bf16[64,2176]{1,0:T(8,128)(2,1)S(1)}, u32[]{:S(2)}, u32[]{:S(2)}) collective-permute-start(bf16[64,2176]{1,0:T(8,128)(2,1)S(1)} %get-tuple-element.52), channel_id=1, source_target_pairs={{0,4},{4,0},{8,12},{12,8},{1,5},{5,1},{9,13},{13,9},{2,6},{6,2},{1... | collective-permute-start | bytes 835592 | tf_op jit(solution)/shard_map/ppermute | solution.py:199
  28.5 13.0 %collective-permute-start.4 = (bf16[64,2176]{1,0:T(8,128)(2,1)S(1)}, bf16[64,2176]{1,0:T(8,128)(2,1)S(1)}, u32[]{:S(2)}, u32[]{:S(2)}) collective-permute-start(bf16[64,2176]{1,0:T(8,128)(2,1)S(1)} %get-tuple-element.50), channel_id=1, source_target_pairs={{0,4},{4,0},{8,12},{12,8},{1,5},{5,1},{9,13},{13,9},{2,6},{6,2},{1... | collective-permute-start | bytes 835592 | tf_op jit(solution)/shard_map/ppermute | solution.py:199
  46.8 10.6 %collective-permute-start.11 = (bf16[32,7424]{1,0:T(8,128)(2,1)S(1)}, bf16[32,7424]{1,0:T(8,128)(2,1)S(1)}, u32[]{:S(2)}, u32[]{:S(2)}) collective-permute-start(bf16[32,7424]{1,0:T(8,128)(2,1)S(1)} %collective-permute-done.3.own_ref), channel_id=1, source_target_pairs={{0,1},{1,0},{2,3},{3,2},{4,5},{5,4},{6,7},{7,6},{8,9},{9,8},{10,11... | collective-permute-start | bytes 1425416 | tf_op jit(solution)/shard_map/ppermute | solution.py:196
  46.9 17.2 %collective-permute-start.10 = (bf16[32,7424]{1,0:T(8,128)(2,1)S(1)}, bf16[32,7424]{1,0:T(8,128)(2,1)S(1)}, u32[]{:S(2)}, u32[]{:S(2)}) collective-permute-start(bf16[32,7424]{1,0:T(8,128)(2,1)S(1)} %get-tuple-element.61), channel_id=1, source_target_pairs={{0,2},{1,3},{2,0},{3,1},{4,6},{5,7},{6,4},{7,5},{8,10},{9,11},{10,... | collective-permute-start | bytes 1425416 | tf_op jit(solution)/shard_map/ppermute | solution.py:193
  48.6 8.7 %collective-permute-start.9 = (bf16[64,2176]{1,0:T(8,128)(2,1)S(1)}, bf16[64,2176]{1,0:T(8,128)(2,1)S(1)}, u32[]{:S(2)}, u32[]{:S(2)}) collective-permute-start(bf16[64,2176]{1,0:T(8,128)(2,1)S(1)} %get-tuple-element.59), channel_id=1, source_target_pairs={{0,4},{4,0},{8,12},{12,8},{1,5},{5,1},{9,13},{13,9},{2,6},{6,2},{1... | collective-permute-start | bytes 835592 | tf_op jit(solution)/shard_map/ppermute | solution.py:199
  64.1 7.6 %collective-permute-start.13 = (bf16[32,7424]{1,0:T(8,128)(2,1)S(1)}, bf16[32,7424]{1,0:T(8,128)(2,1)S(1)}, u32[]{:S(2)}, u32[]{:S(2)}) collective-permute-start(bf16[32,7424]{1,0:T(8,128)(2,1)S(1)} %collective-permute-done.10.own_ref), channel_id=1, source_target_pairs={{0,1},{1,0},{2,3},{3,2},{4,5},{5,4},{6,7},{7,6},{8,9},{9,8},{10,11... | collective-permute-start | bytes 1425416 | tf_op jit(solution)/shard_map/ppermute | solution.py:196
  64.2 7.5 %collective-permute-start.12 = (bf16[32,2176]{1,0:T(8,128)(2,1)S(1)}, bf16[32,2176]{1,0:T(8,128)(2,1)S(1)}, u32[]{:S(2)}, u32[]{:S(2)}) collective-permute-start(bf16[32,2176]{1,0:T(8,128)(2,1)S(1)} %get-tuple-element.66), channel_id=1, source_target_pairs={{0,4},{4,0},{8,12},{12,8},{1,5},{5,1},{9,13},{13,9},{2,6},{6,2},{1... | collective-permute-start | bytes 417800 | tf_op jit(solution)/shard_map/ppermute | solution.py:199
  65.8 21.1 %collective-permute-start.7 = (bf16[64,2176]{1,0:T(8,128)(2,1)S(1)}, bf16[64,2176]{1,0:T(8,128)(2,1)S(1)}, u32[]{:S(2)}, u32[]{:S(2)}) collective-permute-start(bf16[64,2176]{1,0:T(8,128)(2,1)S(1)} %add.5.refs_0_), channel_id=1, source_target_pairs={{2,10},{3,11},{6,14},{7,15},{8,0},{9,1},{12,4},{13,5},{18,26},{19,... | collective-permute-start | bytes 835592 | tf_op jit(solution)/shard_map/ppermute | solution.py:211
  70.3 16.6 %collective-permute-start.8 = (bf16[64,2176]{1,0:T(8,128)(2,1)S(1)}, bf16[64,2176]{1,0:T(8,128)(2,1)S(1)}, u32[]{:S(2)}, u32[]{:S(2)}) collective-permute-start(bf16[64,2176]{1,0:T(8,128)(2,1)S(1)} %add.6.refs_1_), channel_id=1, source_target_pairs={{2,10},{3,11},{6,14},{7,15},{8,0},{9,1},{12,4},{13,5},{18,26},{19,... | collective-permute-start | bytes 835592 | tf_op jit(solution)/shard_map/ppermute | solution.py:211
  71.7 36.0 %copy-start = (bf16[8,64,2048]{2,1,0:T(8,128)(2,1)S(1)}, bf16[8,64,2048]{2,1,0:T(8,128)(2,1)}, u32[]{:S(2)}) copy-start(bf16[8,64,2048]{2,1,0:T(8,128)(2,1)} %param.8) | copy-start | bytes 6291460
  78.4 7.2 %collective-permute-start.14 = (bf16[32,2176]{1,0:T(8,128)(2,1)S(1)}, bf16[32,2176]{1,0:T(8,128)(2,1)S(1)}, u32[]{:S(2)}, u32[]{:S(2)}) collective-permute-start(bf16[32,2176]{1,0:T(8,128)(2,1)S(1)} %get-tuple-element.70), channel_id=1, source_target_pairs={{0,4},{4,0},{8,12},{12,8},{1,5},{5,1},{9,13},{13,9},{2,6},{6,2},{1... | collective-permute-start | bytes 417800 | tf_op jit(solution)/shard_map/ppermute | solution.py:199
  78.9 24.0 %collective-permute-start.15 = (bf16[64,2176]{1,0:T(8,128)(2,1)S(1)}, bf16[64,2176]{1,0:T(8,128)(2,1)S(1)}, u32[]{:S(2)}, u32[]{:S(2)}) collective-permute-start(bf16[64,2176]{1,0:T(8,128)(2,1)S(1)} %add.7.refs_4_), channel_id=1, source_target_pairs={{0,8},{1,9},{4,12},{5,13},{10,2},{11,3},{14,6},{15,7},{16,24},{17,... | collective-permute-start | bytes 835592 | tf_op jit(solution)/shard_map/ppermute | solution.py:211
  80.2 25.7 %collective-permute-start.16 = (bf16[32,2176]{1,0:T(8,128)(2,1)S(1)}, bf16[32,2176]{1,0:T(8,128)(2,1)S(1)}, u32[]{:S(2)}, u32[]{:S(2)}) collective-permute-start(bf16[32,2176]{1,0:T(8,128)(2,1)S(1)} %add.8.refs_5_), channel_id=1, source_target_pairs={{0,8},{1,9},{4,12},{5,13},{10,2},{11,3},{14,6},{15,7},{16,24},{17,... | collective-permute-start | bytes 417800 | tf_op jit(solution)/shard_map/ppermute | solution.py:211
  85.6 22.2 %collective-permute-start.17 = (bf16[32,2176]{1,0:T(8,128)(2,1)S(1)}, bf16[32,2176]{1,0:T(8,128)(2,1)S(1)}, u32[]{:S(2)}, u32[]{:S(2)}) collective-permute-start(bf16[32,2176]{1,0:T(8,128)(2,1)S(1)} %add.9.refs_6_), channel_id=1, source_target_pairs={{0,8},{1,9},{4,12},{5,13},{10,2},{11,3},{14,6},{15,7},{16,24},{17,... | collective-permute-start | bytes 417800 | tf_op jit(solution)/shard_map/ppermute | solution.py:211

commit v3 on v0

v3 whole, which is shorter than its diff:
```python
import functools

import jax
import jax.numpy as jnp
from jax import lax
from jax.experimental import pallas as pl
from jax.experimental.pallas import tpu as pltpu
from jax.sharding import PartitionSpec as P

LANES = 128
PANEL = 512
DEPTH = 1024
TURN = 15
PIECES = (32, 32, 32, 32)
MIB = 1 << 20


def in_vmem():
    return pl.BlockSpec(memory_space=pltpu.VMEM)


def in_hbm():
    return pl.BlockSpec(memory_space=pltpu.HBM)


def left(array):
    return pltpu.with_memory_space_constraint(array, pltpu.HBM)


def turn_kernel(starts, hidden_hbm, ids_hbm, own_ref, *refs):
    *piece_refs, hidden_ref, ids_ref, sems = refs
    units, rows = hidden_hbm.shape
    full = units // LANES
    stops = [at * LANES for at in range(0, full, TURN)] + [units]
    copies = [
        pltpu.make_async_copy(
            hidden_hbm.at[pl.ds(at, to - at)], hidden_ref.at[pl.ds(at, to - at)], sems.at[step]
        )
        for step, (at, to) in enumerate(zip(stops, stops[1:]))
    ]
    ids_copy = pltpu.make_async_copy(ids_hbm, ids_ref, sems.at[len(copies)])
    for copy in copies:
        copy.start()
    ids_copy.start()
    for step, copy in enumerate(copies):
        copy.wait()
        last = step == len(copies) - 1
        if last:
            ids_copy.wait()
        for block in range(stops[step] // LANES, full + 1 if last else stops[step + 1] // LANES):
            if block < full:
                tile = hidden_ref[block * LANES : (block + 1) * LANES, :]
            else:
                ids = jnp.broadcast_to(
                    ids_ref[...].astype(jnp.float32).astype(jnp.bfloat16),
                    ((full + 1) * LANES - units, rows),
                )
                tile = jnp.concatenate([hidden_ref[full * LANES :, :], ids], axis=0)
            turned = tile.T
            at = slice(block * LANES, (block + 1) * LANES)
            own_ref[:, at] = turned
            for first, piece_ref in zip(starts, piece_refs):
                piece_ref[:, at] = turned[first : first + piece_ref.shape[0]]


def load_kernel(w_hbm, s_hbm, token_ref, *refs):
    *panel_refs, spread_ref, s_ref, w_sems, s_sem = refs
    units = w_hbm.shape[0]
    copies = [
        pltpu.make_async_copy(
            w_hbm.at[:, pl.ds(panel * PANEL, PANEL)],
            panel_ref.at[pl.ds(0, units), :],
            w_sems.at[panel],
        )
        for panel, panel_ref in enumerate(panel_refs)
    ]
    s_copy = pltpu.make_async_copy(s_hbm, s_ref, s_sem)
    s_copy.start()
    for copy in copies:
        copy.start()
    token_ref[...] = jnp.zeros_like(token_ref)
    for ref in (spread_ref, *panel_refs):
        ref[units:, :] = jnp.zeros_like(ref[units:, :])
    s_copy.wait()
    for at in range(0, units, DEPTH):
        to = min(at + DEPTH, units)
        spread_ref[at:to, :] = s_ref[:, at:to].T
    for copy in copies:
        copy.wait()


def part_rows(value, cols, send_ref, keep_ref):
    rows = send_ref.shape[0] // 2
    keep_first = lax.rem(lax.axis_index("req"), 2) == lax.rem(lax.axis_index("tensor"), 2)
    value = value.astype(send_ref.dtype)
    for half in range(2):
        first = value[(2 * half) * rows : (2 * half + 1) * rows]
        second = value[(2 * half + 1) * rows : (2 * half + 2) * rows]
        at = slice(half * rows, (half + 1) * rows)
        send_ref[at, cols] = jnp.where(keep_first, second, first)
        keep_ref[at, cols] = jnp.where(keep_first, first, second)


def product_kernel(
    adapters, units, at, _, own_ref, other_ref, direct_ref, passed_ref, *refs
):
    *panel_refs, spread_ref, send_ref, keep_ref = refs
    rows = direct_ref.shape[0]
    width = send_ref.shape[1] - LANES
    wide = spread_ref.shape[1]
    rank = wide // adapters

    def pieces(cols):
        near = [ref[at : at + rows, cols] for ref in (own_ref, other_ref)]
        far = [ref[:, cols] for ref in (direct_ref, passed_ref)]
        return jnp.concatenate(near + far, axis=0)

    every = jnp.dot(pieces(slice(None)), spread_ref[...], preferred_element_type=jnp.float32)
    ids = pieces(slice(units, units + 1)).astype(jnp.float32)
    column = lax.broadcasted_iota(jnp.int32, every.shape, 1) // rank
    picked = jnp.where(column.astype(jnp.float32) == ids, every, 0.0)
    tile = picked[:, :LANES]
    for lane in range(LANES, wide, LANES):
        tile = tile + picked[:, lane : lane + LANES]
    tile = tile + pltpu.roll(tile, rank, 1)
    lane = lax.broadcasted_iota(jnp.int32, tile.shape, 1)
    tile = jnp.where(lane < rank, tile, ids)
    part_rows(tile, slice(width, width + LANES), send_ref, keep_ref)

    for panel, panel_ref in enumerate(panel_refs):
        value = jnp.dot(
            pieces(slice(None)), panel_ref[...], preferred_element_type=jnp.float32
        )
        part_rows(value, slice(panel * PANEL, (panel + 1) * PANEL), send_ref, keep_ref)


def add_kernel(first_ref, second_ref, send_ref, keep_ref):
    rows = send_ref.shape[0]
    keep_near = lax.axis_index("tensor") // 2 == lax.axis_index("req") // 2

    def total(at):
        cut = slice(at, at + rows)
        value = first_ref[cut].astype(jnp.float32) + second_ref[cut].astype(jnp.float32)
        return value.astype(send_ref.dtype)

    near, far = total(0), total(rows)
    send_ref[...] = jnp.where(keep_near, far, near)
    keep_ref[...] = jnp.where(keep_near, near, far)


def last_kernel(n_tensor, adapters, expand_ref, *refs):
    out_ref = refs[-1]
    count = (len(refs) - 1) // 2
    kept, got = refs[:count], refs[count:-1]
    wide, width = expand_ref.shape
    rank = wide // adapters

    def whole(cols):
        parts = [
            first[:, cols].astype(jnp.float32) + second[:, cols].astype(jnp.float32)
            for first, second in zip(kept, got)
        ]
        return jnp.concatenate(parts, axis=0)

    small = whole(slice(width, width + LANES))
    ids = small[:, rank : rank + 1] * (1.0 / n_tensor)
    lane = lax.broadcasted_iota(jnp.int32, small.shape, 1)
    shrink = jnp.where(lane < rank, small, 0.0)
    shrink = shrink + pltpu.roll(shrink, rank, 1)
    spread = jnp.concatenate([shrink] * (wide // LANES), axis=1)
    column = lax.broadcasted_iota(jnp.int32, spread.shape, 1) // rank
    placed = jnp.where(column.astype(jnp.float32) == ids, spread, 0.0).astype(jnp.bfloat16)
    for at in range(0, width, PANEL):
        cols = slice(at, at + PANEL)
        adapter = jnp.dot(placed, expand_ref[:, cols], preferred_element_type=jnp.float32)
        out_ref[:, cols] = (whole(cols) + adapter).astype(out_ref.dtype)


def paired(n_tensor, n_req, hidden, weight, shrink, expand, ids):
    rows, units = hidden.shape
    width = weight.shape[1]
    adapters, rank = shrink.shape[1:]
    wide = adapters * rank
    room = (units // LANES + 1) * LANES
    payload = width + LANES
    bf16 = jnp.bfloat16
    counts = [rows * part // 128 for part in PIECES]
    starts = [sum(counts[:at]) for at in range(len(counts))]
    quick = pl.CostEstimate(flops=1, bytes_accessed=1, transcendentals=0)

    def params(mib):
        return pltpu.CompilerParams(vmem_limit_bytes=mib * MIB)

    def struct(count, lanes):
        return jax.ShapeDtypeStruct((count, lanes), bf16)

    own, *pieces = pl.pallas_call(
        functools.partial(turn_kernel, starts),
        out_shape=[struct(rows, room)] + [struct(count, room) for count in counts],
        in_specs=[in_hbm(), in_hbm()],
        out_specs=[in_vmem()] * (1 + len(counts)),
        scratch_shapes=[
            pltpu.VMEM((units, rows), bf16),
            pltpu.VMEM((1, rows), jnp.int32),
            pltpu.SemaphoreType.DMA((units // LANES // TURN + 2,)),
        ],
        compiler_params=params(4),
        name="turn",
    )(left(hidden.T), left(ids.reshape(1, rows)))

    across = [(i, i ^ 2) for i in range(n_req)]
    beside = [(i, i ^ 1) for i in range(n_req)]
    next_z = [(i, i ^ 1) for i in range(n_tensor)]
    far_z = [(i, i ^ 2) for i in range(n_tensor)]

    direct = [lax.ppermute(pieces[0], "req", across)]
    other = lax.ppermute(own, "req", beside)

    shrink_rows = shrink.transpose(1, 2, 0).reshape(wide, units)
    token, *both = pl.pallas_call(
        load_kernel,
        out_shape=[jax.ShapeDtypeStruct((8, LANES), jnp.float32)]
        + [pltpu.VMEM((room, PANEL), bf16)] * (width // PANEL)
        + [pltpu.VMEM((room, wide), bf16)],
        in_specs=[in_hbm(), in_hbm()],
        out_specs=[in_vmem()] * (2 + width // PANEL),
        scratch_shapes=[
            pltpu.VMEM((wide, units), bf16),
            pltpu.SemaphoreType.DMA((width // PANEL,)),
            pltpu.SemaphoreType.DMA,
        ],
        compiler_params=params(10),
        cost_estimate=quick,
        name="load",
    )(left(weight), left(shrink_rows))

    def product(step, passed, token):
        return pl.pallas_call(
            functools.partial(product_kernel, adapters, units, starts[step]),
            out_shape=[struct(2 * counts[step], payload)] * 2,
            in_specs=[in_vmem()] * (5 + len(both)),
            out_specs=[in_vmem()] * 2,
            compiler_params=params(4),
            cost_estimate=quick,
            name="product",
        )(token, own, other, direct[step], passed, *both)

    def add(step, keep, got):
        return pl.pallas_call(
            add_kernel,
            out_shape=[struct(counts[step], payload)] * 2,
            in_specs=[in_vmem()] * 2,
            out_specs=[in_vmem()] * 2,
            compiler_params=params(4),
            cost_estimate=quick,
            name="add",
        )(keep, got)

    after = lax.optimization_barrier
    steps = len(counts)
    pieces[1], direct[0], token = after((pieces[1], direct[0], token))
    parts, kept, gots = [], [], []

    def add_part(step):
        keep, got = parts[step]
        send, keep = add(step, keep, got)
        kept.append(keep)
        return send

    for step in range(steps):
        if step + 1 < steps:
            direct.append(lax.ppermute(pieces[step + 1], "req", across))
        passed = lax.ppermute(direct[step], "req", beside)
        if step > 1:
            send = add_part(step - 2)
            passed, send = after((passed, send))
            gots.append(lax.ppermute(send, "tensor", far_z))
        send, keep = product(step, passed, token)
        if step + 1 < steps:
            later = pieces[step + 2 : step + 3]
            earlier = parts[step - 1 : step] if step else []
            direct[step + 1], send, later, earlier = after(
                (direct[step + 1], send, later, earlier)
            )
            pieces[step + 2 : step + 3] = later
            if step:
                parts[step - 1] = earlier[0]
        parts.append((keep, lax.ppermute(send, "tensor", next_z)))
    for step in range(steps - 2, steps):
        gots.append(lax.ppermute(add_part(step), "tensor", far_z))

    return pl.pallas_call(
        functools.partial(last_kernel, n_tensor, adapters),
        out_shape=struct(rows, width),
        in_specs=[in_vmem()] * (1 + 2 * steps),
        out_specs=in_vmem(),
        compiler_params=params(8),
        name="last",
    )(expand.reshape(wide, width), *kept, *gots)


def gathered(hidden, weight, shrink, expand, ids):
    rows, units = hidden.shape
    adapters, rank = shrink.shape[1:]
    width = weight.shape[1]
    columns = jnp.arange(adapters, dtype=jnp.int32)[None, :]
    onehot = (ids[:, None] == columns).astype(jnp.float32)
    every = jnp.dot(
        hidden, shrink.reshape(units, adapters * rank), preferred_element_type=jnp.float32
    )
    part = jnp.sum(every.reshape(rows, adapters, rank) * onehot[:, :, None], axis=1)
    all_ids = lax.all_gather(ids, "req", axis=0, tiled=True)
    base = jnp.dot(
        lax.all_gather(hidden, "req", axis=0, tiled=True),
        weight,
        preferred_element_type=jnp.float32,
    )
    base = lax.psum_scatter(
        base.astype(jnp.bfloat16), "tensor", scatter_dimension=0, tiled=True
    ).astype(jnp.float32)
    shrunk = lax.all_gather(
        lax.psum(part.astype(jnp.bfloat16), "tensor"), "req", axis=0, tiled=True
    )
    mine = base.shape[0]
    first = lax.axis_index("tensor") * mine
    shrunk = lax.dynamic_slice_in_dim(shrunk, first, mine, 0)
    mask = lax.dynamic_slice_in_dim(all_ids, first, mine, 0)[:, None] == columns
    placed = (shrunk[:, None, :] * mask.astype(jnp.bfloat16)[:, :, None]).reshape(
        mine, adapters * rank
    )
    adapter = jnp.dot(
        placed, expand.reshape(adapters * rank, width), preferred_element_type=jnp.float32
    )
    return (base + adapter).astype(jnp.bfloat16)


def solution(mesh):
    n_tensor, n_req = mesh.shape["tensor"], mesh.shape["req"]
    if n_tensor == 4 and n_req == 4:
        on_device = functools.partial(paired, n_tensor, n_req)
    else:
        on_device = gathered
    placed = (
        P(("rep", "req"), "tensor"),
        P("tensor", "req"),
        P("tensor", None, None),
        P(None, None, "req"),
        P(("rep", "req")),
    )
    return jax.shard_map(
        on_device,
        mesh=mesh,
        in_specs=placed,
        out_specs=P(("rep", "tensor"), "req"),
        check_vma=False,
    )
```

time: 143 us -> 94 us (0.66)
  Pallas kernels: 0 us -> 35.9 us
  matrix products: 31.1 us -> 0 us
  blocking collectives: 30.3 us -> 0 us
  waiting for transfers between devices: 67.6 us -> 38.4 us
  starting transfers between devices: 0.04 us -> 19.6 us
  between operations: 13.4 us -> 0.1 us
    all_gather x1 -> x0, waiting for transfers between devices: 59 us -> none  [on_device(): lax.all_gather(hidden, 'req', axis=0, tiled=True)]
    ppermute x0 -> x17, waiting for transfers between devices: none -> 38.4 us  [the longest x3 12.8 us: paired(): direct.append(lax.ppermute(pieces[step + 1], 'req', across))]
    pallas_call x0 -> x11, Pallas kernels: none -> 35.9 us  [the longest x4 20.5 us: product(): pl.pallas_call(functools.partial(product_kernel, adapters, units, starts[...]
    dot_general x3 -> x0, matrix products: 31.1 us -> none  [the longest x1 22.6 us: on_device(): jnp.dot(lax.all_gather(hidden, 'req', axis=0, tiled=True), down_projectio...]
    psum x1 -> x0, blocking collectives: 20 us -> none  [on_device(): shrink_full = lax.psum(shrink_part.astype(jnp.bfloat16), 'tensor')]
    ppermute x0 -> x17, starting transfers between devices: none -> 19.6 us  [the longest x4 6.37 us: paired(): parts.append((keep, lax.ppermute(send, 'tensor', next_z)))]
    all_gather x2 -> x0, blocking collectives: 10.3 us -> none  [the longest x1 5.25 us: on_device(): shrink_every = lax.all_gather(shrink_full, 'req', axis=0, tiled=True)]
    reduce_scatter x1 -> x0, waiting for transfers between devices: 7.95 us -> none  [on_device(): lax.psum_scatter(partial_base.astype(jnp.bfloat16), 'tensor', scatter_dim...]
  transfers between devices with their start and end apart: 2 -> 17, of which waited for: 2 -> 11; matrix products, arithmetic and copies ran while one was open for 4% -> 0% of each run, Pallas kernels for 0% -> 35%
where the time goes in v3:
time: 94 us; the launch traced here: 93.9 us
  waiting for transfers between devices  38.4 us (41%)
  Pallas kernels  35.9 us (38%)
  starting transfers between devices  19.6 us (21%)
    pallas_call x4, Pallas kernels, product(): pl.pallas_call(functools.partial(product_kernel, adapters, units, starts[...  20.5 us
    ppermute x3, waiting for transfers between devices, paired(): direct.append(lax.ppermute(pieces[step + 1], 'req', across))  12.8 us
    pallas_call x1, Pallas kernels, paired(): pl.pallas_call(load_kernel, out_shape=[jax.ShapeDtypeStruct((8, LANES), j...  11.9 us
    ppermute x4, waiting for transfers between devices, paired(): parts.append((keep, lax.ppermute(send, 'tensor', next_z)))  11.2 us
    ppermute x2, waiting for transfers between devices, paired(): gots.append(lax.ppermute(add_part(step), 'tensor', far_z))  10.6 us
    ppermute x4, starting transfers between devices, paired(): parts.append((keep, lax.ppermute(send, 'tensor', next_z)))  6.37 us
    ppermute x2, starting transfers between devices, paired(): gots.append(lax.ppermute(send, 'tensor', far_z))  5.07 us
    ppermute x3, starting transfers between devices, paired(): direct.append(lax.ppermute(pieces[step + 1], 'req', across))  3.65 us
  transfers between devices with their start and end apart: 17, of which 11 were waited for; matrix products, arithmetic and copies ran while one was open for 0% of the time, Pallas kernels for 35%

profile of v3, /device:TPU:0, one launch (start us, length us, event | category | flops | bytes accessed | tf_op | source)
XLA Modules:
  0.0 93.9 jit_solution(11687840987001315279)
XLA Ops:
  0.0 1.8 %turn.1 = (bf16[128,7424]{1,0:T(8,128)(2,1)S(1)}, bf16[32,7424]{1,0:T(8,128)(2,1)S(1)}, bf16[32,7424]{1,0:T(8,128)(2,1)S(1)}, bf16[32,7424]{1,0:T(8,128)(2,1)S(1)}, bf16[32,7424]{1,0:T(8,128)(2,1)S(1)}) custom-call(bf16[7392,128]{1,0:T(8,128)(2,1)} %bitcast.8, s32[1,128]{1,0:T(1,128)} %bitcast.9), custom_call_target="tpu_custom_call" | custom-call | tf_op jit(solution)/shard_map/turn/pallas_call | solution.py:197
  2.3 2.6 %collective-permute-start = (bf16[32,7424]{1,0:T(8,128)(2,1)S(1)}, bf16[32,7424]{1,0:T(8,128)(2,1)S(1)}, u32[]{:S(2)}, u32[]{:S(2)}) collective-permute-start(bf16[32,7424]{1,0:T(8,128)(2,1)S(1)} %get-tuple-element.52), channel_id=1, source_target_pairs={{0,2},{1,3},{2,0},{3,1},{4,6},{5,7},{6,4},{7,5},{8,10},{9,11},{10,... | collective-permute-start | bytes 1425416 | tf_op jit(solution)/shard_map/ppermute | solution.py:216
  4.9 11.9 %load.1 = (f32[8,128]{1,0:T(8,128)S(1)}, bf16[7424,512]{1,0:T(8,128)(2,1)S(1)}, bf16[7424,512]{1,0:T(8,128)(2,1)S(1)}, bf16[7424,512]{1,0:T(8,128)(2,1)S(1)}, bf...) custom-call(bf16[7392,2048]{1,0:T(8,128)(2,1)} %w_hbm.1, bf16[512,7392]{1,0:T(8,128)(2,1)} %bitcast.7), custom_call_target="tpu_custom_call" | custom-call | flops 1 | bytes 1 | tf_op jit(solution)/shard_map/load/pallas_call | solution.py:220
  18.7 5.1 %product.4 = (bf16[64,2176]{1,0:T(8,128)(2,1)S(1)}, bf16[64,2176]{1,0:T(8,128)(2,1)S(1)}) custom-call(f32[8,128]{1,0:T(8,128)S(1)} %get-tuple-element.55._, bf16[128,7424]{1,0:T(8,128)(2,1)S(1)} %get-tuple-element.56.own_ref, bf16[128,7424]{1,0:T(8,128)(2,1)S(1)} %collective-permute-done.2.other_ref, bf16[32,7424]{1,0:T(8,128)(2,1)S(1)} %collective-permute-done.direct_ref, ...), custom_call_target="tpu_custom_call" | custom-call | flops 1 | bytes 1 | tf_op jit(solution)/shard_map/product/pallas_call | solution.py:238
  23.8 6.4 %collective-permute-done.1.direct_ref = bf16[32,7424]{1,0:T(8,128)(2,1)S(1)} collective-permute-done((bf16[32,7424]{1,0:T(8,128)(2,1)S(1)}, bf16[32,7424]{1,0:T(8,128)(2,1)S(1)}, u32[]{:S(2)}, u32[]{:S(2)}) %collective-permute-start.1) | collective-permute-done | bytes 475168 | tf_op jit(solution)/shard_map/ppermute | solution.py:272
  30.2 1.3 %collective-permute-start.4 = (bf16[32,7424]{1,0:T(8,128)(2,1)S(1)}, bf16[32,7424]{1,0:T(8,128)(2,1)S(1)}, u32[]{:S(2)}, u32[]{:S(2)}) collective-permute-start(bf16[32,7424]{1,0:T(8,128)(2,1)S(1)} %get-tuple-element.65), channel_id=1, source_target_pairs={{0,2},{1,3},{2,0},{3,1},{4,6},{5,7},{6,4},{7,5},{8,10},{9,11},{10,... | collective-permute-start | bytes 1425416 | tf_op jit(solution)/shard_map/ppermute | solution.py:272
  31.4 1.6 %collective-permute-start.6 = (bf16[64,2176]{1,0:T(8,128)(2,1)S(1)}, bf16[64,2176]{1,0:T(8,128)(2,1)S(1)}, u32[]{:S(2)}, u32[]{:S(2)}) collective-permute-start(bf16[64,2176]{1,0:T(8,128)(2,1)S(1)} %get-tuple-element.70), channel_id=1, source_target_pairs={{0,4},{4,0},{8,12},{12,8},{1,5},{5,1},{9,13},{13,9},{2,6},{6,2},{1... | collective-permute-start | bytes 835592 | tf_op jit(solution)/shard_map/ppermute | solution.py:288
  33.0 5.1 %product.5 = (bf16[64,2176]{1,0:T(8,128)(2,1)S(1)}, bf16[64,2176]{1,0:T(8,128)(2,1)S(1)}) custom-call(f32[8,128]{1,0:T(8,128)S(1)} %get-tuple-element.55._, bf16[128,7424]{1,0:T(8,128)(2,1)S(1)} %get-tuple-element.56.own_ref, bf16[128,7424]{1,0:T(8,128)(2,1)S(1)} %collective-permute-done.2.other_ref, bf16[32,7424]{1,0:T(8,128)(2,1)S(1)} %collective-permute-done.1.direct_ref, ...), custom_call_target="tpu_custom_call" | custom-call | flops 1 | bytes 1 | tf_op jit(solution)/shard_map/product/pallas_call | solution.py:238
  38.1 2.1 %collective-permute-done.6.second_ref = bf16[64,2176]{1,0:T(8,128)(2,1)S(1)} collective-permute-done((bf16[64,2176]{1,0:T(8,128)(2,1)S(1)}, bf16[64,2176]{1,0:T(8,128)(2,1)S(1)}, u32[]{:S(2)}, u32[]{:S(2)}) %collective-permute-start.6) | collective-permute-done | bytes 278560 | tf_op jit(solution)/shard_map/ppermute | solution.py:288
  40.2 3.2 %collective-permute-done.4.direct_ref = bf16[32,7424]{1,0:T(8,128)(2,1)S(1)} collective-permute-done((bf16[32,7424]{1,0:T(8,128)(2,1)S(1)}, bf16[32,7424]{1,0:T(8,128)(2,1)S(1)}, u32[]{:S(2)}, u32[]{:S(2)}) %collective-permute-start.4) | collective-permute-done | bytes 475168 | tf_op jit(solution)/shard_map/ppermute | solution.py:272
  44.7 1.6 %collective-permute-start.9 = (bf16[64,2176]{1,0:T(8,128)(2,1)S(1)}, bf16[64,2176]{1,0:T(8,128)(2,1)S(1)}, u32[]{:S(2)}, u32[]{:S(2)}) collective-permute-start(bf16[64,2176]{1,0:T(8,128)(2,1)S(1)} %get-tuple-element.80), channel_id=1, source_target_pairs={{0,4},{4,0},{8,12},{12,8},{1,5},{5,1},{9,13},{13,9},{2,6},{6,2},{1... | collective-permute-start | bytes 835592 | tf_op jit(solution)/shard_map/ppermute | solution.py:288
  46.4 5.3 %product.6 = (bf16[64,2176]{1,0:T(8,128)(2,1)S(1)}, bf16[64,2176]{1,0:T(8,128)(2,1)S(1)}) custom-call(f32[8,128]{1,0:T(8,128)S(1)} %get-tuple-element.55._, bf16[128,7424]{1,0:T(8,128)(2,1)S(1)} %get-tuple-element.56.own_ref, bf16[128,7424]{1,0:T(8,128)(2,1)S(1)} %collective-permute-done.2.other_ref, bf16[32,7424]{1,0:T(8,128)(2,1)S(1)} %collective-permute-done.4.direct_ref, ...), custom_call_target="tpu_custom_call" | custom-call | flops 1 | bytes 1 | tf_op jit(solution)/shard_map/product/pallas_call | solution.py:238
  51.7 1.8 %collective-permute-done.9.second_ref = bf16[64,2176]{1,0:T(8,128)(2,1)S(1)} collective-permute-done((bf16[64,2176]{1,0:T(8,128)(2,1)S(1)}, bf16[64,2176]{1,0:T(8,128)(2,1)S(1)}, u32[]{:S(2)}, u32[]{:S(2)}) %collective-permute-start.9) | collective-permute-done | bytes 278560 | tf_op jit(solution)/shard_map/ppermute | solution.py:288
  53.5 3.2 %collective-permute-done.7.direct_ref = bf16[32,7424]{1,0:T(8,128)(2,1)S(1)} collective-permute-done((bf16[32,7424]{1,0:T(8,128)(2,1)S(1)}, bf16[32,7424]{1,0:T(8,128)(2,1)S(1)}, u32[]{:S(2)}, u32[]{:S(2)}) %collective-permute-start.7) | collective-permute-done | bytes 475168 | tf_op jit(solution)/shard_map/ppermute | solution.py:272
  56.7 1.6 %collective-permute-start.10 = (bf16[64,2176]{1,0:T(8,128)(2,1)S(1)}, bf16[64,2176]{1,0:T(8,128)(2,1)S(1)}, u32[]{:S(2)}, u32[]{:S(2)}) collective-permute-start(bf16[64,2176]{1,0:T(8,128)(2,1)S(1)} %get-tuple-element.85), channel_id=1, source_target_pairs={{0,4},{4,0},{8,12},{12,8},{1,5},{5,1},{9,13},{13,9},{2,6},{6,2},{1... | collective-permute-start | bytes 835592 | tf_op jit(solution)/shard_map/ppermute | solution.py:288
  58.6 5.1 %product.7 = (bf16[64,2176]{1,0:T(8,128)(2,1)S(1)}, bf16[64,2176]{1,0:T(8,128)(2,1)S(1)}) custom-call(f32[8,128]{1,0:T(8,128)S(1)} %get-tuple-element.55._, bf16[128,7424]{1,0:T(8,128)(2,1)S(1)} %get-tuple-element.56.own_ref, bf16[128,7424]{1,0:T(8,128)(2,1)S(1)} %collective-permute-done.2.other_ref, bf16[32,7424]{1,0:T(8,128)(2,1)S(1)} %collective-permute-done.7.direct_ref, ...), custom_call_target="tpu_custom_call" | custom-call | flops 1 | bytes 1 | tf_op jit(solution)/shard_map/product/pallas_call | solution.py:238
  63.6 1.6 %collective-permute-start.12 = (bf16[64,2176]{1,0:T(8,128)(2,1)S(1)}, bf16[64,2176]{1,0:T(8,128)(2,1)S(1)}, u32[]{:S(2)}, u32[]{:S(2)}) collective-permute-start(bf16[64,2176]{1,0:T(8,128)(2,1)S(1)} %get-tuple-element.91), channel_id=1, source_target_pairs={{0,4},{4,0},{8,12},{12,8},{1,5},{5,1},{9,13},{13,9},{2,6},{6,2},{1... | collective-permute-start | bytes 835592 | tf_op jit(solution)/shard_map/ppermute | solution.py:288
  65.3 2.6 %collective-permute-start.13 = (bf16[32,2176]{1,0:T(8,128)(2,1)S(1)}, bf16[32,2176]{1,0:T(8,128)(2,1)S(1)}, u32[]{:S(2)}, u32[]{:S(2)}) collective-permute-start(bf16[32,2176]{1,0:T(8,128)(2,1)S(1)} %get-tuple-element.93), channel_id=1, source_target_pairs={{0,8},{4,12},{8,0},{12,4},{1,9},{5,13},{9,1},{13,5},{2,10},{6,14},... | collective-permute-start | bytes 417800 | tf_op jit(solution)/shard_map/ppermute | solution.py:277
  68.5 2.4 %collective-permute-start.14 = (bf16[32,2176]{1,0:T(8,128)(2,1)S(1)}, bf16[32,2176]{1,0:T(8,128)(2,1)S(1)}, u32[]{:S(2)}, u32[]{:S(2)}) collective-permute-start(bf16[32,2176]{1,0:T(8,128)(2,1)S(1)} %get-tuple-element.94), channel_id=1, source_target_pairs={{0,8},{4,12},{8,0},{12,4},{1,9},{5,13},{9,1},{13,5},{2,10},{6,14},... | collective-permute-start | bytes 417800 | tf_op jit(solution)/shard_map/ppermute | solution.py:277
  71.0 7.3 %collective-permute-done.12.second_ref = bf16[64,2176]{1,0:T(8,128)(2,1)S(1)} collective-permute-done((bf16[64,2176]{1,0:T(8,128)(2,1)S(1)}, bf16[64,2176]{1,0:T(8,128)(2,1)S(1)}, u32[]{:S(2)}, u32[]{:S(2)}) %collective-permute-start.12) | collective-permute-done | bytes 278560 | tf_op jit(solution)/shard_map/ppermute | solution.py:288
  79.0 8.5 %collective-permute-done.15.refs_6_ = bf16[32,2176]{1,0:T(8,128)(2,1)S(1)} collective-permute-done((bf16[32,2176]{1,0:T(8,128)(2,1)S(1)}, bf16[32,2176]{1,0:T(8,128)(2,1)S(1)}, u32[]{:S(2)}, u32[]{:S(2)}) %collective-permute-start.15) | collective-permute-done | bytes 139296 | tf_op jit(solution)/shard_map/ppermute | solution.py:290
  87.5 3.0 %collective-permute-done.14.refs_5_ = bf16[32,2176]{1,0:T(8,128)(2,1)S(1)} collective-permute-done((bf16[32,2176]{1,0:T(8,128)(2,1)S(1)}, bf16[32,2176]{1,0:T(8,128)(2,1)S(1)}, u32[]{:S(2)}, u32[]{:S(2)}) %collective-permute-start.14) | collective-permute-done | bytes 139296 | tf_op jit(solution)/shard_map/ppermute | solution.py:277
  90.5 2.1 %collective-permute-done.16.refs_7_ = bf16[32,2176]{1,0:T(8,128)(2,1)S(1)} collective-permute-done((bf16[32,2176]{1,0:T(8,128)(2,1)S(1)}, bf16[32,2176]{1,0:T(8,128)(2,1)S(1)}, u32[]{:S(2)}, u32[]{:S(2)}) %collective-permute-start.16) | collective-permute-done | bytes 139296 | tf_op jit(solution)/shard_map/ppermute | solution.py:290
  92.6 1.3 %last.1 = bf16[128,2048]{1,0:T(8,128)(2,1)} custom-call(bf16[512,2048]{1,0:T(8,128)(2,1)S(1)} %bitcast.6, bf16[32,2176]{1,0:T(8,128)(2,1)S(1)} %get-tuple-element.73.refs_0_, bf16[32,2176]{1,0:T(8,128)(2,1)S(1)} %get-tuple-element.83.refs_1_, bf16[32,2176]{1,0:T(8,128)(2,1)S(1)} %get-tuple-element.86.refs_2_, ...), custom_call_target="tpu_custom_call" | custom-call | tf_op jit(solution)/shard_map/last/pallas_call | solution.py:292
  (23 shorter events, 5.4 us)
Async XLA Ops:
  1.8 16.9 %collective-permute-start.2 = (bf16[128,7424]{1,0:T(8,128)(2,1)S(1)}, bf16[128,7424]{1,0:T(8,128)(2,1)S(1)}, u32[]{:S(2)}, u32[]{:S(2)}) collective-permute-start(bf16[128,7424]{1,0:T(8,128)(2,1)S(1)} %get-tuple-element.56.own_ref), channel_id=1, source_target_pairs={{0,1},{1,0},{2,3},{3,2},{4,5},{5,4},{6,7},{7,6},{8,9},{9,8},{10,11... | collective-permute-start | bytes 5701640 | tf_op jit(solution)/shard_map/ppermute | solution.py:217
  2.3 14.4 %collective-permute-start = (bf16[32,7424]{1,0:T(8,128)(2,1)S(1)}, bf16[32,7424]{1,0:T(8,128)(2,1)S(1)}, u32[]{:S(2)}, u32[]{:S(2)}) collective-permute-start(bf16[32,7424]{1,0:T(8,128)(2,1)S(1)} %get-tuple-element.52), channel_id=1, source_target_pairs={{0,2},{1,3},{2,0},{3,1},{4,6},{5,7},{6,4},{7,5},{8,10},{9,11},{10,... | collective-permute-start | bytes 1425416 | tf_op jit(solution)/shard_map/ppermute | solution.py:216
  16.8 1.9 %collective-permute-start.3 = (bf16[32,7424]{1,0:T(8,128)(2,1)S(1)}, bf16[32,7424]{1,0:T(8,128)(2,1)S(1)}, u32[]{:S(2)}, u32[]{:S(2)}) collective-permute-start(bf16[32,7424]{1,0:T(8,128)(2,1)S(1)} %collective-permute-done.direct_ref), channel_id=1, source_target_pairs={{0,1},{1,0},{2,3},{3,2},{4,5},{5,4},{6,7},{7,6},{8,9},{9,8},{10,11... | collective-permute-start | bytes 1425416 | tf_op jit(solution)/shard_map/ppermute | solution.py:273
  17.0 13.1 %collective-permute-start.1 = (bf16[32,7424]{1,0:T(8,128)(2,1)S(1)}, bf16[32,7424]{1,0:T(8,128)(2,1)S(1)}, u32[]{:S(2)}, u32[]{:S(2)}) collective-permute-start(bf16[32,7424]{1,0:T(8,128)(2,1)S(1)} %get-tuple-element.54), channel_id=1, source_target_pairs={{0,2},{1,3},{2,0},{3,1},{4,6},{5,7},{6,4},{7,5},{8,10},{9,11},{10,... | collective-permute-start | bytes 1425416 | tf_op jit(solution)/shard_map/ppermute | solution.py:272
  30.1 2.9 %collective-permute-start.5 = (bf16[32,7424]{1,0:T(8,128)(2,1)S(1)}, bf16[32,7424]{1,0:T(8,128)(2,1)S(1)}, u32[]{:S(2)}, u32[]{:S(2)}) collective-permute-start(bf16[32,7424]{1,0:T(8,128)(2,1)S(1)} %collective-permute-done.1.direct_ref), channel_id=1, source_target_pairs={{0,1},{1,0},{2,3},{3,2},{4,5},{5,4},{6,7},{7,6},{8,9},{9,8},{10,11... | collective-permute-start | bytes 1425416 | tf_op jit(solution)/shard_map/ppermute | solution.py:273
  30.2 13.3 %collective-permute-start.4 = (bf16[32,7424]{1,0:T(8,128)(2,1)S(1)}, bf16[32,7424]{1,0:T(8,128)(2,1)S(1)}, u32[]{:S(2)}, u32[]{:S(2)}) collective-permute-start(bf16[32,7424]{1,0:T(8,128)(2,1)S(1)} %get-tuple-element.65), channel_id=1, source_target_pairs={{0,2},{1,3},{2,0},{3,1},{4,6},{5,7},{6,4},{7,5},{8,10},{9,11},{10,... | collective-permute-start | bytes 1425416 | tf_op jit(solution)/shard_map/ppermute | solution.py:272
  31.4 8.8 %collective-permute-start.6 = (bf16[64,2176]{1,0:T(8,128)(2,1)S(1)}, bf16[64,2176]{1,0:T(8,128)(2,1)S(1)}, u32[]{:S(2)}, u32[]{:S(2)}) collective-permute-start(bf16[64,2176]{1,0:T(8,128)(2,1)S(1)} %get-tuple-element.70), channel_id=1, source_target_pairs={{0,4},{4,0},{8,12},{12,8},{1,5},{5,1},{9,13},{13,9},{2,6},{6,2},{1... | collective-permute-start | bytes 835592 | tf_op jit(solution)/shard_map/ppermute | solution.py:288
  43.4 2.9 %collective-permute-start.8 = (bf16[32,7424]{1,0:T(8,128)(2,1)S(1)}, bf16[32,7424]{1,0:T(8,128)(2,1)S(1)}, u32[]{:S(2)}, u32[]{:S(2)}) collective-permute-start(bf16[32,7424]{1,0:T(8,128)(2,1)S(1)} %collective-permute-done.4.direct_ref), channel_id=1, source_target_pairs={{0,1},{1,0},{2,3},{3,2},{4,5},{5,4},{6,7},{7,6},{8,9},{9,8},{10,11... | collective-permute-start | bytes 1425416 | tf_op jit(solution)/shard_map/ppermute | solution.py:273
  43.4 13.3 %collective-permute-start.7 = (bf16[32,7424]{1,0:T(8,128)(2,1)S(1)}, bf16[32,7424]{1,0:T(8,128)(2,1)S(1)}, u32[]{:S(2)}, u32[]{:S(2)}) collective-permute-start(bf16[32,7424]{1,0:T(8,128)(2,1)S(1)} %get-tuple-element.74), channel_id=1, source_target_pairs={{0,2},{1,3},{2,0},{3,1},{4,6},{5,7},{6,4},{7,5},{8,10},{9,11},{10,... | collective-permute-start | bytes 1425416 | tf_op jit(solution)/shard_map/ppermute | solution.py:272
  44.7 8.8 %collective-permute-start.9 = (bf16[64,2176]{1,0:T(8,128)(2,1)S(1)}, bf16[64,2176]{1,0:T(8,128)(2,1)S(1)}, u32[]{:S(2)}, u32[]{:S(2)}) collective-permute-start(bf16[64,2176]{1,0:T(8,128)(2,1)S(1)} %get-tuple-element.80), channel_id=1, source_target_pairs={{0,4},{4,0},{8,12},{12,8},{1,5},{5,1},{9,13},{13,9},{2,6},{6,2},{1... | collective-permute-start | bytes 835592 | tf_op jit(solution)/shard_map/ppermute | solution.py:288
  56.7 1.8 %collective-permute-start.11 = (bf16[32,7424]{1,0:T(8,128)(2,1)S(1)}, bf16[32,7424]{1,0:T(8,128)(2,1)S(1)}, u32[]{:S(2)}, u32[]{:S(2)}) collective-permute-start(bf16[32,7424]{1,0:T(8,128)(2,1)S(1)} %collective-permute-done.7.direct_ref), channel_id=1, source_target_pairs={{0,1},{1,0},{2,3},{3,2},{4,5},{5,4},{6,7},{7,6},{8,9},{9,8},{10,11... | collective-permute-start | bytes 1425416 | tf_op jit(solution)/shard_map/ppermute | solution.py:273
  56.7 11.2 %collective-permute-start.10 = (bf16[64,2176]{1,0:T(8,128)(2,1)S(1)}, bf16[64,2176]{1,0:T(8,128)(2,1)S(1)}, u32[]{:S(2)}, u32[]{:S(2)}) collective-permute-start(bf16[64,2176]{1,0:T(8,128)(2,1)S(1)} %get-tuple-element.85), channel_id=1, source_target_pairs={{0,4},{4,0},{8,12},{12,8},{1,5},{5,1},{9,13},{13,9},{2,6},{6,2},{1... | collective-permute-start | bytes 835592 | tf_op jit(solution)/shard_map/ppermute | solution.py:288
  58.6 34.0 %copy-start = (bf16[8,64,2048]{2,1,0:T(8,128)(2,1)S(1)}, bf16[8,64,2048]{2,1,0:T(8,128)(2,1)}, u32[]{:S(2)}) copy-start(bf16[8,64,2048]{2,1,0:T(8,128)(2,1)} %param.8) | copy-start | bytes 6291460
  63.6 14.6 %collective-permute-start.12 = (bf16[64,2176]{1,0:T(8,128)(2,1)S(1)}, bf16[64,2176]{1,0:T(8,128)(2,1)S(1)}, u32[]{:S(2)}, u32[]{:S(2)}) collective-permute-start(bf16[64,2176]{1,0:T(8,128)(2,1)S(1)} %get-tuple-element.91), channel_id=1, source_target_pairs={{0,4},{4,0},{8,12},{12,8},{1,5},{5,1},{9,13},{13,9},{2,6},{6,2},{1... | collective-permute-start | bytes 835592 | tf_op jit(solution)/shard_map/ppermute | solution.py:288
  65.3 13.7 %collective-permute-start.13 = (bf16[32,2176]{1,0:T(8,128)(2,1)S(1)}, bf16[32,2176]{1,0:T(8,128)(2,1)S(1)}, u32[]{:S(2)}, u32[]{:S(2)}) collective-permute-start(bf16[32,2176]{1,0:T(8,128)(2,1)S(1)} %get-tuple-element.93), channel_id=1, source_target_pairs={{0,8},{4,12},{8,0},{12,4},{1,9},{5,13},{9,1},{13,5},{2,10},{6,14},... | collective-permute-start | bytes 417800 | tf_op jit(solution)/shard_map/ppermute | solution.py:277
  68.0 19.5 %collective-permute-start.15 = (bf16[32,2176]{1,0:T(8,128)(2,1)S(1)}, bf16[32,2176]{1,0:T(8,128)(2,1)S(1)}, u32[]{:S(2)}, u32[]{:S(2)}) collective-permute-start(bf16[32,2176]{1,0:T(8,128)(2,1)S(1)} %get-tuple-element.95), channel_id=1, source_target_pairs={{0,8},{4,12},{8,0},{12,4},{1,9},{5,13},{9,1},{13,5},{2,10},{6,14},... | collective-permute-start | bytes 417800 | tf_op jit(solution)/shard_map/ppermute | solution.py:290
  68.5 21.9 %collective-permute-start.14 = (bf16[32,2176]{1,0:T(8,128)(2,1)S(1)}, bf16[32,2176]{1,0:T(8,128)(2,1)S(1)}, u32[]{:S(2)}, u32[]{:S(2)}) collective-permute-start(bf16[32,2176]{1,0:T(8,128)(2,1)S(1)} %get-tuple-element.94), channel_id=1, source_target_pairs={{0,8},{4,12},{8,0},{12,4},{1,9},{5,13},{9,1},{13,5},{2,10},{6,14},... | collective-permute-start | bytes 417800 | tf_op jit(solution)/shard_map/ppermute | solution.py:277
  78.4 14.2 %collective-permute-start.16 = (bf16[32,2176]{1,0:T(8,128)(2,1)S(1)}, bf16[32,2176]{1,0:T(8,128)(2,1)S(1)}, u32[]{:S(2)}, u32[]{:S(2)}) collective-permute-start(bf16[32,2176]{1,0:T(8,128)(2,1)S(1)} %get-tuple-element.96), channel_id=1, source_target_pairs={{0,8},{4,12},{8,0},{12,4},{1,9},{5,13},{9,1},{13,5},{2,10},{6,14},... | collective-permute-start | bytes 417800 | tf_op jit(solution)/shard_map/ppermute | solution.py:290

commit v4 on v3

--- a/solution.py
+++ b/solution.py
@@ -102,7 +102,7 @@
 
 
 def product_kernel(
-    adapters, units, at, _, own_ref, other_ref, direct_ref, passed_ref, *refs
+    adapters, units, at, _, own_ref, other_ref, direct_ref, passed_a, passed_b, *refs
 ):
     *panel_refs, spread_ref, send_ref, keep_ref = refs
     rows = direct_ref.shape[0]
@@ -112,7 +112,7 @@
 
     def pieces(cols):
         near = [ref[at : at + rows, cols] for ref in (own_ref, other_ref)]
-        far = [ref[:, cols] for ref in (direct_ref, passed_ref)]
+        far = [ref[:, cols] for ref in (direct_ref, passed_a, passed_b)]
         return jnp.concatenate(near + far, axis=0)
 
     every = jnp.dot(pieces(slice(None)), spread_ref[...], preferred_element_type=jnp.float32)
@@ -238,12 +238,12 @@
         return pl.pallas_call(
             functools.partial(product_kernel, adapters, units, starts[step]),
             out_shape=[struct(2 * counts[step], payload)] * 2,
-            in_specs=[in_vmem()] * (5 + len(both)),
+            in_specs=[in_vmem()] * (6 + len(both)),
             out_specs=[in_vmem()] * 2,
             compiler_params=params(4),
             cost_estimate=quick,
             name="product",
-        )(token, own, other, direct[step], passed, *both)
+        )(token, own, other, direct[step], *passed, *both)
 
     def add(step, keep, got):
         return pl.pallas_call(
@@ -256,9 +256,13 @@
             name="add",
         )(keep, got)
 
+    def over_core(part):
+        half = part.shape[0] // 2
+        return [lax.ppermute(cut, "req", beside) for cut in (part[:half], part[half:])]
+
     after = lax.optimization_barrier
     steps = len(counts)
-    pieces[1], direct[0], token = after((pieces[1], direct[0], token))
+    direct[0], token = after((direct[0], token))
     parts, kept, gots = [], [], []
 
     def add_part(step):
@@ -268,23 +272,25 @@
         return send
 
     for step in range(steps):
+        passed = over_core(direct[step])
         if step + 1 < steps:
             direct.append(lax.ppermute(pieces[step + 1], "req", across))
-        passed = lax.ppermute(direct[step], "req", beside)
         if step > 1:
             send = add_part(step - 2)
             passed, send = after((passed, send))
             gots.append(lax.ppermute(send, "tensor", far_z))
         send, keep = product(step, passed, token)
         if step + 1 < steps:
-            later = pieces[step + 2 : step + 3]
+            if step + 2 < steps:
+                send, pieces[step + 2] = after((send, pieces[step + 2]))
             earlier = parts[step - 1 : step] if step else []
-            direct[step + 1], send, later, earlier = after(
-                (direct[step + 1], send, later, earlier)
+            direct[step + 1], send, earlier, done = after(
+                (direct[step + 1], send, earlier, gots[step - 2 : step - 1] if step > 1 else [])
             )
-            pieces[step + 2 : step + 3] = later
             if step:
                 parts[step - 1] = earlier[0]
+            if done:
+                gots[step - 2] = done[0]
         parts.append((keep, lax.ppermute(send, "tensor", next_z)))
     for step in range(steps - 2, steps):
         gots.append(lax.ppermute(add_part(step), "tensor", far_z))

time: 94 us -> 83.9 us (0.89)
  waiting for transfers between devices: 38.4 us -> 26.4 us
  starting transfers between devices: 19.6 us -> 21.2 us
    ppermute x3, waiting for transfers between devices: 12.8 us -> 4.6 us  [paired(): direct.append(lax.ppermute(pieces[step + 1], 'req', across))]
    ppermute x2, starting transfers between devices: 1.16 us -> 4.31 us  [paired(): gots.append(lax.ppermute(add_part(step), 'tensor', far_z))]
    ppermute x2, waiting for transfers between devices: 10.6 us -> 7.91 us  [paired(): gots.append(lax.ppermute(add_part(step), 'tensor', far_z))]
    ppermute x4 -> x8, waiting for transfers between devices: 0.74 us -> 3.33 us  [over_core(): lax.ppermute(cut, 'req', beside)]
    ppermute x2, waiting for transfers between devices: 2.99 us -> 0.59 us  [paired(): gots.append(lax.ppermute(send, 'tensor', far_z))]
    ppermute x4 -> x8, starting transfers between devices: 0.24 us -> 2.35 us  [over_core(): lax.ppermute(cut, 'req', beside)]
    ppermute x2, starting transfers between devices: 5.07 us -> 3.04 us  [paired(): gots.append(lax.ppermute(send, 'tensor', far_z))]
    ppermute x3, starting transfers between devices: 3.65 us -> 2.16 us  [paired(): direct.append(lax.ppermute(pieces[step + 1], 'req', across))]
  transfers between devices with their start and end apart: 17 -> 21, of which waited for: 11 -> 14; matrix products, arithmetic and copies ran while one was open for 0% -> 0% of each run, Pallas kernels for 35% -> 39%
where the time goes in v4:
time: 83.9 us; the launch traced here: 83.8 us
  Pallas kernels  35.8 us (43%)
  waiting for transfers between devices  26.4 us (31%)
  starting transfers between devices  21.2 us (25%)
    pallas_call x4, Pallas kernels, product(): pl.pallas_call(functools.partial(product_kernel, adapters, units, starts[...  20.5 us
    pallas_call x1, Pallas kernels, paired(): pl.pallas_call(load_kernel, out_shape=[jax.ShapeDtypeStruct((8, LANES), j...  11.9 us
    ppermute x4, waiting for transfers between devices, paired(): parts.append((keep, lax.ppermute(send, 'tensor', next_z)))  10 us
    ppermute x2, waiting for transfers between devices, paired(): gots.append(lax.ppermute(add_part(step), 'tensor', far_z))  7.91 us
    ppermute x4, starting transfers between devices, paired(): parts.append((keep, lax.ppermute(send, 'tensor', next_z)))  6.34 us
    ppermute x3, waiting for transfers between devices, paired(): direct.append(lax.ppermute(pieces[step + 1], 'req', across))  4.6 us
    ppermute x2, starting transfers between devices, paired(): gots.append(lax.ppermute(add_part(step), 'tensor', far_z))  4.31 us
    ppermute x8, waiting for transfers between devices, over_core(): lax.ppermute(cut, 'req', beside)  3.33 us
  transfers between devices with their start and end apart: 21, of which 14 were waited for; matrix products, arithmetic and copies ran while one was open for 0% of the time, Pallas kernels for 39%

profile of v4, /device:TPU:0, one launch (start us, length us, event | category | flops | bytes accessed | tf_op | source)
XLA Modules:
  0.0 83.8 jit_solution(11930866810555588463)
XLA Ops:
  0.0 1.8 %turn.1 = (bf16[128,7424]{1,0:T(8,128)(2,1)S(1)}, bf16[32,7424]{1,0:T(8,128)(2,1)S(1)}, bf16[32,7424]{1,0:T(8,128)(2,1)S(1)}, bf16[32,7424]{1,0:T(8,128)(2,1)S(1)}, bf16[32,7424]{1,0:T(8,128)(2,1)S(1)}) custom-call(bf16[7392,128]{1,0:T(8,128)(2,1)} %bitcast.8, s32[1,128]{1,0:T(1,128)} %bitcast.9), custom_call_target="tpu_custom_call" | custom-call | tf_op jit(solution)/shard_map/turn/pallas_call | solution.py:197
  1.8 3.0 %collective-permute-start = (bf16[32,7424]{1,0:T(8,128)(2,1)S(1)}, bf16[32,7424]{1,0:T(8,128)(2,1)S(1)}, u32[]{:S(2)}, u32[]{:S(2)}) collective-permute-start(bf16[32,7424]{1,0:T(8,128)(2,1)S(1)} %get-tuple-element.55), channel_id=1, source_target_pairs={{0,2},{1,3},{2,0},{3,1},{4,6},{5,7},{6,4},{7,5},{8,10},{9,11},{10,... | collective-permute-start | bytes 1425416 | tf_op jit(solution)/shard_map/ppermute | solution.py:216
  4.9 11.9 %load.1 = (f32[8,128]{1,0:T(8,128)S(1)}, bf16[7424,512]{1,0:T(8,128)(2,1)S(1)}, bf16[7424,512]{1,0:T(8,128)(2,1)S(1)}, bf16[7424,512]{1,0:T(8,128)(2,1)S(1)}, bf...) custom-call(bf16[7392,2048]{1,0:T(8,128)(2,1)} %w_hbm.1, bf16[512,7392]{1,0:T(8,128)(2,1)} %bitcast.7), custom_call_target="tpu_custom_call" | custom-call | flops 1 | bytes 1 | tf_op jit(solution)/shard_map/load/pallas_call | solution.py:220
  17.5 1.0 %collective-permute-done.3.passed_b = bf16[16,7424]{1,0:T(8,128)(2,1)S(1)} collective-permute-done((bf16[16,7424]{1,0:T(8,128)(2,1)S(1)}, bf16[16,7424]{1,0:T(8,128)(2,1)S(1)}, u32[]{:S(2)}, u32[]{:S(2)}) %collective-permute-start.3) | collective-permute-done | bytes 237600 | tf_op jit(solution)/shard_map/ppermute | solution.py:261
  18.9 5.1 %product.4 = (bf16[64,2176]{1,0:T(8,128)(2,1)S(1)}, bf16[64,2176]{1,0:T(8,128)(2,1)S(1)}) custom-call(f32[8,128]{1,0:T(8,128)S(1)} %get-tuple-element.57._, bf16[128,7424]{1,0:T(8,128)(2,1)S(1)} %get-tuple-element.58.own_ref, bf16[128,7424]{1,0:T(8,128)(2,1)S(1)} %collective-permute-done.1.other_ref, bf16[32,7424]{1,0:T(8,128)(2,1)S(1)} %collective-permute-done.direct_ref, ...), custom_call_target="tpu_custom_call" | custom-call | flops 1 | bytes 1 | tf_op jit(solution)/shard_map/product/pallas_call | solution.py:238
  24.0 1.9 %collective-permute-done.5.direct_ref = bf16[32,7424]{1,0:T(8,128)(2,1)S(1)} collective-permute-done((bf16[32,7424]{1,0:T(8,128)(2,1)S(1)}, bf16[32,7424]{1,0:T(8,128)(2,1)S(1)}, u32[]{:S(2)}, u32[]{:S(2)}) %collective-permute-start.5) | collective-permute-done | bytes 475168 | tf_op jit(solution)/shard_map/ppermute | solution.py:277
  25.9 1.8 %collective-permute-start.8 = (bf16[64,2176]{1,0:T(8,128)(2,1)S(1)}, bf16[64,2176]{1,0:T(8,128)(2,1)S(1)}, u32[]{:S(2)}, u32[]{:S(2)}) collective-permute-start(bf16[64,2176]{1,0:T(8,128)(2,1)S(1)} %get-tuple-element.75), channel_id=1, source_target_pairs={{0,4},{4,0},{8,12},{12,8},{1,5},{5,1},{9,13},{13,9},{2,6},{6,2},{1... | collective-permute-start | bytes 835592 | tf_op jit(solution)/shard_map/ppermute | solution.py:294
  27.7 1.5 %collective-permute-start.4 = (bf16[32,7424]{1,0:T(8,128)(2,1)S(1)}, bf16[32,7424]{1,0:T(8,128)(2,1)S(1)}, u32[]{:S(2)}, u32[]{:S(2)}) collective-permute-start(bf16[32,7424]{1,0:T(8,128)(2,1)S(1)} %get-tuple-element.67), channel_id=1, source_target_pairs={{0,2},{1,3},{2,0},{3,1},{4,6},{5,7},{6,4},{7,5},{8,10},{9,11},{10,... | collective-permute-start | bytes 1425416 | tf_op jit(solution)/shard_map/ppermute | solution.py:277
  29.8 1.0 %collective-permute-done.7.passed_b = bf16[16,7424]{1,0:T(8,128)(2,1)S(1)} collective-permute-done((bf16[16,7424]{1,0:T(8,128)(2,1)S(1)}, bf16[16,7424]{1,0:T(8,128)(2,1)S(1)}, u32[]{:S(2)}, u32[]{:S(2)}) %collective-permute-start.7) | collective-permute-done | bytes 237600 | tf_op jit(solution)/shard_map/ppermute | solution.py:261
  31.1 5.1 %product.5 = (bf16[64,2176]{1,0:T(8,128)(2,1)S(1)}, bf16[64,2176]{1,0:T(8,128)(2,1)S(1)}) custom-call(f32[8,128]{1,0:T(8,128)S(1)} %get-tuple-element.57._, bf16[128,7424]{1,0:T(8,128)(2,1)S(1)} %get-tuple-element.58.own_ref, bf16[128,7424]{1,0:T(8,128)(2,1)S(1)} %collective-permute-done.1.other_ref, bf16[32,7424]{1,0:T(8,128)(2,1)S(1)} %collective-permute-done.5.direct_ref, ...), custom_call_target="tpu_custom_call" | custom-call | flops 1 | bytes 1 | tf_op jit(solution)/shard_map/product/pallas_call | solution.py:238
  36.8 2.4 %collective-permute-done.4.direct_ref = bf16[32,7424]{1,0:T(8,128)(2,1)S(1)} collective-permute-done((bf16[32,7424]{1,0:T(8,128)(2,1)S(1)}, bf16[32,7424]{1,0:T(8,128)(2,1)S(1)}, u32[]{:S(2)}, u32[]{:S(2)}) %collective-permute-start.4) | collective-permute-done | bytes 475168 | tf_op jit(solution)/shard_map/ppermute | solution.py:277
  39.8 0.7 collective-permute-start.12
  41.2 2.6 %collective-permute-start.13 = (bf16[32,2176]{1,0:T(8,128)(2,1)S(1)}, bf16[32,2176]{1,0:T(8,128)(2,1)S(1)}, u32[]{:S(2)}, u32[]{:S(2)}) collective-permute-start(bf16[32,2176]{1,0:T(8,128)(2,1)S(1)} %get-tuple-element.87), channel_id=1, source_target_pairs={{0,8},{4,12},{8,0},{12,4},{1,9},{5,13},{9,1},{13,5},{2,10},{6,14},... | collective-permute-start | bytes 417800 | tf_op jit(solution)/shard_map/ppermute | solution.py:281
  43.7 5.3 %product.6 = (bf16[64,2176]{1,0:T(8,128)(2,1)S(1)}, bf16[64,2176]{1,0:T(8,128)(2,1)S(1)}) custom-call(f32[8,128]{1,0:T(8,128)S(1)} %get-tuple-element.57._, bf16[128,7424]{1,0:T(8,128)(2,1)S(1)} %get-tuple-element.58.own_ref, bf16[128,7424]{1,0:T(8,128)(2,1)S(1)} %collective-permute-done.1.other_ref, bf16[32,7424]{1,0:T(8,128)(2,1)S(1)} %collective-permute-done.4.direct_ref, ...), custom_call_target="tpu_custom_call" | custom-call | flops 1 | bytes 1 | tf_op jit(solution)/shard_map/product/pallas_call | solution.py:238
  49.4 2.1 %collective-permute-done.12.second_ref = bf16[64,2176]{1,0:T(8,128)(2,1)S(1)} collective-permute-done((bf16[64,2176]{1,0:T(8,128)(2,1)S(1)}, bf16[64,2176]{1,0:T(8,128)(2,1)S(1)}, u32[]{:S(2)}, u32[]{:S(2)}) %collective-permute-start.12) | collective-permute-done | bytes 278560 | tf_op jit(solution)/shard_map/ppermute | solution.py:294
  52.1 2.6 %collective-permute-start.14 = (bf16[64,2176]{1,0:T(8,128)(2,1)S(1)}, bf16[64,2176]{1,0:T(8,128)(2,1)S(1)}, u32[]{:S(2)}, u32[]{:S(2)}) collective-permute-start(bf16[64,2176]{1,0:T(8,128)(2,1)S(1)} %get-tuple-element.92), channel_id=1, source_target_pairs={{0,4},{4,0},{8,12},{12,8},{1,5},{5,1},{9,13},{13,9},{2,6},{6,2},{1... | collective-permute-start | bytes 835592 | tf_op jit(solution)/shard_map/ppermute | solution.py:294
  54.8 5.1 %product.7 = (bf16[64,2176]{1,0:T(8,128)(2,1)S(1)}, bf16[64,2176]{1,0:T(8,128)(2,1)S(1)}) custom-call(f32[8,128]{1,0:T(8,128)S(1)} %get-tuple-element.57._, bf16[128,7424]{1,0:T(8,128)(2,1)S(1)} %get-tuple-element.58.own_ref, bf16[128,7424]{1,0:T(8,128)(2,1)S(1)} %collective-permute-done.1.other_ref, bf16[32,7424]{1,0:T(8,128)(2,1)S(1)} %collective-permute-done.9.direct_ref, ...), custom_call_target="tpu_custom_call" | custom-call | flops 1 | bytes 1 | tf_op jit(solution)/shard_map/product/pallas_call | solution.py:238
  59.9 1.3 %collective-permute-start.17 = (bf16[64,2176]{1,0:T(8,128)(2,1)S(1)}, bf16[64,2176]{1,0:T(8,128)(2,1)S(1)}, u32[]{:S(2)}, u32[]{:S(2)}) collective-permute-start(bf16[64,2176]{1,0:T(8,128)(2,1)S(1)} %get-tuple-element.99), channel_id=1, source_target_pairs={{0,4},{4,0},{8,12},{12,8},{1,5},{5,1},{9,13},{13,9},{2,6},{6,2},{1... | collective-permute-start | bytes 835592 | tf_op jit(solution)/shard_map/ppermute | solution.py:294
  61.7 2.5 %collective-permute-start.19 = (bf16[32,2176]{1,0:T(8,128)(2,1)S(1)}, bf16[32,2176]{1,0:T(8,128)(2,1)S(1)}, u32[]{:S(2)}, u32[]{:S(2)}) collective-permute-start(bf16[32,2176]{1,0:T(8,128)(2,1)S(1)} %get-tuple-element.103), channel_id=1, source_target_pairs={{0,8},{4,12},{8,0},{12,4},{1,9},{5,13},{9,1},{13,5},{2,10},{6,14},... | collective-permute-start | bytes 417800 | tf_op jit(solution)/shard_map/ppermute | solution.py:296
  64.2 7.9 %collective-permute-done.17.second_ref = bf16[64,2176]{1,0:T(8,128)(2,1)S(1)} collective-permute-done((bf16[64,2176]{1,0:T(8,128)(2,1)S(1)}, bf16[64,2176]{1,0:T(8,128)(2,1)S(1)}, u32[]{:S(2)}, u32[]{:S(2)}) %collective-permute-start.17) | collective-permute-done | bytes 278560 | tf_op jit(solution)/shard_map/ppermute | solution.py:294
  72.2 1.8 %collective-permute-start.20 = (bf16[32,2176]{1,0:T(8,128)(2,1)S(1)}, bf16[32,2176]{1,0:T(8,128)(2,1)S(1)}, u32[]{:S(2)}, u32[]{:S(2)}) collective-permute-start(bf16[32,2176]{1,0:T(8,128)(2,1)S(1)} %get-tuple-element.104), channel_id=1, source_target_pairs={{0,8},{4,12},{8,0},{12,4},{1,9},{5,13},{9,1},{13,5},{2,10},{6,14},... | collective-permute-start | bytes 417800 | tf_op jit(solution)/shard_map/ppermute | solution.py:296
  74.6 6.0 %collective-permute-done.19.refs_6_ = bf16[32,2176]{1,0:T(8,128)(2,1)S(1)} collective-permute-done((bf16[32,2176]{1,0:T(8,128)(2,1)S(1)}, bf16[32,2176]{1,0:T(8,128)(2,1)S(1)}, u32[]{:S(2)}, u32[]{:S(2)}) %collective-permute-start.19) | collective-permute-done | bytes 139296 | tf_op jit(solution)/shard_map/ppermute | solution.py:296
  80.5 1.9 %collective-permute-done.20.refs_7_ = bf16[32,2176]{1,0:T(8,128)(2,1)S(1)} collective-permute-done((bf16[32,2176]{1,0:T(8,128)(2,1)S(1)}, bf16[32,2176]{1,0:T(8,128)(2,1)S(1)}, u32[]{:S(2)}, u32[]{:S(2)}) %collective-permute-start.20) | collective-permute-done | bytes 139296 | tf_op jit(solution)/shard_map/ppermute | solution.py:296
  82.5 1.3 %last.1 = bf16[128,2048]{1,0:T(8,128)(2,1)} custom-call(bf16[512,2048]{1,0:T(8,128)(2,1)S(1)} %bitcast.6, bf16[32,2176]{1,0:T(8,128)(2,1)S(1)} %get-tuple-element.78.refs_0_, bf16[32,2176]{1,0:T(8,128)(2,1)S(1)} %get-tuple-element.90.refs_1_, bf16[32,2176]{1,0:T(8,128)(2,1)S(1)} %get-tuple-element.93.refs_2_, ...), custom_call_target="tpu_custom_call" | custom-call | tf_op jit(solution)/shard_map/last/pallas_call | solution.py:298
  (35 shorter events, 6.2 us)
Async XLA Ops:
  1.8 15.0 %collective-permute-start = (bf16[32,7424]{1,0:T(8,128)(2,1)S(1)}, bf16[32,7424]{1,0:T(8,128)(2,1)S(1)}, u32[]{:S(2)}, u32[]{:S(2)}) collective-permute-start(bf16[32,7424]{1,0:T(8,128)(2,1)S(1)} %get-tuple-element.55), channel_id=1, source_target_pairs={{0,2},{1,3},{2,0},{3,1},{4,6},{5,7},{6,4},{7,5},{8,10},{9,11},{10,... | collective-permute-start | bytes 1425416 | tf_op jit(solution)/shard_map/ppermute | solution.py:216
  4.8 21.1 %collective-permute-start.5 = (bf16[32,7424]{1,0:T(8,128)(2,1)S(1)}, bf16[32,7424]{1,0:T(8,128)(2,1)S(1)}, u32[]{:S(2)}, u32[]{:S(2)}) collective-permute-start(bf16[32,7424]{1,0:T(8,128)(2,1)S(1)} %get-tuple-element.68), channel_id=1, source_target_pairs={{0,2},{1,3},{2,0},{3,1},{4,6},{5,7},{6,4},{7,5},{8,10},{9,11},{10,... | collective-permute-start | bytes 1425416 | tf_op jit(solution)/shard_map/ppermute | solution.py:277
  4.9 14.0 %collective-permute-start.1 = (bf16[128,7424]{1,0:T(8,128)(2,1)S(1)}, bf16[128,7424]{1,0:T(8,128)(2,1)S(1)}, u32[]{:S(2)}, u32[]{:S(2)}) collective-permute-start(bf16[128,7424]{1,0:T(8,128)(2,1)S(1)} %get-tuple-element.58.own_ref), channel_id=1, source_target_pairs={{0,1},{1,0},{2,3},{3,2},{4,5},{5,4},{6,7},{7,6},{8,9},{9,8},{10,11... | collective-permute-start | bytes 5701640 | tf_op jit(solution)/shard_map/ppermute | solution.py:217
  16.8 1.7 %collective-permute-start.3 = (bf16[16,7424]{1,0:T(8,128)(2,1)S(1)}, bf16[16,7424]{1,0:T(8,128)(2,1)S(1)}, u32[]{:S(2)}, u32[]{:S(2)}) collective-permute-start(bf16[16,7424]{1,0:T(8,128)(2,1)S(1)} %get-tuple-element.111), channel_id=1, source_target_pairs={{0,1},{1,0},{2,3},{3,2},{4,5},{5,4},{6,7},{7,6},{8,9},{9,8},{10,11... | collective-permute-start | bytes 712712 | tf_op jit(solution)/shard_map/ppermute | solution.py:261
  17.4 1.5 %collective-permute-start.2 = (bf16[16,7424]{1,0:T(8,128)(2,1)S(1)}, bf16[16,7424]{1,0:T(8,128)(2,1)S(1)}, u32[]{:S(2)}, u32[]{:S(2)}) collective-permute-start(bf16[16,7424]{1,0:T(8,128)(2,1)S(1)} %get-tuple-element.112), channel_id=1, source_target_pairs={{0,1},{1,0},{2,3},{3,2},{4,5},{5,4},{6,7},{7,6},{8,9},{9,8},{10,11... | collective-permute-start | bytes 712712 | tf_op jit(solution)/shard_map/ppermute | solution.py:261
  25.9 10.9 %collective-permute-start.8 = (bf16[64,2176]{1,0:T(8,128)(2,1)S(1)}, bf16[64,2176]{1,0:T(8,128)(2,1)S(1)}, u32[]{:S(2)}, u32[]{:S(2)}) collective-permute-start(bf16[64,2176]{1,0:T(8,128)(2,1)S(1)} %get-tuple-element.75), channel_id=1, source_target_pairs={{0,4},{4,0},{8,12},{12,8},{1,5},{5,1},{9,13},{13,9},{2,6},{6,2},{1... | collective-permute-start | bytes 835592 | tf_op jit(solution)/shard_map/ppermute | solution.py:294
  27.7 11.5 %collective-permute-start.4 = (bf16[32,7424]{1,0:T(8,128)(2,1)S(1)}, bf16[32,7424]{1,0:T(8,128)(2,1)S(1)}, u32[]{:S(2)}, u32[]{:S(2)}) collective-permute-start(bf16[32,7424]{1,0:T(8,128)(2,1)S(1)} %get-tuple-element.67), channel_id=1, source_target_pairs={{0,2},{1,3},{2,0},{3,1},{4,6},{5,7},{6,4},{7,5},{8,10},{9,11},{10,... | collective-permute-start | bytes 1425416 | tf_op jit(solution)/shard_map/ppermute | solution.py:277
  29.2 1.6 %collective-permute-start.7 = (bf16[16,7424]{1,0:T(8,128)(2,1)S(1)}, bf16[16,7424]{1,0:T(8,128)(2,1)S(1)}, u32[]{:S(2)}, u32[]{:S(2)}) collective-permute-start(bf16[16,7424]{1,0:T(8,128)(2,1)S(1)} %get-tuple-element.109), channel_id=1, source_target_pairs={{0,1},{1,0},{2,3},{3,2},{4,5},{5,4},{6,7},{7,6},{8,9},{9,8},{10,11... | collective-permute-start | bytes 712712 | tf_op jit(solution)/shard_map/ppermute | solution.py:261
  29.3 1.8 %collective-permute-start.6 = (bf16[16,7424]{1,0:T(8,128)(2,1)S(1)}, bf16[16,7424]{1,0:T(8,128)(2,1)S(1)}, u32[]{:S(2)}, u32[]{:S(2)}) collective-permute-start(bf16[16,7424]{1,0:T(8,128)(2,1)S(1)} %get-tuple-element.110), channel_id=1, source_target_pairs={{0,1},{1,0},{2,3},{3,2},{4,5},{5,4},{6,7},{7,6},{8,9},{9,8},{10,11... | collective-permute-start | bytes 712712 | tf_op jit(solution)/shard_map/ppermute | solution.py:261
  36.2 13.1 %collective-permute-start.9 = (bf16[32,7424]{1,0:T(8,128)(2,1)S(1)}, bf16[32,7424]{1,0:T(8,128)(2,1)S(1)}, u32[]{:S(2)}, u32[]{:S(2)}) collective-permute-start(bf16[32,7424]{1,0:T(8,128)(2,1)S(1)} %get-tuple-element.79), channel_id=1, source_target_pairs={{0,2},{1,3},{2,0},{3,1},{4,6},{5,7},{6,4},{7,5},{8,10},{9,11},{10,... | collective-permute-start | bytes 1425416 | tf_op jit(solution)/shard_map/ppermute | solution.py:277
  39.3 1.6 %collective-permute-start.11 = (bf16[16,7424]{1,0:T(8,128)(2,1)S(1)}, bf16[16,7424]{1,0:T(8,128)(2,1)S(1)}, u32[]{:S(2)}, u32[]{:S(2)}) collective-permute-start(bf16[16,7424]{1,0:T(8,128)(2,1)S(1)} %get-tuple-element.107), channel_id=1, source_target_pairs={{0,1},{1,0},{2,3},{3,2},{4,5},{5,4},{6,7},{7,6},{8,9},{9,8},{10,11... | collective-permute-start | bytes 712712 | tf_op jit(solution)/shard_map/ppermute | solution.py:261
  39.3 1.8 %collective-permute-start.10 = (bf16[16,7424]{1,0:T(8,128)(2,1)S(1)}, bf16[16,7424]{1,0:T(8,128)(2,1)S(1)}, u32[]{:S(2)}, u32[]{:S(2)}) collective-permute-start(bf16[16,7424]{1,0:T(8,128)(2,1)S(1)} %get-tuple-element.108), channel_id=1, source_target_pairs={{0,1},{1,0},{2,3},{3,2},{4,5},{5,4},{6,7},{7,6},{8,9},{9,8},{10,11... | collective-permute-start | bytes 712712 | tf_op jit(solution)/shard_map/ppermute | solution.py:261
  39.8 11.6 %collective-permute-start.12 = (bf16[64,2176]{1,0:T(8,128)(2,1)S(1)}, bf16[64,2176]{1,0:T(8,128)(2,1)S(1)}, u32[]{:S(2)}, u32[]{:S(2)}) collective-permute-start(bf16[64,2176]{1,0:T(8,128)(2,1)S(1)} %get-tuple-element.86), channel_id=1, source_target_pairs={{0,4},{4,0},{8,12},{12,8},{1,5},{5,1},{9,13},{13,9},{2,6},{6,2},{1... | collective-permute-start | bytes 835592 | tf_op jit(solution)/shard_map/ppermute | solution.py:294
  41.2 10.3 %collective-permute-start.13 = (bf16[32,2176]{1,0:T(8,128)(2,1)S(1)}, bf16[32,2176]{1,0:T(8,128)(2,1)S(1)}, u32[]{:S(2)}, u32[]{:S(2)}) collective-permute-start(bf16[32,2176]{1,0:T(8,128)(2,1)S(1)} %get-tuple-element.87), channel_id=1, source_target_pairs={{0,8},{4,12},{8,0},{12,4},{1,9},{5,13},{9,1},{13,5},{2,10},{6,14},... | collective-permute-start | bytes 417800 | tf_op jit(solution)/shard_map/ppermute | solution.py:281
  51.5 3.3 %collective-permute-start.16 = (bf16[16,7424]{1,0:T(8,128)(2,1)S(1)}, bf16[16,7424]{1,0:T(8,128)(2,1)S(1)}, u32[]{:S(2)}, u32[]{:S(2)}) collective-permute-start(bf16[16,7424]{1,0:T(8,128)(2,1)S(1)} %get-tuple-element.105), channel_id=1, source_target_pairs={{0,1},{1,0},{2,3},{3,2},{4,5},{5,4},{6,7},{7,6},{8,9},{9,8},{10,11... | collective-permute-start | bytes 712712 | tf_op jit(solution)/shard_map/ppermute | solution.py:261
  51.6 3.2 %collective-permute-start.15 = (bf16[16,7424]{1,0:T(8,128)(2,1)S(1)}, bf16[16,7424]{1,0:T(8,128)(2,1)S(1)}, u32[]{:S(2)}, u32[]{:S(2)}) collective-permute-start(bf16[16,7424]{1,0:T(8,128)(2,1)S(1)} %get-tuple-element.106), channel_id=1, source_target_pairs={{0,1},{1,0},{2,3},{3,2},{4,5},{5,4},{6,7},{7,6},{8,9},{9,8},{10,11... | collective-permute-start | bytes 712712 | tf_op jit(solution)/shard_map/ppermute | solution.py:261
  52.1 9.5 %collective-permute-start.14 = (bf16[64,2176]{1,0:T(8,128)(2,1)S(1)}, bf16[64,2176]{1,0:T(8,128)(2,1)S(1)}, u32[]{:S(2)}, u32[]{:S(2)}) collective-permute-start(bf16[64,2176]{1,0:T(8,128)(2,1)S(1)} %get-tuple-element.92), channel_id=1, source_target_pairs={{0,4},{4,0},{8,12},{12,8},{1,5},{5,1},{9,13},{13,9},{2,6},{6,2},{1... | collective-permute-start | bytes 835592 | tf_op jit(solution)/shard_map/ppermute | solution.py:294
  54.8 27.7 %copy-start = (bf16[8,64,2048]{2,1,0:T(8,128)(2,1)S(1)}, bf16[8,64,2048]{2,1,0:T(8,128)(2,1)}, u32[]{:S(2)}) copy-start(bf16[8,64,2048]{2,1,0:T(8,128)(2,1)} %param.8) | copy-start | bytes 6291460
  59.9 12.2 %collective-permute-start.17 = (bf16[64,2176]{1,0:T(8,128)(2,1)S(1)}, bf16[64,2176]{1,0:T(8,128)(2,1)S(1)}, u32[]{:S(2)}, u32[]{:S(2)}) collective-permute-start(bf16[64,2176]{1,0:T(8,128)(2,1)S(1)} %get-tuple-element.99), channel_id=1, source_target_pairs={{0,4},{4,0},{8,12},{12,8},{1,5},{5,1},{9,13},{13,9},{2,6},{6,2},{1... | collective-permute-start | bytes 835592 | tf_op jit(solution)/shard_map/ppermute | solution.py:294
  61.1 13.4 %collective-permute-start.18 = (bf16[32,2176]{1,0:T(8,128)(2,1)S(1)}, bf16[32,2176]{1,0:T(8,128)(2,1)S(1)}, u32[]{:S(2)}, u32[]{:S(2)}) collective-permute-start(bf16[32,2176]{1,0:T(8,128)(2,1)S(1)} %get-tuple-element.102), channel_id=1, source_target_pairs={{0,8},{4,12},{8,0},{12,4},{1,9},{5,13},{9,1},{13,5},{2,10},{6,14},... | collective-permute-start | bytes 417800 | tf_op jit(solution)/shard_map/ppermute | solution.py:281
  61.7 18.8 %collective-permute-start.19 = (bf16[32,2176]{1,0:T(8,128)(2,1)S(1)}, bf16[32,2176]{1,0:T(8,128)(2,1)S(1)}, u32[]{:S(2)}, u32[]{:S(2)}) collective-permute-start(bf16[32,2176]{1,0:T(8,128)(2,1)S(1)} %get-tuple-element.103), channel_id=1, source_target_pairs={{0,8},{4,12},{8,0},{12,4},{1,9},{5,13},{9,1},{13,5},{2,10},{6,14},... | collective-permute-start | bytes 417800 | tf_op jit(solution)/shard_map/ppermute | solution.py:296
  72.2 10.3 %collective-permute-start.20 = (bf16[32,2176]{1,0:T(8,128)(2,1)S(1)}, bf16[32,2176]{1,0:T(8,128)(2,1)S(1)}, u32[]{:S(2)}, u32[]{:S(2)}) collective-permute-start(bf16[32,2176]{1,0:T(8,128)(2,1)S(1)} %get-tuple-element.104), channel_id=1, source_target_pairs={{0,8},{4,12},{8,0},{12,4},{1,9},{5,13},{9,1},{13,5},{2,10},{6,14},... | collective-permute-start | bytes 417800 | tf_op jit(solution)/shard_map/ppermute | solution.py:296

commit v5 on v4

--- a/solution.py
+++ b/solution.py
@@ -280,17 +280,13 @@
             passed, send = after((passed, send))
             gots.append(lax.ppermute(send, "tensor", far_z))
         send, keep = product(step, passed, token)
+        near = slice(step - 2, step - 1) if step > 1 else slice(0, 0)
+        send, gots[near] = after((send, gots[near]))
         if step + 1 < steps:
-            if step + 2 < steps:
-                send, pieces[step + 2] = after((send, pieces[step + 2]))
             earlier = parts[step - 1 : step] if step else []
-            direct[step + 1], send, earlier, done = after(
-                (direct[step + 1], send, earlier, gots[step - 2 : step - 1] if step > 1 else [])
-            )
+            direct[step + 1], send, earlier = after((direct[step + 1], send, earlier))
             if step:
                 parts[step - 1] = earlier[0]
-            if done:
-                gots[step - 2] = done[0]
         parts.append((keep, lax.ppermute(send, "tensor", next_z)))
     for step in range(steps - 2, steps):
         gots.append(lax.ppermute(add_part(step), "tensor", far_z))

time: 83.9 us -> 83.6 us (level)
  waiting for transfers between devices: 26.4 us -> 21.9 us
  starting transfers between devices: 21.2 us -> 25.5 us
    ppermute x2, starting transfers between devices: 3.04 us -> 5.3 us  [paired(): gots.append(lax.ppermute(send, 'tensor', far_z))]
    ppermute x8, waiting for transfers between devices: 3.33 us -> 1.25 us  [over_core(): lax.ppermute(cut, 'req', beside)]
    ppermute x3, waiting for transfers between devices: 4.6 us -> 3.03 us  [paired(): direct.append(lax.ppermute(pieces[step + 1], 'req', across))]
    ppermute x4, waiting for transfers between devices: 10 us -> 8.5 us  [paired(): parts.append((keep, lax.ppermute(send, 'tensor', next_z)))]
    ppermute x3, starting transfers between devices: 2.16 us -> 3.52 us  [paired(): direct.append(lax.ppermute(pieces[step + 1], 'req', across))]
  transfers between devices with their start and end apart: 21 -> 21, of which waited for: 14 -> 10; matrix products, arithmetic and copies ran while one was open for 0% -> 0% of each run, Pallas kernels for 39% -> 39%
where the time goes in v5:
time: 83.6 us; the launch traced here: 83.5 us
  Pallas kernels  35.8 us (43%)
  starting transfers between devices  25.5 us (31%)
  waiting for transfers between devices  21.9 us (26%)
    pallas_call x4, Pallas kernels, product(): pl.pallas_call(functools.partial(product_kernel, adapters, units, starts[...  20.5 us
    pallas_call x1, Pallas kernels, paired(): pl.pallas_call(load_kernel, out_shape=[jax.ShapeDtypeStruct((8, LANES), j...  11.9 us
    ppermute x4, waiting for transfers between devices, paired(): parts.append((keep, lax.ppermute(send, 'tensor', next_z)))  8.5 us
    ppermute x2, waiting for transfers between devices, paired(): gots.append(lax.ppermute(add_part(step), 'tensor', far_z))  7.76 us
    ppermute x4, starting transfers between devices, paired(): parts.append((keep, lax.ppermute(send, 'tensor', next_z)))  6.77 us
    ppermute x2, starting transfers between devices, paired(): gots.append(lax.ppermute(send, 'tensor', far_z))  5.3 us
    ppermute x2, starting transfers between devices, paired(): gots.append(lax.ppermute(add_part(step), 'tensor', far_z))  4.55 us
    ppermute x3, starting transfers between devices, paired(): direct.append(lax.ppermute(pieces[step + 1], 'req', across))  3.52 us
  transfers between devices with their start and end apart: 21, of which 10 were waited for; matrix products, arithmetic and copies ran while one was open for 0% of the time, Pallas kernels for 39%

profile of v5, /device:TPU:0, one launch (start us, length us, event | category | flops | bytes accessed | tf_op | source)
XLA Modules:
  0.0 83.5 jit_solution(12311109743912203199)
XLA Ops:
  0.0 1.8 %turn.1 = (bf16[128,7424]{1,0:T(8,128)(2,1)S(1)}, bf16[32,7424]{1,0:T(8,128)(2,1)S(1)}, bf16[32,7424]{1,0:T(8,128)(2,1)S(1)}, bf16[32,7424]{1,0:T(8,128)(2,1)S(1)}, bf16[32,7424]{1,0:T(8,128)(2,1)S(1)}) custom-call(bf16[7392,128]{1,0:T(8,128)(2,1)} %bitcast.8, s32[1,128]{1,0:T(1,128)} %bitcast.9), custom_call_target="tpu_custom_call" | custom-call | tf_op jit(solution)/shard_map/turn/pallas_call | solution.py:197
  1.8 3.0 %collective-permute-start.1 = (bf16[32,7424]{1,0:T(8,128)(2,1)S(1)}, bf16[32,7424]{1,0:T(8,128)(2,1)S(1)}, u32[]{:S(2)}, u32[]{:S(2)}) collective-permute-start(bf16[32,7424]{1,0:T(8,128)(2,1)S(1)} %get-tuple-element.55), channel_id=1, source_target_pairs={{0,2},{1,3},{2,0},{3,1},{4,6},{5,7},{6,4},{7,5},{8,10},{9,11},{10,... | collective-permute-start | bytes 1425416 | tf_op jit(solution)/shard_map/ppermute | solution.py:216
  4.9 11.9 %load.1 = (f32[8,128]{1,0:T(8,128)S(1)}, bf16[7424,512]{1,0:T(8,128)(2,1)S(1)}, bf16[7424,512]{1,0:T(8,128)(2,1)S(1)}, bf16[7424,512]{1,0:T(8,128)(2,1)S(1)}, bf...) custom-call(bf16[7392,2048]{1,0:T(8,128)(2,1)} %w_hbm.1, bf16[512,7392]{1,0:T(8,128)(2,1)} %bitcast.7), custom_call_target="tpu_custom_call" | custom-call | flops 1 | bytes 1 | tf_op jit(solution)/shard_map/load/pallas_call | solution.py:220
  17.5 1.9 %collective-permute-start = (bf16[32,7424]{1,0:T(8,128)(2,1)S(1)}, bf16[32,7424]{1,0:T(8,128)(2,1)S(1)}, u32[]{:S(2)}, u32[]{:S(2)}) collective-permute-start(bf16[32,7424]{1,0:T(8,128)(2,1)S(1)} %get-tuple-element.54), channel_id=1, source_target_pairs={{0,2},{1,3},{2,0},{3,1},{4,6},{5,7},{6,4},{7,5},{8,10},{9,11},{10,... | collective-permute-start | bytes 1425416 | tf_op jit(solution)/shard_map/ppermute | solution.py:277
  19.5 5.1 %product.4 = (bf16[64,2176]{1,0:T(8,128)(2,1)S(1)}, bf16[64,2176]{1,0:T(8,128)(2,1)S(1)}) custom-call(f32[8,128]{1,0:T(8,128)S(1)} %get-tuple-element.57._, bf16[128,7424]{1,0:T(8,128)(2,1)S(1)} %get-tuple-element.58.own_ref, bf16[128,7424]{1,0:T(8,128)(2,1)S(1)} %collective-permute-done.2.other_ref, bf16[32,7424]{1,0:T(8,128)(2,1)S(1)} %collective-permute-done.1.direct_ref, ...), custom_call_target="tpu_custom_call" | custom-call | flops 1 | bytes 1 | tf_op jit(solution)/shard_map/product/pallas_call | solution.py:238
  24.5 2.2 %collective-permute-done.3.direct_ref = bf16[32,7424]{1,0:T(8,128)(2,1)S(1)} collective-permute-done((bf16[32,7424]{1,0:T(8,128)(2,1)S(1)}, bf16[32,7424]{1,0:T(8,128)(2,1)S(1)}, u32[]{:S(2)}, u32[]{:S(2)}) %collective-permute-start.3) | collective-permute-done | bytes 475168 | tf_op jit(solution)/shard_map/ppermute | solution.py:277
  26.7 2.1 %collective-permute-start.8 = (bf16[64,2176]{1,0:T(8,128)(2,1)S(1)}, bf16[64,2176]{1,0:T(8,128)(2,1)S(1)}, u32[]{:S(2)}, u32[]{:S(2)}) collective-permute-start(bf16[64,2176]{1,0:T(8,128)(2,1)S(1)} %get-tuple-element.70), channel_id=1, source_target_pairs={{0,4},{4,0},{8,12},{12,8},{1,5},{5,1},{9,13},{13,9},{2,6},{6,2},{1... | collective-permute-start | bytes 835592 | tf_op jit(solution)/shard_map/ppermute | solution.py:290
  29.5 1.5 %collective-permute-start.9 = (bf16[32,7424]{1,0:T(8,128)(2,1)S(1)}, bf16[32,7424]{1,0:T(8,128)(2,1)S(1)}, u32[]{:S(2)}, u32[]{:S(2)}) collective-permute-start(bf16[32,7424]{1,0:T(8,128)(2,1)S(1)} %get-tuple-element.74), channel_id=1, source_target_pairs={{0,2},{1,3},{2,0},{3,1},{4,6},{5,7},{6,4},{7,5},{8,10},{9,11},{10,... | collective-permute-start | bytes 1425416 | tf_op jit(solution)/shard_map/ppermute | solution.py:277
  31.0 5.1 %product.5 = (bf16[64,2176]{1,0:T(8,128)(2,1)S(1)}, bf16[64,2176]{1,0:T(8,128)(2,1)S(1)}) custom-call(f32[8,128]{1,0:T(8,128)S(1)} %get-tuple-element.57._, bf16[128,7424]{1,0:T(8,128)(2,1)S(1)} %get-tuple-element.58.own_ref, bf16[128,7424]{1,0:T(8,128)(2,1)S(1)} %collective-permute-done.2.other_ref, bf16[32,7424]{1,0:T(8,128)(2,1)S(1)} %collective-permute-done.3.direct_ref, ...), custom_call_target="tpu_custom_call" | custom-call | flops 1 | bytes 1 | tf_op jit(solution)/shard_map/product/pallas_call | solution.py:238
  36.0 0.9 %collective-permute-done.direct_ref = bf16[32,7424]{1,0:T(8,128)(2,1)S(1)} collective-permute-done((bf16[32,7424]{1,0:T(8,128)(2,1)S(1)}, bf16[32,7424]{1,0:T(8,128)(2,1)S(1)}, u32[]{:S(2)}, u32[]{:S(2)}) %collective-permute-start) | collective-permute-done | bytes 475168 | tf_op jit(solution)/shard_map/ppermute | solution.py:277
  37.5 2.1 %collective-permute-start.13 = (bf16[64,2176]{1,0:T(8,128)(2,1)S(1)}, bf16[64,2176]{1,0:T(8,128)(2,1)S(1)}, u32[]{:S(2)}, u32[]{:S(2)}) collective-permute-start(bf16[64,2176]{1,0:T(8,128)(2,1)S(1)} %get-tuple-element.83), channel_id=1, source_target_pairs={{0,4},{4,0},{8,12},{12,8},{1,5},{5,1},{9,13},{13,9},{2,6},{6,2},{1... | collective-permute-start | bytes 835592 | tf_op jit(solution)/shard_map/ppermute | solution.py:290
  39.8 2.7 %collective-permute-start.12 = (bf16[32,2176]{1,0:T(8,128)(2,1)S(1)}, bf16[32,2176]{1,0:T(8,128)(2,1)S(1)}, u32[]{:S(2)}, u32[]{:S(2)}) collective-permute-start(bf16[32,2176]{1,0:T(8,128)(2,1)S(1)} %get-tuple-element.80), channel_id=1, source_target_pairs={{0,8},{4,12},{8,0},{12,4},{1,9},{5,13},{9,1},{13,5},{2,10},{6,14},... | collective-permute-start | bytes 417800 | tf_op jit(solution)/shard_map/ppermute | solution.py:281
  42.4 5.3 %product.6 = (bf16[64,2176]{1,0:T(8,128)(2,1)S(1)}, bf16[64,2176]{1,0:T(8,128)(2,1)S(1)}) custom-call(f32[8,128]{1,0:T(8,128)S(1)} %get-tuple-element.57._, bf16[128,7424]{1,0:T(8,128)(2,1)S(1)} %get-tuple-element.58.own_ref, bf16[128,7424]{1,0:T(8,128)(2,1)S(1)} %collective-permute-done.2.other_ref, bf16[32,7424]{1,0:T(8,128)(2,1)S(1)} %collective-permute-done.direct_ref, ...), custom_call_target="tpu_custom_call" | custom-call | flops 1 | bytes 1 | tf_op jit(solution)/shard_map/product/pallas_call | solution.py:238
  47.7 1.1 %collective-permute-done.12.refs_4_ = bf16[32,2176]{1,0:T(8,128)(2,1)S(1)} collective-permute-done((bf16[32,2176]{1,0:T(8,128)(2,1)S(1)}, bf16[32,2176]{1,0:T(8,128)(2,1)S(1)}, u32[]{:S(2)}, u32[]{:S(2)}) %collective-permute-start.12) | collective-permute-done | bytes 139296 | tf_op jit(solution)/shard_map/ppermute | solution.py:281
  50.2 0.9 %collective-permute-done.16.passed_b = bf16[16,7424]{1,0:T(8,128)(2,1)S(1)} collective-permute-done((bf16[16,7424]{1,0:T(8,128)(2,1)S(1)}, bf16[16,7424]{1,0:T(8,128)(2,1)S(1)}, u32[]{:S(2)}, u32[]{:S(2)}) %collective-permute-start.16) | collective-permute-done | bytes 237600 | tf_op jit(solution)/shard_map/ppermute | solution.py:261
  51.5 2.7 %collective-permute-start.17 = (bf16[32,2176]{1,0:T(8,128)(2,1)S(1)}, bf16[32,2176]{1,0:T(8,128)(2,1)S(1)}, u32[]{:S(2)}, u32[]{:S(2)}) collective-permute-start(bf16[32,2176]{1,0:T(8,128)(2,1)S(1)} %get-tuple-element.96), channel_id=1, source_target_pairs={{0,8},{4,12},{8,0},{12,4},{1,9},{5,13},{9,1},{13,5},{2,10},{6,14},... | collective-permute-start | bytes 417800 | tf_op jit(solution)/shard_map/ppermute | solution.py:281
  54.1 1.7 %collective-permute-start.14 = (bf16[64,2176]{1,0:T(8,128)(2,1)S(1)}, bf16[64,2176]{1,0:T(8,128)(2,1)S(1)}, u32[]{:S(2)}, u32[]{:S(2)}) collective-permute-start(bf16[64,2176]{1,0:T(8,128)(2,1)S(1)} %get-tuple-element.88), channel_id=1, source_target_pairs={{0,4},{4,0},{8,12},{12,8},{1,5},{5,1},{9,13},{13,9},{2,6},{6,2},{1... | collective-permute-start | bytes 835592 | tf_op jit(solution)/shard_map/ppermute | solution.py:290
  55.8 5.1 %product.7 = (bf16[64,2176]{1,0:T(8,128)(2,1)S(1)}, bf16[64,2176]{1,0:T(8,128)(2,1)S(1)}) custom-call(f32[8,128]{1,0:T(8,128)S(1)} %get-tuple-element.57._, bf16[128,7424]{1,0:T(8,128)(2,1)S(1)} %get-tuple-element.58.own_ref, bf16[128,7424]{1,0:T(8,128)(2,1)S(1)} %collective-permute-done.2.other_ref, bf16[32,7424]{1,0:T(8,128)(2,1)S(1)} %collective-permute-done.9.direct_ref, ...), custom_call_target="tpu_custom_call" | custom-call | flops 1 | bytes 1 | tf_op jit(solution)/shard_map/product/pallas_call | solution.py:238
  61.9 2.4 %collective-permute-done.14.second_ref = bf16[64,2176]{1,0:T(8,128)(2,1)S(1)} collective-permute-done((bf16[64,2176]{1,0:T(8,128)(2,1)S(1)}, bf16[64,2176]{1,0:T(8,128)(2,1)S(1)}, u32[]{:S(2)}, u32[]{:S(2)}) %collective-permute-start.14) | collective-permute-done | bytes 278560 | tf_op jit(solution)/shard_map/ppermute | solution.py:290
  64.4 3.3 %collective-permute-start.19 = (bf16[32,2176]{1,0:T(8,128)(2,1)S(1)}, bf16[32,2176]{1,0:T(8,128)(2,1)S(1)}, u32[]{:S(2)}, u32[]{:S(2)}) collective-permute-start(bf16[32,2176]{1,0:T(8,128)(2,1)S(1)} %get-tuple-element.101), channel_id=1, source_target_pairs={{0,8},{4,12},{8,0},{12,4},{1,9},{5,13},{9,1},{13,5},{2,10},{6,14},... | collective-permute-start | bytes 417800 | tf_op jit(solution)/shard_map/ppermute | solution.py:292
  67.7 5.3 %collective-permute-done.18.second_ref = bf16[64,2176]{1,0:T(8,128)(2,1)S(1)} collective-permute-done((bf16[64,2176]{1,0:T(8,128)(2,1)S(1)}, bf16[64,2176]{1,0:T(8,128)(2,1)S(1)}, u32[]{:S(2)}, u32[]{:S(2)}) %collective-permute-start.18) | collective-permute-done | bytes 278560 | tf_op jit(solution)/shard_map/ppermute | solution.py:290
  73.2 1.3 %collective-permute-start.20 = (bf16[32,2176]{1,0:T(8,128)(2,1)S(1)}, bf16[32,2176]{1,0:T(8,128)(2,1)S(1)}, u32[]{:S(2)}, u32[]{:S(2)}) collective-permute-start(bf16[32,2176]{1,0:T(8,128)(2,1)S(1)} %get-tuple-element.102), channel_id=1, source_target_pairs={{0,8},{4,12},{8,0},{12,4},{1,9},{5,13},{9,1},{13,5},{2,10},{6,14},... | collective-permute-start | bytes 417800 | tf_op jit(solution)/shard_map/ppermute | solution.py:292
  74.4 7.8 %collective-permute-done.20.refs_7_ = bf16[32,2176]{1,0:T(8,128)(2,1)S(1)} collective-permute-done((bf16[32,2176]{1,0:T(8,128)(2,1)S(1)}, bf16[32,2176]{1,0:T(8,128)(2,1)S(1)}, u32[]{:S(2)}, u32[]{:S(2)}) %collective-permute-start.20) | collective-permute-done | bytes 139296 | tf_op jit(solution)/shard_map/ppermute | solution.py:292
  82.2 1.3 %last.1 = bf16[128,2048]{1,0:T(8,128)(2,1)} custom-call(bf16[512,2048]{1,0:T(8,128)(2,1)S(1)} %bitcast.6, bf16[32,2176]{1,0:T(8,128)(2,1)S(1)} %get-tuple-element.73.refs_0_, bf16[32,2176]{1,0:T(8,128)(2,1)S(1)} %get-tuple-element.86.refs_1_, bf16[32,2176]{1,0:T(8,128)(2,1)S(1)} %get-tuple-element.89.refs_2_, ...), custom_call_target="tpu_custom_call" | custom-call | tf_op jit(solution)/shard_map/last/pallas_call | solution.py:294
  (35 shorter events, 5.0 us)
Async XLA Ops:
  1.8 15.0 %collective-permute-start.1 = (bf16[32,7424]{1,0:T(8,128)(2,1)S(1)}, bf16[32,7424]{1,0:T(8,128)(2,1)S(1)}, u32[]{:S(2)}, u32[]{:S(2)}) collective-permute-start(bf16[32,7424]{1,0:T(8,128)(2,1)S(1)} %get-tuple-element.55), channel_id=1, source_target_pairs={{0,2},{1,3},{2,0},{3,1},{4,6},{5,7},{6,4},{7,5},{8,10},{9,11},{10,... | collective-permute-start | bytes 1425416 | tf_op jit(solution)/shard_map/ppermute | solution.py:216
  4.8 21.9 %collective-permute-start.3 = (bf16[32,7424]{1,0:T(8,128)(2,1)S(1)}, bf16[32,7424]{1,0:T(8,128)(2,1)S(1)}, u32[]{:S(2)}, u32[]{:S(2)}) collective-permute-start(bf16[32,7424]{1,0:T(8,128)(2,1)S(1)} %get-tuple-element.59), channel_id=1, source_target_pairs={{0,2},{1,3},{2,0},{3,1},{4,6},{5,7},{6,4},{7,5},{8,10},{9,11},{10,... | collective-permute-start | bytes 1425416 | tf_op jit(solution)/shard_map/ppermute | solution.py:277
  4.9 14.5 %collective-permute-start.2 = (bf16[128,7424]{1,0:T(8,128)(2,1)S(1)}, bf16[128,7424]{1,0:T(8,128)(2,1)S(1)}, u32[]{:S(2)}, u32[]{:S(2)}) collective-permute-start(bf16[128,7424]{1,0:T(8,128)(2,1)S(1)} %get-tuple-element.58.own_ref), channel_id=1, source_target_pairs={{0,1},{1,0},{2,3},{3,2},{4,5},{5,4},{6,7},{7,6},{8,9},{9,8},{10,11... | collective-permute-start | bytes 5701640 | tf_op jit(solution)/shard_map/ppermute | solution.py:217
  16.8 2.6 %collective-permute-start.5 = (bf16[16,7424]{1,0:T(8,128)(2,1)S(1)}, bf16[16,7424]{1,0:T(8,128)(2,1)S(1)}, u32[]{:S(2)}, u32[]{:S(2)}) collective-permute-start(bf16[16,7424]{1,0:T(8,128)(2,1)S(1)} %get-tuple-element.109), channel_id=1, source_target_pairs={{0,1},{1,0},{2,3},{3,2},{4,5},{5,4},{6,7},{7,6},{8,9},{9,8},{10,11... | collective-permute-start | bytes 712712 | tf_op jit(solution)/shard_map/ppermute | solution.py:261
  17.4 2.0 %collective-permute-start.4 = (bf16[16,7424]{1,0:T(8,128)(2,1)S(1)}, bf16[16,7424]{1,0:T(8,128)(2,1)S(1)}, u32[]{:S(2)}, u32[]{:S(2)}) collective-permute-start(bf16[16,7424]{1,0:T(8,128)(2,1)S(1)} %get-tuple-element.110), channel_id=1, source_target_pairs={{0,1},{1,0},{2,3},{3,2},{4,5},{5,4},{6,7},{7,6},{8,9},{9,8},{10,11... | collective-permute-start | bytes 712712 | tf_op jit(solution)/shard_map/ppermute | solution.py:261
  17.5 19.4 %collective-permute-start = (bf16[32,7424]{1,0:T(8,128)(2,1)S(1)}, bf16[32,7424]{1,0:T(8,128)(2,1)S(1)}, u32[]{:S(2)}, u32[]{:S(2)}) collective-permute-start(bf16[32,7424]{1,0:T(8,128)(2,1)S(1)} %get-tuple-element.54), channel_id=1, source_target_pairs={{0,2},{1,3},{2,0},{3,1},{4,6},{5,7},{6,4},{7,5},{8,10},{9,11},{10,... | collective-permute-start | bytes 1425416 | tf_op jit(solution)/shard_map/ppermute | solution.py:277
  26.7 10.2 %collective-permute-start.8 = (bf16[64,2176]{1,0:T(8,128)(2,1)S(1)}, bf16[64,2176]{1,0:T(8,128)(2,1)S(1)}, u32[]{:S(2)}, u32[]{:S(2)}) collective-permute-start(bf16[64,2176]{1,0:T(8,128)(2,1)S(1)} %get-tuple-element.70), channel_id=1, source_target_pairs={{0,4},{4,0},{8,12},{12,8},{1,5},{5,1},{9,13},{13,9},{2,6},{6,2},{1... | collective-permute-start | bytes 835592 | tf_op jit(solution)/shard_map/ppermute | solution.py:290
  28.9 2.1 %collective-permute-start.7 = (bf16[16,7424]{1,0:T(8,128)(2,1)S(1)}, bf16[16,7424]{1,0:T(8,128)(2,1)S(1)}, u32[]{:S(2)}, u32[]{:S(2)}) collective-permute-start(bf16[16,7424]{1,0:T(8,128)(2,1)S(1)} %get-tuple-element.107), channel_id=1, source_target_pairs={{0,1},{1,0},{2,3},{3,2},{4,5},{5,4},{6,7},{7,6},{8,9},{9,8},{10,11... | collective-permute-start | bytes 712712 | tf_op jit(solution)/shard_map/ppermute | solution.py:261
  29.0 2.0 %collective-permute-start.6 = (bf16[16,7424]{1,0:T(8,128)(2,1)S(1)}, bf16[16,7424]{1,0:T(8,128)(2,1)S(1)}, u32[]{:S(2)}, u32[]{:S(2)}) collective-permute-start(bf16[16,7424]{1,0:T(8,128)(2,1)S(1)} %get-tuple-element.108), channel_id=1, source_target_pairs={{0,1},{1,0},{2,3},{3,2},{4,5},{5,4},{6,7},{7,6},{8,9},{9,8},{10,11... | collective-permute-start | bytes 712712 | tf_op jit(solution)/shard_map/ppermute | solution.py:261
  29.5 19.3 %collective-permute-start.9 = (bf16[32,7424]{1,0:T(8,128)(2,1)S(1)}, bf16[32,7424]{1,0:T(8,128)(2,1)S(1)}, u32[]{:S(2)}, u32[]{:S(2)}) collective-permute-start(bf16[32,7424]{1,0:T(8,128)(2,1)S(1)} %get-tuple-element.74), channel_id=1, source_target_pairs={{0,2},{1,3},{2,0},{3,1},{4,6},{5,7},{6,4},{7,5},{8,10},{9,11},{10,... | collective-permute-start | bytes 1425416 | tf_op jit(solution)/shard_map/ppermute | solution.py:277
  36.9 2.8 %collective-permute-start.11 = (bf16[16,7424]{1,0:T(8,128)(2,1)S(1)}, bf16[16,7424]{1,0:T(8,128)(2,1)S(1)}, u32[]{:S(2)}, u32[]{:S(2)}) collective-permute-start(bf16[16,7424]{1,0:T(8,128)(2,1)S(1)} %get-tuple-element.105), channel_id=1, source_target_pairs={{0,1},{1,0},{2,3},{3,2},{4,5},{5,4},{6,7},{7,6},{8,9},{9,8},{10,11... | collective-permute-start | bytes 712712 | tf_op jit(solution)/shard_map/ppermute | solution.py:261
  37.0 2.7 %collective-permute-start.10 = (bf16[16,7424]{1,0:T(8,128)(2,1)S(1)}, bf16[16,7424]{1,0:T(8,128)(2,1)S(1)}, u32[]{:S(2)}, u32[]{:S(2)}) collective-permute-start(bf16[16,7424]{1,0:T(8,128)(2,1)S(1)} %get-tuple-element.106), channel_id=1, source_target_pairs={{0,1},{1,0},{2,3},{3,2},{4,5},{5,4},{6,7},{7,6},{8,9},{9,8},{10,11... | collective-permute-start | bytes 712712 | tf_op jit(solution)/shard_map/ppermute | solution.py:261
  37.5 12.0 %collective-permute-start.13 = (bf16[64,2176]{1,0:T(8,128)(2,1)S(1)}, bf16[64,2176]{1,0:T(8,128)(2,1)S(1)}, u32[]{:S(2)}, u32[]{:S(2)}) collective-permute-start(bf16[64,2176]{1,0:T(8,128)(2,1)S(1)} %get-tuple-element.83), channel_id=1, source_target_pairs={{0,4},{4,0},{8,12},{12,8},{1,5},{5,1},{9,13},{13,9},{2,6},{6,2},{1... | collective-permute-start | bytes 835592 | tf_op jit(solution)/shard_map/ppermute | solution.py:290
  39.8 9.0 %collective-permute-start.12 = (bf16[32,2176]{1,0:T(8,128)(2,1)S(1)}, bf16[32,2176]{1,0:T(8,128)(2,1)S(1)}, u32[]{:S(2)}, u32[]{:S(2)}) collective-permute-start(bf16[32,2176]{1,0:T(8,128)(2,1)S(1)} %get-tuple-element.80), channel_id=1, source_target_pairs={{0,8},{4,12},{8,0},{12,4},{1,9},{5,13},{9,1},{13,5},{2,10},{6,14},... | collective-permute-start | bytes 417800 | tf_op jit(solution)/shard_map/ppermute | solution.py:281
  49.6 1.6 %collective-permute-start.16 = (bf16[16,7424]{1,0:T(8,128)(2,1)S(1)}, bf16[16,7424]{1,0:T(8,128)(2,1)S(1)}, u32[]{:S(2)}, u32[]{:S(2)}) collective-permute-start(bf16[16,7424]{1,0:T(8,128)(2,1)S(1)} %get-tuple-element.103), channel_id=1, source_target_pairs={{0,1},{1,0},{2,3},{3,2},{4,5},{5,4},{6,7},{7,6},{8,9},{9,8},{10,11... | collective-permute-start | bytes 712712 | tf_op jit(solution)/shard_map/ppermute | solution.py:261
  49.6 1.8 %collective-permute-start.15 = (bf16[16,7424]{1,0:T(8,128)(2,1)S(1)}, bf16[16,7424]{1,0:T(8,128)(2,1)S(1)}, u32[]{:S(2)}, u32[]{:S(2)}) collective-permute-start(bf16[16,7424]{1,0:T(8,128)(2,1)S(1)} %get-tuple-element.104), channel_id=1, source_target_pairs={{0,1},{1,0},{2,3},{3,2},{4,5},{5,4},{6,7},{7,6},{8,9},{9,8},{10,11... | collective-permute-start | bytes 712712 | tf_op jit(solution)/shard_map/ppermute | solution.py:261
  51.5 30.7 %copy-start = (bf16[8,64,2048]{2,1,0:T(8,128)(2,1)S(1)}, bf16[8,64,2048]{2,1,0:T(8,128)(2,1)}, u32[]{:S(2)}) copy-start(bf16[8,64,2048]{2,1,0:T(8,128)(2,1)} %param.8) | copy-start | bytes 6291460
  51.5 9.6 %collective-permute-start.17 = (bf16[32,2176]{1,0:T(8,128)(2,1)S(1)}, bf16[32,2176]{1,0:T(8,128)(2,1)S(1)}, u32[]{:S(2)}, u32[]{:S(2)}) collective-permute-start(bf16[32,2176]{1,0:T(8,128)(2,1)S(1)} %get-tuple-element.96), channel_id=1, source_target_pairs={{0,8},{4,12},{8,0},{12,4},{1,9},{5,13},{9,1},{13,5},{2,10},{6,14},... | collective-permute-start | bytes 417800 | tf_op jit(solution)/shard_map/ppermute | solution.py:281
  54.1 10.2 %collective-permute-start.14 = (bf16[64,2176]{1,0:T(8,128)(2,1)S(1)}, bf16[64,2176]{1,0:T(8,128)(2,1)S(1)}, u32[]{:S(2)}, u32[]{:S(2)}) collective-permute-start(bf16[64,2176]{1,0:T(8,128)(2,1)S(1)} %get-tuple-element.88), channel_id=1, source_target_pairs={{0,4},{4,0},{8,12},{12,8},{1,5},{5,1},{9,13},{13,9},{2,6},{6,2},{1... | collective-permute-start | bytes 835592 | tf_op jit(solution)/shard_map/ppermute | solution.py:290
  61.1 12.0 %collective-permute-start.18 = (bf16[64,2176]{1,0:T(8,128)(2,1)S(1)}, bf16[64,2176]{1,0:T(8,128)(2,1)S(1)}, u32[]{:S(2)}, u32[]{:S(2)}) collective-permute-start(bf16[64,2176]{1,0:T(8,128)(2,1)S(1)} %get-tuple-element.97), channel_id=1, source_target_pairs={{0,4},{4,0},{8,12},{12,8},{1,5},{5,1},{9,13},{13,9},{2,6},{6,2},{1... | collective-permute-start | bytes 835592 | tf_op jit(solution)/shard_map/ppermute | solution.py:290
  64.4 10.0 %collective-permute-start.19 = (bf16[32,2176]{1,0:T(8,128)(2,1)S(1)}, bf16[32,2176]{1,0:T(8,128)(2,1)S(1)}, u32[]{:S(2)}, u32[]{:S(2)}) collective-permute-start(bf16[32,2176]{1,0:T(8,128)(2,1)S(1)} %get-tuple-element.101), channel_id=1, source_target_pairs={{0,8},{4,12},{8,0},{12,4},{1,9},{5,13},{9,1},{13,5},{2,10},{6,14},... | collective-permute-start | bytes 417800 | tf_op jit(solution)/shard_map/ppermute | solution.py:292
  73.2 9.0 %collective-permute-start.20 = (bf16[32,2176]{1,0:T(8,128)(2,1)S(1)}, bf16[32,2176]{1,0:T(8,128)(2,1)S(1)}, u32[]{:S(2)}, u32[]{:S(2)}) collective-permute-start(bf16[32,2176]{1,0:T(8,128)(2,1)S(1)} %get-tuple-element.102), channel_id=1, source_target_pairs={{0,8},{4,12},{8,0},{12,4},{1,9},{5,13},{9,1},{13,5},{2,10},{6,14},... | collective-permute-start | bytes 417800 | tf_op jit(solution)/shard_map/ppermute | solution.py:292

commit v6 on v5

--- a/solution.py
+++ b/solution.py
@@ -12,6 +12,7 @@
 DEPTH = 1024
 TURN = 15
 PIECES = (32, 32, 32, 32)
+CUTS = 4
 MIB = 1 << 20
 
 
@@ -101,22 +102,21 @@
         keep_ref[at, cols] = jnp.where(keep_first, first, second)
 
 
-def product_kernel(
-    adapters, units, at, _, own_ref, other_ref, direct_ref, passed_a, passed_b, *refs
-):
+def product_kernel(adapters, units, at, _, own_ref, other_ref, direct_ref, *refs):
+    passed_refs, refs = refs[:CUTS], refs[CUTS:]
     *panel_refs, spread_ref, send_ref, keep_ref = refs
     rows = direct_ref.shape[0]
     width = send_ref.shape[1] - LANES
     wide = spread_ref.shape[1]
     rank = wide // adapters
 
-    def pieces(cols):
-        near = [ref[at : at + rows, cols] for ref in (own_ref, other_ref)]
-        far = [ref[:, cols] for ref in (direct_ref, passed_a, passed_b)]
-        return jnp.concatenate(near + far, axis=0)
-
-    every = jnp.dot(pieces(slice(None)), spread_ref[...], preferred_element_type=jnp.float32)
-    ids = pieces(slice(units, units + 1)).astype(jnp.float32)
+    def piece():
+        near = [own_ref[at : at + rows, :], other_ref[at : at + rows, :]]
+        passed = jnp.concatenate([ref[...] for ref in passed_refs], axis=1)
+        return jnp.concatenate([*near, direct_ref[...], passed], axis=0)
+
+    every = jnp.dot(piece(), spread_ref[...], preferred_element_type=jnp.float32)
+    ids = piece()[:, units : units + 1].astype(jnp.float32)
     column = lax.broadcasted_iota(jnp.int32, every.shape, 1) // rank
     picked = jnp.where(column.astype(jnp.float32) == ids, every, 0.0)
     tile = picked[:, :LANES]
@@ -129,7 +129,7 @@
 
     for panel, panel_ref in enumerate(panel_refs):
         value = jnp.dot(
-            pieces(slice(None)), panel_ref[...], preferred_element_type=jnp.float32
+            piece(), panel_ref[...], preferred_element_type=jnp.float32
         )
         part_rows(value, slice(panel * PANEL, (panel + 1) * PANEL), send_ref, keep_ref)
 
@@ -238,7 +238,7 @@
         return pl.pallas_call(
             functools.partial(product_kernel, adapters, units, starts[step]),
             out_shape=[struct(2 * counts[step], payload)] * 2,
-            in_specs=[in_vmem()] * (6 + len(both)),
+            in_specs=[in_vmem()] * (4 + CUTS + len(both)),
             out_specs=[in_vmem()] * 2,
             compiler_params=params(4),
             cost_estimate=quick,
@@ -257,8 +257,11 @@
         )(keep, got)
 
     def over_core(part):
-        half = part.shape[0] // 2
-        return [lax.ppermute(cut, "req", beside) for cut in (part[:half], part[half:])]
+        tiles = room // LANES
+        ends = [tiles * cut // CUTS * LANES for cut in range(CUTS + 1)]
+        return [
+            lax.ppermute(part[:, at:to], "req", beside) for at, to in zip(ends, ends[1:])
+        ]
 
     after = lax.optimization_barrier
     steps = len(counts)
@@ -280,14 +283,16 @@
             passed, send = after((passed, send))
             gots.append(lax.ppermute(send, "tensor", far_z))
         send, keep = product(step, passed, token)
-        near = slice(step - 2, step - 1) if step > 1 else slice(0, 0)
-        send, gots[near] = after((send, gots[near]))
+        prior, before = slice(max(step - 1, 0), step), slice(max(step - 2, 0), max(step - 1, 0))
         if step + 1 < steps:
-            earlier = parts[step - 1 : step] if step else []
-            direct[step + 1], send, earlier = after((direct[step + 1], send, earlier))
-            if step:
-                parts[step - 1] = earlier[0]
-        parts.append((keep, lax.ppermute(send, "tensor", next_z)))
+            got = lax.ppermute(send, "tensor", next_z)
+            direct[step + 1], keep, parts[prior], gots[before] = after(
+                (direct[step + 1], keep, parts[prior], gots[before])
+            )
+        else:
+            send, parts[prior], gots[before] = after((send, parts[prior], gots[before]))
+            got = lax.ppermute(send, "tensor", next_z)
+        parts.append((keep, got))
     for step in range(steps - 2, steps):
         gots.append(lax.ppermute(add_part(step), "tensor", far_z))
 

time: 83.6 us -> 83 us (level)
  starting transfers between devices: 25.5 us -> 23.7 us
  waiting for transfers between devices: 21.9 us -> 23.2 us
    ppermute x12 -> x20, waiting for transfers between devices: 9.76 us -> 13.1 us  [the longest x4 7.5 us: paired(): got = lax.ppermute(send, 'tensor', next_z)]
    ppermute x3, waiting for transfers between devices: 3.03 us -> 0.15 us  [paired(): direct.append(lax.ppermute(pieces[step + 1], 'req', across))]
    ppermute x2, waiting for transfers between devices: 1.3 us -> 3.66 us  [paired(): gots.append(lax.ppermute(send, 'tensor', far_z))]
    ppermute x2, starting transfers between devices: 5.3 us -> 3.19 us  [paired(): gots.append(lax.ppermute(send, 'tensor', far_z))]
    ppermute x2, waiting for transfers between devices: 7.76 us -> 6.29 us  [paired(): gots.append(lax.ppermute(add_part(step), 'tensor', far_z))]
    ppermute x12 -> x20, starting transfers between devices: 9.13 us -> 8.59 us  [the longest x4 4.89 us: paired(): got = lax.ppermute(send, 'tensor', next_z)]
  transfers between devices with their start and end apart: 21 -> 29, of which waited for: 10 -> 12; matrix products, arithmetic and copies ran while one was open for 0% -> 0% of each run, Pallas kernels for 39% -> 39%
where the time goes in v6:
time: 83 us; the launch traced here: 82.9 us
  Pallas kernels  35.6 us (43%)
  starting transfers between devices  23.7 us (29%)
  waiting for transfers between devices  23.2 us (28%)
    pallas_call x4, Pallas kernels, product(): pl.pallas_call(functools.partial(product_kernel, adapters, units, starts[...  20.3 us
    pallas_call x1, Pallas kernels, paired(): pl.pallas_call(load_kernel, out_shape=[jax.ShapeDtypeStruct((8, LANES), j...  11.9 us
    ppermute x4, waiting for transfers between devices, paired(): got = lax.ppermute(send, 'tensor', next_z)  7.5 us
    ppermute x2, waiting for transfers between devices, paired(): gots.append(lax.ppermute(add_part(step), 'tensor', far_z))  6.29 us
    ppermute x16, waiting for transfers between devices, over_core(): lax.ppermute(part[:, at:to], 'req', beside)  5.61 us
    ppermute x2, starting transfers between devices, paired(): gots.append(lax.ppermute(add_part(step), 'tensor', far_z))  5.31 us
    ppermute x4, starting transfers between devices, paired(): got = lax.ppermute(send, 'tensor', next_z)  4.89 us
    ppermute x16, starting transfers between devices, over_core(): lax.ppermute(part[:, at:to], 'req', beside)  3.7 us
  transfers between devices with their start and end apart: 29, of which 12 were waited for; matrix products, arithmetic and copies ran while one was open for 0% of the time, Pallas kernels for 39%

profile of v6, /device:TPU:0, one launch (start us, length us, event | category | flops | bytes accessed | tf_op | source)
XLA Modules:
  0.0 82.9 jit_solution(3362684922223681944)
XLA Ops:
  0.0 1.8 %turn.1 = (bf16[128,7424]{1,0:T(8,128)(2,1)S(1)}, bf16[32,7424]{1,0:T(8,128)(2,1)S(1)}, bf16[32,7424]{1,0:T(8,128)(2,1)S(1)}, bf16[32,7424]{1,0:T(8,128)(2,1)S(1)}, bf16[32,7424]{1,0:T(8,128)(2,1)S(1)}) custom-call(bf16[7392,128]{1,0:T(8,128)(2,1)} %bitcast.8, s32[1,128]{1,0:T(1,128)} %bitcast.9), custom_call_target="tpu_custom_call" | custom-call | tf_op jit(solution)/shard_map/turn/pallas_call | solution.py:197
  2.3 2.6 %collective-permute-start.1 = (bf16[32,7424]{1,0:T(8,128)(2,1)S(1)}, bf16[32,7424]{1,0:T(8,128)(2,1)S(1)}, u32[]{:S(2)}, u32[]{:S(2)}) collective-permute-start(bf16[32,7424]{1,0:T(8,128)(2,1)S(1)} %get-tuple-element.60), channel_id=1, source_target_pairs={{0,2},{1,3},{2,0},{3,1},{4,6},{5,7},{6,4},{7,5},{8,10},{9,11},{10,... | collective-permute-start | bytes 1425416 | tf_op jit(solution)/shard_map/ppermute | solution.py:216
  5.0 11.9 %load.1 = (f32[8,128]{1,0:T(8,128)S(1)}, bf16[7424,512]{1,0:T(8,128)(2,1)S(1)}, bf16[7424,512]{1,0:T(8,128)(2,1)S(1)}, bf16[7424,512]{1,0:T(8,128)(2,1)S(1)}, bf...) custom-call(bf16[7392,2048]{1,0:T(8,128)(2,1)} %w_hbm.1, bf16[512,7392]{1,0:T(8,128)(2,1)} %bitcast.7), custom_call_target="tpu_custom_call" | custom-call | flops 1 | bytes 1 | tf_op jit(solution)/shard_map/load/pallas_call | solution.py:220
  18.5 1.2 %collective-permute-done.4.refs_0_ = bf16[32,1792]{1,0:T(8,128)(2,1)S(1)} collective-permute-done((bf16[32,1792]{1,0:T(8,128)(2,1)S(1)}, bf16[32,1792]{1,0:T(8,128)(2,1)S(1)}, u32[]{:S(2)}, u32[]{:S(2)}) %collective-permute-start.4) | collective-permute-done | bytes 114720 | tf_op jit(solution)/shard_map/ppermute | solution.py:263
  19.6 1.9 %collective-permute-start = (bf16[32,7424]{1,0:T(8,128)(2,1)S(1)}, bf16[32,7424]{1,0:T(8,128)(2,1)S(1)}, u32[]{:S(2)}, u32[]{:S(2)}) collective-permute-start(bf16[32,7424]{1,0:T(8,128)(2,1)S(1)} %get-tuple-element.59), channel_id=1, source_target_pairs={{0,2},{1,3},{2,0},{3,1},{4,6},{5,7},{6,4},{7,5},{8,10},{9,11},{10,... | collective-permute-start | bytes 1425416 | tf_op jit(solution)/shard_map/ppermute | solution.py:280
  21.6 5.1 %product.4 = (bf16[64,2176]{1,0:T(8,128)(2,1)S(1)}, bf16[64,2176]{1,0:T(8,128)(2,1)S(1)}) custom-call(f32[8,128]{1,0:T(8,128)S(1)} %get-tuple-element.62._, bf16[128,7424]{1,0:T(8,128)(2,1)S(1)} %get-tuple-element.63.own_ref, bf16[128,7424]{1,0:T(8,128)(2,1)S(1)} %collective-permute-done.2.other_ref, bf16[32,7424]{1,0:T(8,128)(2,1)S(1)} %collective-permute-done.1.direct_ref, ...), custom_call_target="tpu_custom_call" | custom-call | flops 1 | bytes 1 | tf_op jit(solution)/shard_map/product/pallas_call | solution.py:238
  26.9 2.1 %collective-permute-start.12 = (bf16[64,2176]{1,0:T(8,128)(2,1)S(1)}, bf16[64,2176]{1,0:T(8,128)(2,1)S(1)}, u32[]{:S(2)}, u32[]{:S(2)}) collective-permute-start(bf16[64,2176]{1,0:T(8,128)(2,1)S(1)} %get-tuple-element.75), channel_id=1, source_target_pairs={{0,4},{4,0},{8,12},{12,8},{1,5},{5,1},{9,13},{13,9},{2,6},{6,2},{1... | collective-permute-start | bytes 835592 | tf_op jit(solution)/shard_map/ppermute | solution.py:288
  29.8 1.2 %collective-permute-done.8.refs_0_ = bf16[32,1792]{1,0:T(8,128)(2,1)S(1)} collective-permute-done((bf16[32,1792]{1,0:T(8,128)(2,1)S(1)}, bf16[32,1792]{1,0:T(8,128)(2,1)S(1)}, u32[]{:S(2)}, u32[]{:S(2)}) %collective-permute-start.8) | collective-permute-done | bytes 114720 | tf_op jit(solution)/shard_map/ppermute | solution.py:263
  30.9 1.5 %collective-permute-start.13 = (bf16[32,7424]{1,0:T(8,128)(2,1)S(1)}, bf16[32,7424]{1,0:T(8,128)(2,1)S(1)}, u32[]{:S(2)}, u32[]{:S(2)}) collective-permute-start(bf16[32,7424]{1,0:T(8,128)(2,1)S(1)} %get-tuple-element.79), channel_id=1, source_target_pairs={{0,2},{1,3},{2,0},{3,1},{4,6},{5,7},{6,4},{7,5},{8,10},{9,11},{10,... | collective-permute-start | bytes 1425416 | tf_op jit(solution)/shard_map/ppermute | solution.py:280
  32.4 5.1 %product.5 = (bf16[64,2176]{1,0:T(8,128)(2,1)S(1)}, bf16[64,2176]{1,0:T(8,128)(2,1)S(1)}) custom-call(f32[8,128]{1,0:T(8,128)S(1)} %get-tuple-element.62._, bf16[128,7424]{1,0:T(8,128)(2,1)S(1)} %get-tuple-element.63.own_ref, bf16[128,7424]{1,0:T(8,128)(2,1)S(1)} %collective-permute-done.2.other_ref, bf16[32,7424]{1,0:T(8,128)(2,1)S(1)} %collective-permute-done.3.direct_ref, ...), custom_call_target="tpu_custom_call" | custom-call | flops 1 | bytes 1 | tf_op jit(solution)/shard_map/product/pallas_call | solution.py:238
  37.5 0.7 collective-permute-start.18
  39.0 0.6 collective-permute-done.16.refs_2_
  39.9 1.1 %collective-permute-done.14.refs_0_ = bf16[32,1792]{1,0:T(8,128)(2,1)S(1)} collective-permute-done((bf16[32,1792]{1,0:T(8,128)(2,1)S(1)}, bf16[32,1792]{1,0:T(8,128)(2,1)S(1)}, u32[]{:S(2)}, u32[]{:S(2)}) %collective-permute-start.14) | collective-permute-done | bytes 114720 | tf_op jit(solution)/shard_map/ppermute | solution.py:263
  41.0 2.6 %collective-permute-start.19 = (bf16[32,2176]{1,0:T(8,128)(2,1)S(1)}, bf16[32,2176]{1,0:T(8,128)(2,1)S(1)}, u32[]{:S(2)}, u32[]{:S(2)}) collective-permute-start(bf16[32,2176]{1,0:T(8,128)(2,1)S(1)} %get-tuple-element.89), channel_id=1, source_target_pairs={{0,8},{4,12},{8,0},{12,4},{1,9},{5,13},{9,1},{13,5},{2,10},{6,14},... | collective-permute-start | bytes 417800 | tf_op jit(solution)/shard_map/ppermute | solution.py:284
  43.6 5.1 %product.6 = (bf16[64,2176]{1,0:T(8,128)(2,1)S(1)}, bf16[64,2176]{1,0:T(8,128)(2,1)S(1)}) custom-call(f32[8,128]{1,0:T(8,128)S(1)} %get-tuple-element.62._, bf16[128,7424]{1,0:T(8,128)(2,1)S(1)} %get-tuple-element.63.own_ref, bf16[128,7424]{1,0:T(8,128)(2,1)S(1)} %collective-permute-done.2.other_ref, bf16[32,7424]{1,0:T(8,128)(2,1)S(1)} %collective-permute-done.direct_ref, ...), custom_call_target="tpu_custom_call" | custom-call | flops 1 | bytes 1 | tf_op jit(solution)/shard_map/product/pallas_call | solution.py:238
  48.7 1.4 %collective-permute-start.24 = (bf16[64,2176]{1,0:T(8,128)(2,1)S(1)}, bf16[64,2176]{1,0:T(8,128)(2,1)S(1)}, u32[]{:S(2)}, u32[]{:S(2)}) collective-permute-start(bf16[64,2176]{1,0:T(8,128)(2,1)S(1)} %get-tuple-element.101), channel_id=1, source_target_pairs={{0,4},{4,0},{8,12},{12,8},{1,5},{5,1},{9,13},{13,9},{2,6},{6,2},{1... | collective-permute-start | bytes 835592 | tf_op jit(solution)/shard_map/ppermute | solution.py:288
  51.4 0.7 collective-permute-done.22.refs_2_
  52.9 5.1 %product.7 = (bf16[64,2176]{1,0:T(8,128)(2,1)S(1)}, bf16[64,2176]{1,0:T(8,128)(2,1)S(1)}) custom-call(f32[8,128]{1,0:T(8,128)S(1)} %get-tuple-element.62._, bf16[128,7424]{1,0:T(8,128)(2,1)S(1)} %get-tuple-element.63.own_ref, bf16[128,7424]{1,0:T(8,128)(2,1)S(1)} %collective-permute-done.2.other_ref, ...), custom_call_target="tpu_custom_call" | custom-call | flops 1 | bytes 1 | tf_op jit(solution)/shard_map/product/pallas_call | solution.py:238
  58.6 3.7 %collective-permute-done.25.refs_5_ = bf16[32,2176]{1,0:T(8,128)(2,1)S(1)} collective-permute-done((bf16[32,2176]{1,0:T(8,128)(2,1)S(1)}, bf16[32,2176]{1,0:T(8,128)(2,1)S(1)}, u32[]{:S(2)}, u32[]{:S(2)}) %collective-permute-start.25) | collective-permute-done | bytes 139296 | tf_op jit(solution)/shard_map/ppermute | solution.py:284
  62.9 3.4 %collective-permute-start.27 = (bf16[32,2176]{1,0:T(8,128)(2,1)S(1)}, bf16[32,2176]{1,0:T(8,128)(2,1)S(1)}, u32[]{:S(2)}, u32[]{:S(2)}) collective-permute-start(bf16[32,2176]{1,0:T(8,128)(2,1)S(1)} %get-tuple-element.111), channel_id=1, source_target_pairs={{0,8},{4,12},{8,0},{12,4},{1,9},{5,13},{9,1},{13,5},{2,10},{6,14},... | collective-permute-start | bytes 417800 | tf_op jit(solution)/shard_map/ppermute | solution.py:297
  66.4 6.9 %collective-permute-done.26.second_ref = bf16[64,2176]{1,0:T(8,128)(2,1)S(1)} collective-permute-done((bf16[64,2176]{1,0:T(8,128)(2,1)S(1)}, bf16[64,2176]{1,0:T(8,128)(2,1)S(1)}, u32[]{:S(2)}, u32[]{:S(2)}) %collective-permute-start.26) | collective-permute-done | bytes 278560 | tf_op jit(solution)/shard_map/ppermute | solution.py:294
  73.4 1.9 %collective-permute-start.28 = (bf16[32,2176]{1,0:T(8,128)(2,1)S(1)}, bf16[32,2176]{1,0:T(8,128)(2,1)S(1)}, u32[]{:S(2)}, u32[]{:S(2)}) collective-permute-start(bf16[32,2176]{1,0:T(8,128)(2,1)S(1)} %get-tuple-element.112), channel_id=1, source_target_pairs={{0,8},{4,12},{8,0},{12,4},{1,9},{5,13},{9,1},{13,5},{2,10},{6,14},... | collective-permute-start | bytes 417800 | tf_op jit(solution)/shard_map/ppermute | solution.py:297
  75.3 6.3 %collective-permute-done.28.refs_7_ = bf16[32,2176]{1,0:T(8,128)(2,1)S(1)} collective-permute-done((bf16[32,2176]{1,0:T(8,128)(2,1)S(1)}, bf16[32,2176]{1,0:T(8,128)(2,1)S(1)}, u32[]{:S(2)}, u32[]{:S(2)}) %collective-permute-start.28) | collective-permute-done | bytes 139296 | tf_op jit(solution)/shard_map/ppermute | solution.py:297
  81.6 1.3 %last.1 = bf16[128,2048]{1,0:T(8,128)(2,1)} custom-call(bf16[512,2048]{1,0:T(8,128)(2,1)S(1)} %bitcast.6, bf16[32,2176]{1,0:T(8,128)(2,1)S(1)} %get-tuple-element.78.refs_0_, bf16[32,2176]{1,0:T(8,128)(2,1)S(1)} %get-tuple-element.92.refs_1_, bf16[32,2176]{1,0:T(8,128)(2,1)S(1)} %get-tuple-element.105.refs_2_, ...), custom_call_target="tpu_custom_call" | custom-call | tf_op jit(solution)/shard_map/last/pallas_call | solution.py:299
  (55 shorter events, 7.6 us)
Async XLA Ops:
  1.8 19.7 %collective-permute-start.2 = (bf16[128,7424]{1,0:T(8,128)(2,1)S(1)}, bf16[128,7424]{1,0:T(8,128)(2,1)S(1)}, u32[]{:S(2)}, u32[]{:S(2)}) collective-permute-start(bf16[128,7424]{1,0:T(8,128)(2,1)S(1)} %get-tuple-element.63.own_ref), channel_id=1, source_target_pairs={{0,1},{1,0},{2,3},{3,2},{4,5},{5,4},{6,7},{7,6},{8,9},{9,8},{10,11... | collective-permute-start | bytes 5701640 | tf_op jit(solution)/shard_map/ppermute | solution.py:217
  2.3 14.5 %collective-permute-start.1 = (bf16[32,7424]{1,0:T(8,128)(2,1)S(1)}, bf16[32,7424]{1,0:T(8,128)(2,1)S(1)}, u32[]{:S(2)}, u32[]{:S(2)}) collective-permute-start(bf16[32,7424]{1,0:T(8,128)(2,1)S(1)} %get-tuple-element.60), channel_id=1, source_target_pairs={{0,2},{1,3},{2,0},{3,1},{4,6},{5,7},{6,4},{7,5},{8,10},{9,11},{10,... | collective-permute-start | bytes 1425416 | tf_op jit(solution)/shard_map/ppermute | solution.py:216
  4.9 21.9 %collective-permute-start.3 = (bf16[32,7424]{1,0:T(8,128)(2,1)S(1)}, bf16[32,7424]{1,0:T(8,128)(2,1)S(1)}, u32[]{:S(2)}, u32[]{:S(2)}) collective-permute-start(bf16[32,7424]{1,0:T(8,128)(2,1)S(1)} %get-tuple-element.64), channel_id=1, source_target_pairs={{0,2},{1,3},{2,0},{3,1},{4,6},{5,7},{6,4},{7,5},{8,10},{9,11},{10,... | collective-permute-start | bytes 1425416 | tf_op jit(solution)/shard_map/ppermute | solution.py:280
  16.9 1.4 %collective-permute-start.6 = (bf16[32,1792]{1,0:T(8,128)(2,1)S(1)}, bf16[32,1792]{1,0:T(8,128)(2,1)S(1)}, u32[]{:S(2)}, u32[]{:S(2)}) collective-permute-start(bf16[32,1792]{1,0:T(8,128)(2,1)S(1)} %get-tuple-element.127), channel_id=1, source_target_pairs={{0,1},{1,0},{2,3},{3,2},{4,5},{5,4},{6,7},{7,6},{8,9},{9,8},{10,11... | collective-permute-start | bytes 344072 | tf_op jit(solution)/shard_map/ppermute | solution.py:263
  17.1 4.5 %collective-permute-start.7 = (bf16[32,1920]{1,0:T(8,128)(2,1)S(1)}, bf16[32,1920]{1,0:T(8,128)(2,1)S(1)}, u32[]{:S(2)}, u32[]{:S(2)}) collective-permute-start(bf16[32,1920]{1,0:T(8,128)(2,1)S(1)} %get-tuple-element.125), channel_id=1, source_target_pairs={{0,1},{1,0},{2,3},{3,2},{4,5},{5,4},{6,7},{7,6},{8,9},{9,8},{10,11... | collective-permute-start | bytes 368648 | tf_op jit(solution)/shard_map/ppermute | solution.py:263
  17.6 4.0 %collective-permute-start.5 = (bf16[32,1920]{1,0:T(8,128)(2,1)S(1)}, bf16[32,1920]{1,0:T(8,128)(2,1)S(1)}, u32[]{:S(2)}, u32[]{:S(2)}) collective-permute-start(bf16[32,1920]{1,0:T(8,128)(2,1)S(1)} %get-tuple-element.126), channel_id=1, source_target_pairs={{0,1},{1,0},{2,3},{3,2},{4,5},{5,4},{6,7},{7,6},{8,9},{9,8},{10,11... | collective-permute-start | bytes 368648 | tf_op jit(solution)/shard_map/ppermute | solution.py:263
  19.6 18.6 %collective-permute-start = (bf16[32,7424]{1,0:T(8,128)(2,1)S(1)}, bf16[32,7424]{1,0:T(8,128)(2,1)S(1)}, u32[]{:S(2)}, u32[]{:S(2)}) collective-permute-start(bf16[32,7424]{1,0:T(8,128)(2,1)S(1)} %get-tuple-element.59), channel_id=1, source_target_pairs={{0,2},{1,3},{2,0},{3,1},{4,6},{5,7},{6,4},{7,5},{8,10},{9,11},{10,... | collective-permute-start | bytes 1425416 | tf_op jit(solution)/shard_map/ppermute | solution.py:280
  26.8 2.8 %collective-permute-start.10 = (bf16[32,1792]{1,0:T(8,128)(2,1)S(1)}, bf16[32,1792]{1,0:T(8,128)(2,1)S(1)}, u32[]{:S(2)}, u32[]{:S(2)}) collective-permute-start(bf16[32,1792]{1,0:T(8,128)(2,1)S(1)} %get-tuple-element.123), channel_id=1, source_target_pairs={{0,1},{1,0},{2,3},{3,2},{4,5},{5,4},{6,7},{7,6},{8,9},{9,8},{10,11... | collective-permute-start | bytes 344072 | tf_op jit(solution)/shard_map/ppermute | solution.py:263
  26.9 11.3 %collective-permute-start.12 = (bf16[64,2176]{1,0:T(8,128)(2,1)S(1)}, bf16[64,2176]{1,0:T(8,128)(2,1)S(1)}, u32[]{:S(2)}, u32[]{:S(2)}) collective-permute-start(bf16[64,2176]{1,0:T(8,128)(2,1)S(1)} %get-tuple-element.75), channel_id=1, source_target_pairs={{0,4},{4,0},{8,12},{12,8},{1,5},{5,1},{9,13},{13,9},{2,6},{6,2},{1... | collective-permute-start | bytes 835592 | tf_op jit(solution)/shard_map/ppermute | solution.py:288
  29.0 3.4 %collective-permute-start.11 = (bf16[32,1920]{1,0:T(8,128)(2,1)S(1)}, bf16[32,1920]{1,0:T(8,128)(2,1)S(1)}, u32[]{:S(2)}, u32[]{:S(2)}) collective-permute-start(bf16[32,1920]{1,0:T(8,128)(2,1)S(1)} %get-tuple-element.121), channel_id=1, source_target_pairs={{0,1},{1,0},{2,3},{3,2},{4,5},{5,4},{6,7},{7,6},{8,9},{9,8},{10,11... | collective-permute-start | bytes 368648 | tf_op jit(solution)/shard_map/ppermute | solution.py:263
  29.3 3.2 %collective-permute-start.9 = (bf16[32,1920]{1,0:T(8,128)(2,1)S(1)}, bf16[32,1920]{1,0:T(8,128)(2,1)S(1)}, u32[]{:S(2)}, u32[]{:S(2)}) collective-permute-start(bf16[32,1920]{1,0:T(8,128)(2,1)S(1)} %get-tuple-element.122), channel_id=1, source_target_pairs={{0,1},{1,0},{2,3},{3,2},{4,5},{5,4},{6,7},{7,6},{8,9},{9,8},{10,11... | collective-permute-start | bytes 368648 | tf_op jit(solution)/shard_map/ppermute | solution.py:263
  30.9 19.2 %collective-permute-start.13 = (bf16[32,7424]{1,0:T(8,128)(2,1)S(1)}, bf16[32,7424]{1,0:T(8,128)(2,1)S(1)}, u32[]{:S(2)}, u32[]{:S(2)}) collective-permute-start(bf16[32,7424]{1,0:T(8,128)(2,1)S(1)} %get-tuple-element.79), channel_id=1, source_target_pairs={{0,2},{1,3},{2,0},{3,1},{4,6},{5,7},{6,4},{7,5},{8,10},{9,11},{10,... | collective-permute-start | bytes 1425416 | tf_op jit(solution)/shard_map/ppermute | solution.py:280
  37.5 12.6 %collective-permute-start.18 = (bf16[64,2176]{1,0:T(8,128)(2,1)S(1)}, bf16[64,2176]{1,0:T(8,128)(2,1)S(1)}, u32[]{:S(2)}, u32[]{:S(2)}) collective-permute-start(bf16[64,2176]{1,0:T(8,128)(2,1)S(1)} %get-tuple-element.88), channel_id=1, source_target_pairs={{0,4},{4,0},{8,12},{12,8},{1,5},{5,1},{9,13},{13,9},{2,6},{6,2},{1... | collective-permute-start | bytes 835592 | tf_op jit(solution)/shard_map/ppermute | solution.py:288
  38.4 2.6 %collective-permute-start.17 = (bf16[32,1920]{1,0:T(8,128)(2,1)S(1)}, bf16[32,1920]{1,0:T(8,128)(2,1)S(1)}, u32[]{:S(2)}, u32[]{:S(2)}) collective-permute-start(bf16[32,1920]{1,0:T(8,128)(2,1)S(1)} %get-tuple-element.117), channel_id=1, source_target_pairs={{0,1},{1,0},{2,3},{3,2},{4,5},{5,4},{6,7},{7,6},{8,9},{9,8},{10,11... | collective-permute-start | bytes 368648 | tf_op jit(solution)/shard_map/ppermute | solution.py:263
  38.9 2.1 %collective-permute-start.15 = (bf16[32,1920]{1,0:T(8,128)(2,1)S(1)}, bf16[32,1920]{1,0:T(8,128)(2,1)S(1)}, u32[]{:S(2)}, u32[]{:S(2)}) collective-permute-start(bf16[32,1920]{1,0:T(8,128)(2,1)S(1)} %get-tuple-element.118), channel_id=1, source_target_pairs={{0,1},{1,0},{2,3},{3,2},{4,5},{5,4},{6,7},{7,6},{8,9},{9,8},{10,11... | collective-permute-start | bytes 368648 | tf_op jit(solution)/shard_map/ppermute | solution.py:263
  41.0 9.1 %collective-permute-start.19 = (bf16[32,2176]{1,0:T(8,128)(2,1)S(1)}, bf16[32,2176]{1,0:T(8,128)(2,1)S(1)}, u32[]{:S(2)}, u32[]{:S(2)}) collective-permute-start(bf16[32,2176]{1,0:T(8,128)(2,1)S(1)} %get-tuple-element.89), channel_id=1, source_target_pairs={{0,8},{4,12},{8,0},{12,4},{1,9},{5,13},{9,1},{13,5},{2,10},{6,14},... | collective-permute-start | bytes 417800 | tf_op jit(solution)/shard_map/ppermute | solution.py:284
  48.7 9.9 %collective-permute-start.24 = (bf16[64,2176]{1,0:T(8,128)(2,1)S(1)}, bf16[64,2176]{1,0:T(8,128)(2,1)S(1)}, u32[]{:S(2)}, u32[]{:S(2)}) collective-permute-start(bf16[64,2176]{1,0:T(8,128)(2,1)S(1)} %get-tuple-element.101), channel_id=1, source_target_pairs={{0,4},{4,0},{8,12},{12,8},{1,5},{5,1},{9,13},{13,9},{2,6},{6,2},{1... | collective-permute-start | bytes 835592 | tf_op jit(solution)/shard_map/ppermute | solution.py:288
  50.1 2.2 %collective-permute-start.23 = (bf16[32,1920]{1,0:T(8,128)(2,1)S(1)}, bf16[32,1920]{1,0:T(8,128)(2,1)S(1)}, u32[]{:S(2)}, u32[]{:S(2)}) collective-permute-start(bf16[32,1920]{1,0:T(8,128)(2,1)S(1)} %get-tuple-element.113), channel_id=1, source_target_pairs={{0,1},{1,0},{2,3},{3,2},{4,5},{5,4},{6,7},{7,6},{8,9},{9,8},{10,11... | collective-permute-start | bytes 368648 | tf_op jit(solution)/shard_map/ppermute | solution.py:263
  50.2 2.1 %collective-permute-start.21 = (bf16[32,1920]{1,0:T(8,128)(2,1)S(1)}, bf16[32,1920]{1,0:T(8,128)(2,1)S(1)}, u32[]{:S(2)}, u32[]{:S(2)}) collective-permute-start(bf16[32,1920]{1,0:T(8,128)(2,1)S(1)} %get-tuple-element.114), channel_id=1, source_target_pairs={{0,1},{1,0},{2,3},{3,2},{4,5},{5,4},{6,7},{7,6},{8,9},{9,8},{10,11... | collective-permute-start | bytes 368648 | tf_op jit(solution)/shard_map/ppermute | solution.py:263
  50.9 1.4 %collective-permute-start.20 = (bf16[32,1792]{1,0:T(8,128)(2,1)S(1)}, bf16[32,1792]{1,0:T(8,128)(2,1)S(1)}, u32[]{:S(2)}, u32[]{:S(2)}) collective-permute-start(bf16[32,1792]{1,0:T(8,128)(2,1)S(1)} %get-tuple-element.116), channel_id=1, source_target_pairs={{0,1},{1,0},{2,3},{3,2},{4,5},{5,4},{6,7},{7,6},{8,9},{9,8},{10,11... | collective-permute-start | bytes 344072 | tf_op jit(solution)/shard_map/ppermute | solution.py:263
  52.3 9.9 %collective-permute-start.25 = (bf16[32,2176]{1,0:T(8,128)(2,1)S(1)}, bf16[32,2176]{1,0:T(8,128)(2,1)S(1)}, u32[]{:S(2)}, u32[]{:S(2)}) collective-permute-start(bf16[32,2176]{1,0:T(8,128)(2,1)S(1)} %get-tuple-element.102), channel_id=1, source_target_pairs={{0,8},{4,12},{8,0},{12,4},{1,9},{5,13},{9,1},{13,5},{2,10},{6,14},... | collective-permute-start | bytes 417800 | tf_op jit(solution)/shard_map/ppermute | solution.py:284
  62.2 11.1 %collective-permute-start.26 = (bf16[64,2176]{1,0:T(8,128)(2,1)S(1)}, bf16[64,2176]{1,0:T(8,128)(2,1)S(1)}, u32[]{:S(2)}, u32[]{:S(2)}) collective-permute-start(bf16[64,2176]{1,0:T(8,128)(2,1)S(1)} %get-tuple-element.107), channel_id=1, source_target_pairs={{0,4},{4,0},{8,12},{12,8},{1,5},{5,1},{9,13},{13,9},{2,6},{6,2},{1... | collective-permute-start | bytes 835592 | tf_op jit(solution)/shard_map/ppermute | solution.py:294
  62.9 12.3 %collective-permute-start.27 = (bf16[32,2176]{1,0:T(8,128)(2,1)S(1)}, bf16[32,2176]{1,0:T(8,128)(2,1)S(1)}, u32[]{:S(2)}, u32[]{:S(2)}) collective-permute-start(bf16[32,2176]{1,0:T(8,128)(2,1)S(1)} %get-tuple-element.111), channel_id=1, source_target_pairs={{0,8},{4,12},{8,0},{12,4},{1,9},{5,13},{9,1},{13,5},{2,10},{6,14},... | collective-permute-start | bytes 417800 | tf_op jit(solution)/shard_map/ppermute | solution.py:297
  73.4 8.2 %collective-permute-start.28 = (bf16[32,2176]{1,0:T(8,128)(2,1)S(1)}, bf16[32,2176]{1,0:T(8,128)(2,1)S(1)}, u32[]{:S(2)}, u32[]{:S(2)}) collective-permute-start(bf16[32,2176]{1,0:T(8,128)(2,1)S(1)} %get-tuple-element.112), channel_id=1, source_target_pairs={{0,8},{4,12},{8,0},{12,4},{1,9},{5,13},{9,1},{13,5},{2,10},{6,14},... | collective-permute-start | bytes 417800 | tf_op jit(solution)/shard_map/ppermute | solution.py:297
  (6 other events, 36.0 us)

commit v7 on v6

--- a/solution.py
+++ b/solution.py
@@ -12,7 +12,7 @@
 DEPTH = 1024
 TURN = 15
 PIECES = (32, 32, 32, 32)
-CUTS = 4
+CUTS = 2
 MIB = 1 << 20
 
 
@@ -278,23 +278,23 @@
         passed = over_core(direct[step])
         if step + 1 < steps:
             direct.append(lax.ppermute(pieces[step + 1], "req", across))
-        if step > 1:
-            send = add_part(step - 2)
-            passed, send = after((passed, send))
-            gots.append(lax.ppermute(send, "tensor", far_z))
         send, keep = product(step, passed, token)
-        prior, before = slice(max(step - 1, 0), step), slice(max(step - 2, 0), max(step - 1, 0))
+        hop = gots[step - 2 :] if step > 1 else []
         if step + 1 < steps:
             got = lax.ppermute(send, "tensor", next_z)
-            direct[step + 1], keep, parts[prior], gots[before] = after(
-                (direct[step + 1], keep, parts[prior], gots[before])
-            )
+            direct[step + 1], keep, parts, hop = after((direct[step + 1], keep, parts, hop))
         else:
-            send, parts[prior], gots[before] = after((send, parts[prior], gots[before]))
+            send, parts, hop = after((send, parts, hop))
             got = lax.ppermute(send, "tensor", next_z)
+        if step > 1:
+            gots[step - 2 :] = hop
+        if step > 0:
+            send = add_part(step - 1)
+            if step + 1 < steps:
+                direct[step + 1], kept[-1] = after((direct[step + 1], kept[-1]))
+            gots.append(lax.ppermute(send, "tensor", far_z))
         parts.append((keep, got))
-    for step in range(steps - 2, steps):
-        gots.append(lax.ppermute(add_part(step), "tensor", far_z))
+    gots.append(lax.ppermute(add_part(steps - 1), "tensor", far_z))
 
     return pl.pallas_call(
         functools.partial(last_kernel, n_tensor, adapters),

time: 83 us -> 79 us (0.952)
  waiting for transfers between devices: 23.2 us -> 19.3 us
    ppermute x16 -> x8, waiting for transfers between devices: 5.61 us -> 0.02 us  [over_core(): lax.ppermute(part[:, at:to], 'req', beside)]
    ppermute x2 -> x1, starting transfers between devices: 5.31 us -> 0.74 us  [paired(): gots.append(lax.ppermute(add_part(steps - 1), 'tensor', far_z))]
    ppermute x3, waiting for transfers between devices: 0.15 us -> 3.59 us  [paired(): direct.append(lax.ppermute(pieces[step + 1], 'req', across))]
    ppermute x2 -> x3, starting transfers between devices: 3.19 us -> 6.47 us  [paired(): gots.append(lax.ppermute(send, 'tensor', far_z))]
    ppermute x2 -> x3, waiting for transfers between devices: 3.66 us -> 0.86 us  [paired(): gots.append(lax.ppermute(send, 'tensor', far_z))]
    ppermute x4, starting transfers between devices: 4.89 us -> 7.26 us  [paired(): got = lax.ppermute(send, 'tensor', next_z)]
    ppermute x16 -> x8, starting transfers between devices: 3.7 us -> 2.28 us  [over_core(): lax.ppermute(part[:, at:to], 'req', beside)]
    ppermute x4, waiting for transfers between devices: 7.5 us -> 8.35 us  [paired(): got = lax.ppermute(send, 'tensor', next_z)]
  transfers between devices with their start and end apart: 29 -> 21, of which waited for: 12 -> 8; matrix products, arithmetic and copies ran while one was open for 0% -> 0% of each run, Pallas kernels for 39% -> 41%
where the time goes in v7:
time: 79 us; the launch traced here: 78.8 us
  Pallas kernels  35.9 us (45%)
  starting transfers between devices  23.4 us (30%)
  waiting for transfers between devices  19.3 us (24%)
    pallas_call x4, Pallas kernels, product(): pl.pallas_call(functools.partial(product_kernel, adapters, units, starts[...  20.5 us
    pallas_call x1, Pallas kernels, paired(): pl.pallas_call(load_kernel, out_shape=[jax.ShapeDtypeStruct((8, LANES), j...  11.9 us
    ppermute x4, waiting for transfers between devices, paired(): got = lax.ppermute(send, 'tensor', next_z)  8.35 us
    ppermute x4, starting transfers between devices, paired(): got = lax.ppermute(send, 'tensor', next_z)  7.26 us
    ppermute x1, waiting for transfers between devices, paired(): gots.append(lax.ppermute(add_part(steps - 1), 'tensor', far_z))  6.49 us
    ppermute x3, starting transfers between devices, paired(): gots.append(lax.ppermute(send, 'tensor', far_z))  6.47 us
    ppermute x3, waiting for transfers between devices, paired(): direct.append(lax.ppermute(pieces[step + 1], 'req', across))  3.59 us
    ppermute x3, starting transfers between devices, paired(): direct.append(lax.ppermute(pieces[step + 1], 'req', across))  3.52 us
  transfers between devices with their start and end apart: 21, of which 8 were waited for; matrix products, arithmetic and copies ran while one was open for 0% of the time, Pallas kernels for 41%

profile of v7, /device:TPU:0, one launch (start us, length us, event | category | flops | bytes accessed | tf_op | source)
XLA Modules:
  0.0 78.8 jit_solution(14938998405976511185)
XLA Ops:
  0.0 1.8 %turn.1 = (bf16[128,7424]{1,0:T(8,128)(2,1)S(1)}, bf16[32,7424]{1,0:T(8,128)(2,1)S(1)}, bf16[32,7424]{1,0:T(8,128)(2,1)S(1)}, bf16[32,7424]{1,0:T(8,128)(2,1)S(1)}, bf16[32,7424]{1,0:T(8,128)(2,1)S(1)}) custom-call(bf16[7392,128]{1,0:T(8,128)(2,1)} %bitcast.8, s32[1,128]{1,0:T(1,128)} %bitcast.9), custom_call_target="tpu_custom_call" | custom-call | tf_op jit(solution)/shard_map/turn/pallas_call | solution.py:197
  2.3 2.6 %collective-permute-start.1 = (bf16[32,7424]{1,0:T(8,128)(2,1)S(1)}, bf16[32,7424]{1,0:T(8,128)(2,1)S(1)}, u32[]{:S(2)}, u32[]{:S(2)}) collective-permute-start(bf16[32,7424]{1,0:T(8,128)(2,1)S(1)} %get-tuple-element.54), channel_id=1, source_target_pairs={{0,2},{1,3},{2,0},{3,1},{4,6},{5,7},{6,4},{7,5},{8,10},{9,11},{10,... | collective-permute-start | bytes 1425416 | tf_op jit(solution)/shard_map/ppermute | solution.py:216
  5.0 11.9 %load.1 = (f32[8,128]{1,0:T(8,128)S(1)}, bf16[7424,512]{1,0:T(8,128)(2,1)S(1)}, bf16[7424,512]{1,0:T(8,128)(2,1)S(1)}, bf16[7424,512]{1,0:T(8,128)(2,1)S(1)}, bf...) custom-call(bf16[7392,2048]{1,0:T(8,128)(2,1)} %w_hbm.1, bf16[512,7392]{1,0:T(8,128)(2,1)} %bitcast.7), custom_call_target="tpu_custom_call" | custom-call | flops 1 | bytes 1 | tf_op jit(solution)/shard_map/load/pallas_call | solution.py:220
  17.5 1.9 %collective-permute-start = (bf16[32,7424]{1,0:T(8,128)(2,1)S(1)}, bf16[32,7424]{1,0:T(8,128)(2,1)S(1)}, u32[]{:S(2)}, u32[]{:S(2)}) collective-permute-start(bf16[32,7424]{1,0:T(8,128)(2,1)S(1)} %get-tuple-element.53), channel_id=1, source_target_pairs={{0,2},{1,3},{2,0},{3,1},{4,6},{5,7},{6,4},{7,5},{8,10},{9,11},{10,... | collective-permute-start | bytes 1425416 | tf_op jit(solution)/shard_map/ppermute | solution.py:280
  19.5 5.1 %product.4 = (bf16[64,2176]{1,0:T(8,128)(2,1)S(1)}, bf16[64,2176]{1,0:T(8,128)(2,1)S(1)}) custom-call(f32[8,128]{1,0:T(8,128)S(1)} %get-tuple-element.56._, bf16[128,7424]{1,0:T(8,128)(2,1)S(1)} %get-tuple-element.57.own_ref, bf16[128,7424]{1,0:T(8,128)(2,1)S(1)} %collective-permute-done.2.other_ref, bf16[32,7424]{1,0:T(8,128)(2,1)S(1)} %collective-permute-done.1.direct_ref, ...), custom_call_target="tpu_custom_call" | custom-call | flops 1 | bytes 1 | tf_op jit(solution)/shard_map/product/pallas_call | solution.py:238
  24.5 2.3 %collective-permute-done.3.direct_ref = bf16[32,7424]{1,0:T(8,128)(2,1)S(1)} collective-permute-done((bf16[32,7424]{1,0:T(8,128)(2,1)S(1)}, bf16[32,7424]{1,0:T(8,128)(2,1)S(1)}, u32[]{:S(2)}, u32[]{:S(2)}) %collective-permute-start.3) | collective-permute-done | bytes 475168 | tf_op jit(solution)/shard_map/ppermute | solution.py:280
  26.8 2.0 %collective-permute-start.8 = (bf16[64,2176]{1,0:T(8,128)(2,1)S(1)}, bf16[64,2176]{1,0:T(8,128)(2,1)S(1)}, u32[]{:S(2)}, u32[]{:S(2)}) collective-permute-start(bf16[64,2176]{1,0:T(8,128)(2,1)S(1)} %get-tuple-element.69), channel_id=1, source_target_pairs={{0,4},{4,0},{8,12},{12,8},{1,5},{5,1},{9,13},{13,9},{2,6},{6,2},{1... | collective-permute-start | bytes 835592 | tf_op jit(solution)/shard_map/ppermute | solution.py:284
  29.5 1.5 %collective-permute-start.9 = (bf16[32,7424]{1,0:T(8,128)(2,1)S(1)}, bf16[32,7424]{1,0:T(8,128)(2,1)S(1)}, u32[]{:S(2)}, u32[]{:S(2)}) collective-permute-start(bf16[32,7424]{1,0:T(8,128)(2,1)S(1)} %get-tuple-element.75), channel_id=1, source_target_pairs={{0,2},{1,3},{2,0},{3,1},{4,6},{5,7},{6,4},{7,5},{8,10},{9,11},{10,... | collective-permute-start | bytes 1425416 | tf_op jit(solution)/shard_map/ppermute | solution.py:280
  31.0 5.1 %product.5 = (bf16[64,2176]{1,0:T(8,128)(2,1)S(1)}, bf16[64,2176]{1,0:T(8,128)(2,1)S(1)}) custom-call(f32[8,128]{1,0:T(8,128)S(1)} %get-tuple-element.56._, bf16[128,7424]{1,0:T(8,128)(2,1)S(1)} %get-tuple-element.57.own_ref, bf16[128,7424]{1,0:T(8,128)(2,1)S(1)} %collective-permute-done.2.other_ref, bf16[32,7424]{1,0:T(8,128)(2,1)S(1)} %collective-permute-done.3.direct_ref, ...), custom_call_target="tpu_custom_call" | custom-call | flops 1 | bytes 1 | tf_op jit(solution)/shard_map/product/pallas_call | solution.py:238
  37.7 3.0 %collective-permute-start.13 = (bf16[32,2176]{1,0:T(8,128)(2,1)S(1)}, bf16[32,2176]{1,0:T(8,128)(2,1)S(1)}, u32[]{:S(2)}, u32[]{:S(2)}) collective-permute-start(bf16[32,2176]{1,0:T(8,128)(2,1)S(1)} %get-tuple-element.80), channel_id=1, source_target_pairs={{0,8},{4,12},{8,0},{12,4},{1,9},{5,13},{9,1},{13,5},{2,10},{6,14},... | collective-permute-start | bytes 417800 | tf_op jit(solution)/shard_map/ppermute | solution.py:295
  40.8 5.3 %product.6 = (bf16[64,2176]{1,0:T(8,128)(2,1)S(1)}, bf16[64,2176]{1,0:T(8,128)(2,1)S(1)}) custom-call(f32[8,128]{1,0:T(8,128)S(1)} %get-tuple-element.56._, bf16[128,7424]{1,0:T(8,128)(2,1)S(1)} %get-tuple-element.57.own_ref, bf16[128,7424]{1,0:T(8,128)(2,1)S(1)} %collective-permute-done.2.other_ref, bf16[32,7424]{1,0:T(8,128)(2,1)S(1)} %collective-permute-done.direct_ref, ...), custom_call_target="tpu_custom_call" | custom-call | flops 1 | bytes 1 | tf_op jit(solution)/shard_map/product/pallas_call | solution.py:238
  46.0 0.9 %collective-permute-done.9.direct_ref = bf16[32,7424]{1,0:T(8,128)(2,1)S(1)} collective-permute-done((bf16[32,7424]{1,0:T(8,128)(2,1)S(1)}, bf16[32,7424]{1,0:T(8,128)(2,1)S(1)}, u32[]{:S(2)}, u32[]{:S(2)}) %collective-permute-start.9) | collective-permute-done | bytes 475168 | tf_op jit(solution)/shard_map/ppermute | solution.py:280
  46.9 0.7 collective-permute-done.12.second_ref
  47.7 2.7 %collective-permute-start.16 = (bf16[64,2176]{1,0:T(8,128)(2,1)S(1)}, bf16[64,2176]{1,0:T(8,128)(2,1)S(1)}, u32[]{:S(2)}, u32[]{:S(2)}) collective-permute-start(bf16[64,2176]{1,0:T(8,128)(2,1)S(1)} %get-tuple-element.89), channel_id=1, source_target_pairs={{0,4},{4,0},{8,12},{12,8},{1,5},{5,1},{9,13},{13,9},{2,6},{6,2},{1... | collective-permute-start | bytes 835592 | tf_op jit(solution)/shard_map/ppermute | solution.py:284
  51.0 1.6 %collective-permute-start.17 = (bf16[32,2176]{1,0:T(8,128)(2,1)S(1)}, bf16[32,2176]{1,0:T(8,128)(2,1)S(1)}, u32[]{:S(2)}, u32[]{:S(2)}) collective-permute-start(bf16[32,2176]{1,0:T(8,128)(2,1)S(1)} %get-tuple-element.90), channel_id=1, source_target_pairs={{0,8},{4,12},{8,0},{12,4},{1,9},{5,13},{9,1},{13,5},{2,10},{6,14},... | collective-permute-start | bytes 417800 | tf_op jit(solution)/shard_map/ppermute | solution.py:295
  52.7 5.1 %product.7 = (bf16[64,2176]{1,0:T(8,128)(2,1)S(1)}, bf16[64,2176]{1,0:T(8,128)(2,1)S(1)}) custom-call(f32[8,128]{1,0:T(8,128)S(1)} %get-tuple-element.56._, bf16[128,7424]{1,0:T(8,128)(2,1)S(1)} %get-tuple-element.57.own_ref, bf16[128,7424]{1,0:T(8,128)(2,1)S(1)} %collective-permute-done.2.other_ref, bf16[32,7424]{1,0:T(8,128)(2,1)S(1)} %collective-permute-done.9.direct_ref, ...), custom_call_target="tpu_custom_call" | custom-call | flops 1 | bytes 1 | tf_op jit(solution)/shard_map/product/pallas_call | solution.py:238
  57.8 0.9 %collective-permute-done.17.refs_5_ = bf16[32,2176]{1,0:T(8,128)(2,1)S(1)} collective-permute-done((bf16[32,2176]{1,0:T(8,128)(2,1)S(1)}, bf16[32,2176]{1,0:T(8,128)(2,1)S(1)}, u32[]{:S(2)}, u32[]{:S(2)}) %collective-permute-start.17) | collective-permute-done | bytes 139296 | tf_op jit(solution)/shard_map/ppermute | solution.py:295
  58.6 0.7 collective-permute-done.16.second_ref
  59.4 2.0 %collective-permute-start.18 = (bf16[64,2176]{1,0:T(8,128)(2,1)S(1)}, bf16[64,2176]{1,0:T(8,128)(2,1)S(1)}, u32[]{:S(2)}, u32[]{:S(2)}) collective-permute-start(bf16[64,2176]{1,0:T(8,128)(2,1)S(1)} %get-tuple-element.95), channel_id=1, source_target_pairs={{0,4},{4,0},{8,12},{12,8},{1,5},{5,1},{9,13},{13,9},{2,6},{6,2},{1... | collective-permute-start | bytes 835592 | tf_op jit(solution)/shard_map/ppermute | solution.py:288
  61.5 1.8 %collective-permute-start.19 = (bf16[32,2176]{1,0:T(8,128)(2,1)S(1)}, bf16[32,2176]{1,0:T(8,128)(2,1)S(1)}, u32[]{:S(2)}, u32[]{:S(2)}) collective-permute-start(bf16[32,2176]{1,0:T(8,128)(2,1)S(1)} %get-tuple-element.99), channel_id=1, source_target_pairs={{0,8},{4,12},{8,0},{12,4},{1,9},{5,13},{9,1},{13,5},{2,10},{6,14},... | collective-permute-start | bytes 417800 | tf_op jit(solution)/shard_map/ppermute | solution.py:295
  63.3 6.9 %collective-permute-done.18.second_ref = bf16[64,2176]{1,0:T(8,128)(2,1)S(1)} collective-permute-done((bf16[64,2176]{1,0:T(8,128)(2,1)S(1)}, bf16[64,2176]{1,0:T(8,128)(2,1)S(1)}, u32[]{:S(2)}, u32[]{:S(2)}) %collective-permute-start.18) | collective-permute-done | bytes 278560 | tf_op jit(solution)/shard_map/ppermute | solution.py:288
  70.3 0.7 collective-permute-start.20
  71.0 6.5 %collective-permute-done.20.refs_7_ = bf16[32,2176]{1,0:T(8,128)(2,1)S(1)} collective-permute-done((bf16[32,2176]{1,0:T(8,128)(2,1)S(1)}, bf16[32,2176]{1,0:T(8,128)(2,1)S(1)}, u32[]{:S(2)}, u32[]{:S(2)}) %collective-permute-start.20) | collective-permute-done | bytes 139296 | tf_op jit(solution)/shard_map/ppermute | solution.py:297
  77.5 1.3 %last.1 = bf16[128,2048]{1,0:T(8,128)(2,1)} custom-call(bf16[512,2048]{1,0:T(8,128)(2,1)S(1)} %bitcast.6, bf16[32,2176]{1,0:T(8,128)(2,1)S(1)} %get-tuple-element.74.refs_0_, bf16[32,2176]{1,0:T(8,128)(2,1)S(1)} %get-tuple-element.85.refs_1_, bf16[32,2176]{1,0:T(8,128)(2,1)S(1)} %get-tuple-element.93.refs_2_, ...), custom_call_target="tpu_custom_call" | custom-call | tf_op jit(solution)/shard_map/last/pallas_call | solution.py:299
  (35 shorter events, 4.4 us)
Async XLA Ops:
  1.8 17.6 %collective-permute-start.2 = (bf16[128,7424]{1,0:T(8,128)(2,1)S(1)}, bf16[128,7424]{1,0:T(8,128)(2,1)S(1)}, u32[]{:S(2)}, u32[]{:S(2)}) collective-permute-start(bf16[128,7424]{1,0:T(8,128)(2,1)S(1)} %get-tuple-element.57.own_ref), channel_id=1, source_target_pairs={{0,1},{1,0},{2,3},{3,2},{4,5},{5,4},{6,7},{7,6},{8,9},{9,8},{10,11... | collective-permute-start | bytes 5701640 | tf_op jit(solution)/shard_map/ppermute | solution.py:217
  2.3 14.5 %collective-permute-start.1 = (bf16[32,7424]{1,0:T(8,128)(2,1)S(1)}, bf16[32,7424]{1,0:T(8,128)(2,1)S(1)}, u32[]{:S(2)}, u32[]{:S(2)}) collective-permute-start(bf16[32,7424]{1,0:T(8,128)(2,1)S(1)} %get-tuple-element.54), channel_id=1, source_target_pairs={{0,2},{1,3},{2,0},{3,1},{4,6},{5,7},{6,4},{7,5},{8,10},{9,11},{10,... | collective-permute-start | bytes 1425416 | tf_op jit(solution)/shard_map/ppermute | solution.py:216
  4.9 21.9 %collective-permute-start.3 = (bf16[32,7424]{1,0:T(8,128)(2,1)S(1)}, bf16[32,7424]{1,0:T(8,128)(2,1)S(1)}, u32[]{:S(2)}, u32[]{:S(2)}) collective-permute-start(bf16[32,7424]{1,0:T(8,128)(2,1)S(1)} %get-tuple-element.58), channel_id=1, source_target_pairs={{0,2},{1,3},{2,0},{3,1},{4,6},{5,7},{6,4},{7,5},{8,10},{9,11},{10,... | collective-permute-start | bytes 1425416 | tf_op jit(solution)/shard_map/ppermute | solution.py:280
  16.9 2.5 %collective-permute-start.5 = (bf16[32,3712]{1,0:T(8,128)(2,1)S(1)}, bf16[32,3712]{1,0:T(8,128)(2,1)S(1)}, u32[]{:S(2)}, u32[]{:S(2)}) collective-permute-start(bf16[32,3712]{1,0:T(8,128)(2,1)S(1)} %get-tuple-element.107), channel_id=1, source_target_pairs={{0,1},{1,0},{2,3},{3,2},{4,5},{5,4},{6,7},{7,6},{8,9},{9,8},{10,11... | collective-permute-start | bytes 712712 | tf_op jit(solution)/shard_map/ppermute | solution.py:263
  17.1 2.4 %collective-permute-start.4 = (bf16[32,3712]{1,0:T(8,128)(2,1)S(1)}, bf16[32,3712]{1,0:T(8,128)(2,1)S(1)}, u32[]{:S(2)}, u32[]{:S(2)}) collective-permute-start(bf16[32,3712]{1,0:T(8,128)(2,1)S(1)} %get-tuple-element.108), channel_id=1, source_target_pairs={{0,1},{1,0},{2,3},{3,2},{4,5},{5,4},{6,7},{7,6},{8,9},{9,8},{10,11... | collective-permute-start | bytes 712712 | tf_op jit(solution)/shard_map/ppermute | solution.py:263
  17.5 19.5 %collective-permute-start = (bf16[32,7424]{1,0:T(8,128)(2,1)S(1)}, bf16[32,7424]{1,0:T(8,128)(2,1)S(1)}, u32[]{:S(2)}, u32[]{:S(2)}) collective-permute-start(bf16[32,7424]{1,0:T(8,128)(2,1)S(1)} %get-tuple-element.53), channel_id=1, source_target_pairs={{0,2},{1,3},{2,0},{3,1},{4,6},{5,7},{6,4},{7,5},{8,10},{9,11},{10,... | collective-permute-start | bytes 1425416 | tf_op jit(solution)/shard_map/ppermute | solution.py:280
  26.8 10.2 %collective-permute-start.8 = (bf16[64,2176]{1,0:T(8,128)(2,1)S(1)}, bf16[64,2176]{1,0:T(8,128)(2,1)S(1)}, u32[]{:S(2)}, u32[]{:S(2)}) collective-permute-start(bf16[64,2176]{1,0:T(8,128)(2,1)S(1)} %get-tuple-element.69), channel_id=1, source_target_pairs={{0,4},{4,0},{8,12},{12,8},{1,5},{5,1},{9,13},{13,9},{2,6},{6,2},{1... | collective-permute-start | bytes 835592 | tf_op jit(solution)/shard_map/ppermute | solution.py:284
  28.9 2.1 %collective-permute-start.7 = (bf16[32,3712]{1,0:T(8,128)(2,1)S(1)}, bf16[32,3712]{1,0:T(8,128)(2,1)S(1)}, u32[]{:S(2)}, u32[]{:S(2)}) collective-permute-start(bf16[32,3712]{1,0:T(8,128)(2,1)S(1)} %get-tuple-element.105), channel_id=1, source_target_pairs={{0,1},{1,0},{2,3},{3,2},{4,5},{5,4},{6,7},{7,6},{8,9},{9,8},{10,11... | collective-permute-start | bytes 712712 | tf_op jit(solution)/shard_map/ppermute | solution.py:263
  29.0 2.0 %collective-permute-start.6 = (bf16[32,3712]{1,0:T(8,128)(2,1)S(1)}, bf16[32,3712]{1,0:T(8,128)(2,1)S(1)}, u32[]{:S(2)}, u32[]{:S(2)}) collective-permute-start(bf16[32,3712]{1,0:T(8,128)(2,1)S(1)} %get-tuple-element.106), channel_id=1, source_target_pairs={{0,1},{1,0},{2,3},{3,2},{4,5},{5,4},{6,7},{7,6},{8,9},{9,8},{10,11... | collective-permute-start | bytes 712712 | tf_op jit(solution)/shard_map/ppermute | solution.py:263
  29.5 17.5 %collective-permute-start.9 = (bf16[32,7424]{1,0:T(8,128)(2,1)S(1)}, bf16[32,7424]{1,0:T(8,128)(2,1)S(1)}, u32[]{:S(2)}, u32[]{:S(2)}) collective-permute-start(bf16[32,7424]{1,0:T(8,128)(2,1)S(1)} %get-tuple-element.75), channel_id=1, source_target_pairs={{0,2},{1,3},{2,0},{3,1},{4,6},{5,7},{6,4},{7,5},{8,10},{9,11},{10,... | collective-permute-start | bytes 1425416 | tf_op jit(solution)/shard_map/ppermute | solution.py:280
  36.0 11.6 %collective-permute-start.12 = (bf16[64,2176]{1,0:T(8,128)(2,1)S(1)}, bf16[64,2176]{1,0:T(8,128)(2,1)S(1)}, u32[]{:S(2)}, u32[]{:S(2)}) collective-permute-start(bf16[64,2176]{1,0:T(8,128)(2,1)S(1)} %get-tuple-element.79), channel_id=1, source_target_pairs={{0,4},{4,0},{8,12},{12,8},{1,5},{5,1},{9,13},{13,9},{2,6},{6,2},{1... | collective-permute-start | bytes 835592 | tf_op jit(solution)/shard_map/ppermute | solution.py:284
  37.1 3.6 %collective-permute-start.11 = (bf16[32,3712]{1,0:T(8,128)(2,1)S(1)}, bf16[32,3712]{1,0:T(8,128)(2,1)S(1)}, u32[]{:S(2)}, u32[]{:S(2)}) collective-permute-start(bf16[32,3712]{1,0:T(8,128)(2,1)S(1)} %get-tuple-element.103), channel_id=1, source_target_pairs={{0,1},{1,0},{2,3},{3,2},{4,5},{5,4},{6,7},{7,6},{8,9},{9,8},{10,11... | collective-permute-start | bytes 712712 | tf_op jit(solution)/shard_map/ppermute | solution.py:263
  37.2 3.6 %collective-permute-start.10 = (bf16[32,3712]{1,0:T(8,128)(2,1)S(1)}, bf16[32,3712]{1,0:T(8,128)(2,1)S(1)}, u32[]{:S(2)}, u32[]{:S(2)}) collective-permute-start(bf16[32,3712]{1,0:T(8,128)(2,1)S(1)} %get-tuple-element.104), channel_id=1, source_target_pairs={{0,1},{1,0},{2,3},{3,2},{4,5},{5,4},{6,7},{7,6},{8,9},{9,8},{10,11... | collective-permute-start | bytes 712712 | tf_op jit(solution)/shard_map/ppermute | solution.py:263
  37.7 9.2 %collective-permute-start.13 = (bf16[32,2176]{1,0:T(8,128)(2,1)S(1)}, bf16[32,2176]{1,0:T(8,128)(2,1)S(1)}, u32[]{:S(2)}, u32[]{:S(2)}) collective-permute-start(bf16[32,2176]{1,0:T(8,128)(2,1)S(1)} %get-tuple-element.80), channel_id=1, source_target_pairs={{0,8},{4,12},{8,0},{12,4},{1,9},{5,13},{9,1},{13,5},{2,10},{6,14},... | collective-permute-start | bytes 417800 | tf_op jit(solution)/shard_map/ppermute | solution.py:295
  47.7 11.6 %collective-permute-start.16 = (bf16[64,2176]{1,0:T(8,128)(2,1)S(1)}, bf16[64,2176]{1,0:T(8,128)(2,1)S(1)}, u32[]{:S(2)}, u32[]{:S(2)}) collective-permute-start(bf16[64,2176]{1,0:T(8,128)(2,1)S(1)} %get-tuple-element.89), channel_id=1, source_target_pairs={{0,4},{4,0},{8,12},{12,8},{1,5},{5,1},{9,13},{13,9},{2,6},{6,2},{1... | collective-permute-start | bytes 835592 | tf_op jit(solution)/shard_map/ppermute | solution.py:284
  50.4 2.2 %collective-permute-start.15 = (bf16[32,3712]{1,0:T(8,128)(2,1)S(1)}, bf16[32,3712]{1,0:T(8,128)(2,1)S(1)}, u32[]{:S(2)}, u32[]{:S(2)}) collective-permute-start(bf16[32,3712]{1,0:T(8,128)(2,1)S(1)} %get-tuple-element.101), channel_id=1, source_target_pairs={{0,1},{1,0},{2,3},{3,2},{4,5},{5,4},{6,7},{7,6},{8,9},{9,8},{10,11... | collective-permute-start | bytes 712712 | tf_op jit(solution)/shard_map/ppermute | solution.py:263
  50.5 2.1 %collective-permute-start.14 = (bf16[32,3712]{1,0:T(8,128)(2,1)S(1)}, bf16[32,3712]{1,0:T(8,128)(2,1)S(1)}, u32[]{:S(2)}, u32[]{:S(2)}) collective-permute-start(bf16[32,3712]{1,0:T(8,128)(2,1)S(1)} %get-tuple-element.102), channel_id=1, source_target_pairs={{0,1},{1,0},{2,3},{3,2},{4,5},{5,4},{6,7},{7,6},{8,9},{9,8},{10,11... | collective-permute-start | bytes 712712 | tf_op jit(solution)/shard_map/ppermute | solution.py:263
  51.0 26.5 %copy-start = (bf16[8,64,2048]{2,1,0:T(8,128)(2,1)S(1)}, bf16[8,64,2048]{2,1,0:T(8,128)(2,1)}, u32[]{:S(2)}) copy-start(bf16[8,64,2048]{2,1,0:T(8,128)(2,1)} %param.8) | copy-start | bytes 6291460
  51.0 7.6 %collective-permute-start.17 = (bf16[32,2176]{1,0:T(8,128)(2,1)S(1)}, bf16[32,2176]{1,0:T(8,128)(2,1)S(1)}, u32[]{:S(2)}, u32[]{:S(2)}) collective-permute-start(bf16[32,2176]{1,0:T(8,128)(2,1)S(1)} %get-tuple-element.90), channel_id=1, source_target_pairs={{0,8},{4,12},{8,0},{12,4},{1,9},{5,13},{9,1},{13,5},{2,10},{6,14},... | collective-permute-start | bytes 417800 | tf_op jit(solution)/shard_map/ppermute | solution.py:295
  59.4 10.8 %collective-permute-start.18 = (bf16[64,2176]{1,0:T(8,128)(2,1)S(1)}, bf16[64,2176]{1,0:T(8,128)(2,1)S(1)}, u32[]{:S(2)}, u32[]{:S(2)}) collective-permute-start(bf16[64,2176]{1,0:T(8,128)(2,1)S(1)} %get-tuple-element.95), channel_id=1, source_target_pairs={{0,4},{4,0},{8,12},{12,8},{1,5},{5,1},{9,13},{13,9},{2,6},{6,2},{1... | collective-permute-start | bytes 835592 | tf_op jit(solution)/shard_map/ppermute | solution.py:288
  61.5 9.5 %collective-permute-start.19 = (bf16[32,2176]{1,0:T(8,128)(2,1)S(1)}, bf16[32,2176]{1,0:T(8,128)(2,1)S(1)}, u32[]{:S(2)}, u32[]{:S(2)}) collective-permute-start(bf16[32,2176]{1,0:T(8,128)(2,1)S(1)} %get-tuple-element.99), channel_id=1, source_target_pairs={{0,8},{4,12},{8,0},{12,4},{1,9},{5,13},{9,1},{13,5},{2,10},{6,14},... | collective-permute-start | bytes 417800 | tf_op jit(solution)/shard_map/ppermute | solution.py:295
  70.3 7.2 %collective-permute-start.20 = (bf16[32,2176]{1,0:T(8,128)(2,1)S(1)}, bf16[32,2176]{1,0:T(8,128)(2,1)S(1)}, u32[]{:S(2)}, u32[]{:S(2)}) collective-permute-start(bf16[32,2176]{1,0:T(8,128)(2,1)S(1)} %get-tuple-element.100), channel_id=1, source_target_pairs={{0,8},{4,12},{8,0},{12,4},{1,9},{5,13},{9,1},{13,5},{2,10},{6,14},... | collective-permute-start | bytes 417800 | tf_op jit(solution)/shard_map/ppermute | solution.py:297

commit v8 on v7

--- a/solution.py
+++ b/solution.py
@@ -11,8 +11,9 @@
 PANEL = 512
 DEPTH = 1024
 TURN = 15
-PIECES = (32, 32, 32, 32)
+PIECES = (48, 32, 32, 16)
 CUTS = 2
+FULL = 128
 MIB = 1 << 20
 
 
@@ -113,7 +114,8 @@
     def piece():
         near = [own_ref[at : at + rows, :], other_ref[at : at + rows, :]]
         passed = jnp.concatenate([ref[...] for ref in passed_refs], axis=1)
-        return jnp.concatenate([*near, direct_ref[...], passed], axis=0)
+        whole = [*near, direct_ref[...], passed]
+        return jnp.concatenate(whole * max(1, FULL // (4 * rows)), axis=0)
 
     every = jnp.dot(piece(), spread_ref[...], preferred_element_type=jnp.float32)
     ids = piece()[:, units : units + 1].astype(jnp.float32)
@@ -279,15 +281,16 @@
         if step + 1 < steps:
             direct.append(lax.ppermute(pieces[step + 1], "req", across))
         send, keep = product(step, passed, token)
-        hop = gots[step - 2 :] if step > 1 else []
+        late = step + 1 == steps
+        hop = gots if late else []
         if step + 1 < steps:
             got = lax.ppermute(send, "tensor", next_z)
             direct[step + 1], keep, parts, hop = after((direct[step + 1], keep, parts, hop))
         else:
-            send, parts, hop = after((send, parts, hop))
             got = lax.ppermute(send, "tensor", next_z)
-        if step > 1:
-            gots[step - 2 :] = hop
+            parts, hop = after((parts, hop))
+        if late:
+            gots = hop
         if step > 0:
             send = add_part(step - 1)
             if step + 1 < steps:

time: 79 us -> 81.4 us (1.030)
  Pallas kernels: 35.9 us -> 38.5 us
  starting transfers between devices: 23.4 us -> 21.2 us
  waiting for transfers between devices: 19.3 us -> 21.3 us
    ppermute x1, waiting for transfers between devices: 0.01 us -> 4.76 us  [paired(): direct = [lax.ppermute(pieces[0], 'req', across)]]
    ppermute x4, waiting for transfers between devices: 8.35 us -> 4.18 us  [paired(): got = lax.ppermute(send, 'tensor', next_z)]
    ppermute x3, waiting for transfers between devices: 3.59 us -> 0.01 us  [paired(): direct.append(lax.ppermute(pieces[step + 1], 'req', across))]
    pallas_call x4, Pallas kernels: 20.5 us -> 23.1 us  [product(): pl.pallas_call(functools.partial(product_kernel, adapters, units, starts[...]
    ppermute x4, starting transfers between devices: 7.26 us -> 4.72 us  [paired(): got = lax.ppermute(send, 'tensor', next_z)]
    ppermute x3, waiting for transfers between devices: 0.86 us -> 3.3 us  [paired(): gots.append(lax.ppermute(send, 'tensor', far_z))]
    ppermute x8, waiting for transfers between devices: 0.02 us -> 1.34 us  [over_core(): lax.ppermute(part[:, at:to], 'req', beside)]
    ppermute x1, waiting for transfers between devices: 6.49 us -> 7.67 us  [paired(): gots.append(lax.ppermute(add_part(steps - 1), 'tensor', far_z))]
  transfers between devices with their start and end apart: 21 -> 21, of which waited for: 8 -> 8; matrix products, arithmetic and copies ran while one was open for 0% -> 0% of each run, Pallas kernels for 41% -> 43%
where the time goes in v8:
time: 81.4 us; the launch traced here: 81.2 us
  Pallas kernels  38.5 us (47%)
  waiting for transfers between devices  21.3 us (26%)
  starting transfers between devices  21.2 us (26%)
    pallas_call x4, Pallas kernels, product(): pl.pallas_call(functools.partial(product_kernel, adapters, units, starts[...  23.1 us
    pallas_call x1, Pallas kernels, paired(): pl.pallas_call(load_kernel, out_shape=[jax.ShapeDtypeStruct((8, LANES), j...  11.9 us
    ppermute x1, waiting for transfers between devices, paired(): gots.append(lax.ppermute(add_part(steps - 1), 'tensor', far_z))  7.67 us
    ppermute x3, starting transfers between devices, paired(): gots.append(lax.ppermute(send, 'tensor', far_z))  5.69 us
    ppermute x1, waiting for transfers between devices, paired(): direct = [lax.ppermute(pieces[0], 'req', across)]  4.76 us
    ppermute x4, starting transfers between devices, paired(): got = lax.ppermute(send, 'tensor', next_z)  4.72 us
    ppermute x4, waiting for transfers between devices, paired(): got = lax.ppermute(send, 'tensor', next_z)  4.18 us
    ppermute x3, starting transfers between devices, paired(): direct.append(lax.ppermute(pieces[step + 1], 'req', across))  3.61 us
  transfers between devices with their start and end apart: 21, of which 8 were waited for; matrix products, arithmetic and copies ran while one was open for 0% of the time, Pallas kernels for 43%

profile of v8, /device:TPU:0, one launch (start us, length us, event | category | flops | bytes accessed | tf_op | source)
XLA Modules:
  0.0 81.2 jit_solution(3657252441223461725)
XLA Ops:
  0.0 1.8 %turn.1 = (bf16[128,7424]{1,0:T(8,128)(2,1)S(1)}, bf16[48,7424]{1,0:T(8,128)(2,1)S(1)}, bf16[32,7424]{1,0:T(8,128)(2,1)S(1)}, bf16[32,7424]{1,0:T(8,128)(2,1)S(1)}, bf16[16,7424]{1,0:T(8,128)(2,1)S(1)}) custom-call(bf16[7392,128]{1,0:T(8,128)(2,1)} %bitcast.8, s32[1,128]{1,0:T(1,128)} %bitcast.9), custom_call_target="tpu_custom_call" | custom-call | tf_op jit(solution)/shard_map/turn/pallas_call | solution.py:199
  1.8 3.0 %collective-permute-start.1 = (bf16[48,7424]{1,0:T(8,128)(2,1)S(1)}, bf16[48,7424]{1,0:T(8,128)(2,1)S(1)}, u32[]{:S(2)}, u32[]{:S(2)}) collective-permute-start(bf16[48,7424]{1,0:T(8,128)(2,1)S(1)} %get-tuple-element.53), channel_id=1, source_target_pairs={{0,2},{1,3},{2,0},{3,1},{4,6},{5,7},{6,4},{7,5},{8,10},{9,11},{10,... | collective-permute-start | bytes 2138120 | tf_op jit(solution)/shard_map/ppermute | solution.py:218
  5.0 11.9 %load.1 = (f32[8,128]{1,0:T(8,128)S(1)}, bf16[7424,512]{1,0:T(8,128)(2,1)S(1)}, bf16[7424,512]{1,0:T(8,128)(2,1)S(1)}, bf16[7424,512]{1,0:T(8,128)(2,1)S(1)}, bf...) custom-call(bf16[7392,2048]{1,0:T(8,128)(2,1)} %w_hbm.1, bf16[512,7392]{1,0:T(8,128)(2,1)} %bitcast.7), custom_call_target="tpu_custom_call" | custom-call | flops 1 | bytes 1 | tf_op jit(solution)/shard_map/load/pallas_call | solution.py:222
  16.9 4.8 %collective-permute-done.1.direct_ref = bf16[48,7424]{1,0:T(8,128)(2,1)S(1)} collective-permute-done((bf16[48,7424]{1,0:T(8,128)(2,1)S(1)}, bf16[48,7424]{1,0:T(8,128)(2,1)S(1)}, u32[]{:S(2)}, u32[]{:S(2)}) %collective-permute-start.1) | collective-permute-done | bytes 712736 | tf_op jit(solution)/shard_map/ppermute | solution.py:218
  22.2 2.1 %collective-permute-start = (bf16[32,7424]{1,0:T(8,128)(2,1)S(1)}, bf16[32,7424]{1,0:T(8,128)(2,1)S(1)}, u32[]{:S(2)}, u32[]{:S(2)}) collective-permute-start(bf16[32,7424]{1,0:T(8,128)(2,1)S(1)} %get-tuple-element.52), channel_id=1, source_target_pairs={{0,2},{1,3},{2,0},{3,1},{4,6},{5,7},{6,4},{7,5},{8,10},{9,11},{10,... | collective-permute-start | bytes 1425416 | tf_op jit(solution)/shard_map/ppermute | solution.py:282
  24.3 7.5 %product.4 = (bf16[96,2176]{1,0:T(8,128)(2,1)S(1)}, bf16[96,2176]{1,0:T(8,128)(2,1)S(1)}) custom-call(f32[8,128]{1,0:T(8,128)S(1)} %get-tuple-element.55._, bf16[128,7424]{1,0:T(8,128)(2,1)S(1)} %get-tuple-element.56.own_ref, bf16[128,7424]{1,0:T(8,128)(2,1)S(1)} %collective-permute-done.2.other_ref, bf16[48,7424]{1,0:T(8,128)(2,1)S(1)} %collective-permute-done.1.direct_ref, ...), custom_call_target="tpu_custom_call" | custom-call | flops 1 | bytes 1 | tf_op jit(solution)/shard_map/product/pallas_call | solution.py:240
  31.9 2.1 %collective-permute-start.8 = (bf16[96,2176]{1,0:T(8,128)(2,1)S(1)}, bf16[96,2176]{1,0:T(8,128)(2,1)S(1)}, u32[]{:S(2)}, u32[]{:S(2)}) collective-permute-start(bf16[96,2176]{1,0:T(8,128)(2,1)S(1)} %get-tuple-element.68), channel_id=1, source_target_pairs={{0,4},{4,0},{8,12},{12,8},{1,5},{5,1},{9,13},{13,9},{2,6},{6,2},{1... | collective-permute-start | bytes 1253384 | tf_op jit(solution)/shard_map/ppermute | solution.py:287
  34.6 1.0 %collective-permute-done.7.refs_1_ = bf16[32,3712]{1,0:T(8,128)(2,1)S(1)} collective-permute-done((bf16[32,3712]{1,0:T(8,128)(2,1)S(1)}, bf16[32,3712]{1,0:T(8,128)(2,1)S(1)}, u32[]{:S(2)}, u32[]{:S(2)}) %collective-permute-start.7) | collective-permute-done | bytes 237600 | tf_op jit(solution)/shard_map/ppermute | solution.py:265
  35.9 5.3 %product.5 = (bf16[64,2176]{1,0:T(8,128)(2,1)S(1)}, bf16[64,2176]{1,0:T(8,128)(2,1)S(1)}) custom-call(f32[8,128]{1,0:T(8,128)S(1)} %get-tuple-element.55._, bf16[128,7424]{1,0:T(8,128)(2,1)S(1)} %get-tuple-element.56.own_ref, bf16[128,7424]{1,0:T(8,128)(2,1)S(1)} %collective-permute-done.2.other_ref, bf16[32,7424]{1,0:T(8,128)(2,1)S(1)} %collective-permute-done.3.direct_ref, ...), custom_call_target="tpu_custom_call" | custom-call | flops 1 | bytes 1 | tf_op jit(solution)/shard_map/product/pallas_call | solution.py:240
  41.3 2.6 %collective-permute-done.8.second_ref = bf16[96,2176]{1,0:T(8,128)(2,1)S(1)} collective-permute-done((bf16[96,2176]{1,0:T(8,128)(2,1)S(1)}, bf16[96,2176]{1,0:T(8,128)(2,1)S(1)}, u32[]{:S(2)}, u32[]{:S(2)}) %collective-permute-start.8) | collective-permute-done | bytes 417824 | tf_op jit(solution)/shard_map/ppermute | solution.py:287
  44.6 1.4 %collective-permute-start.9 = (bf16[16,7424]{1,0:T(8,128)(2,1)S(1)}, bf16[16,7424]{1,0:T(8,128)(2,1)S(1)}, u32[]{:S(2)}, u32[]{:S(2)}) collective-permute-start(bf16[16,7424]{1,0:T(8,128)(2,1)S(1)} %get-tuple-element.74), channel_id=1, source_target_pairs={{0,2},{1,3},{2,0},{3,1},{4,6},{5,7},{6,4},{7,5},{8,10},{9,11},{10,... | collective-permute-start | bytes 712712 | tf_op jit(solution)/shard_map/ppermute | solution.py:282
  46.0 2.6 %collective-permute-start.14 = (bf16[48,2176]{1,0:T(8,128)(2,1)S(1)}, bf16[48,2176]{1,0:T(8,128)(2,1)S(1)}, u32[]{:S(2)}, u32[]{:S(2)}) collective-permute-start(bf16[48,2176]{1,0:T(8,128)(2,1)S(1)} %get-tuple-element.86), channel_id=1, source_target_pairs={{0,8},{4,12},{8,0},{12,4},{1,9},{5,13},{9,1},{13,5},{2,10},{6,14},... | collective-permute-start | bytes 626696 | tf_op jit(solution)/shard_map/ppermute | solution.py:298
  48.6 5.1 %product.6 = (bf16[64,2176]{1,0:T(8,128)(2,1)S(1)}, bf16[64,2176]{1,0:T(8,128)(2,1)S(1)}) custom-call(f32[8,128]{1,0:T(8,128)S(1)} %get-tuple-element.55._, bf16[128,7424]{1,0:T(8,128)(2,1)S(1)} %get-tuple-element.56.own_ref, bf16[128,7424]{1,0:T(8,128)(2,1)S(1)} %collective-permute-done.2.other_ref, bf16[32,7424]{1,0:T(8,128)(2,1)S(1)} %collective-permute-done.direct_ref, ...), custom_call_target="tpu_custom_call" | custom-call | flops 1 | bytes 1 | tf_op jit(solution)/shard_map/product/pallas_call | solution.py:240
  53.9 2.5 %collective-permute-start.13 = (bf16[64,2176]{1,0:T(8,128)(2,1)S(1)}, bf16[64,2176]{1,0:T(8,128)(2,1)S(1)}, u32[]{:S(2)}, u32[]{:S(2)}) collective-permute-start(bf16[64,2176]{1,0:T(8,128)(2,1)S(1)} %get-tuple-element.85), channel_id=1, source_target_pairs={{0,4},{4,0},{8,12},{12,8},{1,5},{5,1},{9,13},{13,9},{2,6},{6,2},{1... | collective-permute-start | bytes 835592 | tf_op jit(solution)/shard_map/ppermute | solution.py:287
  56.5 0.5 collective-permute-start.16
  57.0 1.1 %collective-permute-start.15 = (bf16[32,2176]{1,0:T(8,128)(2,1)S(1)}, bf16[32,2176]{1,0:T(8,128)(2,1)S(1)}, u32[]{:S(2)}, u32[]{:S(2)}) collective-permute-start(bf16[32,2176]{1,0:T(8,128)(2,1)S(1)} %get-tuple-element.87), channel_id=1, source_target_pairs={{0,8},{4,12},{8,0},{12,4},{1,9},{5,13},{9,1},{13,5},{2,10},{6,14},... | collective-permute-start | bytes 417800 | tf_op jit(solution)/shard_map/ppermute | solution.py:298
  58.1 5.1 %product.7 = (bf16[32,2176]{1,0:T(8,128)(2,1)S(1)}, bf16[32,2176]{1,0:T(8,128)(2,1)S(1)}) custom-call(f32[8,128]{1,0:T(8,128)S(1)} %get-tuple-element.55._, bf16[128,7424]{1,0:T(8,128)(2,1)S(1)} %get-tuple-element.56.own_ref, bf16[128,7424]{1,0:T(8,128)(2,1)S(1)} %collective-permute-done.2.other_ref, bf16[16,7424]{1,0:T(8,128)(2,1)S(1)} %collective-permute-done.9.direct_ref, ...), custom_call_target="tpu_custom_call" | custom-call | flops 1 | bytes 1 | tf_op jit(solution)/shard_map/product/pallas_call | solution.py:240
  63.3 3.3 %collective-permute-done.15.refs_5_ = bf16[32,2176]{1,0:T(8,128)(2,1)S(1)} collective-permute-done((bf16[32,2176]{1,0:T(8,128)(2,1)S(1)}, bf16[32,2176]{1,0:T(8,128)(2,1)S(1)}, u32[]{:S(2)}, u32[]{:S(2)}) %collective-permute-start.15) | collective-permute-done | bytes 139296 | tf_op jit(solution)/shard_map/ppermute | solution.py:298
  66.6 0.8 collective-permute-done.13.second_ref
  67.5 2.0 %collective-permute-start.19 = (bf16[32,2176]{1,0:T(8,128)(2,1)S(1)}, bf16[32,2176]{1,0:T(8,128)(2,1)S(1)}, u32[]{:S(2)}, u32[]{:S(2)}) collective-permute-start(bf16[32,2176]{1,0:T(8,128)(2,1)S(1)} %get-tuple-element.97), channel_id=1, source_target_pairs={{0,8},{4,12},{8,0},{12,4},{1,9},{5,13},{9,1},{13,5},{2,10},{6,14},... | collective-permute-start | bytes 417800 | tf_op jit(solution)/shard_map/ppermute | solution.py:298
  69.5 0.8 %collective-permute-done.18.second_ref = bf16[32,2176]{1,0:T(8,128)(2,1)S(1)} collective-permute-done((bf16[32,2176]{1,0:T(8,128)(2,1)S(1)}, bf16[32,2176]{1,0:T(8,128)(2,1)S(1)}, u32[]{:S(2)}, u32[]{:S(2)}) %collective-permute-start.18) | collective-permute-done | bytes 139296 | tf_op jit(solution)/shard_map/ppermute | solution.py:290
  70.3 1.9 %collective-permute-start.20 = (bf16[16,2176]{1,0:T(8,128)(2,1)S(1)}, bf16[16,2176]{1,0:T(8,128)(2,1)S(1)}, u32[]{:S(2)}, u32[]{:S(2)}) collective-permute-start(bf16[16,2176]{1,0:T(8,128)(2,1)S(1)} %get-tuple-element.98), channel_id=1, source_target_pairs={{0,8},{4,12},{8,0},{12,4},{1,9},{5,13},{9,1},{13,5},{2,10},{6,14},... | collective-permute-start | bytes 208904 | tf_op jit(solution)/shard_map/ppermute | solution.py:300
  72.2 7.7 %collective-permute-done.20.refs_7_ = bf16[16,2176]{1,0:T(8,128)(2,1)S(1)} collective-permute-done((bf16[16,2176]{1,0:T(8,128)(2,1)S(1)}, bf16[16,2176]{1,0:T(8,128)(2,1)S(1)}, u32[]{:S(2)}, u32[]{:S(2)}) %collective-permute-start.20) | collective-permute-done | bytes 69664 | tf_op jit(solution)/shard_map/ppermute | solution.py:300
  79.9 1.3 %last.1 = bf16[128,2048]{1,0:T(8,128)(2,1)} custom-call(bf16[512,2048]{1,0:T(8,128)(2,1)S(1)} %bitcast.6, bf16[48,2176]{1,0:T(8,128)(2,1)S(1)} %get-tuple-element.73.refs_0_, bf16[32,2176]{1,0:T(8,128)(2,1)S(1)} %get-tuple-element.83.refs_1_, bf16[32,2176]{1,0:T(8,128)(2,1)S(1)} %get-tuple-element.90.refs_2_, ...), custom_call_target="tpu_custom_call" | custom-call | tf_op jit(solution)/shard_map/last/pallas_call | solution.py:302
  (35 shorter events, 3.0 us)
Async XLA Ops:
  1.8 19.8 %collective-permute-start.1 = (bf16[48,7424]{1,0:T(8,128)(2,1)S(1)}, bf16[48,7424]{1,0:T(8,128)(2,1)S(1)}, u32[]{:S(2)}, u32[]{:S(2)}) collective-permute-start(bf16[48,7424]{1,0:T(8,128)(2,1)S(1)} %get-tuple-element.53), channel_id=1, source_target_pairs={{0,2},{1,3},{2,0},{3,1},{4,6},{5,7},{6,4},{7,5},{8,10},{9,11},{10,... | collective-permute-start | bytes 2138120 | tf_op jit(solution)/shard_map/ppermute | solution.py:218
  4.8 19.5 %collective-permute-start.2 = (bf16[128,7424]{1,0:T(8,128)(2,1)S(1)}, bf16[128,7424]{1,0:T(8,128)(2,1)S(1)}, u32[]{:S(2)}, u32[]{:S(2)}) collective-permute-start(bf16[128,7424]{1,0:T(8,128)(2,1)S(1)} %get-tuple-element.56.own_ref), channel_id=1, source_target_pairs={{0,1},{1,0},{2,3},{3,2},{4,5},{5,4},{6,7},{7,6},{8,9},{9,8},{10,11... | collective-permute-start | bytes 5701640 | tf_op jit(solution)/shard_map/ppermute | solution.py:219
  4.8 27.0 %collective-permute-start.3 = (bf16[32,7424]{1,0:T(8,128)(2,1)S(1)}, bf16[32,7424]{1,0:T(8,128)(2,1)S(1)}, u32[]{:S(2)}, u32[]{:S(2)}) collective-permute-start(bf16[32,7424]{1,0:T(8,128)(2,1)S(1)} %get-tuple-element.57), channel_id=1, source_target_pairs={{0,2},{1,3},{2,0},{3,1},{4,6},{5,7},{6,4},{7,5},{8,10},{9,11},{10,... | collective-permute-start | bytes 1425416 | tf_op jit(solution)/shard_map/ppermute | solution.py:282
  21.7 2.6 %collective-permute-start.5 = (bf16[48,3712]{1,0:T(8,128)(2,1)S(1)}, bf16[48,3712]{1,0:T(8,128)(2,1)S(1)}, u32[]{:S(2)}, u32[]{:S(2)}) collective-permute-start(bf16[48,3712]{1,0:T(8,128)(2,1)S(1)} %get-tuple-element.99), channel_id=1, source_target_pairs={{0,1},{1,0},{2,3},{3,2},{4,5},{5,4},{6,7},{7,6},{8,9},{9,8},{10,11... | collective-permute-start | bytes 1069064 | tf_op jit(solution)/shard_map/ppermute | solution.py:265
  21.8 2.6 %collective-permute-start.4 = (bf16[48,3712]{1,0:T(8,128)(2,1)S(1)}, bf16[48,3712]{1,0:T(8,128)(2,1)S(1)}, u32[]{:S(2)}, u32[]{:S(2)}) collective-permute-start(bf16[48,3712]{1,0:T(8,128)(2,1)S(1)} %get-tuple-element.100), channel_id=1, source_target_pairs={{0,1},{1,0},{2,3},{3,2},{4,5},{5,4},{6,7},{7,6},{8,9},{9,8},{10,11... | collective-permute-start | bytes 1069064 | tf_op jit(solution)/shard_map/ppermute | solution.py:265
  22.2 19.0 %collective-permute-start = (bf16[32,7424]{1,0:T(8,128)(2,1)S(1)}, bf16[32,7424]{1,0:T(8,128)(2,1)S(1)}, u32[]{:S(2)}, u32[]{:S(2)}) collective-permute-start(bf16[32,7424]{1,0:T(8,128)(2,1)S(1)} %get-tuple-element.52), channel_id=1, source_target_pairs={{0,2},{1,3},{2,0},{3,1},{4,6},{5,7},{6,4},{7,5},{8,10},{9,11},{10,... | collective-permute-start | bytes 1425416 | tf_op jit(solution)/shard_map/ppermute | solution.py:282
  31.9 12.0 %collective-permute-start.8 = (bf16[96,2176]{1,0:T(8,128)(2,1)S(1)}, bf16[96,2176]{1,0:T(8,128)(2,1)S(1)}, u32[]{:S(2)}, u32[]{:S(2)}) collective-permute-start(bf16[96,2176]{1,0:T(8,128)(2,1)S(1)} %get-tuple-element.68), channel_id=1, source_target_pairs={{0,4},{4,0},{8,12},{12,8},{1,5},{5,1},{9,13},{13,9},{2,6},{6,2},{1... | collective-permute-start | bytes 1253384 | tf_op jit(solution)/shard_map/ppermute | solution.py:287
  34.0 1.6 %collective-permute-start.7 = (bf16[32,3712]{1,0:T(8,128)(2,1)S(1)}, bf16[32,3712]{1,0:T(8,128)(2,1)S(1)}, u32[]{:S(2)}, u32[]{:S(2)}) collective-permute-start(bf16[32,3712]{1,0:T(8,128)(2,1)S(1)} %get-tuple-element.103), channel_id=1, source_target_pairs={{0,1},{1,0},{2,3},{3,2},{4,5},{5,4},{6,7},{7,6},{8,9},{9,8},{10,11... | collective-permute-start | bytes 712712 | tf_op jit(solution)/shard_map/ppermute | solution.py:265
  34.1 1.8 %collective-permute-start.6 = (bf16[32,3712]{1,0:T(8,128)(2,1)S(1)}, bf16[32,3712]{1,0:T(8,128)(2,1)S(1)}, u32[]{:S(2)}, u32[]{:S(2)}) collective-permute-start(bf16[32,3712]{1,0:T(8,128)(2,1)S(1)} %get-tuple-element.104), channel_id=1, source_target_pairs={{0,1},{1,0},{2,3},{3,2},{4,5},{5,4},{6,7},{7,6},{8,9},{9,8},{10,11... | collective-permute-start | bytes 712712 | tf_op jit(solution)/shard_map/ppermute | solution.py:265
  41.2 12.6 %collective-permute-start.12 = (bf16[64,2176]{1,0:T(8,128)(2,1)S(1)}, bf16[64,2176]{1,0:T(8,128)(2,1)S(1)}, u32[]{:S(2)}, u32[]{:S(2)}) collective-permute-start(bf16[64,2176]{1,0:T(8,128)(2,1)S(1)} %get-tuple-element.78), channel_id=1, source_target_pairs={{0,4},{4,0},{8,12},{12,8},{1,5},{5,1},{9,13},{13,9},{2,6},{6,2},{1... | collective-permute-start | bytes 835592 | tf_op jit(solution)/shard_map/ppermute | solution.py:287
  44.1 4.6 %collective-permute-start.11 = (bf16[32,3712]{1,0:T(8,128)(2,1)S(1)}, bf16[32,3712]{1,0:T(8,128)(2,1)S(1)}, u32[]{:S(2)}, u32[]{:S(2)}) collective-permute-start(bf16[32,3712]{1,0:T(8,128)(2,1)S(1)} %get-tuple-element.101), channel_id=1, source_target_pairs={{0,1},{1,0},{2,3},{3,2},{4,5},{5,4},{6,7},{7,6},{8,9},{9,8},{10,11... | collective-permute-start | bytes 712712 | tf_op jit(solution)/shard_map/ppermute | solution.py:265
  44.1 4.5 %collective-permute-start.10 = (bf16[32,3712]{1,0:T(8,128)(2,1)S(1)}, bf16[32,3712]{1,0:T(8,128)(2,1)S(1)}, u32[]{:S(2)}, u32[]{:S(2)}) collective-permute-start(bf16[32,3712]{1,0:T(8,128)(2,1)S(1)} %get-tuple-element.102), channel_id=1, source_target_pairs={{0,1},{1,0},{2,3},{3,2},{4,5},{5,4},{6,7},{7,6},{8,9},{9,8},{10,11... | collective-permute-start | bytes 712712 | tf_op jit(solution)/shard_map/ppermute | solution.py:265
  44.6 9.1 %collective-permute-start.9 = (bf16[16,7424]{1,0:T(8,128)(2,1)S(1)}, bf16[16,7424]{1,0:T(8,128)(2,1)S(1)}, u32[]{:S(2)}, u32[]{:S(2)}) collective-permute-start(bf16[16,7424]{1,0:T(8,128)(2,1)S(1)} %get-tuple-element.74), channel_id=1, source_target_pairs={{0,2},{1,3},{2,0},{3,1},{4,6},{5,7},{6,4},{7,5},{8,10},{9,11},{10,... | collective-permute-start | bytes 712712 | tf_op jit(solution)/shard_map/ppermute | solution.py:282
  46.0 17.3 %collective-permute-start.14 = (bf16[48,2176]{1,0:T(8,128)(2,1)S(1)}, bf16[48,2176]{1,0:T(8,128)(2,1)S(1)}, u32[]{:S(2)}, u32[]{:S(2)}) collective-permute-start(bf16[48,2176]{1,0:T(8,128)(2,1)S(1)} %get-tuple-element.86), channel_id=1, source_target_pairs={{0,8},{4,12},{8,0},{12,4},{1,9},{5,13},{9,1},{13,5},{2,10},{6,14},... | collective-permute-start | bytes 626696 | tf_op jit(solution)/shard_map/ppermute | solution.py:298
  53.9 13.5 %collective-permute-start.13 = (bf16[64,2176]{1,0:T(8,128)(2,1)S(1)}, bf16[64,2176]{1,0:T(8,128)(2,1)S(1)}, u32[]{:S(2)}, u32[]{:S(2)}) collective-permute-start(bf16[64,2176]{1,0:T(8,128)(2,1)S(1)} %get-tuple-element.85), channel_id=1, source_target_pairs={{0,4},{4,0},{8,12},{12,8},{1,5},{5,1},{9,13},{13,9},{2,6},{6,2},{1... | collective-permute-start | bytes 835592 | tf_op jit(solution)/shard_map/ppermute | solution.py:287
  56.4 1.7 %collective-permute-start.17 = (bf16[16,3712]{1,0:T(8,128)(2,1)S(1)}, bf16[16,3712]{1,0:T(8,128)(2,1)S(1)}, u32[]{:S(2)}, u32[]{:S(2)}) collective-permute-start(bf16[16,3712]{1,0:T(8,128)(2,1)S(1)} %get-tuple-element.105), channel_id=1, source_target_pairs={{0,1},{1,0},{2,3},{3,2},{4,5},{5,4},{6,7},{7,6},{8,9},{9,8},{10,11... | collective-permute-start | bytes 356360 | tf_op jit(solution)/shard_map/ppermute | solution.py:265
  56.5 1.6 %collective-permute-start.16 = (bf16[16,3712]{1,0:T(8,128)(2,1)S(1)}, bf16[16,3712]{1,0:T(8,128)(2,1)S(1)}, u32[]{:S(2)}, u32[]{:S(2)}) collective-permute-start(bf16[16,3712]{1,0:T(8,128)(2,1)S(1)} %get-tuple-element.106), channel_id=1, source_target_pairs={{0,1},{1,0},{2,3},{3,2},{4,5},{5,4},{6,7},{7,6},{8,9},{9,8},{10,11... | collective-permute-start | bytes 356360 | tf_op jit(solution)/shard_map/ppermute | solution.py:265
  57.0 23.0 %copy-start = (bf16[8,64,2048]{2,1,0:T(8,128)(2,1)S(1)}, bf16[8,64,2048]{2,1,0:T(8,128)(2,1)}, u32[]{:S(2)}) copy-start(bf16[8,64,2048]{2,1,0:T(8,128)(2,1)} %param.8) | copy-start | bytes 6291460
  57.0 9.7 %collective-permute-start.15 = (bf16[32,2176]{1,0:T(8,128)(2,1)S(1)}, bf16[32,2176]{1,0:T(8,128)(2,1)S(1)}, u32[]{:S(2)}, u32[]{:S(2)}) collective-permute-start(bf16[32,2176]{1,0:T(8,128)(2,1)S(1)} %get-tuple-element.87), channel_id=1, source_target_pairs={{0,8},{4,12},{8,0},{12,4},{1,9},{5,13},{9,1},{13,5},{2,10},{6,14},... | collective-permute-start | bytes 417800 | tf_op jit(solution)/shard_map/ppermute | solution.py:298
  63.2 7.0 %collective-permute-start.18 = (bf16[32,2176]{1,0:T(8,128)(2,1)S(1)}, bf16[32,2176]{1,0:T(8,128)(2,1)S(1)}, u32[]{:S(2)}, u32[]{:S(2)}) collective-permute-start(bf16[32,2176]{1,0:T(8,128)(2,1)S(1)} %get-tuple-element.93), channel_id=1, source_target_pairs={{0,4},{4,0},{8,12},{12,8},{1,5},{5,1},{9,13},{13,9},{2,6},{6,2},{1... | collective-permute-start | bytes 417800 | tf_op jit(solution)/shard_map/ppermute | solution.py:290
  67.5 12.4 %collective-permute-start.19 = (bf16[32,2176]{1,0:T(8,128)(2,1)S(1)}, bf16[32,2176]{1,0:T(8,128)(2,1)S(1)}, u32[]{:S(2)}, u32[]{:S(2)}) collective-permute-start(bf16[32,2176]{1,0:T(8,128)(2,1)S(1)} %get-tuple-element.97), channel_id=1, source_target_pairs={{0,8},{4,12},{8,0},{12,4},{1,9},{5,13},{9,1},{13,5},{2,10},{6,14},... | collective-permute-start | bytes 417800 | tf_op jit(solution)/shard_map/ppermute | solution.py:298
  70.3 9.6 %collective-permute-start.20 = (bf16[16,2176]{1,0:T(8,128)(2,1)S(1)}, bf16[16,2176]{1,0:T(8,128)(2,1)S(1)}, u32[]{:S(2)}, u32[]{:S(2)}) collective-permute-start(bf16[16,2176]{1,0:T(8,128)(2,1)S(1)} %get-tuple-element.98), channel_id=1, source_target_pairs={{0,8},{4,12},{8,0},{12,4},{1,9},{5,13},{9,1},{13,5},{2,10},{6,14},... | collective-permute-start | bytes 208904 | tf_op jit(solution)/shard_map/ppermute | solution.py:300

commit v9 on v7

--- a/solution.py
+++ b/solution.py
@@ -12,7 +12,8 @@
 DEPTH = 1024
 TURN = 15
 PIECES = (32, 32, 32, 32)
-CUTS = 2
+CUTS = (2, 2, 2, 2)
+HALVES = (1, 1, 1, 2)
 MIB = 1 << 20
 
 
@@ -102,35 +103,38 @@
         keep_ref[at, cols] = jnp.where(keep_first, first, second)
 
 
-def product_kernel(adapters, units, at, _, own_ref, other_ref, direct_ref, *refs):
-    passed_refs, refs = refs[:CUTS], refs[CUTS:]
+def product_kernel(
+    adapters, units, at, cuts, half, halves, _, own_ref, other_ref, direct_ref, *refs
+):
+    passed_refs, refs = refs[:cuts], refs[cuts:]
     *panel_refs, spread_ref, send_ref, keep_ref = refs
+    count = len(panel_refs) // halves
+    panel_refs = panel_refs[half * count : (half + 1) * count]
     rows = direct_ref.shape[0]
-    width = send_ref.shape[1] - LANES
-    wide = spread_ref.shape[1]
-    rank = wide // adapters
 
     def piece():
         near = [own_ref[at : at + rows, :], other_ref[at : at + rows, :]]
         passed = jnp.concatenate([ref[...] for ref in passed_refs], axis=1)
         return jnp.concatenate([*near, direct_ref[...], passed], axis=0)
 
-    every = jnp.dot(piece(), spread_ref[...], preferred_element_type=jnp.float32)
-    ids = piece()[:, units : units + 1].astype(jnp.float32)
-    column = lax.broadcasted_iota(jnp.int32, every.shape, 1) // rank
-    picked = jnp.where(column.astype(jnp.float32) == ids, every, 0.0)
-    tile = picked[:, :LANES]
-    for lane in range(LANES, wide, LANES):
-        tile = tile + picked[:, lane : lane + LANES]
-    tile = tile + pltpu.roll(tile, rank, 1)
-    lane = lax.broadcasted_iota(jnp.int32, tile.shape, 1)
-    tile = jnp.where(lane < rank, tile, ids)
-    part_rows(tile, slice(width, width + LANES), send_ref, keep_ref)
+    if half == 0:
+        width = send_ref.shape[1] - LANES
+        wide = spread_ref.shape[1]
+        rank = wide // adapters
+        every = jnp.dot(piece(), spread_ref[...], preferred_element_type=jnp.float32)
+        ids = piece()[:, units : units + 1].astype(jnp.float32)
+        column = lax.broadcasted_iota(jnp.int32, every.shape, 1) // rank
+        picked = jnp.where(column.astype(jnp.float32) == ids, every, 0.0)
+        tile = picked[:, :LANES]
+        for lane in range(LANES, wide, LANES):
+            tile = tile + picked[:, lane : lane + LANES]
+        tile = tile + pltpu.roll(tile, rank, 1)
+        lane = lax.broadcasted_iota(jnp.int32, tile.shape, 1)
+        tile = jnp.where(lane < rank, tile, ids)
+        part_rows(tile, slice(width, width + LANES), send_ref, keep_ref)
 
     for panel, panel_ref in enumerate(panel_refs):
-        value = jnp.dot(
-            piece(), panel_ref[...], preferred_element_type=jnp.float32
-        )
+        value = jnp.dot(piece(), panel_ref[...], preferred_element_type=jnp.float32)
         part_rows(value, slice(panel * PANEL, (panel + 1) * PANEL), send_ref, keep_ref)
 
 
@@ -148,21 +152,27 @@
     keep_ref[...] = jnp.where(keep_near, near, far)
 
 
-def last_kernel(n_tensor, adapters, expand_ref, *refs):
-    out_ref = refs[-1]
-    count = (len(refs) - 1) // 2
-    kept, got = refs[:count], refs[count:-1]
+def last_kernel(n_tensor, adapters, halves, expand_ref, *refs):
+    *sums, out_ref = refs
     wide, width = expand_ref.shape
     rank = wide // adapters
-
-    def whole(cols):
-        parts = [
-            first[:, cols].astype(jnp.float32) + second[:, cols].astype(jnp.float32)
-            for first, second in zip(kept, got)
-        ]
+    pieces, at = [], 0
+    for count in halves:
+        pieces.append(sums[at : at + 2 * count])
+        at += 2 * count
+
+    def whole(first, lanes):
+        parts = []
+        for piece in pieces:
+            step = 2 * width // len(piece)
+            half = 0 if first == width else first // step
+            start = step if first == width else first % step
+            kept, got = piece[2 * half : 2 * half + 2]
+            cols = slice(start, start + lanes)
+            parts.append(kept[:, cols].astype(jnp.float32) + got[:, cols].astype(jnp.float32))
         return jnp.concatenate(parts, axis=0)
 
-    small = whole(slice(width, width + LANES))
+    small = whole(width, LANES)
     ids = small[:, rank : rank + 1] * (1.0 / n_tensor)
     lane = lax.broadcasted_iota(jnp.int32, small.shape, 1)
     shrink = jnp.where(lane < rank, small, 0.0)
@@ -173,7 +183,7 @@
     for at in range(0, width, PANEL):
         cols = slice(at, at + PANEL)
         adapter = jnp.dot(placed, expand_ref[:, cols], preferred_element_type=jnp.float32)
-        out_ref[:, cols] = (whole(cols) + adapter).astype(out_ref.dtype)
+        out_ref[:, cols] = (whole(at, PANEL) + adapter).astype(out_ref.dtype)
 
 
 def paired(n_tensor, n_req, hidden, weight, shrink, expand, ids):
@@ -234,21 +244,26 @@
         name="load",
     )(left(weight), left(shrink_rows))
 
-    def product(step, passed, token):
+    def product(step, half, passed, token):
+        count = width // PANEL // HALVES[step]
+        lanes = count * PANEL + (LANES if half == 0 else 0)
         return pl.pallas_call(
-            functools.partial(product_kernel, adapters, units, starts[step]),
-            out_shape=[struct(2 * counts[step], payload)] * 2,
-            in_specs=[in_vmem()] * (4 + CUTS + len(both)),
+            functools.partial(
+                product_kernel, adapters, units, starts[step], len(passed), half, HALVES[step]
+            ),
+            out_shape=[struct(2 * counts[step], lanes)] * 2,
+            in_specs=[in_vmem()] * (4 + len(passed) + len(both)),
             out_specs=[in_vmem()] * 2,
             compiler_params=params(4),
             cost_estimate=quick,
             name="product",
         )(token, own, other, direct[step], *passed, *both)
 
-    def add(step, keep, got):
+    def add(keep, got):
+        half = (keep.shape[0] // 2, keep.shape[1])
         return pl.pallas_call(
             add_kernel,
-            out_shape=[struct(counts[step], payload)] * 2,
+            out_shape=[struct(*half)] * 2,
             in_specs=[in_vmem()] * 2,
             out_specs=[in_vmem()] * 2,
             compiler_params=params(4),
@@ -256,54 +271,66 @@
             name="add",
         )(keep, got)
 
-    def over_core(part):
+    def over_core(part, cuts):
         tiles = room // LANES
-        ends = [tiles * cut // CUTS * LANES for cut in range(CUTS + 1)]
+        ends = [tiles * cut // cuts * LANES for cut in range(cuts + 1)]
         return [
             lax.ppermute(part[:, at:to], "req", beside) for at, to in zip(ends, ends[1:])
         ]
+
+    def hop_next(send):
+        return lax.ppermute(send, "tensor", next_z)
+
+    def hop_far(send):
+        return lax.ppermute(send, "tensor", far_z)
 
     after = lax.optimization_barrier
     steps = len(counts)
     direct[0], token = after((direct[0], token))
     parts, kept, gots = [], [], []
-
-    def add_part(step):
-        keep, got = parts[step]
-        send, keep = add(step, keep, got)
-        kept.append(keep)
-        return send
-
-    for step in range(steps):
-        passed = over_core(direct[step])
-        if step + 1 < steps:
-            direct.append(lax.ppermute(pieces[step + 1], "req", across))
-        send, keep = product(step, passed, token)
-        hop = gots[step - 2 :] if step > 1 else []
-        if step + 1 < steps:
-            got = lax.ppermute(send, "tensor", next_z)
-            direct[step + 1], keep, parts, hop = after((direct[step + 1], keep, parts, hop))
+    for step in range(steps - 1):
+        passed = over_core(direct[step], CUTS[step])
+        direct.append(lax.ppermute(pieces[step + 1], "req", across))
+        send, keep = product(step, 0, passed, token)
+        got = hop_next(send)
+        hops = gots[step - 2 :] if step > 1 else []
+        keep, parts, hops = after((keep, parts, hops))
+        if step > 1:
+            gots[step - 2 :] = hops
+        if step > 0:
+            send, stays = add(*parts[step - 1])
+            kept.append(stays)
+            gots.append(hop_far(send))
         else:
-            send, parts, hop = after((send, parts, hop))
-            got = lax.ppermute(send, "tensor", next_z)
-        if step > 1:
-            gots[step - 2 :] = hop
+            stays = keep
+        direct[step + 1], stays = after((direct[step + 1], stays))
         if step > 0:
-            send = add_part(step - 1)
-            if step + 1 < steps:
-                direct[step + 1], kept[-1] = after((direct[step + 1], kept[-1]))
-            gots.append(lax.ppermute(send, "tensor", far_z))
+            kept[-1] = stays
+        else:
+            keep = stays
         parts.append((keep, got))
-    gots.append(lax.ppermute(add_part(steps - 1), "tensor", far_z))
+
+    passed = over_core(direct[-1], CUTS[-1])
+    for half in range(HALVES[-1]):
+        send, keep = product(steps - 1, half, passed, token)
+        if half == 0:
+            send, parts = after((send, parts))
+        passed, keep, gots = after((passed, keep, gots))
+        parts.append((keep, hop_next(send)))
+    for keep, got in parts[steps - 2 :]:
+        send, stays = add(keep, got)
+        kept.append(stays)
+        gots.append(hop_far(send))
+    sums = [array for pair in zip(kept, gots) for array in pair]
 
     return pl.pallas_call(
-        functools.partial(last_kernel, n_tensor, adapters),
+        functools.partial(last_kernel, n_tensor, adapters, HALVES),
         out_shape=struct(rows, width),
-        in_specs=[in_vmem()] * (1 + 2 * steps),
+        in_specs=[in_vmem()] * (1 + len(sums)),
         out_specs=in_vmem(),
         compiler_params=params(8),
         name="last",
-    )(expand.reshape(wide, width), *kept, *gots)
+    )(expand.reshape(wide, width), *sums)
 
 
 def gathered(hidden, weight, shrink, expand, ids):

time: 79 us -> 79.2 us (level)
  starting transfers between devices: 23.4 us -> 27.1 us
  waiting for transfers between devices: 19.3 us -> 15.6 us
    ppermute x8 -> x10, starting transfers between devices: 14.5 us -> 18.2 us  [the longest x5 11.2 us: hop_far(): return lax.ppermute(send, 'tensor', far_z)]
    ppermute x8 -> x10, waiting for transfers between devices: 15.7 us -> 13 us  [the longest x5 7.04 us: hop_next(): return lax.ppermute(send, 'tensor', next_z)]
    ppermute x3, waiting for transfers between devices: 3.59 us -> 2.62 us  [paired(): direct.append(lax.ppermute(pieces[step + 1], 'req', across))]
    pallas_call x4 -> x5, Pallas kernels: 20.5 us -> 20.7 us  [product(): pl.pallas_call(functools.partial(product_kernel, adapters, units, starts[...]
    pallas_call x5 -> x6, Pallas kernels: 1.66 us -> 1.66 us  [the longest x1 1.31 us: paired(): pl.pallas_call(functools.partial(last_kernel, n_tensor, adapters, HALVES)...]
  transfers between devices with their start and end apart: 21 -> 23, of which waited for: 8 -> 9; matrix products, arithmetic and copies ran while one was open for 0% -> 0% of each run, Pallas kernels for 41% -> 42%
where the time goes in v9:
time: 79.2 us; the launch traced here: 79 us
  Pallas kernels  36 us (45%)
  starting transfers between devices  27.1 us (34%)
  waiting for transfers between devices  15.6 us (20%)
    pallas_call x5, Pallas kernels, product(): pl.pallas_call(functools.partial(product_kernel, adapters, units, starts[...  20.7 us
    pallas_call x1, Pallas kernels, paired(): pl.pallas_call(load_kernel, out_shape=[jax.ShapeDtypeStruct((8, LANES), j...  11.9 us
    ppermute x5, starting transfers between devices, hop_far(): return lax.ppermute(send, 'tensor', far_z)  11.2 us
    ppermute x5, waiting for transfers between devices, hop_next(): return lax.ppermute(send, 'tensor', next_z)  7.04 us
    ppermute x5, starting transfers between devices, hop_next(): return lax.ppermute(send, 'tensor', next_z)  7.03 us
    ppermute x5, waiting for transfers between devices, hop_far(): return lax.ppermute(send, 'tensor', far_z)  5.96 us
    ppermute x3, starting transfers between devices, paired(): direct.append(lax.ppermute(pieces[step + 1], 'req', across))  3.52 us
    ppermute x3, waiting for transfers between devices, paired(): direct.append(lax.ppermute(pieces[step + 1], 'req', across))  2.62 us
  transfers between devices with their start and end apart: 23, of which 9 were waited for; matrix products, arithmetic and copies ran while one was open for 0% of the time, Pallas kernels for 42%

profile of v9, /device:TPU:0, one launch (start us, length us, event | category | flops | bytes accessed | tf_op | source)
XLA Modules:
  0.0 79.0 jit_solution(7420724326523290342)
XLA Ops:
  0.0 1.8 %turn.1 = (bf16[128,7424]{1,0:T(8,128)(2,1)S(1)}, bf16[32,7424]{1,0:T(8,128)(2,1)S(1)}, bf16[32,7424]{1,0:T(8,128)(2,1)S(1)}, bf16[32,7424]{1,0:T(8,128)(2,1)S(1)}, bf16[32,7424]{1,0:T(8,128)(2,1)S(1)}) custom-call(bf16[7392,128]{1,0:T(8,128)(2,1)} %bitcast.8, s32[1,128]{1,0:T(1,128)} %bitcast.9), custom_call_target="tpu_custom_call" | custom-call | tf_op jit(solution)/shard_map/turn/pallas_call | solution.py:207
  2.3 2.6 %collective-permute-start.1 = (bf16[32,7424]{1,0:T(8,128)(2,1)S(1)}, bf16[32,7424]{1,0:T(8,128)(2,1)S(1)}, u32[]{:S(2)}, u32[]{:S(2)}) collective-permute-start(bf16[32,7424]{1,0:T(8,128)(2,1)S(1)} %get-tuple-element.63), channel_id=1, source_target_pairs={{0,2},{1,3},{2,0},{3,1},{4,6},{5,7},{6,4},{7,5},{8,10},{9,11},{10,... | collective-permute-start | bytes 1425416 | tf_op jit(solution)/shard_map/ppermute | solution.py:226
  5.0 11.9 %load.1 = (f32[8,128]{1,0:T(8,128)S(1)}, bf16[7424,512]{1,0:T(8,128)(2,1)S(1)}, bf16[7424,512]{1,0:T(8,128)(2,1)S(1)}, bf16[7424,512]{1,0:T(8,128)(2,1)S(1)}, bf...) custom-call(bf16[7392,2048]{1,0:T(8,128)(2,1)} %w_hbm.1, bf16[512,7392]{1,0:T(8,128)(2,1)} %bitcast.7), custom_call_target="tpu_custom_call" | custom-call | flops 1 | bytes 1 | tf_op jit(solution)/shard_map/load/pallas_call | solution.py:230
  17.5 1.9 %collective-permute-start = (bf16[32,7424]{1,0:T(8,128)(2,1)S(1)}, bf16[32,7424]{1,0:T(8,128)(2,1)S(1)}, u32[]{:S(2)}, u32[]{:S(2)}) collective-permute-start(bf16[32,7424]{1,0:T(8,128)(2,1)S(1)} %get-tuple-element.62), channel_id=1, source_target_pairs={{0,2},{1,3},{2,0},{3,1},{4,6},{5,7},{6,4},{7,5},{8,10},{9,11},{10,... | collective-permute-start | bytes 1425416 | tf_op jit(solution)/shard_map/ppermute | solution.py:293
  19.5 5.1 %product.5 = (bf16[64,2176]{1,0:T(8,128)(2,1)S(1)}, bf16[64,2176]{1,0:T(8,128)(2,1)S(1)}) custom-call(f32[8,128]{1,0:T(8,128)S(1)} %get-tuple-element.65._, bf16[128,7424]{1,0:T(8,128)(2,1)S(1)} %get-tuple-element.66.own_ref, bf16[128,7424]{1,0:T(8,128)(2,1)S(1)} %collective-permute-done.2.other_ref, bf16[32,7424]{1,0:T(8,128)(2,1)S(1)} %collective-permute-done.1.direct_ref, ...), custom_call_target="tpu_custom_call" | custom-call | flops 1 | bytes 1 | tf_op jit(solution)/shard_map/product/pallas_call | solution.py:250
  24.5 2.3 %collective-permute-done.3.direct_ref = bf16[32,7424]{1,0:T(8,128)(2,1)S(1)} collective-permute-done((bf16[32,7424]{1,0:T(8,128)(2,1)S(1)}, bf16[32,7424]{1,0:T(8,128)(2,1)S(1)}, u32[]{:S(2)}, u32[]{:S(2)}) %collective-permute-start.3) | collective-permute-done | bytes 475168 | tf_op jit(solution)/shard_map/ppermute | solution.py:293
  26.8 2.0 %collective-permute-start.8 = (bf16[64,2176]{1,0:T(8,128)(2,1)S(1)}, bf16[64,2176]{1,0:T(8,128)(2,1)S(1)}, u32[]{:S(2)}, u32[]{:S(2)}) collective-permute-start(bf16[64,2176]{1,0:T(8,128)(2,1)S(1)} %get-tuple-element.78), channel_id=1, source_target_pairs={{0,4},{4,0},{8,12},{12,8},{1,5},{5,1},{9,13},{13,9},{2,6},{6,2},{1... | collective-permute-start | bytes 835592 | tf_op jit(solution)/shard_map/ppermute | solution.py:282
  29.5 1.5 %collective-permute-start.9 = (bf16[32,7424]{1,0:T(8,128)(2,1)S(1)}, bf16[32,7424]{1,0:T(8,128)(2,1)S(1)}, u32[]{:S(2)}, u32[]{:S(2)}) collective-permute-start(bf16[32,7424]{1,0:T(8,128)(2,1)S(1)} %get-tuple-element.83), channel_id=1, source_target_pairs={{0,2},{1,3},{2,0},{3,1},{4,6},{5,7},{6,4},{7,5},{8,10},{9,11},{10,... | collective-permute-start | bytes 1425416 | tf_op jit(solution)/shard_map/ppermute | solution.py:293
  31.0 5.1 %product.6 = (bf16[64,2176]{1,0:T(8,128)(2,1)S(1)}, bf16[64,2176]{1,0:T(8,128)(2,1)S(1)}) custom-call(f32[8,128]{1,0:T(8,128)S(1)} %get-tuple-element.65._, bf16[128,7424]{1,0:T(8,128)(2,1)S(1)} %get-tuple-element.66.own_ref, bf16[128,7424]{1,0:T(8,128)(2,1)S(1)} %collective-permute-done.2.other_ref, bf16[32,7424]{1,0:T(8,128)(2,1)S(1)} %collective-permute-done.3.direct_ref, ...), custom_call_target="tpu_custom_call" | custom-call | flops 1 | bytes 1 | tf_op jit(solution)/shard_map/product/pallas_call | solution.py:250
  37.6 3.0 %collective-permute-start.13 = (bf16[32,2176]{1,0:T(8,128)(2,1)S(1)}, bf16[32,2176]{1,0:T(8,128)(2,1)S(1)}, u32[]{:S(2)}, u32[]{:S(2)}) collective-permute-start(bf16[32,2176]{1,0:T(8,128)(2,1)S(1)} %get-tuple-element.88), channel_id=1, source_target_pairs={{0,8},{4,12},{8,0},{12,4},{1,9},{5,13},{9,1},{13,5},{2,10},{6,14},... | collective-permute-start | bytes 417800 | tf_op jit(solution)/shard_map/ppermute | solution.py:285
  40.7 5.3 %product.7 = (bf16[64,2176]{1,0:T(8,128)(2,1)S(1)}, bf16[64,2176]{1,0:T(8,128)(2,1)S(1)}) custom-call(f32[8,128]{1,0:T(8,128)S(1)} %get-tuple-element.65._, bf16[128,7424]{1,0:T(8,128)(2,1)S(1)} %get-tuple-element.66.own_ref, bf16[128,7424]{1,0:T(8,128)(2,1)S(1)} %collective-permute-done.2.other_ref, bf16[32,7424]{1,0:T(8,128)(2,1)S(1)} %collective-permute-done.direct_ref, ...), custom_call_target="tpu_custom_call" | custom-call | flops 1 | bytes 1 | tf_op jit(solution)/shard_map/product/pallas_call | solution.py:250
  46.0 1.7 %collective-permute-done.12.second_ref = bf16[64,2176]{1,0:T(8,128)(2,1)S(1)} collective-permute-done((bf16[64,2176]{1,0:T(8,128)(2,1)S(1)}, bf16[64,2176]{1,0:T(8,128)(2,1)S(1)}, u32[]{:S(2)}, u32[]{:S(2)}) %collective-permute-start.12) | collective-permute-done | bytes 278560 | tf_op jit(solution)/shard_map/ppermute | solution.py:282
  47.8 2.7 %collective-permute-start.17 = (bf16[64,2176]{1,0:T(8,128)(2,1)S(1)}, bf16[64,2176]{1,0:T(8,128)(2,1)S(1)}, u32[]{:S(2)}, u32[]{:S(2)}) collective-permute-start(bf16[64,2176]{1,0:T(8,128)(2,1)S(1)} %get-tuple-element.106), channel_id=1, source_target_pairs={{0,4},{4,0},{8,12},{12,8},{1,5},{5,1},{9,13},{13,9},{2,6},{6,2},{1... | collective-permute-start | bytes 835592 | tf_op jit(solution)/shard_map/ppermute | solution.py:282
  51.0 1.5 %collective-permute-start.16 = (bf16[32,2176]{1,0:T(8,128)(2,1)S(1)}, bf16[32,2176]{1,0:T(8,128)(2,1)S(1)}, u32[]{:S(2)}, u32[]{:S(2)}) collective-permute-start(bf16[32,2176]{1,0:T(8,128)(2,1)S(1)} %get-tuple-element.95), channel_id=1, source_target_pairs={{0,8},{4,12},{8,0},{12,4},{1,9},{5,13},{9,1},{13,5},{2,10},{6,14},... | collective-permute-start | bytes 417800 | tf_op jit(solution)/shard_map/ppermute | solution.py:285
  52.6 3.1 %product.8 = (bf16[64,1152]{1,0:T(8,128)(2,1)S(1)}, bf16[64,1152]{1,0:T(8,128)(2,1)S(1)}) custom-call(f32[8,128]{1,0:T(8,128)S(1)} %get-tuple-element.65._, bf16[128,7424]{1,0:T(8,128)(2,1)S(1)} %get-tuple-element.66.own_ref, bf16[128,7424]{1,0:T(8,128)(2,1)S(1)} %collective-permute-done.2.other_ref, bf16[32,7424]{1,0:T(8,128)(2,1)S(1)} %collective-permute-done.9.direct_ref, ...), custom_call_target="tpu_custom_call" | custom-call | flops 1 | bytes 1 | tf_op jit(solution)/shard_map/product/pallas_call | solution.py:250
  55.7 3.7 %collective-permute-done.17.second_ref = bf16[64,2176]{1,0:T(8,128)(2,1)S(1)} collective-permute-done((bf16[64,2176]{1,0:T(8,128)(2,1)S(1)}, bf16[64,2176]{1,0:T(8,128)(2,1)S(1)}, u32[]{:S(2)}, u32[]{:S(2)}) %collective-permute-start.17) | collective-permute-done | bytes 278560 | tf_op jit(solution)/shard_map/ppermute | solution.py:282
  59.9 2.1 %product.9 = (bf16[64,1024]{1,0:T(8,128)(2,1)S(1)}, bf16[64,1024]{1,0:T(8,128)(2,1)S(1)}) custom-call(f32[8,128]{1,0:T(8,128)S(1)} %get-tuple-element.65._, bf16[128,7424]{1,0:T(8,128)(2,1)S(1)} %get-tuple-element.66.own_ref, bf16[128,7424]{1,0:T(8,128)(2,1)S(1)} %collective-permute-done.2.other_ref, bf16[32,7424]{1,0:T(8,128)(2,1)S(1)} %collective-permute-done.9.direct_ref, ...), custom_call_target="tpu_custom_call" | custom-call | flops 1 | bytes 1 | tf_op jit(solution)/shard_map/product/pallas_call | solution.py:250
  62.0 1.6 %collective-permute-start.21 = (bf16[64,1024]{1,0:T(8,128)(2,1)S(1)}, bf16[64,1024]{1,0:T(8,128)(2,1)S(1)}, u32[]{:S(2)}, u32[]{:S(2)}) collective-permute-start(bf16[64,1024]{1,0:T(8,128)(2,1)S(1)} %get-tuple-element.116), channel_id=1, source_target_pairs={{0,4},{4,0},{8,12},{12,8},{1,5},{5,1},{9,13},{13,9},{2,6},{6,2},{1... | collective-permute-start | bytes 393224 | tf_op jit(solution)/shard_map/ppermute | solution.py:282
  63.7 2.0 %collective-permute-start.18 = (bf16[32,2176]{1,0:T(8,128)(2,1)S(1)}, bf16[32,2176]{1,0:T(8,128)(2,1)S(1)}, u32[]{:S(2)}, u32[]{:S(2)}) collective-permute-start(bf16[32,2176]{1,0:T(8,128)(2,1)S(1)} %get-tuple-element.110), channel_id=1, source_target_pairs={{0,8},{4,12},{8,0},{12,4},{1,9},{5,13},{9,1},{13,5},{2,10},{6,14},... | collective-permute-start | bytes 417800 | tf_op jit(solution)/shard_map/ppermute | solution.py:285
  67.1 1.5 %collective-permute-done.21.second_ref = bf16[64,1024]{1,0:T(8,128)(2,1)S(1)} collective-permute-done((bf16[64,1024]{1,0:T(8,128)(2,1)S(1)}, bf16[64,1024]{1,0:T(8,128)(2,1)S(1)}, u32[]{:S(2)}, u32[]{:S(2)}) %collective-permute-start.21) | collective-permute-done | bytes 131104 | tf_op jit(solution)/shard_map/ppermute | solution.py:282
  68.7 3.4 %collective-permute-start.22 = (bf16[32,1024]{1,0:T(8,128)(2,1)S(1)}, bf16[32,1024]{1,0:T(8,128)(2,1)S(1)}, u32[]{:S(2)}, u32[]{:S(2)}) collective-permute-start(bf16[32,1024]{1,0:T(8,128)(2,1)S(1)} %get-tuple-element.118), channel_id=1, source_target_pairs={{0,8},{4,12},{8,0},{12,4},{1,9},{5,13},{9,1},{13,5},{2,10},{6,14},... | collective-permute-start | bytes 196616 | tf_op jit(solution)/shard_map/ppermute | solution.py:285
  72.0 4.0 %collective-permute-done.18.refs_5_ = bf16[32,2176]{1,0:T(8,128)(2,1)S(1)} collective-permute-done((bf16[32,2176]{1,0:T(8,128)(2,1)S(1)}, bf16[32,2176]{1,0:T(8,128)(2,1)S(1)}, u32[]{:S(2)}, u32[]{:S(2)}) %collective-permute-start.18) | collective-permute-done | bytes 139296 | tf_op jit(solution)/shard_map/ppermute | solution.py:285
  76.1 1.7 %collective-permute-done.22.refs_9_ = bf16[32,1024]{1,0:T(8,128)(2,1)S(1)} collective-permute-done((bf16[32,1024]{1,0:T(8,128)(2,1)S(1)}, bf16[32,1024]{1,0:T(8,128)(2,1)S(1)}, u32[]{:S(2)}, u32[]{:S(2)}) %collective-permute-start.22) | collective-permute-done | bytes 65568 | tf_op jit(solution)/shard_map/ppermute | solution.py:285
  77.7 1.3 %last.1 = bf16[128,2048]{1,0:T(8,128)(2,1)} custom-call(bf16[512,2048]{1,0:T(8,128)(2,1)S(1)} %bitcast.6, bf16[32,2176]{1,0:T(8,128)(2,1)S(1)} %get-tuple-element.82.refs_0_, bf16[32,2176]{1,0:T(8,128)(2,1)S(1)} %collective-permute-done.13.refs_1_, bf16[32,2176]{1,0:T(8,128)(2,1)S(1)} %get-tuple-element.102.refs_2_, ...), custom_call_target="tpu_custom_call" | custom-call | tf_op jit(solution)/shard_map/last/pallas_call | solution.py:326
  (41 shorter events, 6.2 us)
Async XLA Ops:
  1.8 17.6 %collective-permute-start.2 = (bf16[128,7424]{1,0:T(8,128)(2,1)S(1)}, bf16[128,7424]{1,0:T(8,128)(2,1)S(1)}, u32[]{:S(2)}, u32[]{:S(2)}) collective-permute-start(bf16[128,7424]{1,0:T(8,128)(2,1)S(1)} %get-tuple-element.66.own_ref), channel_id=1, source_target_pairs={{0,1},{1,0},{2,3},{3,2},{4,5},{5,4},{6,7},{7,6},{8,9},{9,8},{10,11... | collective-permute-start | bytes 5701640 | tf_op jit(solution)/shard_map/ppermute | solution.py:227
  2.3 14.5 %collective-permute-start.1 = (bf16[32,7424]{1,0:T(8,128)(2,1)S(1)}, bf16[32,7424]{1,0:T(8,128)(2,1)S(1)}, u32[]{:S(2)}, u32[]{:S(2)}) collective-permute-start(bf16[32,7424]{1,0:T(8,128)(2,1)S(1)} %get-tuple-element.63), channel_id=1, source_target_pairs={{0,2},{1,3},{2,0},{3,1},{4,6},{5,7},{6,4},{7,5},{8,10},{9,11},{10,... | collective-permute-start | bytes 1425416 | tf_op jit(solution)/shard_map/ppermute | solution.py:226
  4.9 21.9 %collective-permute-start.3 = (bf16[32,7424]{1,0:T(8,128)(2,1)S(1)}, bf16[32,7424]{1,0:T(8,128)(2,1)S(1)}, u32[]{:S(2)}, u32[]{:S(2)}) collective-permute-start(bf16[32,7424]{1,0:T(8,128)(2,1)S(1)} %get-tuple-element.67), channel_id=1, source_target_pairs={{0,2},{1,3},{2,0},{3,1},{4,6},{5,7},{6,4},{7,5},{8,10},{9,11},{10,... | collective-permute-start | bytes 1425416 | tf_op jit(solution)/shard_map/ppermute | solution.py:293
  16.9 2.5 %collective-permute-start.5 = (bf16[32,3712]{1,0:T(8,128)(2,1)S(1)}, bf16[32,3712]{1,0:T(8,128)(2,1)S(1)}, u32[]{:S(2)}, u32[]{:S(2)}) collective-permute-start(bf16[32,3712]{1,0:T(8,128)(2,1)S(1)} %get-tuple-element.125), channel_id=1, source_target_pairs={{0,1},{1,0},{2,3},{3,2},{4,5},{5,4},{6,7},{7,6},{8,9},{9,8},{10,11... | collective-permute-start | bytes 712712 | tf_op jit(solution)/shard_map/ppermute | solution.py:278
  17.1 2.4 %collective-permute-start.4 = (bf16[32,3712]{1,0:T(8,128)(2,1)S(1)}, bf16[32,3712]{1,0:T(8,128)(2,1)S(1)}, u32[]{:S(2)}, u32[]{:S(2)}) collective-permute-start(bf16[32,3712]{1,0:T(8,128)(2,1)S(1)} %get-tuple-element.126), channel_id=1, source_target_pairs={{0,1},{1,0},{2,3},{3,2},{4,5},{5,4},{6,7},{7,6},{8,9},{9,8},{10,11... | collective-permute-start | bytes 712712 | tf_op jit(solution)/shard_map/ppermute | solution.py:278
  17.5 19.5 %collective-permute-start = (bf16[32,7424]{1,0:T(8,128)(2,1)S(1)}, bf16[32,7424]{1,0:T(8,128)(2,1)S(1)}, u32[]{:S(2)}, u32[]{:S(2)}) collective-permute-start(bf16[32,7424]{1,0:T(8,128)(2,1)S(1)} %get-tuple-element.62), channel_id=1, source_target_pairs={{0,2},{1,3},{2,0},{3,1},{4,6},{5,7},{6,4},{7,5},{8,10},{9,11},{10,... | collective-permute-start | bytes 1425416 | tf_op jit(solution)/shard_map/ppermute | solution.py:293
  26.8 9.8 %collective-permute-start.8 = (bf16[64,2176]{1,0:T(8,128)(2,1)S(1)}, bf16[64,2176]{1,0:T(8,128)(2,1)S(1)}, u32[]{:S(2)}, u32[]{:S(2)}) collective-permute-start(bf16[64,2176]{1,0:T(8,128)(2,1)S(1)} %get-tuple-element.78), channel_id=1, source_target_pairs={{0,4},{4,0},{8,12},{12,8},{1,5},{5,1},{9,13},{13,9},{2,6},{6,2},{1... | collective-permute-start | bytes 835592 | tf_op jit(solution)/shard_map/ppermute | solution.py:282
  28.9 2.1 %collective-permute-start.7 = (bf16[32,3712]{1,0:T(8,128)(2,1)S(1)}, bf16[32,3712]{1,0:T(8,128)(2,1)S(1)}, u32[]{:S(2)}, u32[]{:S(2)}) collective-permute-start(bf16[32,3712]{1,0:T(8,128)(2,1)S(1)} %get-tuple-element.123), channel_id=1, source_target_pairs={{0,1},{1,0},{2,3},{3,2},{4,5},{5,4},{6,7},{7,6},{8,9},{9,8},{10,11... | collective-permute-start | bytes 712712 | tf_op jit(solution)/shard_map/ppermute | solution.py:278
  29.0 2.0 %collective-permute-start.6 = (bf16[32,3712]{1,0:T(8,128)(2,1)S(1)}, bf16[32,3712]{1,0:T(8,128)(2,1)S(1)}, u32[]{:S(2)}, u32[]{:S(2)}) collective-permute-start(bf16[32,3712]{1,0:T(8,128)(2,1)S(1)} %get-tuple-element.124), channel_id=1, source_target_pairs={{0,1},{1,0},{2,3},{3,2},{4,5},{5,4},{6,7},{7,6},{8,9},{9,8},{10,11... | collective-permute-start | bytes 712712 | tf_op jit(solution)/shard_map/ppermute | solution.py:278
  29.5 18.3 %collective-permute-start.9 = (bf16[32,7424]{1,0:T(8,128)(2,1)S(1)}, bf16[32,7424]{1,0:T(8,128)(2,1)S(1)}, u32[]{:S(2)}, u32[]{:S(2)}) collective-permute-start(bf16[32,7424]{1,0:T(8,128)(2,1)S(1)} %get-tuple-element.83), channel_id=1, source_target_pairs={{0,2},{1,3},{2,0},{3,1},{4,6},{5,7},{6,4},{7,5},{8,10},{9,11},{10,... | collective-permute-start | bytes 1425416 | tf_op jit(solution)/shard_map/ppermute | solution.py:293
  36.0 11.6 %collective-permute-start.12 = (bf16[64,2176]{1,0:T(8,128)(2,1)S(1)}, bf16[64,2176]{1,0:T(8,128)(2,1)S(1)}, u32[]{:S(2)}, u32[]{:S(2)}) collective-permute-start(bf16[64,2176]{1,0:T(8,128)(2,1)S(1)} %get-tuple-element.87), channel_id=1, source_target_pairs={{0,4},{4,0},{8,12},{12,8},{1,5},{5,1},{9,13},{13,9},{2,6},{6,2},{1... | collective-permute-start | bytes 835592 | tf_op jit(solution)/shard_map/ppermute | solution.py:282
  37.0 3.6 %collective-permute-start.11 = (bf16[32,3712]{1,0:T(8,128)(2,1)S(1)}, bf16[32,3712]{1,0:T(8,128)(2,1)S(1)}, u32[]{:S(2)}, u32[]{:S(2)}) collective-permute-start(bf16[32,3712]{1,0:T(8,128)(2,1)S(1)} %get-tuple-element.121), channel_id=1, source_target_pairs={{0,1},{1,0},{2,3},{3,2},{4,5},{5,4},{6,7},{7,6},{8,9},{9,8},{10,11... | collective-permute-start | bytes 712712 | tf_op jit(solution)/shard_map/ppermute | solution.py:278
  37.1 3.6 %collective-permute-start.10 = (bf16[32,3712]{1,0:T(8,128)(2,1)S(1)}, bf16[32,3712]{1,0:T(8,128)(2,1)S(1)}, u32[]{:S(2)}, u32[]{:S(2)}) collective-permute-start(bf16[32,3712]{1,0:T(8,128)(2,1)S(1)} %get-tuple-element.122), channel_id=1, source_target_pairs={{0,1},{1,0},{2,3},{3,2},{4,5},{5,4},{6,7},{7,6},{8,9},{9,8},{10,11... | collective-permute-start | bytes 712712 | tf_op jit(solution)/shard_map/ppermute | solution.py:278
  37.6 8.3 %collective-permute-start.13 = (bf16[32,2176]{1,0:T(8,128)(2,1)S(1)}, bf16[32,2176]{1,0:T(8,128)(2,1)S(1)}, u32[]{:S(2)}, u32[]{:S(2)}) collective-permute-start(bf16[32,2176]{1,0:T(8,128)(2,1)S(1)} %get-tuple-element.88), channel_id=1, source_target_pairs={{0,8},{4,12},{8,0},{12,4},{1,9},{5,13},{9,1},{13,5},{2,10},{6,14},... | collective-permute-start | bytes 417800 | tf_op jit(solution)/shard_map/ppermute | solution.py:285
  47.8 11.6 %collective-permute-start.17 = (bf16[64,2176]{1,0:T(8,128)(2,1)S(1)}, bf16[64,2176]{1,0:T(8,128)(2,1)S(1)}, u32[]{:S(2)}, u32[]{:S(2)}) collective-permute-start(bf16[64,2176]{1,0:T(8,128)(2,1)S(1)} %get-tuple-element.106), channel_id=1, source_target_pairs={{0,4},{4,0},{8,12},{12,8},{1,5},{5,1},{9,13},{13,9},{2,6},{6,2},{1... | collective-permute-start | bytes 835592 | tf_op jit(solution)/shard_map/ppermute | solution.py:282
  50.5 2.1 %collective-permute-start.15 = (bf16[32,3712]{1,0:T(8,128)(2,1)S(1)}, bf16[32,3712]{1,0:T(8,128)(2,1)S(1)}, u32[]{:S(2)}, u32[]{:S(2)}) collective-permute-start(bf16[32,3712]{1,0:T(8,128)(2,1)S(1)} %get-tuple-element.119), channel_id=1, source_target_pairs={{0,1},{1,0},{2,3},{3,2},{4,5},{5,4},{6,7},{7,6},{8,9},{9,8},{10,11... | collective-permute-start | bytes 712712 | tf_op jit(solution)/shard_map/ppermute | solution.py:278
  50.5 2.0 %collective-permute-start.14 = (bf16[32,3712]{1,0:T(8,128)(2,1)S(1)}, bf16[32,3712]{1,0:T(8,128)(2,1)S(1)}, u32[]{:S(2)}, u32[]{:S(2)}) collective-permute-start(bf16[32,3712]{1,0:T(8,128)(2,1)S(1)} %get-tuple-element.120), channel_id=1, source_target_pairs={{0,1},{1,0},{2,3},{3,2},{4,5},{5,4},{6,7},{7,6},{8,9},{9,8},{10,11... | collective-permute-start | bytes 712712 | tf_op jit(solution)/shard_map/ppermute | solution.py:278
  51.0 8.9 %collective-permute-start.16 = (bf16[32,2176]{1,0:T(8,128)(2,1)S(1)}, bf16[32,2176]{1,0:T(8,128)(2,1)S(1)}, u32[]{:S(2)}, u32[]{:S(2)}) collective-permute-start(bf16[32,2176]{1,0:T(8,128)(2,1)S(1)} %get-tuple-element.95), channel_id=1, source_target_pairs={{0,8},{4,12},{8,0},{12,4},{1,9},{5,13},{9,1},{13,5},{2,10},{6,14},... | collective-permute-start | bytes 417800 | tf_op jit(solution)/shard_map/ppermute | solution.py:285
  59.4 6.4 %collective-permute-start.19 = (bf16[64,1152]{1,0:T(8,128)(2,1)S(1)}, bf16[64,1152]{1,0:T(8,128)(2,1)S(1)}, u32[]{:S(2)}, u32[]{:S(2)}) collective-permute-start(bf16[64,1152]{1,0:T(8,128)(2,1)S(1)} %get-tuple-element.112), channel_id=1, source_target_pairs={{0,4},{4,0},{8,12},{12,8},{1,5},{5,1},{9,13},{13,9},{2,6},{6,2},{1... | collective-permute-start | bytes 442376 | tf_op jit(solution)/shard_map/ppermute | solution.py:282
  59.9 17.8 %copy-start = (bf16[8,64,2048]{2,1,0:T(8,128)(2,1)S(1)}, bf16[8,64,2048]{2,1,0:T(8,128)(2,1)}, u32[]{:S(2)}) copy-start(bf16[8,64,2048]{2,1,0:T(8,128)(2,1)} %param.8) | copy-start | bytes 6291460
  62.0 6.6 %collective-permute-start.21 = (bf16[64,1024]{1,0:T(8,128)(2,1)S(1)}, bf16[64,1024]{1,0:T(8,128)(2,1)S(1)}, u32[]{:S(2)}, u32[]{:S(2)}) collective-permute-start(bf16[64,1024]{1,0:T(8,128)(2,1)S(1)} %get-tuple-element.116), channel_id=1, source_target_pairs={{0,4},{4,0},{8,12},{12,8},{1,5},{5,1},{9,13},{13,9},{2,6},{6,2},{1... | collective-permute-start | bytes 393224 | tf_op jit(solution)/shard_map/ppermute | solution.py:282
  63.7 12.4 %collective-permute-start.18 = (bf16[32,2176]{1,0:T(8,128)(2,1)S(1)}, bf16[32,2176]{1,0:T(8,128)(2,1)S(1)}, u32[]{:S(2)}, u32[]{:S(2)}) collective-permute-start(bf16[32,2176]{1,0:T(8,128)(2,1)S(1)} %get-tuple-element.110), channel_id=1, source_target_pairs={{0,8},{4,12},{8,0},{12,4},{1,9},{5,13},{9,1},{13,5},{2,10},{6,14},... | collective-permute-start | bytes 417800 | tf_op jit(solution)/shard_map/ppermute | solution.py:285
  65.9 11.9 %collective-permute-start.20 = (bf16[32,1152]{1,0:T(8,128)(2,1)S(1)}, bf16[32,1152]{1,0:T(8,128)(2,1)S(1)}, u32[]{:S(2)}, u32[]{:S(2)}) collective-permute-start(bf16[32,1152]{1,0:T(8,128)(2,1)S(1)} %get-tuple-element.114), channel_id=1, source_target_pairs={{0,8},{4,12},{8,0},{12,4},{1,9},{5,13},{9,1},{13,5},{2,10},{6,14},... | collective-permute-start | bytes 221192 | tf_op jit(solution)/shard_map/ppermute | solution.py:285
  68.7 9.1 %collective-permute-start.22 = (bf16[32,1024]{1,0:T(8,128)(2,1)S(1)}, bf16[32,1024]{1,0:T(8,128)(2,1)S(1)}, u32[]{:S(2)}, u32[]{:S(2)}) collective-permute-start(bf16[32,1024]{1,0:T(8,128)(2,1)S(1)} %get-tuple-element.118), channel_id=1, source_target_pairs={{0,8},{4,12},{8,0},{12,4},{1,9},{5,13},{9,1},{13,5},{2,10},{6,14},... | collective-permute-start | bytes 196616 | tf_op jit(solution)/shard_map/ppermute | solution.py:285

commit v10 on v7

--- a/solution.py
+++ b/solution.py
@@ -13,6 +13,8 @@
 TURN = 15
 PIECES = (32, 32, 32, 32)
 CUTS = 2
+FULL = 128
+SLOTS = 3
 MIB = 1 << 20
 
 
@@ -64,57 +66,24 @@
                 piece_ref[:, at] = turned[first : first + piece_ref.shape[0]]
 
 
-def load_kernel(w_hbm, s_hbm, token_ref, *refs):
-    *panel_refs, spread_ref, s_ref, w_sems, s_sem = refs
-    units = w_hbm.shape[0]
-    copies = [
-        pltpu.make_async_copy(
-            w_hbm.at[:, pl.ds(panel * PANEL, PANEL)],
-            panel_ref.at[pl.ds(0, units), :],
-            w_sems.at[panel],
-        )
-        for panel, panel_ref in enumerate(panel_refs)
-    ]
-    s_copy = pltpu.make_async_copy(s_hbm, s_ref, s_sem)
-    s_copy.start()
-    for copy in copies:
-        copy.start()
-    token_ref[...] = jnp.zeros_like(token_ref)
-    for ref in (spread_ref, *panel_refs):
-        ref[units:, :] = jnp.zeros_like(ref[units:, :])
-    s_copy.wait()
-    for at in range(0, units, DEPTH):
-        to = min(at + DEPTH, units)
-        spread_ref[at:to, :] = s_ref[:, at:to].T
-    for copy in copies:
-        copy.wait()
-
-
 def part_rows(value, cols, send_ref, keep_ref):
-    rows = send_ref.shape[0] // 2
+    rows = send_ref.shape[0]
     keep_first = lax.rem(lax.axis_index("req"), 2) == lax.rem(lax.axis_index("tensor"), 2)
     value = value.astype(send_ref.dtype)
-    for half in range(2):
-        first = value[(2 * half) * rows : (2 * half + 1) * rows]
-        second = value[(2 * half + 1) * rows : (2 * half + 2) * rows]
-        at = slice(half * rows, (half + 1) * rows)
-        send_ref[at, cols] = jnp.where(keep_first, second, first)
-        keep_ref[at, cols] = jnp.where(keep_first, first, second)
-
-
-def product_kernel(adapters, units, at, _, own_ref, other_ref, direct_ref, *refs):
-    passed_refs, refs = refs[:CUTS], refs[CUTS:]
-    *panel_refs, spread_ref, send_ref, keep_ref = refs
-    rows = direct_ref.shape[0]
+    first, second = value[:rows], value[rows : 2 * rows]
+    send_ref[:, cols] = jnp.where(keep_first, second, first)
+    keep_ref[:, cols] = jnp.where(keep_first, first, second)
+
+
+def base_panel(panel, piece, panel_ref, send_ref, keep_ref):
+    value = jnp.dot(piece(), panel_ref[...], preferred_element_type=jnp.float32)
+    part_rows(value, slice(panel * PANEL, (panel + 1) * PANEL), send_ref, keep_ref)
+
+
+def shrink_panel(adapters, units, piece, spread_ref, send_ref, keep_ref):
     width = send_ref.shape[1] - LANES
     wide = spread_ref.shape[1]
     rank = wide // adapters
-
-    def piece():
-        near = [own_ref[at : at + rows, :], other_ref[at : at + rows, :]]
-        passed = jnp.concatenate([ref[...] for ref in passed_refs], axis=1)
-        return jnp.concatenate([*near, direct_ref[...], passed], axis=0)
-
     every = jnp.dot(piece(), spread_ref[...], preferred_element_type=jnp.float32)
     ids = piece()[:, units : units + 1].astype(jnp.float32)
     column = lax.broadcasted_iota(jnp.int32, every.shape, 1) // rank
@@ -127,23 +96,74 @@
     tile = jnp.where(lane < rank, tile, ids)
     part_rows(tile, slice(width, width + LANES), send_ref, keep_ref)
 
+
+def near_kernel(adapters, own_ref, other_ref, w_hbm, s_hbm, send_ref, keep_ref, *refs):
+    *panel_refs, spread_ref = refs[: -SLOTS - 3]
+    *stage_refs, tail_ref, w_sems, s_sems = refs[-SLOTS - 3 :]
+    units = w_hbm.shape[0]
+    copies = [
+        pltpu.make_async_copy(
+            w_hbm.at[:, pl.ds(panel * PANEL, PANEL)],
+            panel_ref.at[pl.ds(0, units), :],
+            w_sems.at[panel],
+        )
+        for panel, panel_ref in enumerate(panel_refs)
+    ]
+    cuts = [(at, min(at + DEPTH, units)) for at in range(0, units, DEPTH)]
+    stages = [
+        stage_refs[step % SLOTS] if to - at == DEPTH else tail_ref
+        for step, (at, to) in enumerate(cuts)
+    ]
+    s_copies = [
+        pltpu.make_async_copy(s_hbm.at[:, pl.ds(at, to - at)], stage, s_sems.at[step])
+        for step, ((at, to), stage) in enumerate(zip(cuts, stages))
+    ]
+    for copy in s_copies[:SLOTS]:
+        copy.start()
+    s_copies[-1].start()
+    for copy in copies:
+        copy.start()
+    for ref in (spread_ref, *panel_refs):
+        ref[units:, :] = jnp.zeros_like(ref[units:, :])
+
+    def piece():
+        return jnp.concatenate([own_ref[...], other_ref[...]], axis=0)
+
+    for step, ((at, to), stage) in enumerate(zip(cuts, stages)):
+        s_copies[step].wait()
+        spread_ref[at:to, :] = stage[...].T
+        if step + SLOTS < len(cuts) - 1:
+            s_copies[step + SLOTS].start()
+    shrink_panel(adapters, units, piece, spread_ref, send_ref, keep_ref)
     for panel, panel_ref in enumerate(panel_refs):
-        value = jnp.dot(
-            piece(), panel_ref[...], preferred_element_type=jnp.float32
-        )
-        part_rows(value, slice(panel * PANEL, (panel + 1) * PANEL), send_ref, keep_ref)
-
-
-def add_kernel(first_ref, second_ref, send_ref, keep_ref):
+        copies[panel].wait()
+        base_panel(panel, piece, panel_ref, send_ref, keep_ref)
+
+
+def far_kernel(adapters, units, direct_ref, *refs):
+    passed_refs, refs = refs[:CUTS], refs[CUTS:]
+    *panel_refs, spread_ref, send_ref, keep_ref = refs
+
+    def piece():
+        passed = jnp.concatenate([ref[...] for ref in passed_refs], axis=1)
+        both = jnp.concatenate([direct_ref[...], passed], axis=0)
+        return jnp.concatenate([both] * max(1, FULL // both.shape[0]), axis=0)
+
+    shrink_panel(adapters, units, piece, spread_ref, send_ref, keep_ref)
+    for panel, panel_ref in enumerate(panel_refs):
+        base_panel(panel, piece, panel_ref, send_ref, keep_ref)
+
+
+def add_kernel(at, near_a, near_b, far_a, far_b, send_ref, keep_ref):
     rows = send_ref.shape[0]
     keep_near = lax.axis_index("tensor") // 2 == lax.axis_index("req") // 2
 
-    def total(at):
-        cut = slice(at, at + rows)
+    def total(first_ref, second_ref, cut):
         value = first_ref[cut].astype(jnp.float32) + second_ref[cut].astype(jnp.float32)
         return value.astype(send_ref.dtype)
 
-    near, far = total(0), total(rows)
+    near = total(near_a, near_b, slice(at, at + rows))
+    far = total(far_a, far_b, slice(0, rows))
     send_ref[...] = jnp.where(keep_near, far, near)
     keep_ref[...] = jnp.where(keep_near, near, far)
 
@@ -217,44 +237,45 @@
     other = lax.ppermute(own, "req", beside)
 
     shrink_rows = shrink.transpose(1, 2, 0).reshape(wide, units)
-    token, *both = pl.pallas_call(
-        load_kernel,
-        out_shape=[jax.ShapeDtypeStruct((8, LANES), jnp.float32)]
+    near_send, near_keep, *both = pl.pallas_call(
+        functools.partial(near_kernel, adapters),
+        out_shape=[struct(rows, payload)] * 2
         + [pltpu.VMEM((room, PANEL), bf16)] * (width // PANEL)
         + [pltpu.VMEM((room, wide), bf16)],
-        in_specs=[in_hbm(), in_hbm()],
-        out_specs=[in_vmem()] * (2 + width // PANEL),
+        in_specs=[in_vmem(), in_vmem(), in_hbm(), in_hbm()],
+        out_specs=[in_vmem()] * (3 + width // PANEL),
         scratch_shapes=[
-            pltpu.VMEM((wide, units), bf16),
+            *[pltpu.VMEM((wide, DEPTH), bf16)] * SLOTS,
+            pltpu.VMEM((wide, units % DEPTH), bf16),
             pltpu.SemaphoreType.DMA((width // PANEL,)),
-            pltpu.SemaphoreType.DMA,
+            pltpu.SemaphoreType.DMA((units // DEPTH + 1,)),
         ],
-        compiler_params=params(10),
+        compiler_params=params(6),
         cost_estimate=quick,
-        name="load",
-    )(left(weight), left(shrink_rows))
-
-    def product(step, passed, token):
+        name="near",
+    )(own, other, left(weight), left(shrink_rows))
+
+    def product(step, passed):
         return pl.pallas_call(
-            functools.partial(product_kernel, adapters, units, starts[step]),
-            out_shape=[struct(2 * counts[step], payload)] * 2,
-            in_specs=[in_vmem()] * (4 + CUTS + len(both)),
+            functools.partial(far_kernel, adapters, units),
+            out_shape=[struct(counts[step], payload)] * 2,
+            in_specs=[in_vmem()] * (1 + CUTS + len(both)),
             out_specs=[in_vmem()] * 2,
             compiler_params=params(4),
             cost_estimate=quick,
-            name="product",
-        )(token, own, other, direct[step], *passed, *both)
+            name="far",
+        )(direct[step], *passed, *both)
 
     def add(step, keep, got):
         return pl.pallas_call(
-            add_kernel,
+            functools.partial(add_kernel, starts[step]),
             out_shape=[struct(counts[step], payload)] * 2,
-            in_specs=[in_vmem()] * 2,
+            in_specs=[in_vmem()] * 4,
             out_specs=[in_vmem()] * 2,
             compiler_params=params(4),
             cost_estimate=quick,
             name="add",
-        )(keep, got)
+        )(near_keep, near_got, keep, got)
 
     def over_core(part):
         tiles = room // LANES
@@ -265,12 +286,12 @@
 
     after = lax.optimization_barrier
     steps = len(counts)
-    direct[0], token = after((direct[0], token))
+    near_got = lax.ppermute(near_send, "tensor", next_z)
+    direct[0], near_keep = after((direct[0], near_keep))
     parts, kept, gots = [], [], []
 
     def add_part(step):
-        keep, got = parts[step]
-        send, keep = add(step, keep, got)
+        send, keep = add(step, *parts[step])
         kept.append(keep)
         return send
 
@@ -278,7 +299,7 @@
         passed = over_core(direct[step])
         if step + 1 < steps:
             direct.append(lax.ppermute(pieces[step + 1], "req", across))
-        send, keep = product(step, passed, token)
+        send, keep = product(step, passed)
         hop = gots[step - 2 :] if step > 1 else []
         if step + 1 < steps:
             got = lax.ppermute(send, "tensor", next_z)

time: 79 us -> 89.2 us (1.13)
  Pallas kernels: 35.9 us -> 48.5 us
  starting transfers between devices: 23.4 us -> 21.7 us
    pallas_call x9, Pallas kernels: 32.7 us -> 45.4 us  [the longest x1 23.8 us: paired(): pl.pallas_call(functools.partial(near_kernel, adapters), out_shape=[struc...]
    ppermute x3, waiting for transfers between devices: 0.86 us -> 8.13 us  [paired(): gots.append(lax.ppermute(send, 'tensor', far_z))]
    ppermute x4, starting transfers between devices: 7.26 us -> 2.76 us  [paired(): got = lax.ppermute(send, 'tensor', next_z)]
    ppermute x1, waiting for transfers between devices: 6.49 us -> 2.02 us  [paired(): gots.append(lax.ppermute(add_part(steps - 1), 'tensor', far_z))]
    ppermute x3, waiting for transfers between devices: 3.59 us -> 0.01 us  [paired(): direct.append(lax.ppermute(pieces[step + 1], 'req', across))]
    ppermute x0 -> x1, starting transfers between devices: none -> 1.58 us  [paired(): near_got = lax.ppermute(near_send, 'tensor', next_z)]
    ppermute x4, waiting for transfers between devices: 8.35 us -> 6.97 us  [paired(): got = lax.ppermute(send, 'tensor', next_z)]
    ppermute x3, starting transfers between devices: 6.47 us -> 7.83 us  [paired(): gots.append(lax.ppermute(send, 'tensor', far_z))]
  transfers between devices with their start and end apart: 21 -> 22, of which waited for: 8 -> 9; matrix products, arithmetic and copies ran while one was open for 0% -> 0% of each run, Pallas kernels for 41% -> 51%
where the time goes in v10:
time: 89.2 us; the launch traced here: 89 us
  Pallas kernels  48.5 us (54%)
  starting transfers between devices  21.7 us (24%)
  waiting for transfers between devices  18.5 us (21%)
    pallas_call x1, Pallas kernels, paired(): pl.pallas_call(functools.partial(near_kernel, adapters), out_shape=[struc...  23.8 us
    pallas_call x4, Pallas kernels, product(): pl.pallas_call(functools.partial(far_kernel, adapters, units), out_shape=...  21.2 us
    ppermute x3, waiting for transfers between devices, paired(): gots.append(lax.ppermute(send, 'tensor', far_z))  8.13 us
    ppermute x3, starting transfers between devices, paired(): gots.append(lax.ppermute(send, 'tensor', far_z))  7.83 us
    ppermute x4, waiting for transfers between devices, paired(): got = lax.ppermute(send, 'tensor', next_z)  6.97 us
    ppermute x3, starting transfers between devices, paired(): direct.append(lax.ppermute(pieces[step + 1], 'req', across))  3.48 us
    ppermute x4, starting transfers between devices, paired(): got = lax.ppermute(send, 'tensor', next_z)  2.76 us
    ppermute x1, starting transfers between devices, paired(): direct = [lax.ppermute(pieces[0], 'req', across)]  2.56 us
  transfers between devices with their start and end apart: 22, of which 9 were waited for; matrix products, arithmetic and copies ran while one was open for 0% of the time, Pallas kernels for 51%

profile of v10, /device:TPU:0, one launch (start us, length us, event | category | flops | bytes accessed | tf_op | source)
XLA Modules:
  0.0 89.0 jit_solution(8246176332092664114)
XLA Ops:
  0.0 1.8 %turn.1 = (bf16[128,7424]{1,0:T(8,128)(2,1)S(1)}, bf16[32,7424]{1,0:T(8,128)(2,1)S(1)}, bf16[32,7424]{1,0:T(8,128)(2,1)S(1)}, bf16[32,7424]{1,0:T(8,128)(2,1)S(1)}, bf16[32,7424]{1,0:T(8,128)(2,1)S(1)}) custom-call(bf16[7392,128]{1,0:T(8,128)(2,1)} %bitcast.8, s32[1,128]{1,0:T(1,128)} %bitcast.9), custom_call_target="tpu_custom_call" | custom-call | tf_op jit(solution)/shard_map/turn/pallas_call | solution.py:217
  2.3 2.6 %collective-permute-start.2 = (bf16[32,7424]{1,0:T(8,128)(2,1)S(1)}, bf16[32,7424]{1,0:T(8,128)(2,1)S(1)}, u32[]{:S(2)}, u32[]{:S(2)}) collective-permute-start(bf16[32,7424]{1,0:T(8,128)(2,1)S(1)} %get-tuple-element.56), channel_id=1, source_target_pairs={{0,2},{1,3},{2,0},{3,1},{4,6},{5,7},{6,4},{7,5},{8,10},{9,11},{10,... | collective-permute-start | bytes 1425416 | tf_op jit(solution)/shard_map/ppermute | solution.py:236
  5.0 0.8 collective-permute-done.3.other_ref
  5.9 23.8 %near.1 = (bf16[128,2176]{1,0:T(8,128)(2,1)S(1)}, bf16[128,2176]{1,0:T(8,128)(2,1)S(1)}, bf16[7424,512]{1,0:T(8,128)(2,1)S(1)}, bf16[7424,512]{1,0:T(8,128)(2,1)...) custom-call(bf16[128,7424]{1,0:T(8,128)(2,1)S(1)} %get-tuple-element.57.own_ref, ...), custom_call_target="tpu_custom_call" | custom-call | flops 1 | bytes 1 | tf_op jit(solution)/shard_map/near/pallas_call | solution.py:240
  30.3 2.9 %collective-permute-start = (bf16[32,7424]{1,0:T(8,128)(2,1)S(1)}, bf16[32,7424]{1,0:T(8,128)(2,1)S(1)}, u32[]{:S(2)}, u32[]{:S(2)}) collective-permute-start(bf16[32,7424]{1,0:T(8,128)(2,1)S(1)} %get-tuple-element.54), channel_id=1, source_target_pairs={{0,2},{1,3},{2,0},{3,1},{4,6},{5,7},{6,4},{7,5},{8,10},{9,11},{10,... | collective-permute-start | bytes 1425416 | tf_op jit(solution)/shard_map/ppermute | solution.py:301
  33.2 1.6 %collective-permute-start.9 = (bf16[128,2176]{1,0:T(8,128)(2,1)S(1)}, bf16[128,2176]{1,0:T(8,128)(2,1)S(1)}, u32[]{:S(2)}, u32[]{:S(2)}) collective-permute-start(bf16[128,2176]{1,0:T(8,128)(2,1)S(1)} %get-tuple-element.72), channel_id=1, source_target_pairs={{0,4},{4,0},{8,12},{12,8},{1,5},{5,1},{9,13},{13,9},{2,6},{6,2},{1... | collective-permute-start | bytes 1671176 | tf_op jit(solution)/shard_map/ppermute | solution.py:289
  34.7 5.4 %far.4 = (bf16[32,2176]{1,0:T(8,128)(2,1)S(1)}, bf16[32,2176]{1,0:T(8,128)(2,1)S(1)}) custom-call(bf16[32,7424]{1,0:T(8,128)(2,1)S(1)} %collective-permute-done.2.direct_ref, bf16[32,3712]{1,0:T(8,128)(2,1)S(1)} %collective-permute-done.4.refs_0_, bf16[32,3712]{1,0:T(8,128)(2,1)S(1)} %collective-permute-done.5.refs_1_, ...), custom_call_target="tpu_custom_call" | custom-call | flops 1 | bytes 1 | tf_op jit(solution)/shard_map/far/pallas_call | solution.py:259
  41.2 0.5 collective-permute-done.7.refs_1_
  41.8 0.5 collective-permute-start.10
  42.3 5.2 %far.5 = (bf16[32,2176]{1,0:T(8,128)(2,1)S(1)}, bf16[32,2176]{1,0:T(8,128)(2,1)S(1)}) custom-call(bf16[32,7424]{1,0:T(8,128)(2,1)S(1)} %collective-permute-done.1.direct_ref, bf16[32,3712]{1,0:T(8,128)(2,1)S(1)} %collective-permute-done.6.refs_0_, bf16[32,3712]{1,0:T(8,128)(2,1)S(1)} %collective-permute-done.7.refs_1_, ...), custom_call_target="tpu_custom_call" | custom-call | flops 1 | bytes 1 | tf_op jit(solution)/shard_map/far/pallas_call | solution.py:259
  47.5 3.0 %collective-permute-done.8.far_b = bf16[32,2176]{1,0:T(8,128)(2,1)S(1)} collective-permute-done((bf16[32,2176]{1,0:T(8,128)(2,1)S(1)}, bf16[32,2176]{1,0:T(8,128)(2,1)S(1)}, u32[]{:S(2)}, u32[]{:S(2)}) %collective-permute-start.8) | collective-permute-done | bytes 139296 | tf_op jit(solution)/shard_map/ppermute | solution.py:305
  51.3 1.6 %collective-permute-start.13 = (bf16[32,2176]{1,0:T(8,128)(2,1)S(1)}, bf16[32,2176]{1,0:T(8,128)(2,1)S(1)}, u32[]{:S(2)}, u32[]{:S(2)}) collective-permute-start(bf16[32,2176]{1,0:T(8,128)(2,1)S(1)} %get-tuple-element.81), channel_id=1, source_target_pairs={{0,4},{4,0},{8,12},{12,8},{1,5},{5,1},{9,13},{13,9},{2,6},{6,2},{1... | collective-permute-start | bytes 417800 | tf_op jit(solution)/shard_map/ppermute | solution.py:305
  52.8 2.6 %collective-permute-start.14 = (bf16[32,2176]{1,0:T(8,128)(2,1)S(1)}, bf16[32,2176]{1,0:T(8,128)(2,1)S(1)}, u32[]{:S(2)}, u32[]{:S(2)}) collective-permute-start(bf16[32,2176]{1,0:T(8,128)(2,1)S(1)} %get-tuple-element.82), channel_id=1, source_target_pairs={{0,8},{4,12},{8,0},{12,4},{1,9},{5,13},{9,1},{13,5},{2,10},{6,14},... | collective-permute-start | bytes 417800 | tf_op jit(solution)/shard_map/ppermute | solution.py:316
  55.4 5.4 %far.6 = (bf16[32,2176]{1,0:T(8,128)(2,1)S(1)}, bf16[32,2176]{1,0:T(8,128)(2,1)S(1)}) custom-call(bf16[32,7424]{1,0:T(8,128)(2,1)S(1)} %collective-permute-done.direct_ref, bf16[32,3712]{1,0:T(8,128)(2,1)S(1)} %collective-permute-done.11.refs_0_, bf16[32,3712]{1,0:T(8,128)(2,1)S(1)} %collective-permute-done.12.refs_1_, ...), custom_call_target="tpu_custom_call" | custom-call | flops 1 | bytes 1 | tf_op jit(solution)/shard_map/far/pallas_call | solution.py:259
  60.9 1.3 %collective-permute-done.14.refs_4_ = bf16[32,2176]{1,0:T(8,128)(2,1)S(1)} collective-permute-done((bf16[32,2176]{1,0:T(8,128)(2,1)S(1)}, bf16[32,2176]{1,0:T(8,128)(2,1)S(1)}, u32[]{:S(2)}, u32[]{:S(2)}) %collective-permute-start.14) | collective-permute-done | bytes 139296 | tf_op jit(solution)/shard_map/ppermute | solution.py:316
  63.3 2.6 %collective-permute-start.18 = (bf16[32,2176]{1,0:T(8,128)(2,1)S(1)}, bf16[32,2176]{1,0:T(8,128)(2,1)S(1)}, u32[]{:S(2)}, u32[]{:S(2)}) collective-permute-start(bf16[32,2176]{1,0:T(8,128)(2,1)S(1)} %get-tuple-element.92), channel_id=1, source_target_pairs={{0,8},{4,12},{8,0},{12,4},{1,9},{5,13},{9,1},{13,5},{2,10},{6,14},... | collective-permute-start | bytes 417800 | tf_op jit(solution)/shard_map/ppermute | solution.py:316
  65.9 5.2 %far.7 = (bf16[32,2176]{1,0:T(8,128)(2,1)S(1)}, bf16[32,2176]{1,0:T(8,128)(2,1)S(1)}) custom-call(bf16[32,7424]{1,0:T(8,128)(2,1)S(1)} %collective-permute-done.10.direct_ref, bf16[32,3712]{1,0:T(8,128)(2,1)S(1)} %collective-permute-done.15.refs_0_, bf16[32,3712]{1,0:T(8,128)(2,1)S(1)} %collective-permute-done.16.refs_1_, ...), custom_call_target="tpu_custom_call" | custom-call | flops 1 | bytes 1 | tf_op jit(solution)/shard_map/far/pallas_call | solution.py:259
  71.2 1.4 %collective-permute-done.18.refs_5_ = bf16[32,2176]{1,0:T(8,128)(2,1)S(1)} collective-permute-done((bf16[32,2176]{1,0:T(8,128)(2,1)S(1)}, bf16[32,2176]{1,0:T(8,128)(2,1)S(1)}, u32[]{:S(2)}, u32[]{:S(2)}) %collective-permute-start.18) | collective-permute-done | bytes 139296 | tf_op jit(solution)/shard_map/ppermute | solution.py:316
  73.0 2.7 %collective-permute-start.20 = (bf16[32,2176]{1,0:T(8,128)(2,1)S(1)}, bf16[32,2176]{1,0:T(8,128)(2,1)S(1)}, u32[]{:S(2)}, u32[]{:S(2)}) collective-permute-start(bf16[32,2176]{1,0:T(8,128)(2,1)S(1)} %get-tuple-element.101), channel_id=1, source_target_pairs={{0,8},{4,12},{8,0},{12,4},{1,9},{5,13},{9,1},{13,5},{2,10},{6,14},... | collective-permute-start | bytes 417800 | tf_op jit(solution)/shard_map/ppermute | solution.py:316
  75.6 3.8 %collective-permute-done.19.far_b = bf16[32,2176]{1,0:T(8,128)(2,1)S(1)} collective-permute-done((bf16[32,2176]{1,0:T(8,128)(2,1)S(1)}, bf16[32,2176]{1,0:T(8,128)(2,1)S(1)}, u32[]{:S(2)}, u32[]{:S(2)}) %collective-permute-start.19) | collective-permute-done | bytes 139296 | tf_op jit(solution)/shard_map/ppermute | solution.py:309
  79.6 0.7 collective-permute-start.21
  80.2 5.5 %collective-permute-done.20.refs_6_ = bf16[32,2176]{1,0:T(8,128)(2,1)S(1)} collective-permute-done((bf16[32,2176]{1,0:T(8,128)(2,1)S(1)}, bf16[32,2176]{1,0:T(8,128)(2,1)S(1)}, u32[]{:S(2)}, u32[]{:S(2)}) %collective-permute-start.20) | collective-permute-done | bytes 139296 | tf_op jit(solution)/shard_map/ppermute | solution.py:316
  85.7 2.0 %collective-permute-done.21.refs_7_ = bf16[32,2176]{1,0:T(8,128)(2,1)S(1)} collective-permute-done((bf16[32,2176]{1,0:T(8,128)(2,1)S(1)}, bf16[32,2176]{1,0:T(8,128)(2,1)S(1)}, u32[]{:S(2)}, u32[]{:S(2)}) %collective-permute-start.21) | collective-permute-done | bytes 139296 | tf_op jit(solution)/shard_map/ppermute | solution.py:318
  87.7 1.3 %last.1 = bf16[128,2048]{1,0:T(8,128)(2,1)} custom-call(bf16[512,2048]{1,0:T(8,128)(2,1)S(1)} %bitcast.6, bf16[32,2176]{1,0:T(8,128)(2,1)S(1)} %get-tuple-element.76.refs_0_, bf16[32,2176]{1,0:T(8,128)(2,1)S(1)} %get-tuple-element.87.refs_1_, bf16[32,2176]{1,0:T(8,128)(2,1)S(1)} %get-tuple-element.95.refs_2_, ...), custom_call_target="tpu_custom_call" | custom-call | tf_op jit(solution)/shard_map/last/pallas_call | solution.py:320
  (37 shorter events, 4.7 us)
Async XLA Ops:
  1.8 4.0 %collective-permute-start.3 = (bf16[128,7424]{1,0:T(8,128)(2,1)S(1)}, bf16[128,7424]{1,0:T(8,128)(2,1)S(1)}, u32[]{:S(2)}, u32[]{:S(2)}) collective-permute-start(bf16[128,7424]{1,0:T(8,128)(2,1)S(1)} %get-tuple-element.57.own_ref), channel_id=1, source_target_pairs={{0,1},{1,0},{2,3},{3,2},{4,5},{5,4},{6,7},{7,6},{8,9},{9,8},{10,11... | collective-permute-start | bytes 5701640 | tf_op jit(solution)/shard_map/ppermute | solution.py:237
  2.3 27.3 %collective-permute-start.2 = (bf16[32,7424]{1,0:T(8,128)(2,1)S(1)}, bf16[32,7424]{1,0:T(8,128)(2,1)S(1)}, u32[]{:S(2)}, u32[]{:S(2)}) collective-permute-start(bf16[32,7424]{1,0:T(8,128)(2,1)S(1)} %get-tuple-element.56), channel_id=1, source_target_pairs={{0,2},{1,3},{2,0},{3,1},{4,6},{5,7},{6,4},{7,5},{8,10},{9,11},{10,... | collective-permute-start | bytes 1425416 | tf_op jit(solution)/shard_map/ppermute | solution.py:236
  4.9 35.2 %collective-permute-start.1 = (bf16[32,7424]{1,0:T(8,128)(2,1)S(1)}, bf16[32,7424]{1,0:T(8,128)(2,1)S(1)}, u32[]{:S(2)}, u32[]{:S(2)}) collective-permute-start(bf16[32,7424]{1,0:T(8,128)(2,1)S(1)} %get-tuple-element.55), channel_id=1, source_target_pairs={{0,2},{1,3},{2,0},{3,1},{4,6},{5,7},{6,4},{7,5},{8,10},{9,11},{10,... | collective-permute-start | bytes 1425416 | tf_op jit(solution)/shard_map/ppermute | solution.py:301
  29.7 5.0 %collective-permute-start.5 = (bf16[32,3712]{1,0:T(8,128)(2,1)S(1)}, bf16[32,3712]{1,0:T(8,128)(2,1)S(1)}, u32[]{:S(2)}, u32[]{:S(2)}) collective-permute-start(bf16[32,3712]{1,0:T(8,128)(2,1)S(1)} %get-tuple-element.109), channel_id=1, source_target_pairs={{0,1},{1,0},{2,3},{3,2},{4,5},{5,4},{6,7},{7,6},{8,9},{9,8},{10,11... | collective-permute-start | bytes 712712 | tf_op jit(solution)/shard_map/ppermute | solution.py:284
  30.2 4.6 %collective-permute-start.4 = (bf16[32,3712]{1,0:T(8,128)(2,1)S(1)}, bf16[32,3712]{1,0:T(8,128)(2,1)S(1)}, u32[]{:S(2)}, u32[]{:S(2)}) collective-permute-start(bf16[32,3712]{1,0:T(8,128)(2,1)S(1)} %get-tuple-element.110), channel_id=1, source_target_pairs={{0,1},{1,0},{2,3},{3,2},{4,5},{5,4},{6,7},{7,6},{8,9},{9,8},{10,11... | collective-permute-start | bytes 712712 | tf_op jit(solution)/shard_map/ppermute | solution.py:284
  30.3 17.2 %collective-permute-start = (bf16[32,7424]{1,0:T(8,128)(2,1)S(1)}, bf16[32,7424]{1,0:T(8,128)(2,1)S(1)}, u32[]{:S(2)}, u32[]{:S(2)}) collective-permute-start(bf16[32,7424]{1,0:T(8,128)(2,1)S(1)} %get-tuple-element.54), channel_id=1, source_target_pairs={{0,2},{1,3},{2,0},{3,1},{4,6},{5,7},{6,4},{7,5},{8,10},{9,11},{10,... | collective-permute-start | bytes 1425416 | tf_op jit(solution)/shard_map/ppermute | solution.py:301
  33.2 17.4 %collective-permute-start.9 = (bf16[128,2176]{1,0:T(8,128)(2,1)S(1)}, bf16[128,2176]{1,0:T(8,128)(2,1)S(1)}, u32[]{:S(2)}, u32[]{:S(2)}) collective-permute-start(bf16[128,2176]{1,0:T(8,128)(2,1)S(1)} %get-tuple-element.72), channel_id=1, source_target_pairs={{0,4},{4,0},{8,12},{12,8},{1,5},{5,1},{9,13},{13,9},{2,6},{6,2},{1... | collective-permute-start | bytes 1671176 | tf_op jit(solution)/shard_map/ppermute | solution.py:289
  40.2 1.6 %collective-permute-start.7 = (bf16[32,3712]{1,0:T(8,128)(2,1)S(1)}, bf16[32,3712]{1,0:T(8,128)(2,1)S(1)}, u32[]{:S(2)}, u32[]{:S(2)}) collective-permute-start(bf16[32,3712]{1,0:T(8,128)(2,1)S(1)} %get-tuple-element.107), channel_id=1, source_target_pairs={{0,1},{1,0},{2,3},{3,2},{4,5},{5,4},{6,7},{7,6},{8,9},{9,8},{10,11... | collective-permute-start | bytes 712712 | tf_op jit(solution)/shard_map/ppermute | solution.py:284
  40.3 2.0 %collective-permute-start.6 = (bf16[32,3712]{1,0:T(8,128)(2,1)S(1)}, bf16[32,3712]{1,0:T(8,128)(2,1)S(1)}, u32[]{:S(2)}, u32[]{:S(2)}) collective-permute-start(bf16[32,3712]{1,0:T(8,128)(2,1)S(1)} %get-tuple-element.108), channel_id=1, source_target_pairs={{0,1},{1,0},{2,3},{3,2},{4,5},{5,4},{6,7},{7,6},{8,9},{9,8},{10,11... | collective-permute-start | bytes 712712 | tf_op jit(solution)/shard_map/ppermute | solution.py:284
  40.8 9.8 %collective-permute-start.8 = (bf16[32,2176]{1,0:T(8,128)(2,1)S(1)}, bf16[32,2176]{1,0:T(8,128)(2,1)S(1)}, u32[]{:S(2)}, u32[]{:S(2)}) collective-permute-start(bf16[32,2176]{1,0:T(8,128)(2,1)S(1)} %get-tuple-element.69), channel_id=1, source_target_pairs={{0,4},{4,0},{8,12},{12,8},{1,5},{5,1},{9,13},{13,9},{2,6},{6,2},{1... | collective-permute-start | bytes 417800 | tf_op jit(solution)/shard_map/ppermute | solution.py:305
  41.8 19.1 %collective-permute-start.10 = (bf16[32,7424]{1,0:T(8,128)(2,1)S(1)}, bf16[32,7424]{1,0:T(8,128)(2,1)S(1)}, u32[]{:S(2)}, u32[]{:S(2)}) collective-permute-start(bf16[32,7424]{1,0:T(8,128)(2,1)S(1)} %get-tuple-element.77), channel_id=1, source_target_pairs={{0,2},{1,3},{2,0},{3,1},{4,6},{5,7},{6,4},{7,5},{8,10},{9,11},{10,... | collective-permute-start | bytes 1425416 | tf_op jit(solution)/shard_map/ppermute | solution.py:301
  50.7 4.7 %collective-permute-start.12 = (bf16[32,3712]{1,0:T(8,128)(2,1)S(1)}, bf16[32,3712]{1,0:T(8,128)(2,1)S(1)}, u32[]{:S(2)}, u32[]{:S(2)}) collective-permute-start(bf16[32,3712]{1,0:T(8,128)(2,1)S(1)} %get-tuple-element.105), channel_id=1, source_target_pairs={{0,1},{1,0},{2,3},{3,2},{4,5},{5,4},{6,7},{7,6},{8,9},{9,8},{10,11... | collective-permute-start | bytes 712712 | tf_op jit(solution)/shard_map/ppermute | solution.py:284
  50.8 4.7 %collective-permute-start.11 = (bf16[32,3712]{1,0:T(8,128)(2,1)S(1)}, bf16[32,3712]{1,0:T(8,128)(2,1)S(1)}, u32[]{:S(2)}, u32[]{:S(2)}) collective-permute-start(bf16[32,3712]{1,0:T(8,128)(2,1)S(1)} %get-tuple-element.106), channel_id=1, source_target_pairs={{0,1},{1,0},{2,3},{3,2},{4,5},{5,4},{6,7},{7,6},{8,9},{9,8},{10,11... | collective-permute-start | bytes 712712 | tf_op jit(solution)/shard_map/ppermute | solution.py:284
  51.3 9.6 %collective-permute-start.13 = (bf16[32,2176]{1,0:T(8,128)(2,1)S(1)}, bf16[32,2176]{1,0:T(8,128)(2,1)S(1)}, u32[]{:S(2)}, u32[]{:S(2)}) collective-permute-start(bf16[32,2176]{1,0:T(8,128)(2,1)S(1)} %get-tuple-element.81), channel_id=1, source_target_pairs={{0,4},{4,0},{8,12},{12,8},{1,5},{5,1},{9,13},{13,9},{2,6},{6,2},{1... | collective-permute-start | bytes 417800 | tf_op jit(solution)/shard_map/ppermute | solution.py:305
  52.8 9.3 %collective-permute-start.14 = (bf16[32,2176]{1,0:T(8,128)(2,1)S(1)}, bf16[32,2176]{1,0:T(8,128)(2,1)S(1)}, u32[]{:S(2)}, u32[]{:S(2)}) collective-permute-start(bf16[32,2176]{1,0:T(8,128)(2,1)S(1)} %get-tuple-element.82), channel_id=1, source_target_pairs={{0,8},{4,12},{8,0},{12,4},{1,9},{5,13},{9,1},{13,5},{2,10},{6,14},... | collective-permute-start | bytes 417800 | tf_op jit(solution)/shard_map/ppermute | solution.py:316
  62.3 3.6 %collective-permute-start.16 = (bf16[32,3712]{1,0:T(8,128)(2,1)S(1)}, bf16[32,3712]{1,0:T(8,128)(2,1)S(1)}, u32[]{:S(2)}, u32[]{:S(2)}) collective-permute-start(bf16[32,3712]{1,0:T(8,128)(2,1)S(1)} %get-tuple-element.103), channel_id=1, source_target_pairs={{0,1},{1,0},{2,3},{3,2},{4,5},{5,4},{6,7},{7,6},{8,9},{9,8},{10,11... | collective-permute-start | bytes 712712 | tf_op jit(solution)/shard_map/ppermute | solution.py:284
  62.4 3.5 %collective-permute-start.15 = (bf16[32,3712]{1,0:T(8,128)(2,1)S(1)}, bf16[32,3712]{1,0:T(8,128)(2,1)S(1)}, u32[]{:S(2)}, u32[]{:S(2)}) collective-permute-start(bf16[32,3712]{1,0:T(8,128)(2,1)S(1)} %get-tuple-element.104), channel_id=1, source_target_pairs={{0,1},{1,0},{2,3},{3,2},{4,5},{5,4},{6,7},{7,6},{8,9},{9,8},{10,11... | collective-permute-start | bytes 712712 | tf_op jit(solution)/shard_map/ppermute | solution.py:284
  62.9 8.4 %collective-permute-start.17 = (bf16[32,2176]{1,0:T(8,128)(2,1)S(1)}, bf16[32,2176]{1,0:T(8,128)(2,1)S(1)}, u32[]{:S(2)}, u32[]{:S(2)}) collective-permute-start(bf16[32,2176]{1,0:T(8,128)(2,1)S(1)} %get-tuple-element.91), channel_id=1, source_target_pairs={{0,4},{4,0},{8,12},{12,8},{1,5},{5,1},{9,13},{13,9},{2,6},{6,2},{1... | collective-permute-start | bytes 417800 | tf_op jit(solution)/shard_map/ppermute | solution.py:305
  63.3 24.4 %copy-start = (bf16[8,64,2048]{2,1,0:T(8,128)(2,1)S(1)}, bf16[8,64,2048]{2,1,0:T(8,128)(2,1)}, u32[]{:S(2)}) copy-start(bf16[8,64,2048]{2,1,0:T(8,128)(2,1)} %param.8) | copy-start | bytes 6291460
  63.3 9.3 %collective-permute-start.18 = (bf16[32,2176]{1,0:T(8,128)(2,1)S(1)}, bf16[32,2176]{1,0:T(8,128)(2,1)S(1)}, u32[]{:S(2)}, u32[]{:S(2)}) collective-permute-start(bf16[32,2176]{1,0:T(8,128)(2,1)S(1)} %get-tuple-element.92), channel_id=1, source_target_pairs={{0,8},{4,12},{8,0},{12,4},{1,9},{5,13},{9,1},{13,5},{2,10},{6,14},... | collective-permute-start | bytes 417800 | tf_op jit(solution)/shard_map/ppermute | solution.py:316
  72.6 6.8 %collective-permute-start.19 = (bf16[32,2176]{1,0:T(8,128)(2,1)S(1)}, bf16[32,2176]{1,0:T(8,128)(2,1)S(1)}, u32[]{:S(2)}, u32[]{:S(2)}) collective-permute-start(bf16[32,2176]{1,0:T(8,128)(2,1)S(1)} %get-tuple-element.97), channel_id=1, source_target_pairs={{0,4},{4,0},{8,12},{12,8},{1,5},{5,1},{9,13},{13,9},{2,6},{6,2},{1... | collective-permute-start | bytes 417800 | tf_op jit(solution)/shard_map/ppermute | solution.py:309
  73.0 12.7 %collective-permute-start.20 = (bf16[32,2176]{1,0:T(8,128)(2,1)S(1)}, bf16[32,2176]{1,0:T(8,128)(2,1)S(1)}, u32[]{:S(2)}, u32[]{:S(2)}) collective-permute-start(bf16[32,2176]{1,0:T(8,128)(2,1)S(1)} %get-tuple-element.101), channel_id=1, source_target_pairs={{0,8},{4,12},{8,0},{12,4},{1,9},{5,13},{9,1},{13,5},{2,10},{6,14},... | collective-permute-start | bytes 417800 | tf_op jit(solution)/shard_map/ppermute | solution.py:316
  79.6 8.1 %collective-permute-start.21 = (bf16[32,2176]{1,0:T(8,128)(2,1)S(1)}, bf16[32,2176]{1,0:T(8,128)(2,1)S(1)}, u32[]{:S(2)}, u32[]{:S(2)}) collective-permute-start(bf16[32,2176]{1,0:T(8,128)(2,1)S(1)} %get-tuple-element.102), channel_id=1, source_target_pairs={{0,8},{4,12},{8,0},{12,4},{1,9},{5,13},{9,1},{13,5},{2,10},{6,14},... | collective-permute-start | bytes 417800 | tf_op jit(solution)/shard_map/ppermute | solution.py:318

commit v11 on v10

--- a/solution.py
+++ b/solution.py
@@ -11,7 +11,7 @@
 PANEL = 512
 DEPTH = 1024
 TURN = 15
-PIECES = (32, 32, 32, 32)
+PIECES = (48, 48, 32)
 CUTS = 2
 FULL = 128
 SLOTS = 3
@@ -75,17 +75,25 @@
     keep_ref[:, cols] = jnp.where(keep_first, first, second)
 
 
+def dots(blocks, panel_ref):
+    return jnp.concatenate(
+        [jnp.dot(rows, panel_ref[...], preferred_element_type=jnp.float32) for rows in blocks],
+        axis=0,
+    )
+
+
 def base_panel(panel, piece, panel_ref, send_ref, keep_ref):
-    value = jnp.dot(piece(), panel_ref[...], preferred_element_type=jnp.float32)
-    part_rows(value, slice(panel * PANEL, (panel + 1) * PANEL), send_ref, keep_ref)
+    cols = slice(panel * PANEL, (panel + 1) * PANEL)
+    part_rows(dots(piece(), panel_ref), cols, send_ref, keep_ref)
 
 
 def shrink_panel(adapters, units, piece, spread_ref, send_ref, keep_ref):
     width = send_ref.shape[1] - LANES
     wide = spread_ref.shape[1]
     rank = wide // adapters
-    every = jnp.dot(piece(), spread_ref[...], preferred_element_type=jnp.float32)
-    ids = piece()[:, units : units + 1].astype(jnp.float32)
+    every = dots(piece(), spread_ref)
+    ids = [rows[:, units : units + 1] for rows in piece()]
+    ids = jnp.concatenate(ids, axis=0).astype(jnp.float32)
     column = lax.broadcasted_iota(jnp.int32, every.shape, 1) // rank
     picked = jnp.where(column.astype(jnp.float32) == ids, every, 0.0)
     tile = picked[:, :LANES]
@@ -127,7 +135,7 @@
         ref[units:, :] = jnp.zeros_like(ref[units:, :])
 
     def piece():
-        return jnp.concatenate([own_ref[...], other_ref[...]], axis=0)
+        return [own_ref[...], other_ref[...]]
 
     for step, ((at, to), stage) in enumerate(zip(cuts, stages)):
         s_copies[step].wait()
@@ -146,8 +154,9 @@
 
     def piece():
         passed = jnp.concatenate([ref[...] for ref in passed_refs], axis=1)
-        both = jnp.concatenate([direct_ref[...], passed], axis=0)
-        return jnp.concatenate([both] * max(1, FULL // both.shape[0]), axis=0)
+        rows = jnp.concatenate([direct_ref[...], passed], axis=0)
+        room = max(0, FULL - rows.shape[0])
+        return [jnp.concatenate([rows, rows[:room]], axis=0)]
 
     shrink_panel(adapters, units, piece, spread_ref, send_ref, keep_ref)
     for panel, panel_ref in enumerate(panel_refs):
@@ -288,34 +297,20 @@
     steps = len(counts)
     near_got = lax.ppermute(near_send, "tensor", next_z)
     direct[0], near_keep = after((direct[0], near_keep))
-    parts, kept, gots = [], [], []
-
-    def add_part(step):
-        send, keep = add(step, *parts[step])
-        kept.append(keep)
-        return send
+    kept, gots = [], []
 
     for step in range(steps):
         passed = over_core(direct[step])
         if step + 1 < steps:
             direct.append(lax.ppermute(pieces[step + 1], "req", across))
         send, keep = product(step, passed)
-        hop = gots[step - 2 :] if step > 1 else []
+        got = lax.ppermute(send, "tensor", next_z)
+        keep, got, gots = after((keep, got, gots))
+        send, stays = add(step, keep, got)
         if step + 1 < steps:
-            got = lax.ppermute(send, "tensor", next_z)
-            direct[step + 1], keep, parts, hop = after((direct[step + 1], keep, parts, hop))
-        else:
-            send, parts, hop = after((send, parts, hop))
-            got = lax.ppermute(send, "tensor", next_z)
-        if step > 1:
-            gots[step - 2 :] = hop
-        if step > 0:
-            send = add_part(step - 1)
-            if step + 1 < steps:
-                direct[step + 1], kept[-1] = after((direct[step + 1], kept[-1]))
-            gots.append(lax.ppermute(send, "tensor", far_z))
-        parts.append((keep, got))
-    gots.append(lax.ppermute(add_part(steps - 1), "tensor", far_z))
+            direct[step + 1], stays = after((direct[step + 1], stays))
+        kept.append(stays)
+        gots.append(lax.ppermute(send, "tensor", far_z))
 
     return pl.pallas_call(
         functools.partial(last_kernel, n_tensor, adapters),

time: 89.2 us -> 97.1 us (1.089)
  waiting for transfers between devices: 18.5 us -> 33.2 us
  Pallas kernels: 48.5 us -> 43.3 us
  starting transfers between devices: 21.7 us -> 20.2 us
    ppermute x4 -> x3, waiting for transfers between devices: 6.97 us -> 17.5 us  [paired(): got = lax.ppermute(send, 'tensor', next_z)]
    ppermute x3, waiting for transfers between devices: 8.13 us -> 14.8 us  [paired(): gots.append(lax.ppermute(send, 'tensor', far_z))]
    pallas_call x4 -> x3, Pallas kernels: 21.2 us -> 16 us  [product(): pl.pallas_call(functools.partial(far_kernel, adapters, units), out_shape=...]
    ppermute x4 -> x3, starting transfers between devices: 2.76 us -> 5.91 us  [paired(): got = lax.ppermute(send, 'tensor', next_z)]
    ppermute x3, starting transfers between devices: 7.83 us -> 4.79 us  [paired(): gots.append(lax.ppermute(send, 'tensor', far_z))]
    ppermute x1 -> x0, waiting for transfers between devices: 2.02 us -> none  [paired(): gots.append(lax.ppermute(add_part(steps - 1), 'tensor', far_z))]
    ppermute x3 -> x2, starting transfers between devices: 3.48 us -> 1.76 us  [paired(): direct.append(lax.ppermute(pieces[step + 1], 'req', across))]
    ppermute x1, starting transfers between devices: 1.58 us -> 2.95 us  [paired(): near_got = lax.ppermute(near_send, 'tensor', next_z)]
  transfers between devices with their start and end apart: 22 -> 17, of which waited for: 9 -> 7; matrix products, arithmetic and copies ran while one was open for 0% -> 0% of each run, Pallas kernels for 51% -> 41%
where the time goes in v11:
time: 97.1 us; the launch traced here: 97 us
  Pallas kernels  43.3 us (45%)
  waiting for transfers between devices  33.2 us (34%)
  starting transfers between devices  20.2 us (21%)
    pallas_call x1, Pallas kernels, paired(): pl.pallas_call(functools.partial(near_kernel, adapters), out_shape=[struc...  23.9 us
    ppermute x3, waiting for transfers between devices, paired(): got = lax.ppermute(send, 'tensor', next_z)  17.5 us
    pallas_call x3, Pallas kernels, product(): pl.pallas_call(functools.partial(far_kernel, adapters, units), out_shape=...  16 us
    ppermute x3, waiting for transfers between devices, paired(): gots.append(lax.ppermute(send, 'tensor', far_z))  14.8 us
    ppermute x3, starting transfers between devices, paired(): got = lax.ppermute(send, 'tensor', next_z)  5.91 us
    ppermute x3, starting transfers between devices, paired(): gots.append(lax.ppermute(send, 'tensor', far_z))  4.79 us
    ppermute x1, starting transfers between devices, paired(): near_got = lax.ppermute(near_send, 'tensor', next_z)  2.95 us
    ppermute x1, starting transfers between devices, paired(): direct = [lax.ppermute(pieces[0], 'req', across)]  2.56 us
  transfers between devices with their start and end apart: 17, of which 7 were waited for; matrix products, arithmetic and copies ran while one was open for 0% of the time, Pallas kernels for 41%

profile of v11, /device:TPU:0, one launch (start us, length us, event | category | flops | bytes accessed | tf_op | source)
XLA Modules:
  0.0 97.0 jit_solution(15047587394298099168)
XLA Ops:
  0.0 1.8 %turn.1 = (bf16[128,7424]{1,0:T(8,128)(2,1)S(1)}, bf16[48,7424]{1,0:T(8,128)(2,1)S(1)}, bf16[48,7424]{1,0:T(8,128)(2,1)S(1)}, bf16[32,7424]{1,0:T(8,128)(2,1)S(1)}) custom-call(bf16[7392,128]{1,0:T(8,128)(2,1)} %bitcast.8, s32[1,128]{1,0:T(1,128)} %bitcast.9), custom_call_target="tpu_custom_call" | custom-call | tf_op jit(solution)/shard_map/turn/pallas_call | solution.py:226
  1.8 0.5 collective-permute-start.2
  2.3 2.6 %collective-permute-start.1 = (bf16[48,7424]{1,0:T(8,128)(2,1)S(1)}, bf16[48,7424]{1,0:T(8,128)(2,1)S(1)}, u32[]{:S(2)}, u32[]{:S(2)}) collective-permute-start(bf16[48,7424]{1,0:T(8,128)(2,1)S(1)} %get-tuple-element.44), channel_id=1, source_target_pairs={{0,2},{1,3},{2,0},{3,1},{4,6},{5,7},{6,4},{7,5},{8,10},{9,11},{10,... | collective-permute-start | bytes 2138120 | tf_op jit(solution)/shard_map/ppermute | solution.py:245
  5.0 0.8 collective-permute-done.2.other_ref
  5.9 23.9 %near.1 = (bf16[128,2176]{1,0:T(8,128)(2,1)S(1)}, bf16[128,2176]{1,0:T(8,128)(2,1)S(1)}, bf16[7424,512]{1,0:T(8,128)(2,1)S(1)}, bf16[7424,512]{1,0:T(8,128)(2,1)...) custom-call(bf16[128,7424]{1,0:T(8,128)(2,1)S(1)} %get-tuple-element.45.own_ref, ...), custom_call_target="tpu_custom_call" | custom-call | flops 1 | bytes 1 | tf_op jit(solution)/shard_map/near/pallas_call | solution.py:249
  30.4 3.0 %collective-permute-start.3 = (bf16[128,2176]{1,0:T(8,128)(2,1)S(1)}, bf16[128,2176]{1,0:T(8,128)(2,1)S(1)}, u32[]{:S(2)}, u32[]{:S(2)}) collective-permute-start(bf16[128,2176]{1,0:T(8,128)(2,1)S(1)} %get-tuple-element.48), channel_id=1, source_target_pairs={{0,4},{4,0},{8,12},{12,8},{1,5},{5,1},{9,13},{13,9},{2,6},{6,2},{1... | collective-permute-start | bytes 1671176 | tf_op jit(solution)/shard_map/ppermute | solution.py:298
  33.3 5.4 %far.3 = (bf16[48,2176]{1,0:T(8,128)(2,1)S(1)}, bf16[48,2176]{1,0:T(8,128)(2,1)S(1)}) custom-call(bf16[48,7424]{1,0:T(8,128)(2,1)S(1)} %collective-permute-done.1.direct_ref, bf16[48,3712]{1,0:T(8,128)(2,1)S(1)} %collective-permute-done.4.refs_0_, bf16[48,3712]{1,0:T(8,128)(2,1)S(1)} %collective-permute-done.5.refs_1_, ...), custom_call_target="tpu_custom_call" | custom-call | flops 1 | bytes 1 | tf_op jit(solution)/shard_map/far/pallas_call | solution.py:268
  38.7 1.7 %collective-permute-start.6 = (bf16[48,2176]{1,0:T(8,128)(2,1)S(1)}, bf16[48,2176]{1,0:T(8,128)(2,1)S(1)}, u32[]{:S(2)}, u32[]{:S(2)}) collective-permute-start(bf16[48,2176]{1,0:T(8,128)(2,1)S(1)} %get-tuple-element.56), channel_id=1, source_target_pairs={{0,4},{4,0},{8,12},{12,8},{1,5},{5,1},{9,13},{13,9},{2,6},{6,2},{1... | collective-permute-start | bytes 626696 | tf_op jit(solution)/shard_map/ppermute | solution.py:307
  40.4 10.3 %collective-permute-done.6.far_b = bf16[48,2176]{1,0:T(8,128)(2,1)S(1)} collective-permute-done((bf16[48,2176]{1,0:T(8,128)(2,1)S(1)}, bf16[48,2176]{1,0:T(8,128)(2,1)S(1)}, u32[]{:S(2)}, u32[]{:S(2)}) %collective-permute-start.6) | collective-permute-done | bytes 208928 | tf_op jit(solution)/shard_map/ppermute | solution.py:307
  51.0 0.5 collective-permute-start.8
  51.5 1.7 %collective-permute-start.7 = (bf16[32,7424]{1,0:T(8,128)(2,1)S(1)}, bf16[32,7424]{1,0:T(8,128)(2,1)S(1)}, u32[]{:S(2)}, u32[]{:S(2)}) collective-permute-start(bf16[32,7424]{1,0:T(8,128)(2,1)S(1)} %get-tuple-element.61), channel_id=1, source_target_pairs={{0,2},{1,3},{2,0},{3,1},{4,6},{5,7},{6,4},{7,5},{8,10},{9,11},{10,... | collective-permute-start | bytes 1425416 | tf_op jit(solution)/shard_map/ppermute | solution.py:305
  53.1 2.6 %collective-permute-start.11 = (bf16[48,2176]{1,0:T(8,128)(2,1)S(1)}, bf16[48,2176]{1,0:T(8,128)(2,1)S(1)}, u32[]{:S(2)}, u32[]{:S(2)}) collective-permute-start(bf16[48,2176]{1,0:T(8,128)(2,1)S(1)} %get-tuple-element.65), channel_id=1, source_target_pairs={{0,8},{4,12},{8,0},{12,4},{1,9},{5,13},{9,1},{13,5},{2,10},{6,14},... | collective-permute-start | bytes 626696 | tf_op jit(solution)/shard_map/ppermute | solution.py:313
  55.7 5.2 %far.4 = (bf16[48,2176]{1,0:T(8,128)(2,1)S(1)}, bf16[48,2176]{1,0:T(8,128)(2,1)S(1)}) custom-call(bf16[48,7424]{1,0:T(8,128)(2,1)S(1)} %collective-permute-done.direct_ref, bf16[48,3712]{1,0:T(8,128)(2,1)S(1)} %collective-permute-done.8.refs_0_, bf16[48,3712]{1,0:T(8,128)(2,1)S(1)} %collective-permute-done.9.refs_1_, ...), custom_call_target="tpu_custom_call" | custom-call | flops 1 | bytes 1 | tf_op jit(solution)/shard_map/far/pallas_call | solution.py:268
  60.9 1.6 %collective-permute-start.10 = (bf16[48,2176]{1,0:T(8,128)(2,1)S(1)}, bf16[48,2176]{1,0:T(8,128)(2,1)S(1)}, u32[]{:S(2)}, u32[]{:S(2)}) collective-permute-start(bf16[48,2176]{1,0:T(8,128)(2,1)S(1)} %get-tuple-element.64), channel_id=1, source_target_pairs={{0,4},{4,0},{8,12},{12,8},{1,5},{5,1},{9,13},{13,9},{2,6},{6,2},{1... | collective-permute-start | bytes 626696 | tf_op jit(solution)/shard_map/ppermute | solution.py:307
  62.6 2.9 %collective-permute-done.11.refs_3_ = bf16[48,2176]{1,0:T(8,128)(2,1)S(1)} collective-permute-done((bf16[48,2176]{1,0:T(8,128)(2,1)S(1)}, bf16[48,2176]{1,0:T(8,128)(2,1)S(1)}, u32[]{:S(2)}, u32[]{:S(2)}) %collective-permute-start.11) | collective-permute-done | bytes 208928 | tf_op jit(solution)/shard_map/ppermute | solution.py:313
  65.5 4.4 %collective-permute-done.10.far_b = bf16[48,2176]{1,0:T(8,128)(2,1)S(1)} collective-permute-done((bf16[48,2176]{1,0:T(8,128)(2,1)S(1)}, bf16[48,2176]{1,0:T(8,128)(2,1)S(1)}, u32[]{:S(2)}, u32[]{:S(2)}) %collective-permute-start.10) | collective-permute-done | bytes 208928 | tf_op jit(solution)/shard_map/ppermute | solution.py:307
  70.6 1.6 %collective-permute-start.15 = (bf16[48,2176]{1,0:T(8,128)(2,1)S(1)}, bf16[48,2176]{1,0:T(8,128)(2,1)S(1)}, u32[]{:S(2)}, u32[]{:S(2)}) collective-permute-start(bf16[48,2176]{1,0:T(8,128)(2,1)S(1)} %get-tuple-element.74), channel_id=1, source_target_pairs={{0,8},{4,12},{8,0},{12,4},{1,9},{5,13},{9,1},{13,5},{2,10},{6,14},... | collective-permute-start | bytes 626696 | tf_op jit(solution)/shard_map/ppermute | solution.py:313
  72.2 5.4 %far.5 = (bf16[32,2176]{1,0:T(8,128)(2,1)S(1)}, bf16[32,2176]{1,0:T(8,128)(2,1)S(1)}) custom-call(bf16[32,7424]{1,0:T(8,128)(2,1)S(1)} %collective-permute-done.7.direct_ref, bf16[32,3712]{1,0:T(8,128)(2,1)S(1)} %collective-permute-done.12.refs_0_, bf16[32,3712]{1,0:T(8,128)(2,1)S(1)} %collective-permute-done.13.refs_1_, ...), custom_call_target="tpu_custom_call" | custom-call | flops 1 | bytes 1 | tf_op jit(solution)/shard_map/far/pallas_call | solution.py:268
  77.6 2.5 %collective-permute-start.14 = (bf16[32,2176]{1,0:T(8,128)(2,1)S(1)}, bf16[32,2176]{1,0:T(8,128)(2,1)S(1)}, u32[]{:S(2)}, u32[]{:S(2)}) collective-permute-start(bf16[32,2176]{1,0:T(8,128)(2,1)S(1)} %get-tuple-element.72), channel_id=1, source_target_pairs={{0,4},{4,0},{8,12},{12,8},{1,5},{5,1},{9,13},{13,9},{2,6},{6,2},{1... | collective-permute-start | bytes 417800 | tf_op jit(solution)/shard_map/ppermute | solution.py:307
  80.2 3.1 %collective-permute-done.15.refs_4_ = bf16[48,2176]{1,0:T(8,128)(2,1)S(1)} collective-permute-done((bf16[48,2176]{1,0:T(8,128)(2,1)S(1)}, bf16[48,2176]{1,0:T(8,128)(2,1)S(1)}, u32[]{:S(2)}, u32[]{:S(2)}) %collective-permute-start.15) | collective-permute-done | bytes 208928 | tf_op jit(solution)/shard_map/ppermute | solution.py:313
  83.3 2.9 %collective-permute-done.14.far_b = bf16[32,2176]{1,0:T(8,128)(2,1)S(1)} collective-permute-done((bf16[32,2176]{1,0:T(8,128)(2,1)S(1)}, bf16[32,2176]{1,0:T(8,128)(2,1)S(1)}, u32[]{:S(2)}, u32[]{:S(2)}) %collective-permute-start.14) | collective-permute-done | bytes 139296 | tf_op jit(solution)/shard_map/ppermute | solution.py:307
  86.2 0.6 collective-permute-start.16
  86.9 8.8 %collective-permute-done.16.refs_5_ = bf16[32,2176]{1,0:T(8,128)(2,1)S(1)} collective-permute-done((bf16[32,2176]{1,0:T(8,128)(2,1)S(1)}, bf16[32,2176]{1,0:T(8,128)(2,1)S(1)}, u32[]{:S(2)}, u32[]{:S(2)}) %collective-permute-start.16) | collective-permute-done | bytes 139296 | tf_op jit(solution)/shard_map/ppermute | solution.py:313
  95.6 1.3 %last.1 = bf16[128,2048]{1,0:T(8,128)(2,1)} custom-call(bf16[512,2048]{1,0:T(8,128)(2,1)S(1)} %bitcast.6, bf16[48,2176]{1,0:T(8,128)(2,1)S(1)} %get-tuple-element.60.refs_0_, bf16[48,2176]{1,0:T(8,128)(2,1)S(1)} %get-tuple-element.69.refs_1_, bf16[32,2176]{1,0:T(8,128)(2,1)S(1)} %get-tuple-element.77.refs_2_, ...), custom_call_target="tpu_custom_call" | custom-call | tf_op jit(solution)/shard_map/last/pallas_call | solution.py:315
  (24 shorter events, 1.8 us)
Async XLA Ops:
  1.8 4.0 %collective-permute-start.2 = (bf16[128,7424]{1,0:T(8,128)(2,1)S(1)}, bf16[128,7424]{1,0:T(8,128)(2,1)S(1)}, u32[]{:S(2)}, u32[]{:S(2)}) collective-permute-start(bf16[128,7424]{1,0:T(8,128)(2,1)S(1)} %get-tuple-element.45.own_ref), channel_id=1, source_target_pairs={{0,1},{1,0},{2,3},{3,2},{4,5},{5,4},{6,7},{7,6},{8,9},{9,8},{10,11... | collective-permute-start | bytes 5701640 | tf_op jit(solution)/shard_map/ppermute | solution.py:246
  2.3 27.4 %collective-permute-start.1 = (bf16[48,7424]{1,0:T(8,128)(2,1)S(1)}, bf16[48,7424]{1,0:T(8,128)(2,1)S(1)}, u32[]{:S(2)}, u32[]{:S(2)}) collective-permute-start(bf16[48,7424]{1,0:T(8,128)(2,1)S(1)} %get-tuple-element.44), channel_id=1, source_target_pairs={{0,2},{1,3},{2,0},{3,1},{4,6},{5,7},{6,4},{7,5},{8,10},{9,11},{10,... | collective-permute-start | bytes 2138120 | tf_op jit(solution)/shard_map/ppermute | solution.py:245
  4.9 45.9 %collective-permute-start = (bf16[48,7424]{1,0:T(8,128)(2,1)S(1)}, bf16[48,7424]{1,0:T(8,128)(2,1)S(1)}, u32[]{:S(2)}, u32[]{:S(2)}) collective-permute-start(bf16[48,7424]{1,0:T(8,128)(2,1)S(1)} %get-tuple-element.43), channel_id=1, source_target_pairs={{0,2},{1,3},{2,0},{3,1},{4,6},{5,7},{6,4},{7,5},{8,10},{9,11},{10,... | collective-permute-start | bytes 2138120 | tf_op jit(solution)/shard_map/ppermute | solution.py:305
  29.8 3.5 %collective-permute-start.5 = (bf16[48,3712]{1,0:T(8,128)(2,1)S(1)}, bf16[48,3712]{1,0:T(8,128)(2,1)S(1)}, u32[]{:S(2)}, u32[]{:S(2)}) collective-permute-start(bf16[48,3712]{1,0:T(8,128)(2,1)S(1)} %get-tuple-element.83), channel_id=1, source_target_pairs={{0,1},{1,0},{2,3},{3,2},{4,5},{5,4},{6,7},{7,6},{8,9},{9,8},{10,11... | collective-permute-start | bytes 1069064 | tf_op jit(solution)/shard_map/ppermute | solution.py:293
  30.2 3.1 %collective-permute-start.4 = (bf16[48,3712]{1,0:T(8,128)(2,1)S(1)}, bf16[48,3712]{1,0:T(8,128)(2,1)S(1)}, u32[]{:S(2)}, u32[]{:S(2)}) collective-permute-start(bf16[48,3712]{1,0:T(8,128)(2,1)S(1)} %get-tuple-element.84), channel_id=1, source_target_pairs={{0,1},{1,0},{2,3},{3,2},{4,5},{5,4},{6,7},{7,6},{8,9},{9,8},{10,11... | collective-permute-start | bytes 1069064 | tf_op jit(solution)/shard_map/ppermute | solution.py:293
  30.4 20.3 %collective-permute-start.3 = (bf16[128,2176]{1,0:T(8,128)(2,1)S(1)}, bf16[128,2176]{1,0:T(8,128)(2,1)S(1)}, u32[]{:S(2)}, u32[]{:S(2)}) collective-permute-start(bf16[128,2176]{1,0:T(8,128)(2,1)S(1)} %get-tuple-element.48), channel_id=1, source_target_pairs={{0,4},{4,0},{8,12},{12,8},{1,5},{5,1},{9,13},{13,9},{2,6},{6,2},{1... | collective-permute-start | bytes 1671176 | tf_op jit(solution)/shard_map/ppermute | solution.py:298
  38.7 12.0 %collective-permute-start.6 = (bf16[48,2176]{1,0:T(8,128)(2,1)S(1)}, bf16[48,2176]{1,0:T(8,128)(2,1)S(1)}, u32[]{:S(2)}, u32[]{:S(2)}) collective-permute-start(bf16[48,2176]{1,0:T(8,128)(2,1)S(1)} %get-tuple-element.56), channel_id=1, source_target_pairs={{0,4},{4,0},{8,12},{12,8},{1,5},{5,1},{9,13},{13,9},{2,6},{6,2},{1... | collective-permute-start | bytes 626696 | tf_op jit(solution)/shard_map/ppermute | solution.py:307
  50.9 4.8 %collective-permute-start.9 = (bf16[48,3712]{1,0:T(8,128)(2,1)S(1)}, bf16[48,3712]{1,0:T(8,128)(2,1)S(1)}, u32[]{:S(2)}, u32[]{:S(2)}) collective-permute-start(bf16[48,3712]{1,0:T(8,128)(2,1)S(1)} %get-tuple-element.81), channel_id=1, source_target_pairs={{0,1},{1,0},{2,3},{3,2},{4,5},{5,4},{6,7},{7,6},{8,9},{9,8},{10,11... | collective-permute-start | bytes 1069064 | tf_op jit(solution)/shard_map/ppermute | solution.py:293
  51.0 4.8 %collective-permute-start.8 = (bf16[48,3712]{1,0:T(8,128)(2,1)S(1)}, bf16[48,3712]{1,0:T(8,128)(2,1)S(1)}, u32[]{:S(2)}, u32[]{:S(2)}) collective-permute-start(bf16[48,3712]{1,0:T(8,128)(2,1)S(1)} %get-tuple-element.82), channel_id=1, source_target_pairs={{0,1},{1,0},{2,3},{3,2},{4,5},{5,4},{6,7},{7,6},{8,9},{9,8},{10,11... | collective-permute-start | bytes 1069064 | tf_op jit(solution)/shard_map/ppermute | solution.py:293
  51.5 18.5 %collective-permute-start.7 = (bf16[32,7424]{1,0:T(8,128)(2,1)S(1)}, bf16[32,7424]{1,0:T(8,128)(2,1)S(1)}, u32[]{:S(2)}, u32[]{:S(2)}) collective-permute-start(bf16[32,7424]{1,0:T(8,128)(2,1)S(1)} %get-tuple-element.61), channel_id=1, source_target_pairs={{0,2},{1,3},{2,0},{3,1},{4,6},{5,7},{6,4},{7,5},{8,10},{9,11},{10,... | collective-permute-start | bytes 1425416 | tf_op jit(solution)/shard_map/ppermute | solution.py:305
  53.1 12.3 %collective-permute-start.11 = (bf16[48,2176]{1,0:T(8,128)(2,1)S(1)}, bf16[48,2176]{1,0:T(8,128)(2,1)S(1)}, u32[]{:S(2)}, u32[]{:S(2)}) collective-permute-start(bf16[48,2176]{1,0:T(8,128)(2,1)S(1)} %get-tuple-element.65), channel_id=1, source_target_pairs={{0,8},{4,12},{8,0},{12,4},{1,9},{5,13},{9,1},{13,5},{2,10},{6,14},... | collective-permute-start | bytes 626696 | tf_op jit(solution)/shard_map/ppermute | solution.py:313
  60.9 8.9 %collective-permute-start.10 = (bf16[48,2176]{1,0:T(8,128)(2,1)S(1)}, bf16[48,2176]{1,0:T(8,128)(2,1)S(1)}, u32[]{:S(2)}, u32[]{:S(2)}) collective-permute-start(bf16[48,2176]{1,0:T(8,128)(2,1)S(1)} %get-tuple-element.64), channel_id=1, source_target_pairs={{0,4},{4,0},{8,12},{12,8},{1,5},{5,1},{9,13},{13,9},{2,6},{6,2},{1... | collective-permute-start | bytes 626696 | tf_op jit(solution)/shard_map/ppermute | solution.py:307
  70.1 2.2 %collective-permute-start.13 = (bf16[32,3712]{1,0:T(8,128)(2,1)S(1)}, bf16[32,3712]{1,0:T(8,128)(2,1)S(1)}, u32[]{:S(2)}, u32[]{:S(2)}) collective-permute-start(bf16[32,3712]{1,0:T(8,128)(2,1)S(1)} %get-tuple-element.85), channel_id=1, source_target_pairs={{0,1},{1,0},{2,3},{3,2},{4,5},{5,4},{6,7},{7,6},{8,9},{9,8},{10,11... | collective-permute-start | bytes 712712 | tf_op jit(solution)/shard_map/ppermute | solution.py:293
  70.1 2.1 %collective-permute-start.12 = (bf16[32,3712]{1,0:T(8,128)(2,1)S(1)}, bf16[32,3712]{1,0:T(8,128)(2,1)S(1)}, u32[]{:S(2)}, u32[]{:S(2)}) collective-permute-start(bf16[32,3712]{1,0:T(8,128)(2,1)S(1)} %get-tuple-element.86), channel_id=1, source_target_pairs={{0,1},{1,0},{2,3},{3,2},{4,5},{5,4},{6,7},{7,6},{8,9},{9,8},{10,11... | collective-permute-start | bytes 712712 | tf_op jit(solution)/shard_map/ppermute | solution.py:293
  70.6 25.0 %copy-start = (bf16[8,64,2048]{2,1,0:T(8,128)(2,1)S(1)}, bf16[8,64,2048]{2,1,0:T(8,128)(2,1)}, u32[]{:S(2)}) copy-start(bf16[8,64,2048]{2,1,0:T(8,128)(2,1)} %param.8) | copy-start | bytes 6291460
  70.6 12.6 %collective-permute-start.15 = (bf16[48,2176]{1,0:T(8,128)(2,1)S(1)}, bf16[48,2176]{1,0:T(8,128)(2,1)S(1)}, u32[]{:S(2)}, u32[]{:S(2)}) collective-permute-start(bf16[48,2176]{1,0:T(8,128)(2,1)S(1)} %get-tuple-element.74), channel_id=1, source_target_pairs={{0,8},{4,12},{8,0},{12,4},{1,9},{5,13},{9,1},{13,5},{2,10},{6,14},... | collective-permute-start | bytes 626696 | tf_op jit(solution)/shard_map/ppermute | solution.py:313
  77.6 8.5 %collective-permute-start.14 = (bf16[32,2176]{1,0:T(8,128)(2,1)S(1)}, bf16[32,2176]{1,0:T(8,128)(2,1)S(1)}, u32[]{:S(2)}, u32[]{:S(2)}) collective-permute-start(bf16[32,2176]{1,0:T(8,128)(2,1)S(1)} %get-tuple-element.72), channel_id=1, source_target_pairs={{0,4},{4,0},{8,12},{12,8},{1,5},{5,1},{9,13},{13,9},{2,6},{6,2},{1... | collective-permute-start | bytes 417800 | tf_op jit(solution)/shard_map/ppermute | solution.py:307
  86.2 9.4 %collective-permute-start.16 = (bf16[32,2176]{1,0:T(8,128)(2,1)S(1)}, bf16[32,2176]{1,0:T(8,128)(2,1)S(1)}, u32[]{:S(2)}, u32[]{:S(2)}) collective-permute-start(bf16[32,2176]{1,0:T(8,128)(2,1)S(1)} %get-tuple-element.80), channel_id=1, source_target_pairs={{0,8},{4,12},{8,0},{12,4},{1,9},{5,13},{9,1},{13,5},{2,10},{6,14},... | collective-permute-start | bytes 417800 | tf_op jit(solution)/shard_map/ppermute | solution.py:313

commit v12 on v7

--- a/solution.py
+++ b/solution.py
@@ -12,7 +12,7 @@
 DEPTH = 1024
 TURN = 15
 PIECES = (32, 32, 32, 32)
-CUTS = 2
+CUTS = (2, 2, 4, 4)
 MIB = 1 << 20
 
 
@@ -102,8 +102,8 @@
         keep_ref[at, cols] = jnp.where(keep_first, first, second)
 
 
-def product_kernel(adapters, units, at, _, own_ref, other_ref, direct_ref, *refs):
-    passed_refs, refs = refs[:CUTS], refs[CUTS:]
+def product_kernel(adapters, units, at, cuts, _, own_ref, other_ref, direct_ref, *refs):
+    passed_refs, refs = refs[:cuts], refs[cuts:]
     *panel_refs, spread_ref, send_ref, keep_ref = refs
     rows = direct_ref.shape[0]
     width = send_ref.shape[1] - LANES
@@ -236,9 +236,9 @@
 
     def product(step, passed, token):
         return pl.pallas_call(
-            functools.partial(product_kernel, adapters, units, starts[step]),
+            functools.partial(product_kernel, adapters, units, starts[step], len(passed)),
             out_shape=[struct(2 * counts[step], payload)] * 2,
-            in_specs=[in_vmem()] * (4 + CUTS + len(both)),
+            in_specs=[in_vmem()] * (4 + len(passed) + len(both)),
             out_specs=[in_vmem()] * 2,
             compiler_params=params(4),
             cost_estimate=quick,
@@ -256,9 +256,9 @@
             name="add",
         )(keep, got)
 
-    def over_core(part):
+    def over_core(part, cuts):
         tiles = room // LANES
-        ends = [tiles * cut // CUTS * LANES for cut in range(CUTS + 1)]
+        ends = [tiles * cut // cuts * LANES for cut in range(cuts + 1)]
         return [
             lax.ppermute(part[:, at:to], "req", beside) for at, to in zip(ends, ends[1:])
         ]
@@ -275,7 +275,7 @@
         return send
 
     for step in range(steps):
-        passed = over_core(direct[step])
+        passed = over_core(direct[step], CUTS[step])
         if step + 1 < steps:
             direct.append(lax.ppermute(pieces[step + 1], "req", across))
         send, keep = product(step, passed, token)

time: 79 us -> 81 us (1.025)
  waiting for transfers between devices: 19.3 us -> 23.8 us
  starting transfers between devices: 23.4 us -> 21 us
    ppermute x8 -> x12, waiting for transfers between devices: 0.02 us -> 3.64 us  [over_core(): lax.ppermute(part[:, at:to], 'req', beside)]
    ppermute x4, starting transfers between devices: 7.26 us -> 4.38 us  [paired(): got = lax.ppermute(send, 'tensor', next_z)]
    ppermute x4, waiting for transfers between devices: 8.35 us -> 9.36 us  [paired(): got = lax.ppermute(send, 'tensor', next_z)]
    ppermute x3, waiting for transfers between devices: 3.59 us -> 2.71 us  [paired(): direct.append(lax.ppermute(pieces[step + 1], 'req', across))]
    ppermute x8 -> x12, starting transfers between devices: 2.28 us -> 3.07 us  [over_core(): lax.ppermute(part[:, at:to], 'req', beside)]
  transfers between devices with their start and end apart: 21 -> 25, of which waited for: 8 -> 11; matrix products, arithmetic and copies ran while one was open for 0% -> 0% of each run, Pallas kernels for 41% -> 40%
where the time goes in v12:
time: 81 us; the launch traced here: 80.9 us
  Pallas kernels  35.8 us (44%)
  waiting for transfers between devices  23.8 us (29%)
  starting transfers between devices  21 us (26%)
    pallas_call x4, Pallas kernels, product(): pl.pallas_call(functools.partial(product_kernel, adapters, units, starts[...  20.5 us
    pallas_call x1, Pallas kernels, paired(): pl.pallas_call(load_kernel, out_shape=[jax.ShapeDtypeStruct((8, LANES), j...  11.9 us
    ppermute x4, waiting for transfers between devices, paired(): got = lax.ppermute(send, 'tensor', next_z)  9.36 us
    ppermute x1, waiting for transfers between devices, paired(): gots.append(lax.ppermute(add_part(steps - 1), 'tensor', far_z))  7 us
    ppermute x3, starting transfers between devices, paired(): gots.append(lax.ppermute(send, 'tensor', far_z))  5.89 us
    ppermute x4, starting transfers between devices, paired(): got = lax.ppermute(send, 'tensor', next_z)  4.38 us
    ppermute x12, waiting for transfers between devices, over_core(): lax.ppermute(part[:, at:to], 'req', beside)  3.64 us
    ppermute x3, starting transfers between devices, paired(): direct.append(lax.ppermute(pieces[step + 1], 'req', across))  3.52 us
  transfers between devices with their start and end apart: 25, of which 11 were waited for; matrix products, arithmetic and copies ran while one was open for 0% of the time, Pallas kernels for 40%

profile of v12, /device:TPU:0, one launch (start us, length us, event | category | flops | bytes accessed | tf_op | source)
XLA Modules:
  0.0 80.9 jit_solution(13807434661553491557)
XLA Ops:
  0.0 1.8 %turn.1 = (bf16[128,7424]{1,0:T(8,128)(2,1)S(1)}, bf16[32,7424]{1,0:T(8,128)(2,1)S(1)}, bf16[32,7424]{1,0:T(8,128)(2,1)S(1)}, bf16[32,7424]{1,0:T(8,128)(2,1)S(1)}, bf16[32,7424]{1,0:T(8,128)(2,1)S(1)}) custom-call(bf16[7392,128]{1,0:T(8,128)(2,1)} %bitcast.8, s32[1,128]{1,0:T(1,128)} %bitcast.9), custom_call_target="tpu_custom_call" | custom-call | tf_op jit(solution)/shard_map/turn/pallas_call | solution.py:197
  2.3 2.6 %collective-permute-start.1 = (bf16[32,7424]{1,0:T(8,128)(2,1)S(1)}, bf16[32,7424]{1,0:T(8,128)(2,1)S(1)}, u32[]{:S(2)}, u32[]{:S(2)}) collective-permute-start(bf16[32,7424]{1,0:T(8,128)(2,1)S(1)} %get-tuple-element.54), channel_id=1, source_target_pairs={{0,2},{1,3},{2,0},{3,1},{4,6},{5,7},{6,4},{7,5},{8,10},{9,11},{10,... | collective-permute-start | bytes 1425416 | tf_op jit(solution)/shard_map/ppermute | solution.py:216
  5.0 11.9 %load.1 = (f32[8,128]{1,0:T(8,128)S(1)}, bf16[7424,512]{1,0:T(8,128)(2,1)S(1)}, bf16[7424,512]{1,0:T(8,128)(2,1)S(1)}, bf16[7424,512]{1,0:T(8,128)(2,1)S(1)}, bf...) custom-call(bf16[7392,2048]{1,0:T(8,128)(2,1)} %w_hbm.1, bf16[512,7392]{1,0:T(8,128)(2,1)} %bitcast.7), custom_call_target="tpu_custom_call" | custom-call | flops 1 | bytes 1 | tf_op jit(solution)/shard_map/load/pallas_call | solution.py:220
  17.5 1.9 %collective-permute-start = (bf16[32,7424]{1,0:T(8,128)(2,1)S(1)}, bf16[32,7424]{1,0:T(8,128)(2,1)S(1)}, u32[]{:S(2)}, u32[]{:S(2)}) collective-permute-start(bf16[32,7424]{1,0:T(8,128)(2,1)S(1)} %get-tuple-element.53), channel_id=1, source_target_pairs={{0,2},{1,3},{2,0},{3,1},{4,6},{5,7},{6,4},{7,5},{8,10},{9,11},{10,... | collective-permute-start | bytes 1425416 | tf_op jit(solution)/shard_map/ppermute | solution.py:280
  19.5 5.1 %product.4 = (bf16[64,2176]{1,0:T(8,128)(2,1)S(1)}, bf16[64,2176]{1,0:T(8,128)(2,1)S(1)}) custom-call(f32[8,128]{1,0:T(8,128)S(1)} %get-tuple-element.56._, bf16[128,7424]{1,0:T(8,128)(2,1)S(1)} %get-tuple-element.57.own_ref, bf16[128,7424]{1,0:T(8,128)(2,1)S(1)} %collective-permute-done.2.other_ref, bf16[32,7424]{1,0:T(8,128)(2,1)S(1)} %collective-permute-done.1.direct_ref, ...), custom_call_target="tpu_custom_call" | custom-call | flops 1 | bytes 1 | tf_op jit(solution)/shard_map/product/pallas_call | solution.py:238
  24.5 2.3 %collective-permute-done.3.direct_ref = bf16[32,7424]{1,0:T(8,128)(2,1)S(1)} collective-permute-done((bf16[32,7424]{1,0:T(8,128)(2,1)S(1)}, bf16[32,7424]{1,0:T(8,128)(2,1)S(1)}, u32[]{:S(2)}, u32[]{:S(2)}) %collective-permute-start.3) | collective-permute-done | bytes 475168 | tf_op jit(solution)/shard_map/ppermute | solution.py:280
  26.8 2.0 %collective-permute-start.8 = (bf16[64,2176]{1,0:T(8,128)(2,1)S(1)}, bf16[64,2176]{1,0:T(8,128)(2,1)S(1)}, u32[]{:S(2)}, u32[]{:S(2)}) collective-permute-start(bf16[64,2176]{1,0:T(8,128)(2,1)S(1)} %get-tuple-element.69), channel_id=1, source_target_pairs={{0,4},{4,0},{8,12},{12,8},{1,5},{5,1},{9,13},{13,9},{2,6},{6,2},{1... | collective-permute-start | bytes 835592 | tf_op jit(solution)/shard_map/ppermute | solution.py:284
  29.5 1.5 %collective-permute-start.9 = (bf16[32,7424]{1,0:T(8,128)(2,1)S(1)}, bf16[32,7424]{1,0:T(8,128)(2,1)S(1)}, u32[]{:S(2)}, u32[]{:S(2)}) collective-permute-start(bf16[32,7424]{1,0:T(8,128)(2,1)S(1)} %get-tuple-element.75), channel_id=1, source_target_pairs={{0,2},{1,3},{2,0},{3,1},{4,6},{5,7},{6,4},{7,5},{8,10},{9,11},{10,... | collective-permute-start | bytes 1425416 | tf_op jit(solution)/shard_map/ppermute | solution.py:280
  31.0 5.1 %product.5 = (bf16[64,2176]{1,0:T(8,128)(2,1)S(1)}, bf16[64,2176]{1,0:T(8,128)(2,1)S(1)}) custom-call(f32[8,128]{1,0:T(8,128)S(1)} %get-tuple-element.56._, bf16[128,7424]{1,0:T(8,128)(2,1)S(1)} %get-tuple-element.57.own_ref, bf16[128,7424]{1,0:T(8,128)(2,1)S(1)} %collective-permute-done.2.other_ref, bf16[32,7424]{1,0:T(8,128)(2,1)S(1)} %collective-permute-done.3.direct_ref, ...), custom_call_target="tpu_custom_call" | custom-call | flops 1 | bytes 1 | tf_op jit(solution)/shard_map/product/pallas_call | solution.py:238
  37.1 3.1 %collective-permute-start.15 = (bf16[32,2176]{1,0:T(8,128)(2,1)S(1)}, bf16[32,2176]{1,0:T(8,128)(2,1)S(1)}, u32[]{:S(2)}, u32[]{:S(2)}) collective-permute-start(bf16[32,2176]{1,0:T(8,128)(2,1)S(1)} %get-tuple-element.80), channel_id=1, source_target_pairs={{0,8},{4,12},{8,0},{12,4},{1,9},{5,13},{9,1},{13,5},{2,10},{6,14},... | collective-permute-start | bytes 417800 | tf_op jit(solution)/shard_map/ppermute | solution.py:295
  40.8 0.8 collective-permute-done.12.refs_2_
  42.1 0.8 %collective-permute-done.13.refs_3_ = bf16[32,1920]{1,0:T(8,128)(2,1)S(1)} collective-permute-done((bf16[32,1920]{1,0:T(8,128)(2,1)S(1)}, bf16[32,1920]{1,0:T(8,128)(2,1)S(1)}, u32[]{:S(2)}, u32[]{:S(2)}) %collective-permute-start.13) | collective-permute-done | bytes 122912 | tf_op jit(solution)/shard_map/ppermute | solution.py:263
  43.1 5.3 %product.6 = (bf16[64,2176]{1,0:T(8,128)(2,1)S(1)}, bf16[64,2176]{1,0:T(8,128)(2,1)S(1)}) custom-call(f32[8,128]{1,0:T(8,128)S(1)} %get-tuple-element.56._, bf16[128,7424]{1,0:T(8,128)(2,1)S(1)} %get-tuple-element.57.own_ref, bf16[128,7424]{1,0:T(8,128)(2,1)S(1)} %collective-permute-done.2.other_ref, bf16[32,7424]{1,0:T(8,128)(2,1)S(1)} %collective-permute-done.direct_ref, ...), custom_call_target="tpu_custom_call" | custom-call | flops 1 | bytes 1 | tf_op jit(solution)/shard_map/product/pallas_call | solution.py:238
  48.4 1.6 %collective-permute-start.20 = (bf16[64,2176]{1,0:T(8,128)(2,1)S(1)}, bf16[64,2176]{1,0:T(8,128)(2,1)S(1)}, u32[]{:S(2)}, u32[]{:S(2)}) collective-permute-start(bf16[64,2176]{1,0:T(8,128)(2,1)S(1)} %get-tuple-element.89), channel_id=1, source_target_pairs={{0,4},{4,0},{8,12},{12,8},{1,5},{5,1},{9,13},{13,9},{2,6},{6,2},{1... | collective-permute-start | bytes 835592 | tf_op jit(solution)/shard_map/ppermute | solution.py:284
  51.3 0.6 collective-permute-done.18.refs_2_
  52.1 1.2 %collective-permute-done.16.refs_0_ = bf16[32,1792]{1,0:T(8,128)(2,1)S(1)} collective-permute-done((bf16[32,1792]{1,0:T(8,128)(2,1)S(1)}, bf16[32,1792]{1,0:T(8,128)(2,1)S(1)}, u32[]{:S(2)}, u32[]{:S(2)}) %collective-permute-start.16) | collective-permute-done | bytes 114720 | tf_op jit(solution)/shard_map/ppermute | solution.py:263
  53.3 5.1 %product.7 = (bf16[64,2176]{1,0:T(8,128)(2,1)S(1)}, bf16[64,2176]{1,0:T(8,128)(2,1)S(1)}) custom-call(f32[8,128]{1,0:T(8,128)S(1)} %get-tuple-element.56._, bf16[128,7424]{1,0:T(8,128)(2,1)S(1)} %get-tuple-element.57.own_ref, bf16[128,7424]{1,0:T(8,128)(2,1)S(1)} %collective-permute-done.2.other_ref, bf16[32,7424]{1,0:T(8,128)(2,1)S(1)} %collective-permute-done.9.direct_ref, ...), custom_call_target="tpu_custom_call" | custom-call | flops 1 | bytes 1 | tf_op jit(solution)/shard_map/product/pallas_call | solution.py:238
  58.4 1.1 %collective-permute-done.21.refs_5_ = bf16[32,2176]{1,0:T(8,128)(2,1)S(1)} collective-permute-done((bf16[32,2176]{1,0:T(8,128)(2,1)S(1)}, bf16[32,2176]{1,0:T(8,128)(2,1)S(1)}, u32[]{:S(2)}, u32[]{:S(2)}) %collective-permute-start.21) | collective-permute-done | bytes 139296 | tf_op jit(solution)/shard_map/ppermute | solution.py:295
  59.4 0.9 %collective-permute-done.20.second_ref = bf16[64,2176]{1,0:T(8,128)(2,1)S(1)} collective-permute-done((bf16[64,2176]{1,0:T(8,128)(2,1)S(1)}, bf16[64,2176]{1,0:T(8,128)(2,1)S(1)}, u32[]{:S(2)}, u32[]{:S(2)}) %collective-permute-start.20) | collective-permute-done | bytes 278560 | tf_op jit(solution)/shard_map/ppermute | solution.py:284
  60.6 2.4 %collective-permute-start.23 = (bf16[32,2176]{1,0:T(8,128)(2,1)S(1)}, bf16[32,2176]{1,0:T(8,128)(2,1)S(1)}, u32[]{:S(2)}, u32[]{:S(2)}) collective-permute-start(bf16[32,2176]{1,0:T(8,128)(2,1)S(1)} %get-tuple-element.99), channel_id=1, source_target_pairs={{0,8},{4,12},{8,0},{12,4},{1,9},{5,13},{9,1},{13,5},{2,10},{6,14},... | collective-permute-start | bytes 417800 | tf_op jit(solution)/shard_map/ppermute | solution.py:295
  63.0 8.5 %collective-permute-done.22.second_ref = bf16[64,2176]{1,0:T(8,128)(2,1)S(1)} collective-permute-done((bf16[64,2176]{1,0:T(8,128)(2,1)S(1)}, bf16[64,2176]{1,0:T(8,128)(2,1)S(1)}, u32[]{:S(2)}, u32[]{:S(2)}) %collective-permute-start.22) | collective-permute-done | bytes 278560 | tf_op jit(solution)/shard_map/ppermute | solution.py:288
  71.5 1.0 %collective-permute-start.24 = (bf16[32,2176]{1,0:T(8,128)(2,1)S(1)}, bf16[32,2176]{1,0:T(8,128)(2,1)S(1)}, u32[]{:S(2)}, u32[]{:S(2)}) collective-permute-start(bf16[32,2176]{1,0:T(8,128)(2,1)S(1)} %get-tuple-element.100), channel_id=1, source_target_pairs={{0,8},{4,12},{8,0},{12,4},{1,9},{5,13},{9,1},{13,5},{2,10},{6,14},... | collective-permute-start | bytes 417800 | tf_op jit(solution)/shard_map/ppermute | solution.py:297
  72.6 7.0 %collective-permute-done.24.refs_7_ = bf16[32,2176]{1,0:T(8,128)(2,1)S(1)} collective-permute-done((bf16[32,2176]{1,0:T(8,128)(2,1)S(1)}, bf16[32,2176]{1,0:T(8,128)(2,1)S(1)}, u32[]{:S(2)}, u32[]{:S(2)}) %collective-permute-start.24) | collective-permute-done | bytes 139296 | tf_op jit(solution)/shard_map/ppermute | solution.py:297
  79.6 1.3 %last.1 = bf16[128,2048]{1,0:T(8,128)(2,1)} custom-call(bf16[512,2048]{1,0:T(8,128)(2,1)S(1)} %bitcast.6, bf16[32,2176]{1,0:T(8,128)(2,1)S(1)} %get-tuple-element.74.refs_0_, bf16[32,2176]{1,0:T(8,128)(2,1)S(1)} %get-tuple-element.85.refs_1_, bf16[32,2176]{1,0:T(8,128)(2,1)S(1)} %get-tuple-element.93.refs_2_, ...), custom_call_target="tpu_custom_call" | custom-call | tf_op jit(solution)/shard_map/last/pallas_call | solution.py:299
  (45 shorter events, 5.9 us)
Async XLA Ops:
  1.8 17.6 %collective-permute-start.2 = (bf16[128,7424]{1,0:T(8,128)(2,1)S(1)}, bf16[128,7424]{1,0:T(8,128)(2,1)S(1)}, u32[]{:S(2)}, u32[]{:S(2)}) collective-permute-start(bf16[128,7424]{1,0:T(8,128)(2,1)S(1)} %get-tuple-element.57.own_ref), channel_id=1, source_target_pairs={{0,1},{1,0},{2,3},{3,2},{4,5},{5,4},{6,7},{7,6},{8,9},{9,8},{10,11... | collective-permute-start | bytes 5701640 | tf_op jit(solution)/shard_map/ppermute | solution.py:217
  2.3 14.5 %collective-permute-start.1 = (bf16[32,7424]{1,0:T(8,128)(2,1)S(1)}, bf16[32,7424]{1,0:T(8,128)(2,1)S(1)}, u32[]{:S(2)}, u32[]{:S(2)}) collective-permute-start(bf16[32,7424]{1,0:T(8,128)(2,1)S(1)} %get-tuple-element.54), channel_id=1, source_target_pairs={{0,2},{1,3},{2,0},{3,1},{4,6},{5,7},{6,4},{7,5},{8,10},{9,11},{10,... | collective-permute-start | bytes 1425416 | tf_op jit(solution)/shard_map/ppermute | solution.py:216
  4.9 21.9 %collective-permute-start.3 = (bf16[32,7424]{1,0:T(8,128)(2,1)S(1)}, bf16[32,7424]{1,0:T(8,128)(2,1)S(1)}, u32[]{:S(2)}, u32[]{:S(2)}) collective-permute-start(bf16[32,7424]{1,0:T(8,128)(2,1)S(1)} %get-tuple-element.58), channel_id=1, source_target_pairs={{0,2},{1,3},{2,0},{3,1},{4,6},{5,7},{6,4},{7,5},{8,10},{9,11},{10,... | collective-permute-start | bytes 1425416 | tf_op jit(solution)/shard_map/ppermute | solution.py:280
  16.9 2.5 %collective-permute-start.5 = (bf16[32,3712]{1,0:T(8,128)(2,1)S(1)}, bf16[32,3712]{1,0:T(8,128)(2,1)S(1)}, u32[]{:S(2)}, u32[]{:S(2)}) collective-permute-start(bf16[32,3712]{1,0:T(8,128)(2,1)S(1)} %get-tuple-element.111), channel_id=1, source_target_pairs={{0,1},{1,0},{2,3},{3,2},{4,5},{5,4},{6,7},{7,6},{8,9},{9,8},{10,11... | collective-permute-start | bytes 712712 | tf_op jit(solution)/shard_map/ppermute | solution.py:263
  17.1 2.4 %collective-permute-start.4 = (bf16[32,3712]{1,0:T(8,128)(2,1)S(1)}, bf16[32,3712]{1,0:T(8,128)(2,1)S(1)}, u32[]{:S(2)}, u32[]{:S(2)}) collective-permute-start(bf16[32,3712]{1,0:T(8,128)(2,1)S(1)} %get-tuple-element.112), channel_id=1, source_target_pairs={{0,1},{1,0},{2,3},{3,2},{4,5},{5,4},{6,7},{7,6},{8,9},{9,8},{10,11... | collective-permute-start | bytes 712712 | tf_op jit(solution)/shard_map/ppermute | solution.py:263
  17.5 19.5 %collective-permute-start = (bf16[32,7424]{1,0:T(8,128)(2,1)S(1)}, bf16[32,7424]{1,0:T(8,128)(2,1)S(1)}, u32[]{:S(2)}, u32[]{:S(2)}) collective-permute-start(bf16[32,7424]{1,0:T(8,128)(2,1)S(1)} %get-tuple-element.53), channel_id=1, source_target_pairs={{0,2},{1,3},{2,0},{3,1},{4,6},{5,7},{6,4},{7,5},{8,10},{9,11},{10,... | collective-permute-start | bytes 1425416 | tf_op jit(solution)/shard_map/ppermute | solution.py:280
  26.8 10.2 %collective-permute-start.8 = (bf16[64,2176]{1,0:T(8,128)(2,1)S(1)}, bf16[64,2176]{1,0:T(8,128)(2,1)S(1)}, u32[]{:S(2)}, u32[]{:S(2)}) collective-permute-start(bf16[64,2176]{1,0:T(8,128)(2,1)S(1)} %get-tuple-element.69), channel_id=1, source_target_pairs={{0,4},{4,0},{8,12},{12,8},{1,5},{5,1},{9,13},{13,9},{2,6},{6,2},{1... | collective-permute-start | bytes 835592 | tf_op jit(solution)/shard_map/ppermute | solution.py:284
  28.9 2.1 %collective-permute-start.7 = (bf16[32,3712]{1,0:T(8,128)(2,1)S(1)}, bf16[32,3712]{1,0:T(8,128)(2,1)S(1)}, u32[]{:S(2)}, u32[]{:S(2)}) collective-permute-start(bf16[32,3712]{1,0:T(8,128)(2,1)S(1)} %get-tuple-element.109), channel_id=1, source_target_pairs={{0,1},{1,0},{2,3},{3,2},{4,5},{5,4},{6,7},{7,6},{8,9},{9,8},{10,11... | collective-permute-start | bytes 712712 | tf_op jit(solution)/shard_map/ppermute | solution.py:263
  29.0 2.0 %collective-permute-start.6 = (bf16[32,3712]{1,0:T(8,128)(2,1)S(1)}, bf16[32,3712]{1,0:T(8,128)(2,1)S(1)}, u32[]{:S(2)}, u32[]{:S(2)}) collective-permute-start(bf16[32,3712]{1,0:T(8,128)(2,1)S(1)} %get-tuple-element.110), channel_id=1, source_target_pairs={{0,1},{1,0},{2,3},{3,2},{4,5},{5,4},{6,7},{7,6},{8,9},{9,8},{10,11... | collective-permute-start | bytes 712712 | tf_op jit(solution)/shard_map/ppermute | solution.py:263
  29.5 20.6 %collective-permute-start.9 = (bf16[32,7424]{1,0:T(8,128)(2,1)S(1)}, bf16[32,7424]{1,0:T(8,128)(2,1)S(1)}, u32[]{:S(2)}, u32[]{:S(2)}) collective-permute-start(bf16[32,7424]{1,0:T(8,128)(2,1)S(1)} %get-tuple-element.75), channel_id=1, source_target_pairs={{0,2},{1,3},{2,0},{3,1},{4,6},{5,7},{6,4},{7,5},{8,10},{9,11},{10,... | collective-permute-start | bytes 1425416 | tf_op jit(solution)/shard_map/ppermute | solution.py:280
  36.0 14.0 %collective-permute-start.14 = (bf16[64,2176]{1,0:T(8,128)(2,1)S(1)}, bf16[64,2176]{1,0:T(8,128)(2,1)S(1)}, u32[]{:S(2)}, u32[]{:S(2)}) collective-permute-start(bf16[64,2176]{1,0:T(8,128)(2,1)S(1)} %get-tuple-element.79), channel_id=1, source_target_pairs={{0,4},{4,0},{8,12},{12,8},{1,5},{5,1},{9,13},{13,9},{2,6},{6,2},{1... | collective-permute-start | bytes 835592 | tf_op jit(solution)/shard_map/ppermute | solution.py:284
  37.1 13.0 %collective-permute-start.15 = (bf16[32,2176]{1,0:T(8,128)(2,1)S(1)}, bf16[32,2176]{1,0:T(8,128)(2,1)S(1)}, u32[]{:S(2)}, u32[]{:S(2)}) collective-permute-start(bf16[32,2176]{1,0:T(8,128)(2,1)S(1)} %get-tuple-element.80), channel_id=1, source_target_pairs={{0,8},{4,12},{8,0},{12,4},{1,9},{5,13},{9,1},{13,5},{2,10},{6,14},... | collective-permute-start | bytes 417800 | tf_op jit(solution)/shard_map/ppermute | solution.py:295
  40.2 1.4 %collective-permute-start.12 = (bf16[32,1792]{1,0:T(8,128)(2,1)S(1)}, bf16[32,1792]{1,0:T(8,128)(2,1)S(1)}, u32[]{:S(2)}, u32[]{:S(2)}) collective-permute-start(bf16[32,1792]{1,0:T(8,128)(2,1)S(1)} %get-tuple-element.107), channel_id=1, source_target_pairs={{0,1},{1,0},{2,3},{3,2},{4,5},{5,4},{6,7},{7,6},{8,9},{9,8},{10,11... | collective-permute-start | bytes 344072 | tf_op jit(solution)/shard_map/ppermute | solution.py:263
  40.3 1.5 %collective-permute-start.10 = (bf16[32,1792]{1,0:T(8,128)(2,1)S(1)}, bf16[32,1792]{1,0:T(8,128)(2,1)S(1)}, u32[]{:S(2)}, u32[]{:S(2)}) collective-permute-start(bf16[32,1792]{1,0:T(8,128)(2,1)S(1)} %get-tuple-element.108), channel_id=1, source_target_pairs={{0,1},{1,0},{2,3},{3,2},{4,5},{5,4},{6,7},{7,6},{8,9},{9,8},{10,11... | collective-permute-start | bytes 344072 | tf_op jit(solution)/shard_map/ppermute | solution.py:263
  41.6 1.3 %collective-permute-start.13 = (bf16[32,1920]{1,0:T(8,128)(2,1)S(1)}, bf16[32,1920]{1,0:T(8,128)(2,1)S(1)}, u32[]{:S(2)}, u32[]{:S(2)}) collective-permute-start(bf16[32,1920]{1,0:T(8,128)(2,1)S(1)} %get-tuple-element.105), channel_id=1, source_target_pairs={{0,1},{1,0},{2,3},{3,2},{4,5},{5,4},{6,7},{7,6},{8,9},{9,8},{10,11... | collective-permute-start | bytes 368648 | tf_op jit(solution)/shard_map/ppermute | solution.py:263
  41.8 1.3 %collective-permute-start.11 = (bf16[32,1920]{1,0:T(8,128)(2,1)S(1)}, bf16[32,1920]{1,0:T(8,128)(2,1)S(1)}, u32[]{:S(2)}, u32[]{:S(2)}) collective-permute-start(bf16[32,1920]{1,0:T(8,128)(2,1)S(1)} %get-tuple-element.106), channel_id=1, source_target_pairs={{0,1},{1,0},{2,3},{3,2},{4,5},{5,4},{6,7},{7,6},{8,9},{9,8},{10,11... | collective-permute-start | bytes 368648 | tf_op jit(solution)/shard_map/ppermute | solution.py:263
  48.4 12.0 %collective-permute-start.20 = (bf16[64,2176]{1,0:T(8,128)(2,1)S(1)}, bf16[64,2176]{1,0:T(8,128)(2,1)S(1)}, u32[]{:S(2)}, u32[]{:S(2)}) collective-permute-start(bf16[64,2176]{1,0:T(8,128)(2,1)S(1)} %get-tuple-element.89), channel_id=1, source_target_pairs={{0,4},{4,0},{8,12},{12,8},{1,5},{5,1},{9,13},{13,9},{2,6},{6,2},{1... | collective-permute-start | bytes 835592 | tf_op jit(solution)/shard_map/ppermute | solution.py:284
  50.1 9.3 %collective-permute-start.21 = (bf16[32,2176]{1,0:T(8,128)(2,1)S(1)}, bf16[32,2176]{1,0:T(8,128)(2,1)S(1)}, u32[]{:S(2)}, u32[]{:S(2)}) collective-permute-start(bf16[32,2176]{1,0:T(8,128)(2,1)S(1)} %get-tuple-element.90), channel_id=1, source_target_pairs={{0,8},{4,12},{8,0},{12,4},{1,9},{5,13},{9,1},{13,5},{2,10},{6,14},... | collective-permute-start | bytes 417800 | tf_op jit(solution)/shard_map/ppermute | solution.py:295
  50.6 1.4 %collective-permute-start.18 = (bf16[32,1792]{1,0:T(8,128)(2,1)S(1)}, bf16[32,1792]{1,0:T(8,128)(2,1)S(1)}, u32[]{:S(2)}, u32[]{:S(2)}) collective-permute-start(bf16[32,1792]{1,0:T(8,128)(2,1)S(1)} %get-tuple-element.103), channel_id=1, source_target_pairs={{0,1},{1,0},{2,3},{3,2},{4,5},{5,4},{6,7},{7,6},{8,9},{9,8},{10,11... | collective-permute-start | bytes 344072 | tf_op jit(solution)/shard_map/ppermute | solution.py:263
  50.7 2.6 %collective-permute-start.19 = (bf16[32,1920]{1,0:T(8,128)(2,1)S(1)}, bf16[32,1920]{1,0:T(8,128)(2,1)S(1)}, u32[]{:S(2)}, u32[]{:S(2)}) collective-permute-start(bf16[32,1920]{1,0:T(8,128)(2,1)S(1)} %get-tuple-element.101), channel_id=1, source_target_pairs={{0,1},{1,0},{2,3},{3,2},{4,5},{5,4},{6,7},{7,6},{8,9},{9,8},{10,11... | collective-permute-start | bytes 368648 | tf_op jit(solution)/shard_map/ppermute | solution.py:263
  51.2 2.1 %collective-permute-start.17 = (bf16[32,1920]{1,0:T(8,128)(2,1)S(1)}, bf16[32,1920]{1,0:T(8,128)(2,1)S(1)}, u32[]{:S(2)}, u32[]{:S(2)}) collective-permute-start(bf16[32,1920]{1,0:T(8,128)(2,1)S(1)} %get-tuple-element.102), channel_id=1, source_target_pairs={{0,1},{1,0},{2,3},{3,2},{4,5},{5,4},{6,7},{7,6},{8,9},{9,8},{10,11... | collective-permute-start | bytes 368648 | tf_op jit(solution)/shard_map/ppermute | solution.py:263
  60.4 11.1 %collective-permute-start.22 = (bf16[64,2176]{1,0:T(8,128)(2,1)S(1)}, bf16[64,2176]{1,0:T(8,128)(2,1)S(1)}, u32[]{:S(2)}, u32[]{:S(2)}) collective-permute-start(bf16[64,2176]{1,0:T(8,128)(2,1)S(1)} %get-tuple-element.95), channel_id=1, source_target_pairs={{0,4},{4,0},{8,12},{12,8},{1,5},{5,1},{9,13},{13,9},{2,6},{6,2},{1... | collective-permute-start | bytes 835592 | tf_op jit(solution)/shard_map/ppermute | solution.py:288
  60.6 12.0 %collective-permute-start.23 = (bf16[32,2176]{1,0:T(8,128)(2,1)S(1)}, bf16[32,2176]{1,0:T(8,128)(2,1)S(1)}, u32[]{:S(2)}, u32[]{:S(2)}) collective-permute-start(bf16[32,2176]{1,0:T(8,128)(2,1)S(1)} %get-tuple-element.99), channel_id=1, source_target_pairs={{0,8},{4,12},{8,0},{12,4},{1,9},{5,13},{9,1},{13,5},{2,10},{6,14},... | collective-permute-start | bytes 417800 | tf_op jit(solution)/shard_map/ppermute | solution.py:295
  71.5 8.0 %collective-permute-start.24 = (bf16[32,2176]{1,0:T(8,128)(2,1)S(1)}, bf16[32,2176]{1,0:T(8,128)(2,1)S(1)}, u32[]{:S(2)}, u32[]{:S(2)}) collective-permute-start(bf16[32,2176]{1,0:T(8,128)(2,1)S(1)} %get-tuple-element.100), channel_id=1, source_target_pairs={{0,8},{4,12},{8,0},{12,4},{1,9},{5,13},{9,1},{13,5},{2,10},{6,14},... | collective-permute-start | bytes 417800 | tf_op jit(solution)/shard_map/ppermute | solution.py:297
  (2 other events, 28.9 us)

commit v13 on v7

--- a/solution.py
+++ b/solution.py
@@ -13,6 +13,7 @@
 TURN = 15
 PIECES = (32, 32, 32, 32)
 CUTS = 2
+FULL = 128
 MIB = 1 << 20
 
 
@@ -90,19 +91,16 @@
         copy.wait()
 
 
-def part_rows(value, cols, send_ref, keep_ref):
-    rows = send_ref.shape[0] // 2
+def part_rows(rows, value, cols, send_ref, keep_ref):
     keep_first = lax.rem(lax.axis_index("req"), 2) == lax.rem(lax.axis_index("tensor"), 2)
     value = value.astype(send_ref.dtype)
-    for half in range(2):
-        first = value[(2 * half) * rows : (2 * half + 1) * rows]
-        second = value[(2 * half + 1) * rows : (2 * half + 2) * rows]
-        at = slice(half * rows, (half + 1) * rows)
-        send_ref[at, cols] = jnp.where(keep_first, second, first)
-        keep_ref[at, cols] = jnp.where(keep_first, first, second)
-
-
-def product_kernel(adapters, units, at, _, own_ref, other_ref, direct_ref, *refs):
+    for at in range(0, send_ref.shape[0], rows):
+        first, second = value[2 * at : 2 * at + rows], value[2 * at + rows : 2 * at + 2 * rows]
+        send_ref[at : at + rows, cols] = jnp.where(keep_first, second, first)
+        keep_ref[at : at + rows, cols] = jnp.where(keep_first, first, second)
+
+
+def product_kernel(adapters, units, nears, _, own_ref, other_ref, direct_ref, *refs):
     passed_refs, refs = refs[:CUTS], refs[CUTS:]
     *panel_refs, spread_ref, send_ref, keep_ref = refs
     rows = direct_ref.shape[0]
@@ -111,9 +109,11 @@
     rank = wide // adapters
 
     def piece():
-        near = [own_ref[at : at + rows, :], other_ref[at : at + rows, :]]
         passed = jnp.concatenate([ref[...] for ref in passed_refs], axis=1)
-        return jnp.concatenate([*near, direct_ref[...], passed], axis=0)
+        whole = [direct_ref[...], passed]
+        for at in nears:
+            whole += [ref[at : at + rows, :] for ref in (own_ref, other_ref)]
+        return jnp.concatenate(whole * max(1, FULL // (rows * len(whole))), axis=0)
 
     every = jnp.dot(piece(), spread_ref[...], preferred_element_type=jnp.float32)
     ids = piece()[:, units : units + 1].astype(jnp.float32)
@@ -125,25 +125,25 @@
     tile = tile + pltpu.roll(tile, rank, 1)
     lane = lax.broadcasted_iota(jnp.int32, tile.shape, 1)
     tile = jnp.where(lane < rank, tile, ids)
-    part_rows(tile, slice(width, width + LANES), send_ref, keep_ref)
+    part_rows(rows, tile, slice(width, width + LANES), send_ref, keep_ref)
 
     for panel, panel_ref in enumerate(panel_refs):
         value = jnp.dot(
             piece(), panel_ref[...], preferred_element_type=jnp.float32
         )
-        part_rows(value, slice(panel * PANEL, (panel + 1) * PANEL), send_ref, keep_ref)
-
-
-def add_kernel(first_ref, second_ref, send_ref, keep_ref):
+        part_rows(rows, value, slice(panel * PANEL, (panel + 1) * PANEL), send_ref, keep_ref)
+
+
+def add_kernel(near_at, near_a, near_b, far_a, far_b, send_ref, keep_ref):
     rows = send_ref.shape[0]
     keep_near = lax.axis_index("tensor") // 2 == lax.axis_index("req") // 2
 
-    def total(at):
+    def total(first_ref, second_ref, at):
         cut = slice(at, at + rows)
         value = first_ref[cut].astype(jnp.float32) + second_ref[cut].astype(jnp.float32)
         return value.astype(send_ref.dtype)
 
-    near, far = total(0), total(rows)
+    near, far = total(near_a, near_b, near_at), total(far_a, far_b, 0)
     send_ref[...] = jnp.where(keep_near, far, near)
     keep_ref[...] = jnp.where(keep_near, near, far)
 
@@ -235,9 +235,11 @@
     )(left(weight), left(shrink_rows))
 
     def product(step, passed, token):
+        nears = [starts[step]] if step + 1 < len(counts) else []
+        nears += [starts[-1]] if step == 0 else []
         return pl.pallas_call(
-            functools.partial(product_kernel, adapters, units, starts[step]),
-            out_shape=[struct(2 * counts[step], payload)] * 2,
+            functools.partial(product_kernel, adapters, units, nears),
+            out_shape=[struct((1 + len(nears)) * counts[step], payload)] * 2,
             in_specs=[in_vmem()] * (4 + CUTS + len(both)),
             out_specs=[in_vmem()] * 2,
             compiler_params=params(4),
@@ -245,16 +247,18 @@
             name="product",
         )(token, own, other, direct[step], *passed, *both)
 
-    def add(step, keep, got):
+    def add(step):
+        last = step + 1 == len(counts)
+        near_at = counts[step] * (2 if last else 1)
         return pl.pallas_call(
-            add_kernel,
+            functools.partial(add_kernel, near_at),
             out_shape=[struct(counts[step], payload)] * 2,
-            in_specs=[in_vmem()] * 2,
+            in_specs=[in_vmem()] * 4,
             out_specs=[in_vmem()] * 2,
             compiler_params=params(4),
             cost_estimate=quick,
             name="add",
-        )(keep, got)
+        )(*parts[0 if last else step], *parts[step])
 
     def over_core(part):
         tiles = room // LANES
@@ -269,8 +273,7 @@
     parts, kept, gots = [], [], []
 
     def add_part(step):
-        keep, got = parts[step]
-        send, keep = add(step, keep, got)
+        send, keep = add(step)
         kept.append(keep)
         return send
 
@@ -284,8 +287,8 @@
             got = lax.ppermute(send, "tensor", next_z)
             direct[step + 1], keep, parts, hop = after((direct[step + 1], keep, parts, hop))
         else:
-            send, parts, hop = after((send, parts, hop))
             got = lax.ppermute(send, "tensor", next_z)
+            parts, hop = after((parts, hop))
         if step > 1:
             gots[step - 2 :] = hop
         if step > 0:

time: 79 us -> 78 us (0.987)
  waiting for transfers between devices: 19.3 us -> 15.8 us
  Pallas kernels: 35.9 us -> 38.4 us
    ppermute x3, waiting for transfers between devices: 0.86 us -> 8.03 us  [paired(): gots.append(lax.ppermute(send, 'tensor', far_z))]
    ppermute x1, waiting for transfers between devices: 6.49 us -> 2.47 us  [paired(): gots.append(lax.ppermute(add_part(steps - 1), 'tensor', far_z))]
    ppermute x3, waiting for transfers between devices: 3.59 us -> 0.24 us  [paired(): direct.append(lax.ppermute(pieces[step + 1], 'req', across))]
    ppermute x4, waiting for transfers between devices: 8.35 us -> 5.08 us  [paired(): got = lax.ppermute(send, 'tensor', next_z)]
    ppermute x3, starting transfers between devices: 6.47 us -> 9.19 us  [paired(): gots.append(lax.ppermute(send, 'tensor', far_z))]
    pallas_call x8, Pallas kernels: 20.9 us -> 23.4 us  [the longest x4 23 us: product(): pl.pallas_call(functools.partial(product_kernel, adapters, units, nears),...]
    ppermute x4, starting transfers between devices: 7.26 us -> 5.05 us  [paired(): got = lax.ppermute(send, 'tensor', next_z)]
  transfers between devices with their start and end apart: 21 -> 21, of which waited for: 8 -> 7; matrix products, arithmetic and copies ran while one was open for 0% -> 0% of each run, Pallas kernels for 41% -> 45%
where the time goes in v13:
time: 78 us; the launch traced here: 77.8 us
  Pallas kernels  38.4 us (49%)
  starting transfers between devices  23.3 us (30%)
  waiting for transfers between devices  15.8 us (20%)
    pallas_call x4, Pallas kernels, product(): pl.pallas_call(functools.partial(product_kernel, adapters, units, nears),...  23 us
    pallas_call x1, Pallas kernels, paired(): pl.pallas_call(load_kernel, out_shape=[jax.ShapeDtypeStruct((8, LANES), j...  11.9 us
    ppermute x3, starting transfers between devices, paired(): gots.append(lax.ppermute(send, 'tensor', far_z))  9.19 us
    ppermute x3, waiting for transfers between devices, paired(): gots.append(lax.ppermute(send, 'tensor', far_z))  8.03 us
    ppermute x4, waiting for transfers between devices, paired(): got = lax.ppermute(send, 'tensor', next_z)  5.08 us
    ppermute x4, starting transfers between devices, paired(): got = lax.ppermute(send, 'tensor', next_z)  5.05 us
    ppermute x3, starting transfers between devices, paired(): direct.append(lax.ppermute(pieces[step + 1], 'req', across))  3.52 us
    ppermute x1, starting transfers between devices, paired(): direct = [lax.ppermute(pieces[0], 'req', across)]  2.56 us
  transfers between devices with their start and end apart: 21, of which 7 were waited for; matrix products, arithmetic and copies ran while one was open for 0% of the time, Pallas kernels for 45%

profile of v13, /device:TPU:0, one launch (start us, length us, event | category | flops | bytes accessed | tf_op | source)
XLA Modules:
  0.0 77.8 jit_solution(3409894014723519795)
XLA Ops:
  0.0 1.8 %turn.1 = (bf16[128,7424]{1,0:T(8,128)(2,1)S(1)}, bf16[32,7424]{1,0:T(8,128)(2,1)S(1)}, bf16[32,7424]{1,0:T(8,128)(2,1)S(1)}, bf16[32,7424]{1,0:T(8,128)(2,1)S(1)}, bf16[32,7424]{1,0:T(8,128)(2,1)S(1)}) custom-call(bf16[7392,128]{1,0:T(8,128)(2,1)} %bitcast.8, s32[1,128]{1,0:T(1,128)} %bitcast.9), custom_call_target="tpu_custom_call" | custom-call | tf_op jit(solution)/shard_map/turn/pallas_call | solution.py:197
  1.8 0.5 collective-permute-start.2
  2.3 2.6 %collective-permute-start.1 = (bf16[32,7424]{1,0:T(8,128)(2,1)S(1)}, bf16[32,7424]{1,0:T(8,128)(2,1)S(1)}, u32[]{:S(2)}, u32[]{:S(2)}) collective-permute-start(bf16[32,7424]{1,0:T(8,128)(2,1)S(1)} %get-tuple-element.57), channel_id=1, source_target_pairs={{0,2},{1,3},{2,0},{3,1},{4,6},{5,7},{6,4},{7,5},{8,10},{9,11},{10,... | collective-permute-start | bytes 1425416 | tf_op jit(solution)/shard_map/ppermute | solution.py:216
  5.0 11.9 %load.1 = (f32[8,128]{1,0:T(8,128)S(1)}, bf16[7424,512]{1,0:T(8,128)(2,1)S(1)}, bf16[7424,512]{1,0:T(8,128)(2,1)S(1)}, bf16[7424,512]{1,0:T(8,128)(2,1)S(1)}, bf...) custom-call(bf16[7392,2048]{1,0:T(8,128)(2,1)} %w_hbm.1, bf16[512,7392]{1,0:T(8,128)(2,1)} %bitcast.7), custom_call_target="tpu_custom_call" | custom-call | flops 1 | bytes 1 | tf_op jit(solution)/shard_map/load/pallas_call | solution.py:220
  17.5 1.9 %collective-permute-start = (bf16[32,7424]{1,0:T(8,128)(2,1)S(1)}, bf16[32,7424]{1,0:T(8,128)(2,1)S(1)}, u32[]{:S(2)}, u32[]{:S(2)}) collective-permute-start(bf16[32,7424]{1,0:T(8,128)(2,1)S(1)} %get-tuple-element.56), channel_id=1, source_target_pairs={{0,2},{1,3},{2,0},{3,1},{4,6},{5,7},{6,4},{7,5},{8,10},{9,11},{10,... | collective-permute-start | bytes 1425416 | tf_op jit(solution)/shard_map/ppermute | solution.py:283
  19.5 7.5 %product.4 = (bf16[96,2176]{1,0:T(8,128)(2,1)S(1)}, bf16[96,2176]{1,0:T(8,128)(2,1)S(1)}) custom-call(f32[8,128]{1,0:T(8,128)S(1)} %get-tuple-element.59._, bf16[128,7424]{1,0:T(8,128)(2,1)S(1)} %get-tuple-element.60.own_ref, bf16[128,7424]{1,0:T(8,128)(2,1)S(1)} %collective-permute-done.2.other_ref, bf16[32,7424]{1,0:T(8,128)(2,1)S(1)} %collective-permute-done.1.direct_ref, ...), custom_call_target="tpu_custom_call" | custom-call | flops 1 | bytes 1 | tf_op jit(solution)/shard_map/product/pallas_call | solution.py:240
  27.0 1.9 %collective-permute-start.8 = (bf16[96,2176]{1,0:T(8,128)(2,1)S(1)}, bf16[96,2176]{1,0:T(8,128)(2,1)S(1)}, u32[]{:S(2)}, u32[]{:S(2)}) collective-permute-start(bf16[96,2176]{1,0:T(8,128)(2,1)S(1)} %get-tuple-element.72), channel_id=1, source_target_pairs={{0,4},{4,0},{8,12},{12,8},{1,5},{5,1},{9,13},{13,9},{2,6},{6,2},{1... | collective-permute-start | bytes 1253384 | tf_op jit(solution)/shard_map/ppermute | solution.py:287
  29.0 0.5 collective-permute-start.6
  29.5 1.5 %collective-permute-start.9 = (bf16[32,7424]{1,0:T(8,128)(2,1)S(1)}, bf16[32,7424]{1,0:T(8,128)(2,1)S(1)}, u32[]{:S(2)}, u32[]{:S(2)}) collective-permute-start(bf16[32,7424]{1,0:T(8,128)(2,1)S(1)} %get-tuple-element.78), channel_id=1, source_target_pairs={{0,2},{1,3},{2,0},{3,1},{4,6},{5,7},{6,4},{7,5},{8,10},{9,11},{10,... | collective-permute-start | bytes 1425416 | tf_op jit(solution)/shard_map/ppermute | solution.py:283
  31.0 5.3 %product.5 = (bf16[64,2176]{1,0:T(8,128)(2,1)S(1)}, bf16[64,2176]{1,0:T(8,128)(2,1)S(1)}) custom-call(f32[8,128]{1,0:T(8,128)S(1)} %get-tuple-element.59._, bf16[128,7424]{1,0:T(8,128)(2,1)S(1)} %get-tuple-element.60.own_ref, bf16[128,7424]{1,0:T(8,128)(2,1)S(1)} %collective-permute-done.2.other_ref, bf16[32,7424]{1,0:T(8,128)(2,1)S(1)} %collective-permute-done.3.direct_ref, ...), custom_call_target="tpu_custom_call" | custom-call | flops 1 | bytes 1 | tf_op jit(solution)/shard_map/product/pallas_call | solution.py:240
  36.2 0.5 collective-permute-start.12
  37.0 1.6 %collective-permute-done.8.near_b.far_b = bf16[96,2176]{1,0:T(8,128)(2,1)S(1)} collective-permute-done((bf16[96,2176]{1,0:T(8,128)(2,1)S(1)}, bf16[96,2176]{1,0:T(8,128)(2,1)S(1)}, u32[]{:S(2)}, u32[]{:S(2)}) %collective-permute-start.8) | collective-permute-done | bytes 417824 | tf_op jit(solution)/shard_map/ppermute | solution.py:287
  39.3 2.6 %collective-permute-start.13 = (bf16[32,2176]{1,0:T(8,128)(2,1)S(1)}, bf16[32,2176]{1,0:T(8,128)(2,1)S(1)}, u32[]{:S(2)}, u32[]{:S(2)}) collective-permute-start(bf16[32,2176]{1,0:T(8,128)(2,1)S(1)} %get-tuple-element.83), channel_id=1, source_target_pairs={{0,8},{4,12},{8,0},{12,4},{1,9},{5,13},{9,1},{13,5},{2,10},{6,14},... | collective-permute-start | bytes 417800 | tf_op jit(solution)/shard_map/ppermute | solution.py:298
  41.9 5.1 %product.6 = (bf16[64,2176]{1,0:T(8,128)(2,1)S(1)}, bf16[64,2176]{1,0:T(8,128)(2,1)S(1)}) custom-call(f32[8,128]{1,0:T(8,128)S(1)} %get-tuple-element.59._, bf16[128,7424]{1,0:T(8,128)(2,1)S(1)} %get-tuple-element.60.own_ref, bf16[128,7424]{1,0:T(8,128)(2,1)S(1)} %collective-permute-done.2.other_ref, bf16[32,7424]{1,0:T(8,128)(2,1)S(1)} %collective-permute-done.direct_ref, ...), custom_call_target="tpu_custom_call" | custom-call | flops 1 | bytes 1 | tf_op jit(solution)/shard_map/product/pallas_call | solution.py:240
  47.0 0.9 %collective-permute-done.12.near_b.far_b = bf16[64,2176]{1,0:T(8,128)(2,1)S(1)} collective-permute-done((bf16[64,2176]{1,0:T(8,128)(2,1)S(1)}, bf16[64,2176]{1,0:T(8,128)(2,1)S(1)}, u32[]{:S(2)}, u32[]{:S(2)}) %collective-permute-start.12) | collective-permute-done | bytes 278560 | tf_op jit(solution)/shard_map/ppermute | solution.py:287
  48.6 2.6 %collective-permute-start.14 = (bf16[64,2176]{1,0:T(8,128)(2,1)S(1)}, bf16[64,2176]{1,0:T(8,128)(2,1)S(1)}, u32[]{:S(2)}, u32[]{:S(2)}) collective-permute-start(bf16[64,2176]{1,0:T(8,128)(2,1)S(1)} %get-tuple-element.92), channel_id=1, source_target_pairs={{0,4},{4,0},{8,12},{12,8},{1,5},{5,1},{9,13},{13,9},{2,6},{6,2},{1... | collective-permute-start | bytes 835592 | tf_op jit(solution)/shard_map/ppermute | solution.py:287
  51.2 3.2 %collective-permute-start.15 = (bf16[32,2176]{1,0:T(8,128)(2,1)S(1)}, bf16[32,2176]{1,0:T(8,128)(2,1)S(1)}, u32[]{:S(2)}, u32[]{:S(2)}) collective-permute-start(bf16[32,2176]{1,0:T(8,128)(2,1)S(1)} %get-tuple-element.93), channel_id=1, source_target_pairs={{0,8},{4,12},{8,0},{12,4},{1,9},{5,13},{9,1},{13,5},{2,10},{6,14},... | collective-permute-start | bytes 417800 | tf_op jit(solution)/shard_map/ppermute | solution.py:298
  54.4 5.2 %product.7 = (bf16[32,2176]{1,0:T(8,128)(2,1)S(1)}, bf16[32,2176]{1,0:T(8,128)(2,1)S(1)}) custom-call(f32[8,128]{1,0:T(8,128)S(1)} %get-tuple-element.59._, bf16[128,7424]{1,0:T(8,128)(2,1)S(1)} %get-tuple-element.60.own_ref, bf16[128,7424]{1,0:T(8,128)(2,1)S(1)} %collective-permute-done.2.other_ref, bf16[32,7424]{1,0:T(8,128)(2,1)S(1)} %collective-permute-done.9.direct_ref, ...), custom_call_target="tpu_custom_call" | custom-call | flops 1 | bytes 1 | tf_op jit(solution)/shard_map/product/pallas_call | solution.py:240
  59.6 1.4 %collective-permute-done.15.refs_5_ = bf16[32,2176]{1,0:T(8,128)(2,1)S(1)} collective-permute-done((bf16[32,2176]{1,0:T(8,128)(2,1)S(1)}, bf16[32,2176]{1,0:T(8,128)(2,1)S(1)}, u32[]{:S(2)}, u32[]{:S(2)}) %collective-permute-start.15) | collective-permute-done | bytes 139296 | tf_op jit(solution)/shard_map/ppermute | solution.py:298
  61.1 3.4 %collective-permute-start.19 = (bf16[32,2176]{1,0:T(8,128)(2,1)S(1)}, bf16[32,2176]{1,0:T(8,128)(2,1)S(1)}, u32[]{:S(2)}, u32[]{:S(2)}) collective-permute-start(bf16[32,2176]{1,0:T(8,128)(2,1)S(1)} %get-tuple-element.105), channel_id=1, source_target_pairs={{0,8},{4,12},{8,0},{12,4},{1,9},{5,13},{9,1},{13,5},{2,10},{6,14},... | collective-permute-start | bytes 417800 | tf_op jit(solution)/shard_map/ppermute | solution.py:298
  64.5 2.6 %collective-permute-done.18.far_b = bf16[32,2176]{1,0:T(8,128)(2,1)S(1)} collective-permute-done((bf16[32,2176]{1,0:T(8,128)(2,1)S(1)}, bf16[32,2176]{1,0:T(8,128)(2,1)S(1)}, u32[]{:S(2)}, u32[]{:S(2)}) %collective-permute-start.18) | collective-permute-done | bytes 139296 | tf_op jit(solution)/shard_map/ppermute | solution.py:290
  67.4 6.7 %collective-permute-done.19.refs_6_ = bf16[32,2176]{1,0:T(8,128)(2,1)S(1)} collective-permute-done((bf16[32,2176]{1,0:T(8,128)(2,1)S(1)}, bf16[32,2176]{1,0:T(8,128)(2,1)S(1)}, u32[]{:S(2)}, u32[]{:S(2)}) %collective-permute-start.19) | collective-permute-done | bytes 139296 | tf_op jit(solution)/shard_map/ppermute | solution.py:298
  74.1 2.5 %collective-permute-done.20.refs_7_ = bf16[32,2176]{1,0:T(8,128)(2,1)S(1)} collective-permute-done((bf16[32,2176]{1,0:T(8,128)(2,1)S(1)}, bf16[32,2176]{1,0:T(8,128)(2,1)S(1)}, u32[]{:S(2)}, u32[]{:S(2)}) %collective-permute-start.20) | collective-permute-done | bytes 139296 | tf_op jit(solution)/shard_map/ppermute | solution.py:300
  76.5 1.3 %last.1 = bf16[128,2048]{1,0:T(8,128)(2,1)} custom-call(bf16[512,2048]{1,0:T(8,128)(2,1)S(1)} %bitcast.6, bf16[32,2176]{1,0:T(8,128)(2,1)S(1)} %get-tuple-element.77.refs_0_, bf16[32,2176]{1,0:T(8,128)(2,1)S(1)} %get-tuple-element.88.refs_1_, bf16[32,2176]{1,0:T(8,128)(2,1)S(1)} %get-tuple-element.96.refs_2_, ...), custom_call_target="tpu_custom_call" | custom-call | tf_op jit(solution)/shard_map/last/pallas_call | solution.py:302
  (35 shorter events, 2.9 us)
Async XLA Ops:
  1.8 17.6 %collective-permute-start.2 = (bf16[128,7424]{1,0:T(8,128)(2,1)S(1)}, bf16[128,7424]{1,0:T(8,128)(2,1)S(1)}, u32[]{:S(2)}, u32[]{:S(2)}) collective-permute-start(bf16[128,7424]{1,0:T(8,128)(2,1)S(1)} %get-tuple-element.60.own_ref), channel_id=1, source_target_pairs={{0,1},{1,0},{2,3},{3,2},{4,5},{5,4},{6,7},{7,6},{8,9},{9,8},{10,11... | collective-permute-start | bytes 5701640 | tf_op jit(solution)/shard_map/ppermute | solution.py:217
  2.3 14.5 %collective-permute-start.1 = (bf16[32,7424]{1,0:T(8,128)(2,1)S(1)}, bf16[32,7424]{1,0:T(8,128)(2,1)S(1)}, u32[]{:S(2)}, u32[]{:S(2)}) collective-permute-start(bf16[32,7424]{1,0:T(8,128)(2,1)S(1)} %get-tuple-element.57), channel_id=1, source_target_pairs={{0,2},{1,3},{2,0},{3,1},{4,6},{5,7},{6,4},{7,5},{8,10},{9,11},{10,... | collective-permute-start | bytes 1425416 | tf_op jit(solution)/shard_map/ppermute | solution.py:216
  4.9 22.1 %collective-permute-start.3 = (bf16[32,7424]{1,0:T(8,128)(2,1)S(1)}, bf16[32,7424]{1,0:T(8,128)(2,1)S(1)}, u32[]{:S(2)}, u32[]{:S(2)}) collective-permute-start(bf16[32,7424]{1,0:T(8,128)(2,1)S(1)} %get-tuple-element.61), channel_id=1, source_target_pairs={{0,2},{1,3},{2,0},{3,1},{4,6},{5,7},{6,4},{7,5},{8,10},{9,11},{10,... | collective-permute-start | bytes 1425416 | tf_op jit(solution)/shard_map/ppermute | solution.py:283
  16.9 2.5 %collective-permute-start.5 = (bf16[32,3712]{1,0:T(8,128)(2,1)S(1)}, bf16[32,3712]{1,0:T(8,128)(2,1)S(1)}, u32[]{:S(2)}, u32[]{:S(2)}) collective-permute-start(bf16[32,3712]{1,0:T(8,128)(2,1)S(1)} %get-tuple-element.113), channel_id=1, source_target_pairs={{0,1},{1,0},{2,3},{3,2},{4,5},{5,4},{6,7},{7,6},{8,9},{9,8},{10,11... | collective-permute-start | bytes 712712 | tf_op jit(solution)/shard_map/ppermute | solution.py:267
  17.1 2.4 %collective-permute-start.4 = (bf16[32,3712]{1,0:T(8,128)(2,1)S(1)}, bf16[32,3712]{1,0:T(8,128)(2,1)S(1)}, u32[]{:S(2)}, u32[]{:S(2)}) collective-permute-start(bf16[32,3712]{1,0:T(8,128)(2,1)S(1)} %get-tuple-element.114), channel_id=1, source_target_pairs={{0,1},{1,0},{2,3},{3,2},{4,5},{5,4},{6,7},{7,6},{8,9},{9,8},{10,11... | collective-permute-start | bytes 712712 | tf_op jit(solution)/shard_map/ppermute | solution.py:267
  17.5 19.5 %collective-permute-start = (bf16[32,7424]{1,0:T(8,128)(2,1)S(1)}, bf16[32,7424]{1,0:T(8,128)(2,1)S(1)}, u32[]{:S(2)}, u32[]{:S(2)}) collective-permute-start(bf16[32,7424]{1,0:T(8,128)(2,1)S(1)} %get-tuple-element.56), channel_id=1, source_target_pairs={{0,2},{1,3},{2,0},{3,1},{4,6},{5,7},{6,4},{7,5},{8,10},{9,11},{10,... | collective-permute-start | bytes 1425416 | tf_op jit(solution)/shard_map/ppermute | solution.py:283
  27.0 11.6 %collective-permute-start.8 = (bf16[96,2176]{1,0:T(8,128)(2,1)S(1)}, bf16[96,2176]{1,0:T(8,128)(2,1)S(1)}, u32[]{:S(2)}, u32[]{:S(2)}) collective-permute-start(bf16[96,2176]{1,0:T(8,128)(2,1)S(1)} %get-tuple-element.72), channel_id=1, source_target_pairs={{0,4},{4,0},{8,12},{12,8},{1,5},{5,1},{9,13},{13,9},{2,6},{6,2},{1... | collective-permute-start | bytes 1253384 | tf_op jit(solution)/shard_map/ppermute | solution.py:287
  28.9 2.1 %collective-permute-start.7 = (bf16[32,3712]{1,0:T(8,128)(2,1)S(1)}, bf16[32,3712]{1,0:T(8,128)(2,1)S(1)}, u32[]{:S(2)}, u32[]{:S(2)}) collective-permute-start(bf16[32,3712]{1,0:T(8,128)(2,1)S(1)} %get-tuple-element.111), channel_id=1, source_target_pairs={{0,1},{1,0},{2,3},{3,2},{4,5},{5,4},{6,7},{7,6},{8,9},{9,8},{10,11... | collective-permute-start | bytes 712712 | tf_op jit(solution)/shard_map/ppermute | solution.py:267
  29.0 2.0 %collective-permute-start.6 = (bf16[32,3712]{1,0:T(8,128)(2,1)S(1)}, bf16[32,3712]{1,0:T(8,128)(2,1)S(1)}, u32[]{:S(2)}, u32[]{:S(2)}) collective-permute-start(bf16[32,3712]{1,0:T(8,128)(2,1)S(1)} %get-tuple-element.112), channel_id=1, source_target_pairs={{0,1},{1,0},{2,3},{3,2},{4,5},{5,4},{6,7},{7,6},{8,9},{9,8},{10,11... | collective-permute-start | bytes 712712 | tf_op jit(solution)/shard_map/ppermute | solution.py:267
  29.5 17.5 %collective-permute-start.9 = (bf16[32,7424]{1,0:T(8,128)(2,1)S(1)}, bf16[32,7424]{1,0:T(8,128)(2,1)S(1)}, u32[]{:S(2)}, u32[]{:S(2)}) collective-permute-start(bf16[32,7424]{1,0:T(8,128)(2,1)S(1)} %get-tuple-element.78), channel_id=1, source_target_pairs={{0,2},{1,3},{2,0},{3,1},{4,6},{5,7},{6,4},{7,5},{8,10},{9,11},{10,... | collective-permute-start | bytes 1425416 | tf_op jit(solution)/shard_map/ppermute | solution.py:283
  36.2 11.6 %collective-permute-start.12 = (bf16[64,2176]{1,0:T(8,128)(2,1)S(1)}, bf16[64,2176]{1,0:T(8,128)(2,1)S(1)}, u32[]{:S(2)}, u32[]{:S(2)}) collective-permute-start(bf16[64,2176]{1,0:T(8,128)(2,1)S(1)} %get-tuple-element.82), channel_id=1, source_target_pairs={{0,4},{4,0},{8,12},{12,8},{1,5},{5,1},{9,13},{13,9},{2,6},{6,2},{1... | collective-permute-start | bytes 835592 | tf_op jit(solution)/shard_map/ppermute | solution.py:287
  38.7 3.2 %collective-permute-start.11 = (bf16[32,3712]{1,0:T(8,128)(2,1)S(1)}, bf16[32,3712]{1,0:T(8,128)(2,1)S(1)}, u32[]{:S(2)}, u32[]{:S(2)}) collective-permute-start(bf16[32,3712]{1,0:T(8,128)(2,1)S(1)} %get-tuple-element.109), channel_id=1, source_target_pairs={{0,1},{1,0},{2,3},{3,2},{4,5},{5,4},{6,7},{7,6},{8,9},{9,8},{10,11... | collective-permute-start | bytes 712712 | tf_op jit(solution)/shard_map/ppermute | solution.py:267
  38.8 3.1 %collective-permute-start.10 = (bf16[32,3712]{1,0:T(8,128)(2,1)S(1)}, bf16[32,3712]{1,0:T(8,128)(2,1)S(1)}, u32[]{:S(2)}, u32[]{:S(2)}) collective-permute-start(bf16[32,3712]{1,0:T(8,128)(2,1)S(1)} %get-tuple-element.110), channel_id=1, source_target_pairs={{0,1},{1,0},{2,3},{3,2},{4,5},{5,4},{6,7},{7,6},{8,9},{9,8},{10,11... | collective-permute-start | bytes 712712 | tf_op jit(solution)/shard_map/ppermute | solution.py:267
  39.3 8.5 %collective-permute-start.13 = (bf16[32,2176]{1,0:T(8,128)(2,1)S(1)}, bf16[32,2176]{1,0:T(8,128)(2,1)S(1)}, u32[]{:S(2)}, u32[]{:S(2)}) collective-permute-start(bf16[32,2176]{1,0:T(8,128)(2,1)S(1)} %get-tuple-element.83), channel_id=1, source_target_pairs={{0,8},{4,12},{8,0},{12,4},{1,9},{5,13},{9,1},{13,5},{2,10},{6,14},... | collective-permute-start | bytes 417800 | tf_op jit(solution)/shard_map/ppermute | solution.py:298
  48.0 6.4 %collective-permute-start.17 = (bf16[32,3712]{1,0:T(8,128)(2,1)S(1)}, bf16[32,3712]{1,0:T(8,128)(2,1)S(1)}, u32[]{:S(2)}, u32[]{:S(2)}) collective-permute-start(bf16[32,3712]{1,0:T(8,128)(2,1)S(1)} %get-tuple-element.107), channel_id=1, source_target_pairs={{0,1},{1,0},{2,3},{3,2},{4,5},{5,4},{6,7},{7,6},{8,9},{9,8},{10,11... | collective-permute-start | bytes 712712 | tf_op jit(solution)/shard_map/ppermute | solution.py:267
  48.1 6.3 %collective-permute-start.16 = (bf16[32,3712]{1,0:T(8,128)(2,1)S(1)}, bf16[32,3712]{1,0:T(8,128)(2,1)S(1)}, u32[]{:S(2)}, u32[]{:S(2)}) collective-permute-start(bf16[32,3712]{1,0:T(8,128)(2,1)S(1)} %get-tuple-element.108), channel_id=1, source_target_pairs={{0,1},{1,0},{2,3},{3,2},{4,5},{5,4},{6,7},{7,6},{8,9},{9,8},{10,11... | collective-permute-start | bytes 712712 | tf_op jit(solution)/shard_map/ppermute | solution.py:267
  48.6 12.5 %collective-permute-start.14 = (bf16[64,2176]{1,0:T(8,128)(2,1)S(1)}, bf16[64,2176]{1,0:T(8,128)(2,1)S(1)}, u32[]{:S(2)}, u32[]{:S(2)}) collective-permute-start(bf16[64,2176]{1,0:T(8,128)(2,1)S(1)} %get-tuple-element.92), channel_id=1, source_target_pairs={{0,4},{4,0},{8,12},{12,8},{1,5},{5,1},{9,13},{13,9},{2,6},{6,2},{1... | collective-permute-start | bytes 835592 | tf_op jit(solution)/shard_map/ppermute | solution.py:287
  51.2 25.4 %copy-start = (bf16[8,64,2048]{2,1,0:T(8,128)(2,1)S(1)}, bf16[8,64,2048]{2,1,0:T(8,128)(2,1)}, u32[]{:S(2)}) copy-start(bf16[8,64,2048]{2,1,0:T(8,128)(2,1)} %param.8) | copy-start | bytes 6291460
  51.2 9.8 %collective-permute-start.15 = (bf16[32,2176]{1,0:T(8,128)(2,1)S(1)}, bf16[32,2176]{1,0:T(8,128)(2,1)S(1)}, u32[]{:S(2)}, u32[]{:S(2)}) collective-permute-start(bf16[32,2176]{1,0:T(8,128)(2,1)S(1)} %get-tuple-element.93), channel_id=1, source_target_pairs={{0,8},{4,12},{8,0},{12,4},{1,9},{5,13},{9,1},{13,5},{2,10},{6,14},... | collective-permute-start | bytes 417800 | tf_op jit(solution)/shard_map/ppermute | solution.py:298
  59.6 7.6 %collective-permute-start.18 = (bf16[32,2176]{1,0:T(8,128)(2,1)S(1)}, bf16[32,2176]{1,0:T(8,128)(2,1)S(1)}, u32[]{:S(2)}, u32[]{:S(2)}) collective-permute-start(bf16[32,2176]{1,0:T(8,128)(2,1)S(1)} %get-tuple-element.101), channel_id=1, source_target_pairs={{0,4},{4,0},{8,12},{12,8},{1,5},{5,1},{9,13},{13,9},{2,6},{6,2},{1... | collective-permute-start | bytes 417800 | tf_op jit(solution)/shard_map/ppermute | solution.py:290
  61.1 12.9 %collective-permute-start.19 = (bf16[32,2176]{1,0:T(8,128)(2,1)S(1)}, bf16[32,2176]{1,0:T(8,128)(2,1)S(1)}, u32[]{:S(2)}, u32[]{:S(2)}) collective-permute-start(bf16[32,2176]{1,0:T(8,128)(2,1)S(1)} %get-tuple-element.105), channel_id=1, source_target_pairs={{0,8},{4,12},{8,0},{12,4},{1,9},{5,13},{9,1},{13,5},{2,10},{6,14},... | collective-permute-start | bytes 417800 | tf_op jit(solution)/shard_map/ppermute | solution.py:298
  67.2 9.3 %collective-permute-start.20 = (bf16[32,2176]{1,0:T(8,128)(2,1)S(1)}, bf16[32,2176]{1,0:T(8,128)(2,1)S(1)}, u32[]{:S(2)}, u32[]{:S(2)}) collective-permute-start(bf16[32,2176]{1,0:T(8,128)(2,1)S(1)} %get-tuple-element.106), channel_id=1, source_target_pairs={{0,8},{4,12},{8,0},{12,4},{1,9},{5,13},{9,1},{13,5},{2,10},{6,14},... | collective-permute-start | bytes 417800 | tf_op jit(solution)/shard_map/ppermute | solution.py:300

commit v14 on v13

--- a/solution.py
+++ b/solution.py
@@ -14,6 +14,7 @@
 PIECES = (32, 32, 32, 32)
 CUTS = 2
 FULL = 128
+EARLY = 2
 MIB = 1 << 20
 
 
@@ -100,17 +101,17 @@
         keep_ref[at : at + rows, cols] = jnp.where(keep_first, first, second)
 
 
-def product_kernel(adapters, units, nears, _, own_ref, other_ref, direct_ref, *refs):
-    passed_refs, refs = refs[:CUTS], refs[CUTS:]
+def product_kernel(adapters, units, rows, far, nears, _, own_ref, other_ref, *refs):
+    far_refs, refs = refs[: far * (1 + CUTS)], refs[far * (1 + CUTS) :]
     *panel_refs, spread_ref, send_ref, keep_ref = refs
-    rows = direct_ref.shape[0]
     width = send_ref.shape[1] - LANES
     wide = spread_ref.shape[1]
     rank = wide // adapters
 
     def piece():
-        passed = jnp.concatenate([ref[...] for ref in passed_refs], axis=1)
-        whole = [direct_ref[...], passed]
+        whole = []
+        if far:
+            whole = [far_refs[0][...], jnp.concatenate([ref[...] for ref in far_refs[1:]], axis=1)]
         for at in nears:
             whole += [ref[at : at + rows, :] for ref in (own_ref, other_ref)]
         return jnp.concatenate(whole * max(1, FULL // (rows * len(whole))), axis=0)
@@ -234,22 +235,19 @@
         name="load",
     )(left(weight), left(shrink_rows))
 
-    def product(step, passed, token):
-        nears = [starts[step]] if step + 1 < len(counts) else []
-        nears += [starts[-1]] if step == 0 else []
+    def product(rows, nears, *far):
         return pl.pallas_call(
-            functools.partial(product_kernel, adapters, units, nears),
-            out_shape=[struct((1 + len(nears)) * counts[step], payload)] * 2,
-            in_specs=[in_vmem()] * (4 + CUTS + len(both)),
+            functools.partial(product_kernel, adapters, units, rows, len(far) > 0, nears),
+            out_shape=[struct((len(nears) + (len(far) > 0)) * rows, payload)] * 2,
+            in_specs=[in_vmem()] * (3 + len(far) + len(both)),
             out_specs=[in_vmem()] * 2,
             compiler_params=params(4),
             cost_estimate=quick,
             name="product",
-        )(token, own, other, direct[step], *passed, *both)
+        )(token, own, other, *far, *both)
 
     def add(step):
-        last = step + 1 == len(counts)
-        near_at = counts[step] * (2 if last else 1)
+        near, near_at = (parts[step], counts[step]) if step < EARLY else (late, late_at[step])
         return pl.pallas_call(
             functools.partial(add_kernel, near_at),
             out_shape=[struct(counts[step], payload)] * 2,
@@ -258,7 +256,7 @@
             compiler_params=params(4),
             cost_estimate=quick,
             name="add",
-        )(*parts[0 if last else step], *parts[step])
+        )(*near, *parts[step])
 
     def over_core(part):
         tiles = room // LANES
@@ -277,17 +275,26 @@
         kept.append(keep)
         return send
 
+    late_at = {step: starts[step] - starts[EARLY] for step in range(EARLY, steps)}
+    late_send, late_keep = product(counts[-1], starts[EARLY:])
+    late = (late_keep, lax.ppermute(late_send, "tensor", next_z))
     for step in range(steps):
         passed = over_core(direct[step])
+        if step == 0:
+            passed, late_keep = after((passed, late_keep))
+            late = (late_keep, late[1])
         if step + 1 < steps:
             direct.append(lax.ppermute(pieces[step + 1], "req", across))
-        send, keep = product(step, passed, token)
+        send, keep = product(
+            counts[step], starts[step : step + 1] if step < EARLY else [], direct[step], *passed
+        )
         hop = gots[step - 2 :] if step > 1 else []
+        got = lax.ppermute(send, "tensor", next_z)
         if step + 1 < steps:
-            got = lax.ppermute(send, "tensor", next_z)
             direct[step + 1], keep, parts, hop = after((direct[step + 1], keep, parts, hop))
+            if step == 0:
+                direct[1], late = after((direct[1], late))
         else:
-            got = lax.ppermute(send, "tensor", next_z)
             parts, hop = after((parts, hop))
         if step > 1:
             gots[step - 2 :] = hop

time: 78 us -> 91.3 us (1.17)
  local copies, waits for them, and re-layouts: 0.14 us -> 12.1 us
  Pallas kernels: 38.4 us -> 41.2 us
  starting transfers between devices: 23.3 us -> 21.7 us
    unnamed x2 -> x16, local copies, waits for them, and re-layouts: 0.01 us -> 11.9 us
    ppermute x3, starting transfers between devices: 9.19 us -> 4.61 us  [paired(): gots.append(lax.ppermute(send, 'tensor', far_z))]
    pallas_call x4 -> x5, Pallas kernels: 23 us -> 25.9 us  [product(): pl.pallas_call(functools.partial(product_kernel, adapters, units, rows, l...]
    ppermute x1, starting transfers between devices: 0.18 us -> 2.53 us  [paired(): gots.append(lax.ppermute(add_part(steps - 1), 'tensor', far_z))]
    ppermute x0 -> x1, starting transfers between devices: none -> 2.02 us  [paired(): late = (late_keep, lax.ppermute(late_send, 'tensor', next_z))]
    ppermute x3, waiting for transfers between devices: 8.03 us -> 9.33 us  [paired(): gots.append(lax.ppermute(send, 'tensor', far_z))]
  transfers between devices with their start and end apart: 21 -> 22, of which waited for: 7 -> 7; matrix products, arithmetic and copies ran while one was open for 0% -> 0% of each run, Pallas kernels for 45% -> 42%
where the time goes in v14:
time: 91.3 us; the launch traced here: 91 us
  Pallas kernels  41.2 us (45%)
  starting transfers between devices  21.7 us (24%)
  waiting for transfers between devices  15.8 us (17%)
  local copies, waits for them, and re-layouts  12.1 us (13%)
    pallas_call x5, Pallas kernels, product(): pl.pallas_call(functools.partial(product_kernel, adapters, units, rows, l...  25.9 us
    unnamed x16, local copies, waits for them, and re-layouts  11.9 us
    pallas_call x1, Pallas kernels, paired(): pl.pallas_call(load_kernel, out_shape=[jax.ShapeDtypeStruct((8, LANES), j...  11.9 us
    ppermute x3, waiting for transfers between devices, paired(): gots.append(lax.ppermute(send, 'tensor', far_z))  9.33 us
    ppermute x3, starting transfers between devices, paired(): gots.append(lax.ppermute(send, 'tensor', far_z))  4.61 us
    ppermute x4, waiting for transfers between devices, paired(): got = lax.ppermute(send, 'tensor', next_z)  4.46 us
    ppermute x4, starting transfers between devices, paired(): got = lax.ppermute(send, 'tensor', next_z)  4.3 us
    ppermute x3, starting transfers between devices, paired(): direct.append(lax.ppermute(pieces[step + 1], 'req', across))  2.91 us
  transfers between devices with their start and end apart: 22, of which 7 were waited for; matrix products, arithmetic and copies ran while one was open for 0% of the time, Pallas kernels for 42%

profile of v14, /device:TPU:0, one launch (start us, length us, event | category | flops | bytes accessed | tf_op | source)
XLA Modules:
  0.0 91.0 jit_solution(13745875748240540063)
XLA Ops:
  0.0 1.8 %turn.1 = (bf16[128,7424]{1,0:T(8,128)(2,1)S(1)}, bf16[32,7424]{1,0:T(8,128)(2,1)S(1)}, bf16[32,7424]{1,0:T(8,128)(2,1)S(1)}, bf16[32,7424]{1,0:T(8,128)(2,1)S(1)}, bf16[32,7424]{1,0:T(8,128)(2,1)S(1)}) custom-call(bf16[7392,128]{1,0:T(8,128)(2,1)} %bitcast.8, s32[1,128]{1,0:T(1,128)} %bitcast.9), custom_call_target="tpu_custom_call" | custom-call | tf_op jit(solution)/shard_map/turn/pallas_call | solution.py:198
  2.3 2.6 %collective-permute-start.1 = (bf16[32,7424]{1,0:T(8,128)(2,1)S(1)}, bf16[32,7424]{1,0:T(8,128)(2,1)S(1)}, u32[]{:S(2)}, u32[]{:S(2)}) collective-permute-start(bf16[32,7424]{1,0:T(8,128)(2,1)S(1)} %get-tuple-element.61), channel_id=1, source_target_pairs={{0,2},{1,3},{2,0},{3,1},{4,6},{5,7},{6,4},{7,5},{8,10},{9,11},{10,... | collective-permute-start | bytes 1425416 | tf_op jit(solution)/shard_map/ppermute | solution.py:217
  5.0 11.9 %load.1 = (f32[8,128]{1,0:T(8,128)S(1)}, bf16[7424,512]{1,0:T(8,128)(2,1)S(1)}, bf16[7424,512]{1,0:T(8,128)(2,1)S(1)}, bf16[7424,512]{1,0:T(8,128)(2,1)S(1)}, bf...) custom-call(bf16[7392,2048]{1,0:T(8,128)(2,1)} %w_hbm.1, bf16[512,7392]{1,0:T(8,128)(2,1)} %bitcast.7), custom_call_target="tpu_custom_call" | custom-call | flops 1 | bytes 1 | tf_op jit(solution)/shard_map/load/pallas_call | solution.py:221
  16.9 5.1 %product.5 = (bf16[64,2176]{1,0:T(8,128)(2,1)S(1)}, bf16[64,2176]{1,0:T(8,128)(2,1)S(1)}) custom-call(f32[8,128]{1,0:T(8,128)S(1)} %get-tuple-element.63._, bf16[128,7424]{1,0:T(8,128)(2,1)S(1)} %get-tuple-element.64.own_ref, bf16[128,7424]{1,0:T(8,128)(2,1)S(1)} %collective-permute-done.2.other_ref, ...), custom_call_target="tpu_custom_call" | custom-call | flops 1 | bytes 1 | tf_op jit(solution)/shard_map/product/pallas_call | solution.py:239
  22.2 2.2 %copy-done.5 = bf16[7424,512]{1,0:T(8,128)(2,1)} copy-done((bf16[7424,512]{1,0:T(8,128)(2,1)}, bf16[7424,512]{1,0:T(8,128)(2,1)S(1)}, u32[]{:S(2)}) %copy-start.5) | copy-done | bytes 7602200
  24.5 2.0 %collective-permute-start.6 = (bf16[64,2176]{1,0:T(8,128)(2,1)S(1)}, bf16[64,2176]{1,0:T(8,128)(2,1)S(1)}, u32[]{:S(2)}, u32[]{:S(2)}) collective-permute-start(bf16[64,2176]{1,0:T(8,128)(2,1)S(1)} %get-tuple-element.78), channel_id=1, source_target_pairs={{0,4},{4,0},{8,12},{12,8},{1,5},{5,1},{9,13},{13,9},{2,6},{6,2},{1... | collective-permute-start | bytes 835592 | tf_op jit(solution)/shard_map/ppermute | solution.py:280
  27.1 1.5 %collective-permute-start = (bf16[32,7424]{1,0:T(8,128)(2,1)S(1)}, bf16[32,7424]{1,0:T(8,128)(2,1)S(1)}, u32[]{:S(2)}, u32[]{:S(2)}) collective-permute-start(bf16[32,7424]{1,0:T(8,128)(2,1)S(1)} %get-tuple-element.60), channel_id=1, source_target_pairs={{0,2},{1,3},{2,0},{3,1},{4,6},{5,7},{6,4},{7,5},{8,10},{9,11},{10,... | collective-permute-start | bytes 1425416 | tf_op jit(solution)/shard_map/ppermute | solution.py:287
  28.6 3.2 %copy-done.1 = bf16[7424,512]{1,0:T(8,128)(2,1)S(1)} copy-done((bf16[7424,512]{1,0:T(8,128)(2,1)S(1)}, bf16[7424,512]{1,0:T(8,128)(2,1)}, u32[]{:S(2)}) %copy-start.1) | copy-done | bytes 7602200
  31.7 3.2 %copy-done.4 = bf16[7424,512]{1,0:T(8,128)(2,1)S(1)} copy-done((bf16[7424,512]{1,0:T(8,128)(2,1)S(1)}, bf16[7424,512]{1,0:T(8,128)(2,1)}, u32[]{:S(2)}) %copy-start.4) | copy-done | bytes 7602200
  34.9 3.2 %copy-done.6 = bf16[7424,512]{1,0:T(8,128)(2,1)S(1)} copy-done((bf16[7424,512]{1,0:T(8,128)(2,1)S(1)}, bf16[7424,512]{1,0:T(8,128)(2,1)}, u32[]{:S(2)}) %copy-start.6) | copy-done | bytes 7602200
  38.1 5.1 %product.6 = (bf16[64,2176]{1,0:T(8,128)(2,1)S(1)}, bf16[64,2176]{1,0:T(8,128)(2,1)S(1)}) custom-call(f32[8,128]{1,0:T(8,128)S(1)} %get-tuple-element.63._, bf16[128,7424]{1,0:T(8,128)(2,1)S(1)} %get-tuple-element.64.own_ref, bf16[128,7424]{1,0:T(8,128)(2,1)S(1)} %collective-permute-done.2.other_ref, bf16[32,7424]{1,0:T(8,128)(2,1)S(1)} %collective-permute-done.1.refs_0_, ...), custom_call_target="tpu_custom_call" | custom-call | flops 1 | bytes 1 | tf_op jit(solution)/shard_map/product/pallas_call | solution.py:239
  44.3 1.3 %collective-permute-start.10 = (bf16[32,7424]{1,0:T(8,128)(2,1)S(1)}, bf16[32,7424]{1,0:T(8,128)(2,1)S(1)}, u32[]{:S(2)}, u32[]{:S(2)}) collective-permute-start(bf16[32,7424]{1,0:T(8,128)(2,1)S(1)} %get-tuple-element.88), channel_id=1, source_target_pairs={{0,2},{1,3},{2,0},{3,1},{4,6},{5,7},{6,4},{7,5},{8,10},{9,11},{10,... | collective-permute-start | bytes 1425416 | tf_op jit(solution)/shard_map/ppermute | solution.py:287
  45.6 5.3 %product.7 = (bf16[64,2176]{1,0:T(8,128)(2,1)S(1)}, bf16[64,2176]{1,0:T(8,128)(2,1)S(1)}) custom-call(f32[8,128]{1,0:T(8,128)S(1)} %get-tuple-element.63._, bf16[128,7424]{1,0:T(8,128)(2,1)S(1)} %get-tuple-element.64.own_ref, bf16[128,7424]{1,0:T(8,128)(2,1)S(1)} %collective-permute-done.2.other_ref, bf16[32,7424]{1,0:T(8,128)(2,1)S(1)} %collective-permute-done.3.refs_0_, ...), custom_call_target="tpu_custom_call" | custom-call | flops 1 | bytes 1 | tf_op jit(solution)/shard_map/product/pallas_call | solution.py:239
  53.3 2.6 %collective-permute-start.14 = (bf16[32,2176]{1,0:T(8,128)(2,1)S(1)}, bf16[32,2176]{1,0:T(8,128)(2,1)S(1)}, u32[]{:S(2)}, u32[]{:S(2)}) collective-permute-start(bf16[32,2176]{1,0:T(8,128)(2,1)S(1)} %get-tuple-element.93), channel_id=1, source_target_pairs={{0,8},{4,12},{8,0},{12,4},{1,9},{5,13},{9,1},{13,5},{2,10},{6,14},... | collective-permute-start | bytes 417800 | tf_op jit(solution)/shard_map/ppermute | solution.py:305
  55.9 5.1 %product.8 = (bf16[32,2176]{1,0:T(8,128)(2,1)S(1)}, bf16[32,2176]{1,0:T(8,128)(2,1)S(1)}) custom-call(f32[8,128]{1,0:T(8,128)S(1)} %get-tuple-element.63._, bf16[128,7424]{1,0:T(8,128)(2,1)S(1)} %get-tuple-element.64.own_ref, bf16[128,7424]{1,0:T(8,128)(2,1)S(1)} %collective-permute-done.2.other_ref, bf16[32,7424]{1,0:T(8,128)(2,1)S(1)} %collective-permute-done.refs_0_, ...), custom_call_target="tpu_custom_call" | custom-call | flops 1 | bytes 1 | tf_op jit(solution)/shard_map/product/pallas_call | solution.py:239
  63.5 2.6 %collective-permute-start.15 = (bf16[32,2176]{1,0:T(8,128)(2,1)S(1)}, bf16[32,2176]{1,0:T(8,128)(2,1)S(1)}, u32[]{:S(2)}, u32[]{:S(2)}) collective-permute-start(bf16[32,2176]{1,0:T(8,128)(2,1)S(1)} %get-tuple-element.102), channel_id=1, source_target_pairs={{0,4},{4,0},{8,12},{12,8},{1,5},{5,1},{9,13},{13,9},{2,6},{6,2},{1... | collective-permute-start | bytes 417800 | tf_op jit(solution)/shard_map/ppermute | solution.py:292
  66.1 1.6 %collective-permute-start.16 = (bf16[32,2176]{1,0:T(8,128)(2,1)S(1)}, bf16[32,2176]{1,0:T(8,128)(2,1)S(1)}, u32[]{:S(2)}, u32[]{:S(2)}) collective-permute-start(bf16[32,2176]{1,0:T(8,128)(2,1)S(1)} %get-tuple-element.103), channel_id=1, source_target_pairs={{0,8},{4,12},{8,0},{12,4},{1,9},{5,13},{9,1},{13,5},{2,10},{6,14},... | collective-permute-start | bytes 417800 | tf_op jit(solution)/shard_map/ppermute | solution.py:305
  67.7 5.4 %product.9 = (bf16[32,2176]{1,0:T(8,128)(2,1)S(1)}, bf16[32,2176]{1,0:T(8,128)(2,1)S(1)}) custom-call(f32[8,128]{1,0:T(8,128)S(1)} %get-tuple-element.63._, bf16[128,7424]{1,0:T(8,128)(2,1)S(1)} %get-tuple-element.64.own_ref, bf16[128,7424]{1,0:T(8,128)(2,1)S(1)} %collective-permute-done.2.other_ref, bf16[32,7424]{1,0:T(8,128)(2,1)S(1)} %collective-permute-done.10.refs_0_, ...), custom_call_target="tpu_custom_call" | custom-call | flops 1 | bytes 1 | tf_op jit(solution)/shard_map/product/pallas_call | solution.py:239
  73.5 1.9 %collective-permute-done.16.refs_5_ = bf16[32,2176]{1,0:T(8,128)(2,1)S(1)} collective-permute-done((bf16[32,2176]{1,0:T(8,128)(2,1)S(1)}, bf16[32,2176]{1,0:T(8,128)(2,1)S(1)}, u32[]{:S(2)}, u32[]{:S(2)}) %collective-permute-start.16) | collective-permute-done | bytes 139296 | tf_op jit(solution)/shard_map/ppermute | solution.py:305
  75.9 2.7 %collective-permute-done.19.far_b = bf16[32,2176]{1,0:T(8,128)(2,1)S(1)} collective-permute-done((bf16[32,2176]{1,0:T(8,128)(2,1)S(1)}, bf16[32,2176]{1,0:T(8,128)(2,1)S(1)}, u32[]{:S(2)}, u32[]{:S(2)}) %collective-permute-start.19) | collective-permute-done | bytes 139296 | tf_op jit(solution)/shard_map/ppermute | solution.py:292
  78.7 2.5 %collective-permute-start.21 = (bf16[32,2176]{1,0:T(8,128)(2,1)S(1)}, bf16[32,2176]{1,0:T(8,128)(2,1)S(1)}, u32[]{:S(2)}, u32[]{:S(2)}) collective-permute-start(bf16[32,2176]{1,0:T(8,128)(2,1)S(1)} %get-tuple-element.114), channel_id=1, source_target_pairs={{0,8},{4,12},{8,0},{12,4},{1,9},{5,13},{9,1},{13,5},{2,10},{6,14},... | collective-permute-start | bytes 417800 | tf_op jit(solution)/shard_map/ppermute | solution.py:307
  81.2 6.5 %collective-permute-done.20.refs_6_ = bf16[32,2176]{1,0:T(8,128)(2,1)S(1)} collective-permute-done((bf16[32,2176]{1,0:T(8,128)(2,1)S(1)}, bf16[32,2176]{1,0:T(8,128)(2,1)S(1)}, u32[]{:S(2)}, u32[]{:S(2)}) %collective-permute-start.20) | collective-permute-done | bytes 139296 | tf_op jit(solution)/shard_map/ppermute | solution.py:305
  87.7 2.0 %collective-permute-done.21.refs_7_ = bf16[32,2176]{1,0:T(8,128)(2,1)S(1)} collective-permute-done((bf16[32,2176]{1,0:T(8,128)(2,1)S(1)}, bf16[32,2176]{1,0:T(8,128)(2,1)S(1)}, u32[]{:S(2)}, u32[]{:S(2)}) %collective-permute-start.21) | collective-permute-done | bytes 139296 | tf_op jit(solution)/shard_map/ppermute | solution.py:307
  89.7 1.3 %last.1 = bf16[128,2048]{1,0:T(8,128)(2,1)} custom-call(bf16[512,2048]{1,0:T(8,128)(2,1)S(1)} %bitcast.6, bf16[32,2176]{1,0:T(8,128)(2,1)S(1)} %get-tuple-element.87.refs_0_, bf16[32,2176]{1,0:T(8,128)(2,1)S(1)} %get-tuple-element.98.refs_1_, bf16[32,2176]{1,0:T(8,128)(2,1)S(1)} %get-tuple-element.106.refs_2_, ...), custom_call_target="tpu_custom_call" | custom-call | tf_op jit(solution)/shard_map/last/pallas_call | solution.py:309
  (52 shorter events, 8.4 us)
Async XLA Ops:
  1.8 15.1 %collective-permute-start.2 = (bf16[128,7424]{1,0:T(8,128)(2,1)S(1)}, bf16[128,7424]{1,0:T(8,128)(2,1)S(1)}, u32[]{:S(2)}, u32[]{:S(2)}) collective-permute-start(bf16[128,7424]{1,0:T(8,128)(2,1)S(1)} %get-tuple-element.64.own_ref), channel_id=1, source_target_pairs={{0,1},{1,0},{2,3},{3,2},{4,5},{5,4},{6,7},{7,6},{8,9},{9,8},{10,11... | collective-permute-start | bytes 5701640 | tf_op jit(solution)/shard_map/ppermute | solution.py:218
  2.3 14.6 %collective-permute-start.1 = (bf16[32,7424]{1,0:T(8,128)(2,1)S(1)}, bf16[32,7424]{1,0:T(8,128)(2,1)S(1)}, u32[]{:S(2)}, u32[]{:S(2)}) collective-permute-start(bf16[32,7424]{1,0:T(8,128)(2,1)S(1)} %get-tuple-element.61), channel_id=1, source_target_pairs={{0,2},{1,3},{2,0},{3,1},{4,6},{5,7},{6,4},{7,5},{8,10},{9,11},{10,... | collective-permute-start | bytes 1425416 | tf_op jit(solution)/shard_map/ppermute | solution.py:217
  4.9 38.2 %collective-permute-start.3 = (bf16[32,7424]{1,0:T(8,128)(2,1)S(1)}, bf16[32,7424]{1,0:T(8,128)(2,1)S(1)}, u32[]{:S(2)}, u32[]{:S(2)}) collective-permute-start(bf16[32,7424]{1,0:T(8,128)(2,1)S(1)} %get-tuple-element.65), channel_id=1, source_target_pairs={{0,2},{1,3},{2,0},{3,1},{4,6},{5,7},{6,4},{7,5},{8,10},{9,11},{10,... | collective-permute-start | bytes 1425416 | tf_op jit(solution)/shard_map/ppermute | solution.py:287
  24.5 19.2 %collective-permute-start.6 = (bf16[64,2176]{1,0:T(8,128)(2,1)S(1)}, bf16[64,2176]{1,0:T(8,128)(2,1)S(1)}, u32[]{:S(2)}, u32[]{:S(2)}) collective-permute-start(bf16[64,2176]{1,0:T(8,128)(2,1)S(1)} %get-tuple-element.78), channel_id=1, source_target_pairs={{0,4},{4,0},{8,12},{12,8},{1,5},{5,1},{9,13},{13,9},{2,6},{6,2},{1... | collective-permute-start | bytes 835592 | tf_op jit(solution)/shard_map/ppermute | solution.py:280
  26.5 2.1 %collective-permute-start.5 = (bf16[32,3712]{1,0:T(8,128)(2,1)S(1)}, bf16[32,3712]{1,0:T(8,128)(2,1)S(1)}, u32[]{:S(2)}, u32[]{:S(2)}) collective-permute-start(bf16[32,3712]{1,0:T(8,128)(2,1)S(1)} %get-tuple-element.121), channel_id=1, source_target_pairs={{0,1},{1,0},{2,3},{3,2},{4,5},{5,4},{6,7},{7,6},{8,9},{9,8},{10,11... | collective-permute-start | bytes 712712 | tf_op jit(solution)/shard_map/ppermute | solution.py:265
  26.6 2.0 %collective-permute-start.4 = (bf16[32,3712]{1,0:T(8,128)(2,1)S(1)}, bf16[32,3712]{1,0:T(8,128)(2,1)S(1)}, u32[]{:S(2)}, u32[]{:S(2)}) collective-permute-start(bf16[32,3712]{1,0:T(8,128)(2,1)S(1)} %get-tuple-element.122), channel_id=1, source_target_pairs={{0,1},{1,0},{2,3},{3,2},{4,5},{5,4},{6,7},{7,6},{8,9},{9,8},{10,11... | collective-permute-start | bytes 712712 | tf_op jit(solution)/shard_map/ppermute | solution.py:265
  27.1 23.8 %collective-permute-start = (bf16[32,7424]{1,0:T(8,128)(2,1)S(1)}, bf16[32,7424]{1,0:T(8,128)(2,1)S(1)}, u32[]{:S(2)}, u32[]{:S(2)}) collective-permute-start(bf16[32,7424]{1,0:T(8,128)(2,1)S(1)} %get-tuple-element.60), channel_id=1, source_target_pairs={{0,2},{1,3},{2,0},{3,1},{4,6},{5,7},{6,4},{7,5},{8,10},{9,11},{10,... | collective-permute-start | bytes 1425416 | tf_op jit(solution)/shard_map/ppermute | solution.py:287
  38.1 7.6 %copy-start.2 = (bf16[7424,512]{1,0:T(8,128)(2,1)S(1)}, bf16[7424,512]{1,0:T(8,128)(2,1)}, u32[]{:S(2)}) copy-start(bf16[7424,512]{1,0:T(8,128)(2,1)} %copy-done) | copy-start | bytes 22806532
  43.1 8.6 %collective-permute-start.9 = (bf16[64,2176]{1,0:T(8,128)(2,1)S(1)}, bf16[64,2176]{1,0:T(8,128)(2,1)S(1)}, u32[]{:S(2)}, u32[]{:S(2)}) collective-permute-start(bf16[64,2176]{1,0:T(8,128)(2,1)S(1)} %get-tuple-element.82), channel_id=1, source_target_pairs={{0,4},{4,0},{8,12},{12,8},{1,5},{5,1},{9,13},{13,9},{2,6},{6,2},{1... | collective-permute-start | bytes 835592 | tf_op jit(solution)/shard_map/ppermute | solution.py:292
  43.7 1.9 %collective-permute-start.8 = (bf16[32,3712]{1,0:T(8,128)(2,1)S(1)}, bf16[32,3712]{1,0:T(8,128)(2,1)S(1)}, u32[]{:S(2)}, u32[]{:S(2)}) collective-permute-start(bf16[32,3712]{1,0:T(8,128)(2,1)S(1)} %get-tuple-element.119), channel_id=1, source_target_pairs={{0,1},{1,0},{2,3},{3,2},{4,5},{5,4},{6,7},{7,6},{8,9},{9,8},{10,11... | collective-permute-start | bytes 712712 | tf_op jit(solution)/shard_map/ppermute | solution.py:265
  43.8 1.8 %collective-permute-start.7 = (bf16[32,3712]{1,0:T(8,128)(2,1)S(1)}, bf16[32,3712]{1,0:T(8,128)(2,1)S(1)}, u32[]{:S(2)}, u32[]{:S(2)}) collective-permute-start(bf16[32,3712]{1,0:T(8,128)(2,1)S(1)} %get-tuple-element.120), channel_id=1, source_target_pairs={{0,1},{1,0},{2,3},{3,2},{4,5},{5,4},{6,7},{7,6},{8,9},{9,8},{10,11... | collective-permute-start | bytes 712712 | tf_op jit(solution)/shard_map/ppermute | solution.py:265
  44.3 16.7 %collective-permute-start.10 = (bf16[32,7424]{1,0:T(8,128)(2,1)S(1)}, bf16[32,7424]{1,0:T(8,128)(2,1)S(1)}, u32[]{:S(2)}, u32[]{:S(2)}) collective-permute-start(bf16[32,7424]{1,0:T(8,128)(2,1)S(1)} %get-tuple-element.88), channel_id=1, source_target_pairs={{0,2},{1,3},{2,0},{3,1},{4,6},{5,7},{6,4},{7,5},{8,10},{9,11},{10,... | collective-permute-start | bytes 1425416 | tf_op jit(solution)/shard_map/ppermute | solution.py:287
  51.9 10.9 %collective-permute-start.13 = (bf16[64,2176]{1,0:T(8,128)(2,1)S(1)}, bf16[64,2176]{1,0:T(8,128)(2,1)S(1)}, u32[]{:S(2)}, u32[]{:S(2)}) collective-permute-start(bf16[64,2176]{1,0:T(8,128)(2,1)S(1)} %get-tuple-element.92), channel_id=1, source_target_pairs={{0,4},{4,0},{8,12},{12,8},{1,5},{5,1},{9,13},{13,9},{2,6},{6,2},{1... | collective-permute-start | bytes 835592 | tf_op jit(solution)/shard_map/ppermute | solution.py:292
  52.7 3.2 %collective-permute-start.12 = (bf16[32,3712]{1,0:T(8,128)(2,1)S(1)}, bf16[32,3712]{1,0:T(8,128)(2,1)S(1)}, u32[]{:S(2)}, u32[]{:S(2)}) collective-permute-start(bf16[32,3712]{1,0:T(8,128)(2,1)S(1)} %get-tuple-element.117), channel_id=1, source_target_pairs={{0,1},{1,0},{2,3},{3,2},{4,5},{5,4},{6,7},{7,6},{8,9},{9,8},{10,11... | collective-permute-start | bytes 712712 | tf_op jit(solution)/shard_map/ppermute | solution.py:265
  52.8 3.1 %collective-permute-start.11 = (bf16[32,3712]{1,0:T(8,128)(2,1)S(1)}, bf16[32,3712]{1,0:T(8,128)(2,1)S(1)}, u32[]{:S(2)}, u32[]{:S(2)}) collective-permute-start(bf16[32,3712]{1,0:T(8,128)(2,1)S(1)} %get-tuple-element.118), channel_id=1, source_target_pairs={{0,1},{1,0},{2,3},{3,2},{4,5},{5,4},{6,7},{7,6},{8,9},{9,8},{10,11... | collective-permute-start | bytes 712712 | tf_op jit(solution)/shard_map/ppermute | solution.py:265
  53.3 8.6 %collective-permute-start.14 = (bf16[32,2176]{1,0:T(8,128)(2,1)S(1)}, bf16[32,2176]{1,0:T(8,128)(2,1)S(1)}, u32[]{:S(2)}, u32[]{:S(2)}) collective-permute-start(bf16[32,2176]{1,0:T(8,128)(2,1)S(1)} %get-tuple-element.93), channel_id=1, source_target_pairs={{0,8},{4,12},{8,0},{12,4},{1,9},{5,13},{9,1},{13,5},{2,10},{6,14},... | collective-permute-start | bytes 417800 | tf_op jit(solution)/shard_map/ppermute | solution.py:305
  62.9 4.8 %collective-permute-start.18 = (bf16[32,3712]{1,0:T(8,128)(2,1)S(1)}, bf16[32,3712]{1,0:T(8,128)(2,1)S(1)}, u32[]{:S(2)}, u32[]{:S(2)}) collective-permute-start(bf16[32,3712]{1,0:T(8,128)(2,1)S(1)} %get-tuple-element.115), channel_id=1, source_target_pairs={{0,1},{1,0},{2,3},{3,2},{4,5},{5,4},{6,7},{7,6},{8,9},{9,8},{10,11... | collective-permute-start | bytes 712712 | tf_op jit(solution)/shard_map/ppermute | solution.py:265
  63.0 4.7 %collective-permute-start.17 = (bf16[32,3712]{1,0:T(8,128)(2,1)S(1)}, bf16[32,3712]{1,0:T(8,128)(2,1)S(1)}, u32[]{:S(2)}, u32[]{:S(2)}) collective-permute-start(bf16[32,3712]{1,0:T(8,128)(2,1)S(1)} %get-tuple-element.116), channel_id=1, source_target_pairs={{0,1},{1,0},{2,3},{3,2},{4,5},{5,4},{6,7},{7,6},{8,9},{9,8},{10,11... | collective-permute-start | bytes 712712 | tf_op jit(solution)/shard_map/ppermute | solution.py:265
  63.5 10.0 %collective-permute-start.15 = (bf16[32,2176]{1,0:T(8,128)(2,1)S(1)}, bf16[32,2176]{1,0:T(8,128)(2,1)S(1)}, u32[]{:S(2)}, u32[]{:S(2)}) collective-permute-start(bf16[32,2176]{1,0:T(8,128)(2,1)S(1)} %get-tuple-element.102), channel_id=1, source_target_pairs={{0,4},{4,0},{8,12},{12,8},{1,5},{5,1},{9,13},{13,9},{2,6},{6,2},{1... | collective-permute-start | bytes 417800 | tf_op jit(solution)/shard_map/ppermute | solution.py:292
  66.1 23.6 %copy-start.7 = (bf16[8,64,2048]{2,1,0:T(8,128)(2,1)S(1)}, bf16[8,64,2048]{2,1,0:T(8,128)(2,1)}, u32[]{:S(2)}) copy-start(bf16[8,64,2048]{2,1,0:T(8,128)(2,1)} %param.8) | copy-start | bytes 6291460
  66.1 9.3 %collective-permute-start.16 = (bf16[32,2176]{1,0:T(8,128)(2,1)S(1)}, bf16[32,2176]{1,0:T(8,128)(2,1)S(1)}, u32[]{:S(2)}, u32[]{:S(2)}) collective-permute-start(bf16[32,2176]{1,0:T(8,128)(2,1)S(1)} %get-tuple-element.103), channel_id=1, source_target_pairs={{0,8},{4,12},{8,0},{12,4},{1,9},{5,13},{9,1},{13,5},{2,10},{6,14},... | collective-permute-start | bytes 417800 | tf_op jit(solution)/shard_map/ppermute | solution.py:305
  73.0 5.5 %collective-permute-start.19 = (bf16[32,2176]{1,0:T(8,128)(2,1)S(1)}, bf16[32,2176]{1,0:T(8,128)(2,1)S(1)}, u32[]{:S(2)}, u32[]{:S(2)}) collective-permute-start(bf16[32,2176]{1,0:T(8,128)(2,1)S(1)} %get-tuple-element.109), channel_id=1, source_target_pairs={{0,4},{4,0},{8,12},{12,8},{1,5},{5,1},{9,13},{13,9},{2,6},{6,2},{1... | collective-permute-start | bytes 417800 | tf_op jit(solution)/shard_map/ppermute | solution.py:292
  75.5 12.3 %collective-permute-start.20 = (bf16[32,2176]{1,0:T(8,128)(2,1)S(1)}, bf16[32,2176]{1,0:T(8,128)(2,1)S(1)}, u32[]{:S(2)}, u32[]{:S(2)}) collective-permute-start(bf16[32,2176]{1,0:T(8,128)(2,1)S(1)} %get-tuple-element.113), channel_id=1, source_target_pairs={{0,8},{4,12},{8,0},{12,4},{1,9},{5,13},{9,1},{13,5},{2,10},{6,14},... | collective-permute-start | bytes 417800 | tf_op jit(solution)/shard_map/ppermute | solution.py:305
  78.7 11.0 %collective-permute-start.21 = (bf16[32,2176]{1,0:T(8,128)(2,1)S(1)}, bf16[32,2176]{1,0:T(8,128)(2,1)S(1)}, u32[]{:S(2)}, u32[]{:S(2)}) collective-permute-start(bf16[32,2176]{1,0:T(8,128)(2,1)S(1)} %get-tuple-element.114), channel_id=1, source_target_pairs={{0,8},{4,12},{8,0},{12,4},{1,9},{5,13},{9,1},{13,5},{2,10},{6,14},... | collective-permute-start | bytes 417800 | tf_op jit(solution)/shard_map/ppermute | solution.py:307
  (6 other events, 27.5 us)

commit v15 on v13

--- a/solution.py
+++ b/solution.py
@@ -288,8 +288,7 @@
             direct[step + 1], keep, parts, hop = after((direct[step + 1], keep, parts, hop))
         else:
             got = lax.ppermute(send, "tensor", next_z)
-            parts, hop = after((parts, hop))
-        if step > 1:
+        if step > 1 and step + 1 < steps:
             gots[step - 2 :] = hop
         if step > 0:
             send = add_part(step - 1)
@@ -297,6 +296,7 @@
                 direct[step + 1], kept[-1] = after((direct[step + 1], kept[-1]))
             gots.append(lax.ppermute(send, "tensor", far_z))
         parts.append((keep, got))
+    parts[-1], gots[-2] = after((parts[-1], gots[-2]))
     gots.append(lax.ppermute(add_part(steps - 1), "tensor", far_z))
 
     return pl.pallas_call(

time: 78 us -> 78 us (level)
  starting transfers between devices: 23.3 us -> 24.6 us
  waiting for transfers between devices: 15.8 us -> 14.5 us
    ppermute x3, waiting for transfers between devices: 8.03 us -> 6.34 us  [paired(): gots.append(lax.ppermute(send, 'tensor', far_z))]
    ppermute x1, starting transfers between devices: 0.18 us -> 1.5 us  [paired(): gots.append(lax.ppermute(add_part(steps - 1), 'tensor', far_z))]
where the time goes in v15:
time: 78 us; the launch traced here: 77.8 us
  Pallas kernels  38.4 us (49%)
  starting transfers between devices  24.6 us (32%)
  waiting for transfers between devices  14.5 us (19%)
    pallas_call x4, Pallas kernels, product(): pl.pallas_call(functools.partial(product_kernel, adapters, units, nears),...  23 us
    pallas_call x1, Pallas kernels, paired(): pl.pallas_call(load_kernel, out_shape=[jax.ShapeDtypeStruct((8, LANES), j...  11.9 us
    ppermute x3, starting transfers between devices, paired(): gots.append(lax.ppermute(send, 'tensor', far_z))  9.19 us
    ppermute x3, waiting for transfers between devices, paired(): gots.append(lax.ppermute(send, 'tensor', far_z))  6.34 us
    ppermute x4, waiting for transfers between devices, paired(): got = lax.ppermute(send, 'tensor', next_z)  5.67 us
    ppermute x4, starting transfers between devices, paired(): got = lax.ppermute(send, 'tensor', next_z)  5.05 us
    ppermute x3, starting transfers between devices, paired(): direct.append(lax.ppermute(pieces[step + 1], 'req', across))  3.52 us
    ppermute x1, starting transfers between devices, paired(): direct = [lax.ppermute(pieces[0], 'req', across)]  2.56 us
  transfers between devices with their start and end apart: 21, of which 7 were waited for; matrix products, arithmetic and copies ran while one was open for 0% of the time, Pallas kernels for 45%

profile of v15, /device:TPU:0, one launch (start us, length us, event | category | flops | bytes accessed | tf_op | source)
XLA Modules:
  0.0 77.8 jit_solution(8257958510781322552)
XLA Ops:
  0.0 1.8 %turn.1 = (bf16[128,7424]{1,0:T(8,128)(2,1)S(1)}, bf16[32,7424]{1,0:T(8,128)(2,1)S(1)}, bf16[32,7424]{1,0:T(8,128)(2,1)S(1)}, bf16[32,7424]{1,0:T(8,128)(2,1)S(1)}, bf16[32,7424]{1,0:T(8,128)(2,1)S(1)}) custom-call(bf16[7392,128]{1,0:T(8,128)(2,1)} %bitcast.8, s32[1,128]{1,0:T(1,128)} %bitcast.9), custom_call_target="tpu_custom_call" | custom-call | tf_op jit(solution)/shard_map/turn/pallas_call | solution.py:197
  1.8 0.5 collective-permute-start.2
  2.3 2.6 %collective-permute-start.1 = (bf16[32,7424]{1,0:T(8,128)(2,1)S(1)}, bf16[32,7424]{1,0:T(8,128)(2,1)S(1)}, u32[]{:S(2)}, u32[]{:S(2)}) collective-permute-start(bf16[32,7424]{1,0:T(8,128)(2,1)S(1)} %get-tuple-element.55), channel_id=1, source_target_pairs={{0,2},{1,3},{2,0},{3,1},{4,6},{5,7},{6,4},{7,5},{8,10},{9,11},{10,... | collective-permute-start | bytes 1425416 | tf_op jit(solution)/shard_map/ppermute | solution.py:216
  5.0 11.9 %load.1 = (f32[8,128]{1,0:T(8,128)S(1)}, bf16[7424,512]{1,0:T(8,128)(2,1)S(1)}, bf16[7424,512]{1,0:T(8,128)(2,1)S(1)}, bf16[7424,512]{1,0:T(8,128)(2,1)S(1)}, bf...) custom-call(bf16[7392,2048]{1,0:T(8,128)(2,1)} %w_hbm.1, bf16[512,7392]{1,0:T(8,128)(2,1)} %bitcast.7), custom_call_target="tpu_custom_call" | custom-call | flops 1 | bytes 1 | tf_op jit(solution)/shard_map/load/pallas_call | solution.py:220
  17.5 1.9 %collective-permute-start = (bf16[32,7424]{1,0:T(8,128)(2,1)S(1)}, bf16[32,7424]{1,0:T(8,128)(2,1)S(1)}, u32[]{:S(2)}, u32[]{:S(2)}) collective-permute-start(bf16[32,7424]{1,0:T(8,128)(2,1)S(1)} %get-tuple-element.54), channel_id=1, source_target_pairs={{0,2},{1,3},{2,0},{3,1},{4,6},{5,7},{6,4},{7,5},{8,10},{9,11},{10,... | collective-permute-start | bytes 1425416 | tf_op jit(solution)/shard_map/ppermute | solution.py:283
  19.5 7.5 %product.4 = (bf16[96,2176]{1,0:T(8,128)(2,1)S(1)}, bf16[96,2176]{1,0:T(8,128)(2,1)S(1)}) custom-call(f32[8,128]{1,0:T(8,128)S(1)} %get-tuple-element.57._, bf16[128,7424]{1,0:T(8,128)(2,1)S(1)} %get-tuple-element.58.own_ref, bf16[128,7424]{1,0:T(8,128)(2,1)S(1)} %collective-permute-done.2.other_ref, bf16[32,7424]{1,0:T(8,128)(2,1)S(1)} %collective-permute-done.1.direct_ref, ...), custom_call_target="tpu_custom_call" | custom-call | flops 1 | bytes 1 | tf_op jit(solution)/shard_map/product/pallas_call | solution.py:240
  27.0 1.9 %collective-permute-start.8 = (bf16[96,2176]{1,0:T(8,128)(2,1)S(1)}, bf16[96,2176]{1,0:T(8,128)(2,1)S(1)}, u32[]{:S(2)}, u32[]{:S(2)}) collective-permute-start(bf16[96,2176]{1,0:T(8,128)(2,1)S(1)} %get-tuple-element.70), channel_id=1, source_target_pairs={{0,4},{4,0},{8,12},{12,8},{1,5},{5,1},{9,13},{13,9},{2,6},{6,2},{1... | collective-permute-start | bytes 1253384 | tf_op jit(solution)/shard_map/ppermute | solution.py:287
  29.5 1.5 %collective-permute-start.9 = (bf16[32,7424]{1,0:T(8,128)(2,1)S(1)}, bf16[32,7424]{1,0:T(8,128)(2,1)S(1)}, u32[]{:S(2)}, u32[]{:S(2)}) collective-permute-start(bf16[32,7424]{1,0:T(8,128)(2,1)S(1)} %get-tuple-element.76), channel_id=1, source_target_pairs={{0,2},{1,3},{2,0},{3,1},{4,6},{5,7},{6,4},{7,5},{8,10},{9,11},{10,... | collective-permute-start | bytes 1425416 | tf_op jit(solution)/shard_map/ppermute | solution.py:283
  31.0 5.3 %product.5 = (bf16[64,2176]{1,0:T(8,128)(2,1)S(1)}, bf16[64,2176]{1,0:T(8,128)(2,1)S(1)}) custom-call(f32[8,128]{1,0:T(8,128)S(1)} %get-tuple-element.57._, bf16[128,7424]{1,0:T(8,128)(2,1)S(1)} %get-tuple-element.58.own_ref, bf16[128,7424]{1,0:T(8,128)(2,1)S(1)} %collective-permute-done.2.other_ref, bf16[32,7424]{1,0:T(8,128)(2,1)S(1)} %collective-permute-done.3.direct_ref, ...), custom_call_target="tpu_custom_call" | custom-call | flops 1 | bytes 1 | tf_op jit(solution)/shard_map/product/pallas_call | solution.py:240
  36.2 0.5 collective-permute-start.12
  37.0 1.6 %collective-permute-done.8.near_b.far_b = bf16[96,2176]{1,0:T(8,128)(2,1)S(1)} collective-permute-done((bf16[96,2176]{1,0:T(8,128)(2,1)S(1)}, bf16[96,2176]{1,0:T(8,128)(2,1)S(1)}, u32[]{:S(2)}, u32[]{:S(2)}) %collective-permute-start.8) | collective-permute-done | bytes 417824 | tf_op jit(solution)/shard_map/ppermute | solution.py:287
  39.3 2.6 %collective-permute-start.13 = (bf16[32,2176]{1,0:T(8,128)(2,1)S(1)}, bf16[32,2176]{1,0:T(8,128)(2,1)S(1)}, u32[]{:S(2)}, u32[]{:S(2)}) collective-permute-start(bf16[32,2176]{1,0:T(8,128)(2,1)S(1)} %get-tuple-element.81), channel_id=1, source_target_pairs={{0,8},{4,12},{8,0},{12,4},{1,9},{5,13},{9,1},{13,5},{2,10},{6,14},... | collective-permute-start | bytes 417800 | tf_op jit(solution)/shard_map/ppermute | solution.py:297
  41.9 5.1 %product.6 = (bf16[64,2176]{1,0:T(8,128)(2,1)S(1)}, bf16[64,2176]{1,0:T(8,128)(2,1)S(1)}) custom-call(f32[8,128]{1,0:T(8,128)S(1)} %get-tuple-element.57._, bf16[128,7424]{1,0:T(8,128)(2,1)S(1)} %get-tuple-element.58.own_ref, bf16[128,7424]{1,0:T(8,128)(2,1)S(1)} %collective-permute-done.2.other_ref, bf16[32,7424]{1,0:T(8,128)(2,1)S(1)} %collective-permute-done.direct_ref, ...), custom_call_target="tpu_custom_call" | custom-call | flops 1 | bytes 1 | tf_op jit(solution)/shard_map/product/pallas_call | solution.py:240
  47.0 0.9 %collective-permute-done.12.near_b.far_b = bf16[64,2176]{1,0:T(8,128)(2,1)S(1)} collective-permute-done((bf16[64,2176]{1,0:T(8,128)(2,1)S(1)}, bf16[64,2176]{1,0:T(8,128)(2,1)S(1)}, u32[]{:S(2)}, u32[]{:S(2)}) %collective-permute-start.12) | collective-permute-done | bytes 278560 | tf_op jit(solution)/shard_map/ppermute | solution.py:287
  48.6 2.6 %collective-permute-start.14 = (bf16[64,2176]{1,0:T(8,128)(2,1)S(1)}, bf16[64,2176]{1,0:T(8,128)(2,1)S(1)}, u32[]{:S(2)}, u32[]{:S(2)}) collective-permute-start(bf16[64,2176]{1,0:T(8,128)(2,1)S(1)} %get-tuple-element.88), channel_id=1, source_target_pairs={{0,4},{4,0},{8,12},{12,8},{1,5},{5,1},{9,13},{13,9},{2,6},{6,2},{1... | collective-permute-start | bytes 835592 | tf_op jit(solution)/shard_map/ppermute | solution.py:287
  51.2 3.2 %collective-permute-start.18 = (bf16[32,2176]{1,0:T(8,128)(2,1)S(1)}, bf16[32,2176]{1,0:T(8,128)(2,1)S(1)}, u32[]{:S(2)}, u32[]{:S(2)}) collective-permute-start(bf16[32,2176]{1,0:T(8,128)(2,1)S(1)} %get-tuple-element.95), channel_id=1, source_target_pairs={{0,8},{4,12},{8,0},{12,4},{1,9},{5,13},{9,1},{13,5},{2,10},{6,14},... | collective-permute-start | bytes 417800 | tf_op jit(solution)/shard_map/ppermute | solution.py:297
  54.4 5.2 %product.7 = (bf16[32,2176]{1,0:T(8,128)(2,1)S(1)}, bf16[32,2176]{1,0:T(8,128)(2,1)S(1)}) custom-call(f32[8,128]{1,0:T(8,128)S(1)} %get-tuple-element.57._, bf16[128,7424]{1,0:T(8,128)(2,1)S(1)} %get-tuple-element.58.own_ref, bf16[128,7424]{1,0:T(8,128)(2,1)S(1)} %collective-permute-done.2.other_ref, bf16[32,7424]{1,0:T(8,128)(2,1)S(1)} %collective-permute-done.9.direct_ref, ...), custom_call_target="tpu_custom_call" | custom-call | flops 1 | bytes 1 | tf_op jit(solution)/shard_map/product/pallas_call | solution.py:240
  59.6 1.4 %collective-permute-done.14.near_b.far_b = bf16[64,2176]{1,0:T(8,128)(2,1)S(1)} collective-permute-done((bf16[64,2176]{1,0:T(8,128)(2,1)S(1)}, bf16[64,2176]{1,0:T(8,128)(2,1)S(1)}, u32[]{:S(2)}, u32[]{:S(2)}) %collective-permute-start.14) | collective-permute-done | bytes 278560 | tf_op jit(solution)/shard_map/ppermute | solution.py:287
  61.1 3.4 %collective-permute-start.19 = (bf16[32,2176]{1,0:T(8,128)(2,1)S(1)}, bf16[32,2176]{1,0:T(8,128)(2,1)S(1)}, u32[]{:S(2)}, u32[]{:S(2)}) collective-permute-start(bf16[32,2176]{1,0:T(8,128)(2,1)S(1)} %get-tuple-element.101), channel_id=1, source_target_pairs={{0,8},{4,12},{8,0},{12,4},{1,9},{5,13},{9,1},{13,5},{2,10},{6,14},... | collective-permute-start | bytes 417800 | tf_op jit(solution)/shard_map/ppermute | solution.py:297
  64.5 1.8 %collective-permute-done.17.far_b = bf16[32,2176]{1,0:T(8,128)(2,1)S(1)} collective-permute-done((bf16[32,2176]{1,0:T(8,128)(2,1)S(1)}, bf16[32,2176]{1,0:T(8,128)(2,1)S(1)}, u32[]{:S(2)}, u32[]{:S(2)}) %collective-permute-start.17) | collective-permute-done | bytes 139296 | tf_op jit(solution)/shard_map/ppermute | solution.py:290
  66.5 1.5 %collective-permute-start.20 = (bf16[32,2176]{1,0:T(8,128)(2,1)S(1)}, bf16[32,2176]{1,0:T(8,128)(2,1)S(1)}, u32[]{:S(2)}, u32[]{:S(2)}) collective-permute-start(bf16[32,2176]{1,0:T(8,128)(2,1)S(1)} %get-tuple-element.102), channel_id=1, source_target_pairs={{0,8},{4,12},{8,0},{12,4},{1,9},{5,13},{9,1},{13,5},{2,10},{6,14},... | collective-permute-start | bytes 417800 | tf_op jit(solution)/shard_map/ppermute | solution.py:300
  67.9 6.3 %collective-permute-done.19.refs_6_ = bf16[32,2176]{1,0:T(8,128)(2,1)S(1)} collective-permute-done((bf16[32,2176]{1,0:T(8,128)(2,1)S(1)}, bf16[32,2176]{1,0:T(8,128)(2,1)S(1)}, u32[]{:S(2)}, u32[]{:S(2)}) %collective-permute-start.19) | collective-permute-done | bytes 139296 | tf_op jit(solution)/shard_map/ppermute | solution.py:297
  74.3 2.2 %collective-permute-done.20.refs_7_ = bf16[32,2176]{1,0:T(8,128)(2,1)S(1)} collective-permute-done((bf16[32,2176]{1,0:T(8,128)(2,1)S(1)}, bf16[32,2176]{1,0:T(8,128)(2,1)S(1)}, u32[]{:S(2)}, u32[]{:S(2)}) %collective-permute-start.20) | collective-permute-done | bytes 139296 | tf_op jit(solution)/shard_map/ppermute | solution.py:300
  76.5 1.3 %last.1 = bf16[128,2048]{1,0:T(8,128)(2,1)} custom-call(bf16[512,2048]{1,0:T(8,128)(2,1)S(1)} %bitcast.6, bf16[32,2176]{1,0:T(8,128)(2,1)S(1)} %get-tuple-element.75.refs_0_, bf16[32,2176]{1,0:T(8,128)(2,1)S(1)} %get-tuple-element.86.refs_1_, bf16[32,2176]{1,0:T(8,128)(2,1)S(1)} %get-tuple-element.89.refs_2_, ...), custom_call_target="tpu_custom_call" | custom-call | tf_op jit(solution)/shard_map/last/pallas_call | solution.py:302
  (35 shorter events, 3.2 us)
Async XLA Ops:
  1.8 17.6 %collective-permute-start.2 = (bf16[128,7424]{1,0:T(8,128)(2,1)S(1)}, bf16[128,7424]{1,0:T(8,128)(2,1)S(1)}, u32[]{:S(2)}, u32[]{:S(2)}) collective-permute-start(bf16[128,7424]{1,0:T(8,128)(2,1)S(1)} %get-tuple-element.58.own_ref), channel_id=1, source_target_pairs={{0,1},{1,0},{2,3},{3,2},{4,5},{5,4},{6,7},{7,6},{8,9},{9,8},{10,11... | collective-permute-start | bytes 5701640 | tf_op jit(solution)/shard_map/ppermute | solution.py:217
  2.3 14.5 %collective-permute-start.1 = (bf16[32,7424]{1,0:T(8,128)(2,1)S(1)}, bf16[32,7424]{1,0:T(8,128)(2,1)S(1)}, u32[]{:S(2)}, u32[]{:S(2)}) collective-permute-start(bf16[32,7424]{1,0:T(8,128)(2,1)S(1)} %get-tuple-element.55), channel_id=1, source_target_pairs={{0,2},{1,3},{2,0},{3,1},{4,6},{5,7},{6,4},{7,5},{8,10},{9,11},{10,... | collective-permute-start | bytes 1425416 | tf_op jit(solution)/shard_map/ppermute | solution.py:216
  4.9 22.1 %collective-permute-start.3 = (bf16[32,7424]{1,0:T(8,128)(2,1)S(1)}, bf16[32,7424]{1,0:T(8,128)(2,1)S(1)}, u32[]{:S(2)}, u32[]{:S(2)}) collective-permute-start(bf16[32,7424]{1,0:T(8,128)(2,1)S(1)} %get-tuple-element.59), channel_id=1, source_target_pairs={{0,2},{1,3},{2,0},{3,1},{4,6},{5,7},{6,4},{7,5},{8,10},{9,11},{10,... | collective-permute-start | bytes 1425416 | tf_op jit(solution)/shard_map/ppermute | solution.py:283
  16.9 2.5 %collective-permute-start.5 = (bf16[32,3712]{1,0:T(8,128)(2,1)S(1)}, bf16[32,3712]{1,0:T(8,128)(2,1)S(1)}, u32[]{:S(2)}, u32[]{:S(2)}) collective-permute-start(bf16[32,3712]{1,0:T(8,128)(2,1)S(1)} %get-tuple-element.109), channel_id=1, source_target_pairs={{0,1},{1,0},{2,3},{3,2},{4,5},{5,4},{6,7},{7,6},{8,9},{9,8},{10,11... | collective-permute-start | bytes 712712 | tf_op jit(solution)/shard_map/ppermute | solution.py:267
  17.1 2.4 %collective-permute-start.4 = (bf16[32,3712]{1,0:T(8,128)(2,1)S(1)}, bf16[32,3712]{1,0:T(8,128)(2,1)S(1)}, u32[]{:S(2)}, u32[]{:S(2)}) collective-permute-start(bf16[32,3712]{1,0:T(8,128)(2,1)S(1)} %get-tuple-element.110), channel_id=1, source_target_pairs={{0,1},{1,0},{2,3},{3,2},{4,5},{5,4},{6,7},{7,6},{8,9},{9,8},{10,11... | collective-permute-start | bytes 712712 | tf_op jit(solution)/shard_map/ppermute | solution.py:267
  17.5 19.5 %collective-permute-start = (bf16[32,7424]{1,0:T(8,128)(2,1)S(1)}, bf16[32,7424]{1,0:T(8,128)(2,1)S(1)}, u32[]{:S(2)}, u32[]{:S(2)}) collective-permute-start(bf16[32,7424]{1,0:T(8,128)(2,1)S(1)} %get-tuple-element.54), channel_id=1, source_target_pairs={{0,2},{1,3},{2,0},{3,1},{4,6},{5,7},{6,4},{7,5},{8,10},{9,11},{10,... | collective-permute-start | bytes 1425416 | tf_op jit(solution)/shard_map/ppermute | solution.py:283
  27.0 11.6 %collective-permute-start.8 = (bf16[96,2176]{1,0:T(8,128)(2,1)S(1)}, bf16[96,2176]{1,0:T(8,128)(2,1)S(1)}, u32[]{:S(2)}, u32[]{:S(2)}) collective-permute-start(bf16[96,2176]{1,0:T(8,128)(2,1)S(1)} %get-tuple-element.70), channel_id=1, source_target_pairs={{0,4},{4,0},{8,12},{12,8},{1,5},{5,1},{9,13},{13,9},{2,6},{6,2},{1... | collective-permute-start | bytes 1253384 | tf_op jit(solution)/shard_map/ppermute | solution.py:287
  28.9 2.1 %collective-permute-start.7 = (bf16[32,3712]{1,0:T(8,128)(2,1)S(1)}, bf16[32,3712]{1,0:T(8,128)(2,1)S(1)}, u32[]{:S(2)}, u32[]{:S(2)}) collective-permute-start(bf16[32,3712]{1,0:T(8,128)(2,1)S(1)} %get-tuple-element.107), channel_id=1, source_target_pairs={{0,1},{1,0},{2,3},{3,2},{4,5},{5,4},{6,7},{7,6},{8,9},{9,8},{10,11... | collective-permute-start | bytes 712712 | tf_op jit(solution)/shard_map/ppermute | solution.py:267
  29.0 2.0 %collective-permute-start.6 = (bf16[32,3712]{1,0:T(8,128)(2,1)S(1)}, bf16[32,3712]{1,0:T(8,128)(2,1)S(1)}, u32[]{:S(2)}, u32[]{:S(2)}) collective-permute-start(bf16[32,3712]{1,0:T(8,128)(2,1)S(1)} %get-tuple-element.108), channel_id=1, source_target_pairs={{0,1},{1,0},{2,3},{3,2},{4,5},{5,4},{6,7},{7,6},{8,9},{9,8},{10,11... | collective-permute-start | bytes 712712 | tf_op jit(solution)/shard_map/ppermute | solution.py:267
  29.5 17.5 %collective-permute-start.9 = (bf16[32,7424]{1,0:T(8,128)(2,1)S(1)}, bf16[32,7424]{1,0:T(8,128)(2,1)S(1)}, u32[]{:S(2)}, u32[]{:S(2)}) collective-permute-start(bf16[32,7424]{1,0:T(8,128)(2,1)S(1)} %get-tuple-element.76), channel_id=1, source_target_pairs={{0,2},{1,3},{2,0},{3,1},{4,6},{5,7},{6,4},{7,5},{8,10},{9,11},{10,... | collective-permute-start | bytes 1425416 | tf_op jit(solution)/shard_map/ppermute | solution.py:283
  36.2 11.6 %collective-permute-start.12 = (bf16[64,2176]{1,0:T(8,128)(2,1)S(1)}, bf16[64,2176]{1,0:T(8,128)(2,1)S(1)}, u32[]{:S(2)}, u32[]{:S(2)}) collective-permute-start(bf16[64,2176]{1,0:T(8,128)(2,1)S(1)} %get-tuple-element.80), channel_id=1, source_target_pairs={{0,4},{4,0},{8,12},{12,8},{1,5},{5,1},{9,13},{13,9},{2,6},{6,2},{1... | collective-permute-start | bytes 835592 | tf_op jit(solution)/shard_map/ppermute | solution.py:287
  38.7 3.2 %collective-permute-start.11 = (bf16[32,3712]{1,0:T(8,128)(2,1)S(1)}, bf16[32,3712]{1,0:T(8,128)(2,1)S(1)}, u32[]{:S(2)}, u32[]{:S(2)}) collective-permute-start(bf16[32,3712]{1,0:T(8,128)(2,1)S(1)} %get-tuple-element.105), channel_id=1, source_target_pairs={{0,1},{1,0},{2,3},{3,2},{4,5},{5,4},{6,7},{7,6},{8,9},{9,8},{10,11... | collective-permute-start | bytes 712712 | tf_op jit(solution)/shard_map/ppermute | solution.py:267
  38.8 3.1 %collective-permute-start.10 = (bf16[32,3712]{1,0:T(8,128)(2,1)S(1)}, bf16[32,3712]{1,0:T(8,128)(2,1)S(1)}, u32[]{:S(2)}, u32[]{:S(2)}) collective-permute-start(bf16[32,3712]{1,0:T(8,128)(2,1)S(1)} %get-tuple-element.106), channel_id=1, source_target_pairs={{0,1},{1,0},{2,3},{3,2},{4,5},{5,4},{6,7},{7,6},{8,9},{9,8},{10,11... | collective-permute-start | bytes 712712 | tf_op jit(solution)/shard_map/ppermute | solution.py:267
  39.3 8.5 %collective-permute-start.13 = (bf16[32,2176]{1,0:T(8,128)(2,1)S(1)}, bf16[32,2176]{1,0:T(8,128)(2,1)S(1)}, u32[]{:S(2)}, u32[]{:S(2)}) collective-permute-start(bf16[32,2176]{1,0:T(8,128)(2,1)S(1)} %get-tuple-element.81), channel_id=1, source_target_pairs={{0,8},{4,12},{8,0},{12,4},{1,9},{5,13},{9,1},{13,5},{2,10},{6,14},... | collective-permute-start | bytes 417800 | tf_op jit(solution)/shard_map/ppermute | solution.py:297
  48.0 6.4 %collective-permute-start.16 = (bf16[32,3712]{1,0:T(8,128)(2,1)S(1)}, bf16[32,3712]{1,0:T(8,128)(2,1)S(1)}, u32[]{:S(2)}, u32[]{:S(2)}) collective-permute-start(bf16[32,3712]{1,0:T(8,128)(2,1)S(1)} %get-tuple-element.103), channel_id=1, source_target_pairs={{0,1},{1,0},{2,3},{3,2},{4,5},{5,4},{6,7},{7,6},{8,9},{9,8},{10,11... | collective-permute-start | bytes 712712 | tf_op jit(solution)/shard_map/ppermute | solution.py:267
  48.1 6.3 %collective-permute-start.15 = (bf16[32,3712]{1,0:T(8,128)(2,1)S(1)}, bf16[32,3712]{1,0:T(8,128)(2,1)S(1)}, u32[]{:S(2)}, u32[]{:S(2)}) collective-permute-start(bf16[32,3712]{1,0:T(8,128)(2,1)S(1)} %get-tuple-element.104), channel_id=1, source_target_pairs={{0,1},{1,0},{2,3},{3,2},{4,5},{5,4},{6,7},{7,6},{8,9},{9,8},{10,11... | collective-permute-start | bytes 712712 | tf_op jit(solution)/shard_map/ppermute | solution.py:267
  48.6 12.5 %collective-permute-start.14 = (bf16[64,2176]{1,0:T(8,128)(2,1)S(1)}, bf16[64,2176]{1,0:T(8,128)(2,1)S(1)}, u32[]{:S(2)}, u32[]{:S(2)}) collective-permute-start(bf16[64,2176]{1,0:T(8,128)(2,1)S(1)} %get-tuple-element.88), channel_id=1, source_target_pairs={{0,4},{4,0},{8,12},{12,8},{1,5},{5,1},{9,13},{13,9},{2,6},{6,2},{1... | collective-permute-start | bytes 835592 | tf_op jit(solution)/shard_map/ppermute | solution.py:287
  51.2 25.4 %copy-start = (bf16[8,64,2048]{2,1,0:T(8,128)(2,1)S(1)}, bf16[8,64,2048]{2,1,0:T(8,128)(2,1)}, u32[]{:S(2)}) copy-start(bf16[8,64,2048]{2,1,0:T(8,128)(2,1)} %param.8) | copy-start | bytes 6291460
  51.2 13.4 %collective-permute-start.18 = (bf16[32,2176]{1,0:T(8,128)(2,1)S(1)}, bf16[32,2176]{1,0:T(8,128)(2,1)S(1)}, u32[]{:S(2)}, u32[]{:S(2)}) collective-permute-start(bf16[32,2176]{1,0:T(8,128)(2,1)S(1)} %get-tuple-element.95), channel_id=1, source_target_pairs={{0,8},{4,12},{8,0},{12,4},{1,9},{5,13},{9,1},{13,5},{2,10},{6,14},... | collective-permute-start | bytes 417800 | tf_op jit(solution)/shard_map/ppermute | solution.py:297
  59.6 6.8 %collective-permute-start.17 = (bf16[32,2176]{1,0:T(8,128)(2,1)S(1)}, bf16[32,2176]{1,0:T(8,128)(2,1)S(1)}, u32[]{:S(2)}, u32[]{:S(2)}) collective-permute-start(bf16[32,2176]{1,0:T(8,128)(2,1)S(1)} %get-tuple-element.94), channel_id=1, source_target_pairs={{0,4},{4,0},{8,12},{12,8},{1,5},{5,1},{9,13},{13,9},{2,6},{6,2},{1... | collective-permute-start | bytes 417800 | tf_op jit(solution)/shard_map/ppermute | solution.py:290
  61.1 13.2 %collective-permute-start.19 = (bf16[32,2176]{1,0:T(8,128)(2,1)S(1)}, bf16[32,2176]{1,0:T(8,128)(2,1)S(1)}, u32[]{:S(2)}, u32[]{:S(2)}) collective-permute-start(bf16[32,2176]{1,0:T(8,128)(2,1)S(1)} %get-tuple-element.101), channel_id=1, source_target_pairs={{0,8},{4,12},{8,0},{12,4},{1,9},{5,13},{9,1},{13,5},{2,10},{6,14},... | collective-permute-start | bytes 417800 | tf_op jit(solution)/shard_map/ppermute | solution.py:297
  66.5 10.1 %collective-permute-start.20 = (bf16[32,2176]{1,0:T(8,128)(2,1)S(1)}, bf16[32,2176]{1,0:T(8,128)(2,1)S(1)}, u32[]{:S(2)}, u32[]{:S(2)}) collective-permute-start(bf16[32,2176]{1,0:T(8,128)(2,1)S(1)} %get-tuple-element.102), channel_id=1, source_target_pairs={{0,8},{4,12},{8,0},{12,4},{1,9},{5,13},{9,1},{13,5},{2,10},{6,14},... | collective-permute-start | bytes 417800 | tf_op jit(solution)/shard_map/ppermute | solution.py:300

commit v16 on v15

--- a/solution.py
+++ b/solution.py
@@ -12,7 +12,7 @@
 DEPTH = 1024
 TURN = 15
 PIECES = (32, 32, 32, 32)
-CUTS = 2
+CUTS = (2, 2, 2, 1)
 FULL = 128
 MIB = 1 << 20
 
@@ -100,8 +100,8 @@
         keep_ref[at : at + rows, cols] = jnp.where(keep_first, first, second)
 
 
-def product_kernel(adapters, units, nears, _, own_ref, other_ref, direct_ref, *refs):
-    passed_refs, refs = refs[:CUTS], refs[CUTS:]
+def product_kernel(adapters, units, cuts, nears, _, own_ref, other_ref, direct_ref, *refs):
+    passed_refs, refs = refs[:cuts], refs[cuts:]
     *panel_refs, spread_ref, send_ref, keep_ref = refs
     rows = direct_ref.shape[0]
     width = send_ref.shape[1] - LANES
@@ -238,9 +238,9 @@
         nears = [starts[step]] if step + 1 < len(counts) else []
         nears += [starts[-1]] if step == 0 else []
         return pl.pallas_call(
-            functools.partial(product_kernel, adapters, units, nears),
+            functools.partial(product_kernel, adapters, units, len(passed), nears),
             out_shape=[struct((1 + len(nears)) * counts[step], payload)] * 2,
-            in_specs=[in_vmem()] * (4 + CUTS + len(both)),
+            in_specs=[in_vmem()] * (4 + len(passed) + len(both)),
             out_specs=[in_vmem()] * 2,
             compiler_params=params(4),
             cost_estimate=quick,
@@ -260,9 +260,9 @@
             name="add",
         )(*parts[0 if last else step], *parts[step])
 
-    def over_core(part):
+    def over_core(part, cuts):
         tiles = room // LANES
-        ends = [tiles * cut // CUTS * LANES for cut in range(CUTS + 1)]
+        ends = [tiles * cut // cuts * LANES for cut in range(cuts + 1)]
         return [
             lax.ppermute(part[:, at:to], "req", beside) for at, to in zip(ends, ends[1:])
         ]
@@ -278,7 +278,7 @@
         return send
 
     for step in range(steps):
-        passed = over_core(direct[step])
+        passed = over_core(direct[step], CUTS[step])
         if step + 1 < steps:
             direct.append(lax.ppermute(pieces[step + 1], "req", across))
         send, keep = product(step, passed, token)

time: 78 us -> 77.9 us (level)
  starting transfers between devices: 24.6 us -> 23.3 us
  waiting for transfers between devices: 14.5 us -> 15.8 us
    ppermute x4, waiting for transfers between devices: 5.67 us -> 6.64 us  [paired(): got = lax.ppermute(send, 'tensor', next_z)]
    ppermute x8 -> x7, starting transfers between devices: 2.28 us -> 1.78 us  [over_core(): lax.ppermute(part[:, at:to], 'req', beside)]
  transfers between devices with their start and end apart: 21 -> 20, of which waited for: 7 -> 7; matrix products, arithmetic and copies ran while one was open for 0% -> 0% of each run, Pallas kernels for 45% -> 45%
where the time goes in v16:
time: 77.9 us; the launch traced here: 77.7 us
  Pallas kernels  38.3 us (49%)
  starting transfers between devices  23.3 us (30%)
  waiting for transfers between devices  15.8 us (20%)
    pallas_call x4, Pallas kernels, product(): pl.pallas_call(functools.partial(product_kernel, adapters, units, len(pas...  23 us
    pallas_call x1, Pallas kernels, paired(): pl.pallas_call(load_kernel, out_shape=[jax.ShapeDtypeStruct((8, LANES), j...  11.9 us
    ppermute x3, starting transfers between devices, paired(): gots.append(lax.ppermute(send, 'tensor', far_z))  8.78 us
    ppermute x4, waiting for transfers between devices, paired(): got = lax.ppermute(send, 'tensor', next_z)  6.64 us
    ppermute x3, waiting for transfers between devices, paired(): gots.append(lax.ppermute(send, 'tensor', far_z))  6.64 us
    ppermute x4, starting transfers between devices, paired(): got = lax.ppermute(send, 'tensor', next_z)  5.19 us
    ppermute x3, starting transfers between devices, paired(): direct.append(lax.ppermute(pieces[step + 1], 'req', across))  3.52 us
    ppermute x1, starting transfers between devices, paired(): direct = [lax.ppermute(pieces[0], 'req', across)]  2.56 us
  transfers between devices with their start and end apart: 20, of which 7 were waited for; matrix products, arithmetic and copies ran while one was open for 0% of the time, Pallas kernels for 45%

profile of v16, /device:TPU:0, one launch (start us, length us, event | category | flops | bytes accessed | tf_op | source)
XLA Modules:
  0.0 77.7 jit_solution(9055302131393942632)
XLA Ops:
  0.0 1.8 %turn.1 = (bf16[128,7424]{1,0:T(8,128)(2,1)S(1)}, bf16[32,7424]{1,0:T(8,128)(2,1)S(1)}, bf16[32,7424]{1,0:T(8,128)(2,1)S(1)}, bf16[32,7424]{1,0:T(8,128)(2,1)S(1)}, bf16[32,7424]{1,0:T(8,128)(2,1)S(1)}) custom-call(bf16[7392,128]{1,0:T(8,128)(2,1)} %bitcast.8, s32[1,128]{1,0:T(1,128)} %bitcast.9), custom_call_target="tpu_custom_call" | custom-call | tf_op jit(solution)/shard_map/turn/pallas_call | solution.py:197
  1.8 0.5 collective-permute-start.2
  2.3 2.6 %collective-permute-start.1 = (bf16[32,7424]{1,0:T(8,128)(2,1)S(1)}, bf16[32,7424]{1,0:T(8,128)(2,1)S(1)}, u32[]{:S(2)}, u32[]{:S(2)}) collective-permute-start(bf16[32,7424]{1,0:T(8,128)(2,1)S(1)} %get-tuple-element.55), channel_id=1, source_target_pairs={{0,2},{1,3},{2,0},{3,1},{4,6},{5,7},{6,4},{7,5},{8,10},{9,11},{10,... | collective-permute-start | bytes 1425416 | tf_op jit(solution)/shard_map/ppermute | solution.py:216
  5.0 11.9 %load.1 = (f32[8,128]{1,0:T(8,128)S(1)}, bf16[7424,512]{1,0:T(8,128)(2,1)S(1)}, bf16[7424,512]{1,0:T(8,128)(2,1)S(1)}, bf16[7424,512]{1,0:T(8,128)(2,1)S(1)}, bf...) custom-call(bf16[7392,2048]{1,0:T(8,128)(2,1)} %w_hbm.1, bf16[512,7392]{1,0:T(8,128)(2,1)} %bitcast.7), custom_call_target="tpu_custom_call" | custom-call | flops 1 | bytes 1 | tf_op jit(solution)/shard_map/load/pallas_call | solution.py:220
  17.5 1.9 %collective-permute-start = (bf16[32,7424]{1,0:T(8,128)(2,1)S(1)}, bf16[32,7424]{1,0:T(8,128)(2,1)S(1)}, u32[]{:S(2)}, u32[]{:S(2)}) collective-permute-start(bf16[32,7424]{1,0:T(8,128)(2,1)S(1)} %get-tuple-element.54), channel_id=1, source_target_pairs={{0,2},{1,3},{2,0},{3,1},{4,6},{5,7},{6,4},{7,5},{8,10},{9,11},{10,... | collective-permute-start | bytes 1425416 | tf_op jit(solution)/shard_map/ppermute | solution.py:283
  19.5 7.5 %product.4 = (bf16[96,2176]{1,0:T(8,128)(2,1)S(1)}, bf16[96,2176]{1,0:T(8,128)(2,1)S(1)}) custom-call(f32[8,128]{1,0:T(8,128)S(1)} %get-tuple-element.57._, bf16[128,7424]{1,0:T(8,128)(2,1)S(1)} %get-tuple-element.58.own_ref, bf16[128,7424]{1,0:T(8,128)(2,1)S(1)} %collective-permute-done.2.other_ref, bf16[32,7424]{1,0:T(8,128)(2,1)S(1)} %collective-permute-done.1.direct_ref, ...), custom_call_target="tpu_custom_call" | custom-call | flops 1 | bytes 1 | tf_op jit(solution)/shard_map/product/pallas_call | solution.py:240
  27.0 1.9 %collective-permute-start.8 = (bf16[96,2176]{1,0:T(8,128)(2,1)S(1)}, bf16[96,2176]{1,0:T(8,128)(2,1)S(1)}, u32[]{:S(2)}, u32[]{:S(2)}) collective-permute-start(bf16[96,2176]{1,0:T(8,128)(2,1)S(1)} %get-tuple-element.70), channel_id=1, source_target_pairs={{0,4},{4,0},{8,12},{12,8},{1,5},{5,1},{9,13},{13,9},{2,6},{6,2},{1... | collective-permute-start | bytes 1253384 | tf_op jit(solution)/shard_map/ppermute | solution.py:287
  29.5 1.5 %collective-permute-start.9 = (bf16[32,7424]{1,0:T(8,128)(2,1)S(1)}, bf16[32,7424]{1,0:T(8,128)(2,1)S(1)}, u32[]{:S(2)}, u32[]{:S(2)}) collective-permute-start(bf16[32,7424]{1,0:T(8,128)(2,1)S(1)} %get-tuple-element.76), channel_id=1, source_target_pairs={{0,2},{1,3},{2,0},{3,1},{4,6},{5,7},{6,4},{7,5},{8,10},{9,11},{10,... | collective-permute-start | bytes 1425416 | tf_op jit(solution)/shard_map/ppermute | solution.py:283
  31.0 5.3 %product.5 = (bf16[64,2176]{1,0:T(8,128)(2,1)S(1)}, bf16[64,2176]{1,0:T(8,128)(2,1)S(1)}) custom-call(f32[8,128]{1,0:T(8,128)S(1)} %get-tuple-element.57._, bf16[128,7424]{1,0:T(8,128)(2,1)S(1)} %get-tuple-element.58.own_ref, bf16[128,7424]{1,0:T(8,128)(2,1)S(1)} %collective-permute-done.2.other_ref, bf16[32,7424]{1,0:T(8,128)(2,1)S(1)} %collective-permute-done.3.direct_ref, ...), custom_call_target="tpu_custom_call" | custom-call | flops 1 | bytes 1 | tf_op jit(solution)/shard_map/product/pallas_call | solution.py:240
  36.2 0.5 collective-permute-start.12
  37.0 1.6 %collective-permute-done.8.near_b.far_b = bf16[96,2176]{1,0:T(8,128)(2,1)S(1)} collective-permute-done((bf16[96,2176]{1,0:T(8,128)(2,1)S(1)}, bf16[96,2176]{1,0:T(8,128)(2,1)S(1)}, u32[]{:S(2)}, u32[]{:S(2)}) %collective-permute-start.8) | collective-permute-done | bytes 417824 | tf_op jit(solution)/shard_map/ppermute | solution.py:287
  39.3 2.6 %collective-permute-start.13 = (bf16[32,2176]{1,0:T(8,128)(2,1)S(1)}, bf16[32,2176]{1,0:T(8,128)(2,1)S(1)}, u32[]{:S(2)}, u32[]{:S(2)}) collective-permute-start(bf16[32,2176]{1,0:T(8,128)(2,1)S(1)} %get-tuple-element.81), channel_id=1, source_target_pairs={{0,8},{4,12},{8,0},{12,4},{1,9},{5,13},{9,1},{13,5},{2,10},{6,14},... | collective-permute-start | bytes 417800 | tf_op jit(solution)/shard_map/ppermute | solution.py:297
  41.9 5.1 %product.6 = (bf16[64,2176]{1,0:T(8,128)(2,1)S(1)}, bf16[64,2176]{1,0:T(8,128)(2,1)S(1)}) custom-call(f32[8,128]{1,0:T(8,128)S(1)} %get-tuple-element.57._, bf16[128,7424]{1,0:T(8,128)(2,1)S(1)} %get-tuple-element.58.own_ref, bf16[128,7424]{1,0:T(8,128)(2,1)S(1)} %collective-permute-done.2.other_ref, bf16[32,7424]{1,0:T(8,128)(2,1)S(1)} %collective-permute-done.direct_ref, ...), custom_call_target="tpu_custom_call" | custom-call | flops 1 | bytes 1 | tf_op jit(solution)/shard_map/product/pallas_call | solution.py:240
  47.0 0.9 %collective-permute-done.12.near_b.far_b = bf16[64,2176]{1,0:T(8,128)(2,1)S(1)} collective-permute-done((bf16[64,2176]{1,0:T(8,128)(2,1)S(1)}, bf16[64,2176]{1,0:T(8,128)(2,1)S(1)}, u32[]{:S(2)}, u32[]{:S(2)}) %collective-permute-start.12) | collective-permute-done | bytes 278560 | tf_op jit(solution)/shard_map/ppermute | solution.py:287
  48.0 2.7 %collective-permute-start.14 = (bf16[64,2176]{1,0:T(8,128)(2,1)S(1)}, bf16[64,2176]{1,0:T(8,128)(2,1)S(1)}, u32[]{:S(2)}, u32[]{:S(2)}) collective-permute-start(bf16[64,2176]{1,0:T(8,128)(2,1)S(1)} %get-tuple-element.88), channel_id=1, source_target_pairs={{0,4},{4,0},{8,12},{12,8},{1,5},{5,1},{9,13},{13,9},{2,6},{6,2},{1... | collective-permute-start | bytes 835592 | tf_op jit(solution)/shard_map/ppermute | solution.py:287
  50.7 3.2 %collective-permute-start.17 = (bf16[32,2176]{1,0:T(8,128)(2,1)S(1)}, bf16[32,2176]{1,0:T(8,128)(2,1)S(1)}, u32[]{:S(2)}, u32[]{:S(2)}) collective-permute-start(bf16[32,2176]{1,0:T(8,128)(2,1)S(1)} %get-tuple-element.95), channel_id=1, source_target_pairs={{0,8},{4,12},{8,0},{12,4},{1,9},{5,13},{9,1},{13,5},{2,10},{6,14},... | collective-permute-start | bytes 417800 | tf_op jit(solution)/shard_map/ppermute | solution.py:297
  53.9 5.1 %product.7 = (bf16[32,2176]{1,0:T(8,128)(2,1)S(1)}, bf16[32,2176]{1,0:T(8,128)(2,1)S(1)}) custom-call(f32[8,128]{1,0:T(8,128)S(1)} %get-tuple-element.57._, bf16[128,7424]{1,0:T(8,128)(2,1)S(1)} %get-tuple-element.58.own_ref, bf16[128,7424]{1,0:T(8,128)(2,1)S(1)} %collective-permute-done.2.other_ref, bf16[32,7424]{1,0:T(8,128)(2,1)S(1)} %collective-permute-done.9.direct_ref, ...), custom_call_target="tpu_custom_call" | custom-call | flops 1 | bytes 1 | tf_op jit(solution)/shard_map/product/pallas_call | solution.py:240
  59.2 1.7 %collective-permute-done.14.near_b.far_b = bf16[64,2176]{1,0:T(8,128)(2,1)S(1)} collective-permute-done((bf16[64,2176]{1,0:T(8,128)(2,1)S(1)}, bf16[64,2176]{1,0:T(8,128)(2,1)S(1)}, u32[]{:S(2)}, u32[]{:S(2)}) %collective-permute-start.14) | collective-permute-done | bytes 278560 | tf_op jit(solution)/shard_map/ppermute | solution.py:287
  61.0 3.0 %collective-permute-start.18 = (bf16[32,2176]{1,0:T(8,128)(2,1)S(1)}, bf16[32,2176]{1,0:T(8,128)(2,1)S(1)}, u32[]{:S(2)}, u32[]{:S(2)}) collective-permute-start(bf16[32,2176]{1,0:T(8,128)(2,1)S(1)} %get-tuple-element.101), channel_id=1, source_target_pairs={{0,8},{4,12},{8,0},{12,4},{1,9},{5,13},{9,1},{13,5},{2,10},{6,14},... | collective-permute-start | bytes 417800 | tf_op jit(solution)/shard_map/ppermute | solution.py:297
  64.0 2.4 %collective-permute-done.16.far_b = bf16[32,2176]{1,0:T(8,128)(2,1)S(1)} collective-permute-done((bf16[32,2176]{1,0:T(8,128)(2,1)S(1)}, bf16[32,2176]{1,0:T(8,128)(2,1)S(1)}, u32[]{:S(2)}, u32[]{:S(2)}) %collective-permute-start.16) | collective-permute-done | bytes 139296 | tf_op jit(solution)/shard_map/ppermute | solution.py:290
  66.5 1.0 %collective-permute-start.19 = (bf16[32,2176]{1,0:T(8,128)(2,1)S(1)}, bf16[32,2176]{1,0:T(8,128)(2,1)S(1)}, u32[]{:S(2)}, u32[]{:S(2)}) collective-permute-start(bf16[32,2176]{1,0:T(8,128)(2,1)S(1)} %get-tuple-element.102), channel_id=1, source_target_pairs={{0,8},{4,12},{8,0},{12,4},{1,9},{5,13},{9,1},{13,5},{2,10},{6,14},... | collective-permute-start | bytes 417800 | tf_op jit(solution)/shard_map/ppermute | solution.py:300
  67.5 6.6 %collective-permute-done.18.refs_6_ = bf16[32,2176]{1,0:T(8,128)(2,1)S(1)} collective-permute-done((bf16[32,2176]{1,0:T(8,128)(2,1)S(1)}, bf16[32,2176]{1,0:T(8,128)(2,1)S(1)}, u32[]{:S(2)}, u32[]{:S(2)}) %collective-permute-start.18) | collective-permute-done | bytes 139296 | tf_op jit(solution)/shard_map/ppermute | solution.py:297
  74.2 2.2 %collective-permute-done.19.refs_7_ = bf16[32,2176]{1,0:T(8,128)(2,1)S(1)} collective-permute-done((bf16[32,2176]{1,0:T(8,128)(2,1)S(1)}, bf16[32,2176]{1,0:T(8,128)(2,1)S(1)}, u32[]{:S(2)}, u32[]{:S(2)}) %collective-permute-start.19) | collective-permute-done | bytes 139296 | tf_op jit(solution)/shard_map/ppermute | solution.py:300
  76.4 1.3 %last.1 = bf16[128,2048]{1,0:T(8,128)(2,1)} custom-call(bf16[512,2048]{1,0:T(8,128)(2,1)S(1)} %bitcast.6, bf16[32,2176]{1,0:T(8,128)(2,1)S(1)} %get-tuple-element.75.refs_0_, bf16[32,2176]{1,0:T(8,128)(2,1)S(1)} %get-tuple-element.86.refs_1_, bf16[32,2176]{1,0:T(8,128)(2,1)S(1)} %get-tuple-element.89.refs_2_, ...), custom_call_target="tpu_custom_call" | custom-call | tf_op jit(solution)/shard_map/last/pallas_call | solution.py:302
  (32 shorter events, 2.8 us)
Async XLA Ops:
  1.8 17.6 %collective-permute-start.2 = (bf16[128,7424]{1,0:T(8,128)(2,1)S(1)}, bf16[128,7424]{1,0:T(8,128)(2,1)S(1)}, u32[]{:S(2)}, u32[]{:S(2)}) collective-permute-start(bf16[128,7424]{1,0:T(8,128)(2,1)S(1)} %get-tuple-element.58.own_ref), channel_id=1, source_target_pairs={{0,1},{1,0},{2,3},{3,2},{4,5},{5,4},{6,7},{7,6},{8,9},{9,8},{10,11... | collective-permute-start | bytes 5701640 | tf_op jit(solution)/shard_map/ppermute | solution.py:217
  2.3 14.5 %collective-permute-start.1 = (bf16[32,7424]{1,0:T(8,128)(2,1)S(1)}, bf16[32,7424]{1,0:T(8,128)(2,1)S(1)}, u32[]{:S(2)}, u32[]{:S(2)}) collective-permute-start(bf16[32,7424]{1,0:T(8,128)(2,1)S(1)} %get-tuple-element.55), channel_id=1, source_target_pairs={{0,2},{1,3},{2,0},{3,1},{4,6},{5,7},{6,4},{7,5},{8,10},{9,11},{10,... | collective-permute-start | bytes 1425416 | tf_op jit(solution)/shard_map/ppermute | solution.py:216
  4.9 22.1 %collective-permute-start.3 = (bf16[32,7424]{1,0:T(8,128)(2,1)S(1)}, bf16[32,7424]{1,0:T(8,128)(2,1)S(1)}, u32[]{:S(2)}, u32[]{:S(2)}) collective-permute-start(bf16[32,7424]{1,0:T(8,128)(2,1)S(1)} %get-tuple-element.59), channel_id=1, source_target_pairs={{0,2},{1,3},{2,0},{3,1},{4,6},{5,7},{6,4},{7,5},{8,10},{9,11},{10,... | collective-permute-start | bytes 1425416 | tf_op jit(solution)/shard_map/ppermute | solution.py:283
  16.9 2.5 %collective-permute-start.5 = (bf16[32,3712]{1,0:T(8,128)(2,1)S(1)}, bf16[32,3712]{1,0:T(8,128)(2,1)S(1)}, u32[]{:S(2)}, u32[]{:S(2)}) collective-permute-start(bf16[32,3712]{1,0:T(8,128)(2,1)S(1)} %get-tuple-element.107), channel_id=1, source_target_pairs={{0,1},{1,0},{2,3},{3,2},{4,5},{5,4},{6,7},{7,6},{8,9},{9,8},{10,11... | collective-permute-start | bytes 712712 | tf_op jit(solution)/shard_map/ppermute | solution.py:267
  17.1 2.4 %collective-permute-start.4 = (bf16[32,3712]{1,0:T(8,128)(2,1)S(1)}, bf16[32,3712]{1,0:T(8,128)(2,1)S(1)}, u32[]{:S(2)}, u32[]{:S(2)}) collective-permute-start(bf16[32,3712]{1,0:T(8,128)(2,1)S(1)} %get-tuple-element.108), channel_id=1, source_target_pairs={{0,1},{1,0},{2,3},{3,2},{4,5},{5,4},{6,7},{7,6},{8,9},{9,8},{10,11... | collective-permute-start | bytes 712712 | tf_op jit(solution)/shard_map/ppermute | solution.py:267
  17.5 19.5 %collective-permute-start = (bf16[32,7424]{1,0:T(8,128)(2,1)S(1)}, bf16[32,7424]{1,0:T(8,128)(2,1)S(1)}, u32[]{:S(2)}, u32[]{:S(2)}) collective-permute-start(bf16[32,7424]{1,0:T(8,128)(2,1)S(1)} %get-tuple-element.54), channel_id=1, source_target_pairs={{0,2},{1,3},{2,0},{3,1},{4,6},{5,7},{6,4},{7,5},{8,10},{9,11},{10,... | collective-permute-start | bytes 1425416 | tf_op jit(solution)/shard_map/ppermute | solution.py:283
  27.0 11.6 %collective-permute-start.8 = (bf16[96,2176]{1,0:T(8,128)(2,1)S(1)}, bf16[96,2176]{1,0:T(8,128)(2,1)S(1)}, u32[]{:S(2)}, u32[]{:S(2)}) collective-permute-start(bf16[96,2176]{1,0:T(8,128)(2,1)S(1)} %get-tuple-element.70), channel_id=1, source_target_pairs={{0,4},{4,0},{8,12},{12,8},{1,5},{5,1},{9,13},{13,9},{2,6},{6,2},{1... | collective-permute-start | bytes 1253384 | tf_op jit(solution)/shard_map/ppermute | solution.py:287
  28.9 2.1 %collective-permute-start.7 = (bf16[32,3712]{1,0:T(8,128)(2,1)S(1)}, bf16[32,3712]{1,0:T(8,128)(2,1)S(1)}, u32[]{:S(2)}, u32[]{:S(2)}) collective-permute-start(bf16[32,3712]{1,0:T(8,128)(2,1)S(1)} %get-tuple-element.105), channel_id=1, source_target_pairs={{0,1},{1,0},{2,3},{3,2},{4,5},{5,4},{6,7},{7,6},{8,9},{9,8},{10,11... | collective-permute-start | bytes 712712 | tf_op jit(solution)/shard_map/ppermute | solution.py:267
  29.0 2.0 %collective-permute-start.6 = (bf16[32,3712]{1,0:T(8,128)(2,1)S(1)}, bf16[32,3712]{1,0:T(8,128)(2,1)S(1)}, u32[]{:S(2)}, u32[]{:S(2)}) collective-permute-start(bf16[32,3712]{1,0:T(8,128)(2,1)S(1)} %get-tuple-element.106), channel_id=1, source_target_pairs={{0,1},{1,0},{2,3},{3,2},{4,5},{5,4},{6,7},{7,6},{8,9},{9,8},{10,11... | collective-permute-start | bytes 712712 | tf_op jit(solution)/shard_map/ppermute | solution.py:267
  29.5 17.5 %collective-permute-start.9 = (bf16[32,7424]{1,0:T(8,128)(2,1)S(1)}, bf16[32,7424]{1,0:T(8,128)(2,1)S(1)}, u32[]{:S(2)}, u32[]{:S(2)}) collective-permute-start(bf16[32,7424]{1,0:T(8,128)(2,1)S(1)} %get-tuple-element.76), channel_id=1, source_target_pairs={{0,2},{1,3},{2,0},{3,1},{4,6},{5,7},{6,4},{7,5},{8,10},{9,11},{10,... | collective-permute-start | bytes 1425416 | tf_op jit(solution)/shard_map/ppermute | solution.py:283
  36.2 11.6 %collective-permute-start.12 = (bf16[64,2176]{1,0:T(8,128)(2,1)S(1)}, bf16[64,2176]{1,0:T(8,128)(2,1)S(1)}, u32[]{:S(2)}, u32[]{:S(2)}) collective-permute-start(bf16[64,2176]{1,0:T(8,128)(2,1)S(1)} %get-tuple-element.80), channel_id=1, source_target_pairs={{0,4},{4,0},{8,12},{12,8},{1,5},{5,1},{9,13},{13,9},{2,6},{6,2},{1... | collective-permute-start | bytes 835592 | tf_op jit(solution)/shard_map/ppermute | solution.py:287
  38.7 3.2 %collective-permute-start.11 = (bf16[32,3712]{1,0:T(8,128)(2,1)S(1)}, bf16[32,3712]{1,0:T(8,128)(2,1)S(1)}, u32[]{:S(2)}, u32[]{:S(2)}) collective-permute-start(bf16[32,3712]{1,0:T(8,128)(2,1)S(1)} %get-tuple-element.103), channel_id=1, source_target_pairs={{0,1},{1,0},{2,3},{3,2},{4,5},{5,4},{6,7},{7,6},{8,9},{9,8},{10,11... | collective-permute-start | bytes 712712 | tf_op jit(solution)/shard_map/ppermute | solution.py:267
  38.8 3.1 %collective-permute-start.10 = (bf16[32,3712]{1,0:T(8,128)(2,1)S(1)}, bf16[32,3712]{1,0:T(8,128)(2,1)S(1)}, u32[]{:S(2)}, u32[]{:S(2)}) collective-permute-start(bf16[32,3712]{1,0:T(8,128)(2,1)S(1)} %get-tuple-element.104), channel_id=1, source_target_pairs={{0,1},{1,0},{2,3},{3,2},{4,5},{5,4},{6,7},{7,6},{8,9},{9,8},{10,11... | collective-permute-start | bytes 712712 | tf_op jit(solution)/shard_map/ppermute | solution.py:267
  39.3 8.5 %collective-permute-start.13 = (bf16[32,2176]{1,0:T(8,128)(2,1)S(1)}, bf16[32,2176]{1,0:T(8,128)(2,1)S(1)}, u32[]{:S(2)}, u32[]{:S(2)}) collective-permute-start(bf16[32,2176]{1,0:T(8,128)(2,1)S(1)} %get-tuple-element.81), channel_id=1, source_target_pairs={{0,8},{4,12},{8,0},{12,4},{1,9},{5,13},{9,1},{13,5},{2,10},{6,14},... | collective-permute-start | bytes 417800 | tf_op jit(solution)/shard_map/ppermute | solution.py:297
  47.9 5.9 %collective-permute-start.15 = (bf16[32,7424]{1,0:T(8,128)(2,1)S(1)}, bf16[32,7424]{1,0:T(8,128)(2,1)S(1)}, u32[]{:S(2)}, u32[]{:S(2)}) collective-permute-start(bf16[32,7424]{1,0:T(8,128)(2,1)S(1)} %collective-permute-done.9.direct_ref), channel_id=1, source_target_pairs={{0,1},{1,0},{2,3},{3,2},{4,5},{5,4},{6,7},{7,6},{8,9},{9,8},{10,11... | collective-permute-start | bytes 1425416 | tf_op jit(solution)/shard_map/ppermute | solution.py:267
  48.0 12.9 %collective-permute-start.14 = (bf16[64,2176]{1,0:T(8,128)(2,1)S(1)}, bf16[64,2176]{1,0:T(8,128)(2,1)S(1)}, u32[]{:S(2)}, u32[]{:S(2)}) collective-permute-start(bf16[64,2176]{1,0:T(8,128)(2,1)S(1)} %get-tuple-element.88), channel_id=1, source_target_pairs={{0,4},{4,0},{8,12},{12,8},{1,5},{5,1},{9,13},{13,9},{2,6},{6,2},{1... | collective-permute-start | bytes 835592 | tf_op jit(solution)/shard_map/ppermute | solution.py:287
  50.7 25.7 %copy-start = (bf16[8,64,2048]{2,1,0:T(8,128)(2,1)S(1)}, bf16[8,64,2048]{2,1,0:T(8,128)(2,1)}, u32[]{:S(2)}) copy-start(bf16[8,64,2048]{2,1,0:T(8,128)(2,1)} %param.8) | copy-start | bytes 6291460
  50.7 13.3 %collective-permute-start.17 = (bf16[32,2176]{1,0:T(8,128)(2,1)S(1)}, bf16[32,2176]{1,0:T(8,128)(2,1)S(1)}, u32[]{:S(2)}, u32[]{:S(2)}) collective-permute-start(bf16[32,2176]{1,0:T(8,128)(2,1)S(1)} %get-tuple-element.95), channel_id=1, source_target_pairs={{0,8},{4,12},{8,0},{12,4},{1,9},{5,13},{9,1},{13,5},{2,10},{6,14},... | collective-permute-start | bytes 417800 | tf_op jit(solution)/shard_map/ppermute | solution.py:297
  59.0 7.4 %collective-permute-start.16 = (bf16[32,2176]{1,0:T(8,128)(2,1)S(1)}, bf16[32,2176]{1,0:T(8,128)(2,1)S(1)}, u32[]{:S(2)}, u32[]{:S(2)}) collective-permute-start(bf16[32,2176]{1,0:T(8,128)(2,1)S(1)} %get-tuple-element.94), channel_id=1, source_target_pairs={{0,4},{4,0},{8,12},{12,8},{1,5},{5,1},{9,13},{13,9},{2,6},{6,2},{1... | collective-permute-start | bytes 417800 | tf_op jit(solution)/shard_map/ppermute | solution.py:290
  61.0 13.1 %collective-permute-start.18 = (bf16[32,2176]{1,0:T(8,128)(2,1)S(1)}, bf16[32,2176]{1,0:T(8,128)(2,1)S(1)}, u32[]{:S(2)}, u32[]{:S(2)}) collective-permute-start(bf16[32,2176]{1,0:T(8,128)(2,1)S(1)} %get-tuple-element.101), channel_id=1, source_target_pairs={{0,8},{4,12},{8,0},{12,4},{1,9},{5,13},{9,1},{13,5},{2,10},{6,14},... | collective-permute-start | bytes 417800 | tf_op jit(solution)/shard_map/ppermute | solution.py:297
  66.5 9.9 %collective-permute-start.19 = (bf16[32,2176]{1,0:T(8,128)(2,1)S(1)}, bf16[32,2176]{1,0:T(8,128)(2,1)S(1)}, u32[]{:S(2)}, u32[]{:S(2)}) collective-permute-start(bf16[32,2176]{1,0:T(8,128)(2,1)S(1)} %get-tuple-element.102), channel_id=1, source_target_pairs={{0,8},{4,12},{8,0},{12,4},{1,9},{5,13},{9,1},{13,5},{2,10},{6,14},... | collective-permute-start | bytes 417800 | tf_op jit(solution)/shard_map/ppermute | solution.py:300

commit v17 on v16

--- a/solution.py
+++ b/solution.py
@@ -91,20 +91,23 @@
         copy.wait()
 
 
-def part_rows(rows, value, cols, send_ref, keep_ref):
+def part_rows(rows, value, cols, outs):
     keep_first = lax.rem(lax.axis_index("req"), 2) == lax.rem(lax.axis_index("tensor"), 2)
-    value = value.astype(send_ref.dtype)
-    for at in range(0, send_ref.shape[0], rows):
-        first, second = value[2 * at : 2 * at + rows], value[2 * at + rows : 2 * at + 2 * rows]
-        send_ref[at : at + rows, cols] = jnp.where(keep_first, second, first)
-        keep_ref[at : at + rows, cols] = jnp.where(keep_first, first, second)
-
-
-def product_kernel(adapters, units, cuts, nears, _, own_ref, other_ref, direct_ref, *refs):
+    value = value.astype(outs[0].dtype)
+    base = 0
+    for send_ref, keep_ref in zip(outs[::2], outs[1::2]):
+        for at in range(0, send_ref.shape[0], rows):
+            first, second = value[base : base + rows], value[base + rows : base + 2 * rows]
+            send_ref[at : at + rows, cols] = jnp.where(keep_first, second, first)
+            keep_ref[at : at + rows, cols] = jnp.where(keep_first, first, second)
+            base += 2 * rows
+
+
+def product_kernel(adapters, units, cuts, nears, n_outs, _, own_ref, other_ref, direct_ref, *refs):
     passed_refs, refs = refs[:cuts], refs[cuts:]
-    *panel_refs, spread_ref, send_ref, keep_ref = refs
+    outs, (*panel_refs, spread_ref) = refs[-n_outs:], refs[:-n_outs]
     rows = direct_ref.shape[0]
-    width = send_ref.shape[1] - LANES
+    width = outs[0].shape[1] - LANES
     wide = spread_ref.shape[1]
     rank = wide // adapters
 
@@ -125,13 +128,13 @@
     tile = tile + pltpu.roll(tile, rank, 1)
     lane = lax.broadcasted_iota(jnp.int32, tile.shape, 1)
     tile = jnp.where(lane < rank, tile, ids)
-    part_rows(rows, tile, slice(width, width + LANES), send_ref, keep_ref)
+    part_rows(rows, tile, slice(width, width + LANES), outs)
 
     for panel, panel_ref in enumerate(panel_refs):
         value = jnp.dot(
             piece(), panel_ref[...], preferred_element_type=jnp.float32
         )
-        part_rows(rows, value, slice(panel * PANEL, (panel + 1) * PANEL), send_ref, keep_ref)
+        part_rows(rows, value, slice(panel * PANEL, (panel + 1) * PANEL), outs)
 
 
 def add_kernel(near_at, near_a, near_b, far_a, far_b, send_ref, keep_ref):
@@ -236,12 +239,15 @@
 
     def product(step, passed, token):
         nears = [starts[step]] if step + 1 < len(counts) else []
-        nears += [starts[-1]] if step == 0 else []
+        shapes = [struct((1 + len(nears)) * counts[step], payload)] * 2
+        if step == 0:
+            nears.append(starts[-1])
+            shapes += [struct(counts[step], payload)] * 2
         return pl.pallas_call(
-            functools.partial(product_kernel, adapters, units, len(passed), nears),
-            out_shape=[struct((1 + len(nears)) * counts[step], payload)] * 2,
+            functools.partial(product_kernel, adapters, units, len(passed), nears, len(shapes)),
+            out_shape=shapes,
             in_specs=[in_vmem()] * (4 + len(passed) + len(both)),
-            out_specs=[in_vmem()] * 2,
+            out_specs=[in_vmem()] * len(shapes),
             compiler_params=params(4),
             cost_estimate=quick,
             name="product",
@@ -249,7 +255,7 @@
 
     def add(step):
         last = step + 1 == len(counts)
-        near_at = counts[step] * (2 if last else 1)
+        near_at = 0 if last else counts[step]
         return pl.pallas_call(
             functools.partial(add_kernel, near_at),
             out_shape=[struct(counts[step], payload)] * 2,
@@ -258,7 +264,7 @@
             compiler_params=params(4),
             cost_estimate=quick,
             name="add",
-        )(*parts[0 if last else step], *parts[step])
+        )(*(late if last else parts[step]), *parts[step])
 
     def over_core(part, cuts):
         tiles = room // LANES
@@ -281,11 +287,15 @@
         passed = over_core(direct[step], CUTS[step])
         if step + 1 < steps:
             direct.append(lax.ppermute(pieces[step + 1], "req", across))
-        send, keep = product(step, passed, token)
+        send, keep, *extra = product(step, passed, token)
+        if extra:
+            late = (extra[1], lax.ppermute(extra[0], "tensor", next_z))
         hop = gots[step - 2 :] if step > 1 else []
         if step + 1 < steps:
             got = lax.ppermute(send, "tensor", next_z)
             direct[step + 1], keep, parts, hop = after((direct[step + 1], keep, parts, hop))
+            if step + 2 == steps:
+                direct[step + 1], late = after((direct[step + 1], late))
         else:
             got = lax.ppermute(send, "tensor", next_z)
         if step > 1 and step + 1 < steps:

time: 77.9 us -> 81.5 us (1.046)
  starting transfers between devices: 23.3 us -> 25.6 us
  waiting for transfers between devices: 15.8 us -> 17.1 us
    ppermute x4, waiting for transfers between devices: 6.64 us -> 3.08 us  [paired(): got = lax.ppermute(send, 'tensor', next_z)]
    ppermute x0 -> x1, waiting for transfers between devices: none -> 2.73 us  [paired(): late = (extra[1], lax.ppermute(extra[0], 'tensor', next_z))]
    ppermute x1, starting transfers between devices: 0.98 us -> 3.25 us  [paired(): gots.append(lax.ppermute(add_part(steps - 1), 'tensor', far_z))]
    ppermute x3, waiting for transfers between devices: 6.64 us -> 8.48 us  [paired(): gots.append(lax.ppermute(send, 'tensor', far_z))]
    ppermute x3, starting transfers between devices: 8.78 us -> 7.56 us  [paired(): gots.append(lax.ppermute(send, 'tensor', far_z))]
    ppermute x4, starting transfers between devices: 5.19 us -> 6.3 us  [paired(): got = lax.ppermute(send, 'tensor', next_z)]
  transfers between devices with their start and end apart: 20 -> 21, of which waited for: 7 -> 8; matrix products, arithmetic and copies ran while one was open for 0% -> 0% of each run, Pallas kernels for 45% -> 43%
where the time goes in v17:
time: 81.5 us; the launch traced here: 81.3 us
  Pallas kernels  38.3 us (47%)
  starting transfers between devices  25.6 us (31%)
  waiting for transfers between devices  17.1 us (21%)
    pallas_call x4, Pallas kernels, product(): pl.pallas_call(functools.partial(product_kernel, adapters, units, len(pas...  23 us
    pallas_call x1, Pallas kernels, paired(): pl.pallas_call(load_kernel, out_shape=[jax.ShapeDtypeStruct((8, LANES), j...  11.9 us
    ppermute x3, waiting for transfers between devices, paired(): gots.append(lax.ppermute(send, 'tensor', far_z))  8.48 us
    ppermute x3, starting transfers between devices, paired(): gots.append(lax.ppermute(send, 'tensor', far_z))  7.56 us
    ppermute x4, starting transfers between devices, paired(): got = lax.ppermute(send, 'tensor', next_z)  6.3 us
    ppermute x3, starting transfers between devices, paired(): direct.append(lax.ppermute(pieces[step + 1], 'req', across))  3.52 us
    ppermute x1, starting transfers between devices, paired(): gots.append(lax.ppermute(add_part(steps - 1), 'tensor', far_z))  3.25 us
    ppermute x4, waiting for transfers between devices, paired(): got = lax.ppermute(send, 'tensor', next_z)  3.08 us
  transfers between devices with their start and end apart: 21, of which 8 were waited for; matrix products, arithmetic and copies ran while one was open for 0% of the time, Pallas kernels for 43%

profile of v17, /device:TPU:0, one launch (start us, length us, event | category | flops | bytes accessed | tf_op | source)
XLA Modules:
  0.0 81.3 jit_solution(18038634317466923702)
XLA Ops:
  0.0 1.8 %turn.1 = (bf16[128,7424]{1,0:T(8,128)(2,1)S(1)}, bf16[32,7424]{1,0:T(8,128)(2,1)S(1)}, bf16[32,7424]{1,0:T(8,128)(2,1)S(1)}, bf16[32,7424]{1,0:T(8,128)(2,1)S(1)}, bf16[32,7424]{1,0:T(8,128)(2,1)S(1)}) custom-call(bf16[7392,128]{1,0:T(8,128)(2,1)} %bitcast.8, s32[1,128]{1,0:T(1,128)} %bitcast.9), custom_call_target="tpu_custom_call" | custom-call | tf_op jit(solution)/shard_map/turn/pallas_call | solution.py:200
  2.3 2.6 %collective-permute-start.1 = (bf16[32,7424]{1,0:T(8,128)(2,1)S(1)}, bf16[32,7424]{1,0:T(8,128)(2,1)S(1)}, u32[]{:S(2)}, u32[]{:S(2)}) collective-permute-start(bf16[32,7424]{1,0:T(8,128)(2,1)S(1)} %get-tuple-element.58), channel_id=1, source_target_pairs={{0,2},{1,3},{2,0},{3,1},{4,6},{5,7},{6,4},{7,5},{8,10},{9,11},{10,... | collective-permute-start | bytes 1425416 | tf_op jit(solution)/shard_map/ppermute | solution.py:219
  5.0 11.9 %load.1 = (f32[8,128]{1,0:T(8,128)S(1)}, bf16[7424,512]{1,0:T(8,128)(2,1)S(1)}, bf16[7424,512]{1,0:T(8,128)(2,1)S(1)}, bf16[7424,512]{1,0:T(8,128)(2,1)S(1)}, bf...) custom-call(bf16[7392,2048]{1,0:T(8,128)(2,1)} %w_hbm.1, bf16[512,7392]{1,0:T(8,128)(2,1)} %bitcast.7), custom_call_target="tpu_custom_call" | custom-call | flops 1 | bytes 1 | tf_op jit(solution)/shard_map/load/pallas_call | solution.py:223
  17.5 1.9 %collective-permute-start = (bf16[32,7424]{1,0:T(8,128)(2,1)S(1)}, bf16[32,7424]{1,0:T(8,128)(2,1)S(1)}, u32[]{:S(2)}, u32[]{:S(2)}) collective-permute-start(bf16[32,7424]{1,0:T(8,128)(2,1)S(1)} %get-tuple-element.57), channel_id=1, source_target_pairs={{0,2},{1,3},{2,0},{3,1},{4,6},{5,7},{6,4},{7,5},{8,10},{9,11},{10,... | collective-permute-start | bytes 1425416 | tf_op jit(solution)/shard_map/ppermute | solution.py:289
  19.5 7.5 %product.4 = (bf16[64,2176]{1,0:T(8,128)(2,1)S(1)}, bf16[64,2176]{1,0:T(8,128)(2,1)S(1)}, bf16[32,2176]{1,0:T(8,128)(2,1)S(1)}, bf16[32,2176]{1,0:T(8,128)(2,1)S(1)}) custom-call(f32[8,128]{1,0:T(8,128)S(1)} %get-tuple-element.60._, bf16[128,7424]{1,0:T(8,128)(2,1)S(1)} %get-tuple-element.61.own_ref, bf16[128,7424]{1,0:T(8,128)(2,1)S(1)} %collective-permute-done.2.other_ref, ...), custom_call_target="tpu_custom_call" | custom-call | flops 1 | bytes 1 | tf_op jit(solution)/shard_map/product/pallas_call | solution.py:246
  27.0 1.9 %collective-permute-start.8 = (bf16[64,2176]{1,0:T(8,128)(2,1)S(1)}, bf16[64,2176]{1,0:T(8,128)(2,1)S(1)}, u32[]{:S(2)}, u32[]{:S(2)}) collective-permute-start(bf16[64,2176]{1,0:T(8,128)(2,1)S(1)} %get-tuple-element.73), channel_id=1, source_target_pairs={{0,4},{4,0},{8,12},{12,8},{1,5},{5,1},{9,13},{13,9},{2,6},{6,2},{1... | collective-permute-start | bytes 835592 | tf_op jit(solution)/shard_map/ppermute | solution.py:295
  29.5 1.5 %collective-permute-start.9 = (bf16[32,7424]{1,0:T(8,128)(2,1)S(1)}, bf16[32,7424]{1,0:T(8,128)(2,1)S(1)}, u32[]{:S(2)}, u32[]{:S(2)}) collective-permute-start(bf16[32,7424]{1,0:T(8,128)(2,1)S(1)} %get-tuple-element.79), channel_id=1, source_target_pairs={{0,2},{1,3},{2,0},{3,1},{4,6},{5,7},{6,4},{7,5},{8,10},{9,11},{10,... | collective-permute-start | bytes 1425416 | tf_op jit(solution)/shard_map/ppermute | solution.py:289
  31.0 5.3 %product.5 = (bf16[64,2176]{1,0:T(8,128)(2,1)S(1)}, bf16[64,2176]{1,0:T(8,128)(2,1)S(1)}) custom-call(f32[8,128]{1,0:T(8,128)S(1)} %get-tuple-element.60._, bf16[128,7424]{1,0:T(8,128)(2,1)S(1)} %get-tuple-element.61.own_ref, bf16[128,7424]{1,0:T(8,128)(2,1)S(1)} %collective-permute-done.2.other_ref, bf16[32,7424]{1,0:T(8,128)(2,1)S(1)} %collective-permute-done.3.direct_ref, ...), custom_call_target="tpu_custom_call" | custom-call | flops 1 | bytes 1 | tf_op jit(solution)/shard_map/product/pallas_call | solution.py:246
  36.2 0.8 collective-permute-done.direct_ref
  37.2 2.1 %collective-permute-start.12 = (bf16[64,2176]{1,0:T(8,128)(2,1)S(1)}, bf16[64,2176]{1,0:T(8,128)(2,1)S(1)}, u32[]{:S(2)}, u32[]{:S(2)}) collective-permute-start(bf16[64,2176]{1,0:T(8,128)(2,1)S(1)} %get-tuple-element.83), channel_id=1, source_target_pairs={{0,4},{4,0},{8,12},{12,8},{1,5},{5,1},{9,13},{13,9},{2,6},{6,2},{1... | collective-permute-start | bytes 835592 | tf_op jit(solution)/shard_map/ppermute | solution.py:295
  39.5 2.6 %collective-permute-start.13 = (bf16[32,2176]{1,0:T(8,128)(2,1)S(1)}, bf16[32,2176]{1,0:T(8,128)(2,1)S(1)}, u32[]{:S(2)}, u32[]{:S(2)}) collective-permute-start(bf16[32,2176]{1,0:T(8,128)(2,1)S(1)} %get-tuple-element.84), channel_id=1, source_target_pairs={{0,8},{4,12},{8,0},{12,4},{1,9},{5,13},{9,1},{13,5},{2,10},{6,14},... | collective-permute-start | bytes 417800 | tf_op jit(solution)/shard_map/ppermute | solution.py:307
  42.5 5.1 %product.6 = (bf16[64,2176]{1,0:T(8,128)(2,1)S(1)}, bf16[64,2176]{1,0:T(8,128)(2,1)S(1)}) custom-call(f32[8,128]{1,0:T(8,128)S(1)} %get-tuple-element.60._, bf16[128,7424]{1,0:T(8,128)(2,1)S(1)} %get-tuple-element.61.own_ref, bf16[128,7424]{1,0:T(8,128)(2,1)S(1)} %collective-permute-done.2.other_ref, bf16[32,7424]{1,0:T(8,128)(2,1)S(1)} %collective-permute-done.direct_ref, ...), custom_call_target="tpu_custom_call" | custom-call | flops 1 | bytes 1 | tf_op jit(solution)/shard_map/product/pallas_call | solution.py:246
  47.6 1.7 %collective-permute-done.13.refs_4_ = bf16[32,2176]{1,0:T(8,128)(2,1)S(1)} collective-permute-done((bf16[32,2176]{1,0:T(8,128)(2,1)S(1)}, bf16[32,2176]{1,0:T(8,128)(2,1)S(1)}, u32[]{:S(2)}, u32[]{:S(2)}) %collective-permute-start.13) | collective-permute-done | bytes 139296 | tf_op jit(solution)/shard_map/ppermute | solution.py:307
  49.8 2.7 %collective-permute-done.14.near_b = bf16[32,2176]{1,0:T(8,128)(2,1)S(1)} collective-permute-done((bf16[32,2176]{1,0:T(8,128)(2,1)S(1)}, bf16[32,2176]{1,0:T(8,128)(2,1)S(1)}, u32[]{:S(2)}, u32[]{:S(2)}) %collective-permute-start.14) | collective-permute-done | bytes 139296 | tf_op jit(solution)/shard_map/ppermute | solution.py:292
  52.7 1.8 %collective-permute-start.15 = (bf16[64,2176]{1,0:T(8,128)(2,1)S(1)}, bf16[64,2176]{1,0:T(8,128)(2,1)S(1)}, u32[]{:S(2)}, u32[]{:S(2)}) collective-permute-start(bf16[64,2176]{1,0:T(8,128)(2,1)S(1)} %get-tuple-element.94), channel_id=1, source_target_pairs={{0,4},{4,0},{8,12},{12,8},{1,5},{5,1},{9,13},{13,9},{2,6},{6,2},{1... | collective-permute-start | bytes 835592 | tf_op jit(solution)/shard_map/ppermute | solution.py:295
  54.5 2.6 %collective-permute-start.18 = (bf16[32,2176]{1,0:T(8,128)(2,1)S(1)}, bf16[32,2176]{1,0:T(8,128)(2,1)S(1)}, u32[]{:S(2)}, u32[]{:S(2)}) collective-permute-start(bf16[32,2176]{1,0:T(8,128)(2,1)S(1)} %get-tuple-element.101), channel_id=1, source_target_pairs={{0,8},{4,12},{8,0},{12,4},{1,9},{5,13},{9,1},{13,5},{2,10},{6,14},... | collective-permute-start | bytes 417800 | tf_op jit(solution)/shard_map/ppermute | solution.py:307
  57.1 5.1 %product.7 = (bf16[32,2176]{1,0:T(8,128)(2,1)S(1)}, bf16[32,2176]{1,0:T(8,128)(2,1)S(1)}) custom-call(f32[8,128]{1,0:T(8,128)S(1)} %get-tuple-element.60._, bf16[128,7424]{1,0:T(8,128)(2,1)S(1)} %get-tuple-element.61.own_ref, bf16[128,7424]{1,0:T(8,128)(2,1)S(1)} %collective-permute-done.2.other_ref, bf16[32,7424]{1,0:T(8,128)(2,1)S(1)} %collective-permute-done.9.direct_ref, ...), custom_call_target="tpu_custom_call" | custom-call | flops 1 | bytes 1 | tf_op jit(solution)/shard_map/product/pallas_call | solution.py:246
  62.8 2.0 %collective-permute-done.15.near_b.far_b = bf16[64,2176]{1,0:T(8,128)(2,1)S(1)} collective-permute-done((bf16[64,2176]{1,0:T(8,128)(2,1)S(1)}, bf16[64,2176]{1,0:T(8,128)(2,1)S(1)}, u32[]{:S(2)}, u32[]{:S(2)}) %collective-permute-start.15) | collective-permute-done | bytes 278560 | tf_op jit(solution)/shard_map/ppermute | solution.py:295
  64.9 2.4 %collective-permute-start.19 = (bf16[32,2176]{1,0:T(8,128)(2,1)S(1)}, bf16[32,2176]{1,0:T(8,128)(2,1)S(1)}, u32[]{:S(2)}, u32[]{:S(2)}) collective-permute-start(bf16[32,2176]{1,0:T(8,128)(2,1)S(1)} %get-tuple-element.107), channel_id=1, source_target_pairs={{0,8},{4,12},{8,0},{12,4},{1,9},{5,13},{9,1},{13,5},{2,10},{6,14},... | collective-permute-start | bytes 417800 | tf_op jit(solution)/shard_map/ppermute | solution.py:307
  67.2 0.5 collective-permute-done.17.far_b
  67.9 3.3 %collective-permute-start.20 = (bf16[32,2176]{1,0:T(8,128)(2,1)S(1)}, bf16[32,2176]{1,0:T(8,128)(2,1)S(1)}, u32[]{:S(2)}, u32[]{:S(2)}) collective-permute-start(bf16[32,2176]{1,0:T(8,128)(2,1)S(1)} %get-tuple-element.108), channel_id=1, source_target_pairs={{0,8},{4,12},{8,0},{12,4},{1,9},{5,13},{9,1},{13,5},{2,10},{6,14},... | collective-permute-start | bytes 417800 | tf_op jit(solution)/shard_map/ppermute | solution.py:310
  71.1 6.8 %collective-permute-done.19.refs_6_ = bf16[32,2176]{1,0:T(8,128)(2,1)S(1)} collective-permute-done((bf16[32,2176]{1,0:T(8,128)(2,1)S(1)}, bf16[32,2176]{1,0:T(8,128)(2,1)S(1)}, u32[]{:S(2)}, u32[]{:S(2)}) %collective-permute-start.19) | collective-permute-done | bytes 139296 | tf_op jit(solution)/shard_map/ppermute | solution.py:307
  78.0 2.1 %collective-permute-done.20.refs_7_ = bf16[32,2176]{1,0:T(8,128)(2,1)S(1)} collective-permute-done((bf16[32,2176]{1,0:T(8,128)(2,1)S(1)}, bf16[32,2176]{1,0:T(8,128)(2,1)S(1)}, u32[]{:S(2)}, u32[]{:S(2)}) %collective-permute-start.20) | collective-permute-done | bytes 139296 | tf_op jit(solution)/shard_map/ppermute | solution.py:310
  80.0 1.3 %last.1 = bf16[128,2048]{1,0:T(8,128)(2,1)} custom-call(bf16[512,2048]{1,0:T(8,128)(2,1)S(1)} %bitcast.6, bf16[32,2176]{1,0:T(8,128)(2,1)S(1)} %get-tuple-element.78.refs_0_, bf16[32,2176]{1,0:T(8,128)(2,1)S(1)} %get-tuple-element.92.refs_1_, bf16[32,2176]{1,0:T(8,128)(2,1)S(1)} %get-tuple-element.95.refs_2_, ...), custom_call_target="tpu_custom_call" | custom-call | tf_op jit(solution)/shard_map/last/pallas_call | solution.py:312
  (34 shorter events, 4.1 us)
Async XLA Ops:
  1.8 17.6 %collective-permute-start.2 = (bf16[128,7424]{1,0:T(8,128)(2,1)S(1)}, bf16[128,7424]{1,0:T(8,128)(2,1)S(1)}, u32[]{:S(2)}, u32[]{:S(2)}) collective-permute-start(bf16[128,7424]{1,0:T(8,128)(2,1)S(1)} %get-tuple-element.61.own_ref), channel_id=1, source_target_pairs={{0,1},{1,0},{2,3},{3,2},{4,5},{5,4},{6,7},{7,6},{8,9},{9,8},{10,11... | collective-permute-start | bytes 5701640 | tf_op jit(solution)/shard_map/ppermute | solution.py:220
  2.3 14.5 %collective-permute-start.1 = (bf16[32,7424]{1,0:T(8,128)(2,1)S(1)}, bf16[32,7424]{1,0:T(8,128)(2,1)S(1)}, u32[]{:S(2)}, u32[]{:S(2)}) collective-permute-start(bf16[32,7424]{1,0:T(8,128)(2,1)S(1)} %get-tuple-element.58), channel_id=1, source_target_pairs={{0,2},{1,3},{2,0},{3,1},{4,6},{5,7},{6,4},{7,5},{8,10},{9,11},{10,... | collective-permute-start | bytes 1425416 | tf_op jit(solution)/shard_map/ppermute | solution.py:219
  4.9 22.1 %collective-permute-start.3 = (bf16[32,7424]{1,0:T(8,128)(2,1)S(1)}, bf16[32,7424]{1,0:T(8,128)(2,1)S(1)}, u32[]{:S(2)}, u32[]{:S(2)}) collective-permute-start(bf16[32,7424]{1,0:T(8,128)(2,1)S(1)} %get-tuple-element.62), channel_id=1, source_target_pairs={{0,2},{1,3},{2,0},{3,1},{4,6},{5,7},{6,4},{7,5},{8,10},{9,11},{10,... | collective-permute-start | bytes 1425416 | tf_op jit(solution)/shard_map/ppermute | solution.py:289
  16.9 2.5 %collective-permute-start.5 = (bf16[32,3712]{1,0:T(8,128)(2,1)S(1)}, bf16[32,3712]{1,0:T(8,128)(2,1)S(1)}, u32[]{:S(2)}, u32[]{:S(2)}) collective-permute-start(bf16[32,3712]{1,0:T(8,128)(2,1)S(1)} %get-tuple-element.113), channel_id=1, source_target_pairs={{0,1},{1,0},{2,3},{3,2},{4,5},{5,4},{6,7},{7,6},{8,9},{9,8},{10,11... | collective-permute-start | bytes 712712 | tf_op jit(solution)/shard_map/ppermute | solution.py:273
  17.1 2.4 %collective-permute-start.4 = (bf16[32,3712]{1,0:T(8,128)(2,1)S(1)}, bf16[32,3712]{1,0:T(8,128)(2,1)S(1)}, u32[]{:S(2)}, u32[]{:S(2)}) collective-permute-start(bf16[32,3712]{1,0:T(8,128)(2,1)S(1)} %get-tuple-element.114), channel_id=1, source_target_pairs={{0,1},{1,0},{2,3},{3,2},{4,5},{5,4},{6,7},{7,6},{8,9},{9,8},{10,11... | collective-permute-start | bytes 712712 | tf_op jit(solution)/shard_map/ppermute | solution.py:273
  17.5 19.5 %collective-permute-start = (bf16[32,7424]{1,0:T(8,128)(2,1)S(1)}, bf16[32,7424]{1,0:T(8,128)(2,1)S(1)}, u32[]{:S(2)}, u32[]{:S(2)}) collective-permute-start(bf16[32,7424]{1,0:T(8,128)(2,1)S(1)} %get-tuple-element.57), channel_id=1, source_target_pairs={{0,2},{1,3},{2,0},{3,1},{4,6},{5,7},{6,4},{7,5},{8,10},{9,11},{10,... | collective-permute-start | bytes 1425416 | tf_op jit(solution)/shard_map/ppermute | solution.py:289
  27.0 10.0 %collective-permute-start.8 = (bf16[64,2176]{1,0:T(8,128)(2,1)S(1)}, bf16[64,2176]{1,0:T(8,128)(2,1)S(1)}, u32[]{:S(2)}, u32[]{:S(2)}) collective-permute-start(bf16[64,2176]{1,0:T(8,128)(2,1)S(1)} %get-tuple-element.73), channel_id=1, source_target_pairs={{0,4},{4,0},{8,12},{12,8},{1,5},{5,1},{9,13},{13,9},{2,6},{6,2},{1... | collective-permute-start | bytes 835592 | tf_op jit(solution)/shard_map/ppermute | solution.py:295
  28.9 2.1 %collective-permute-start.7 = (bf16[32,3712]{1,0:T(8,128)(2,1)S(1)}, bf16[32,3712]{1,0:T(8,128)(2,1)S(1)}, u32[]{:S(2)}, u32[]{:S(2)}) collective-permute-start(bf16[32,3712]{1,0:T(8,128)(2,1)S(1)} %get-tuple-element.111), channel_id=1, source_target_pairs={{0,1},{1,0},{2,3},{3,2},{4,5},{5,4},{6,7},{7,6},{8,9},{9,8},{10,11... | collective-permute-start | bytes 712712 | tf_op jit(solution)/shard_map/ppermute | solution.py:273
  29.0 2.0 %collective-permute-start.6 = (bf16[32,3712]{1,0:T(8,128)(2,1)S(1)}, bf16[32,3712]{1,0:T(8,128)(2,1)S(1)}, u32[]{:S(2)}, u32[]{:S(2)}) collective-permute-start(bf16[32,3712]{1,0:T(8,128)(2,1)S(1)} %get-tuple-element.112), channel_id=1, source_target_pairs={{0,1},{1,0},{2,3},{3,2},{4,5},{5,4},{6,7},{7,6},{8,9},{9,8},{10,11... | collective-permute-start | bytes 712712 | tf_op jit(solution)/shard_map/ppermute | solution.py:273
  29.5 18.1 %collective-permute-start.9 = (bf16[32,7424]{1,0:T(8,128)(2,1)S(1)}, bf16[32,7424]{1,0:T(8,128)(2,1)S(1)}, u32[]{:S(2)}, u32[]{:S(2)}) collective-permute-start(bf16[32,7424]{1,0:T(8,128)(2,1)S(1)} %get-tuple-element.79), channel_id=1, source_target_pairs={{0,2},{1,3},{2,0},{3,1},{4,6},{5,7},{6,4},{7,5},{8,10},{9,11},{10,... | collective-permute-start | bytes 1425416 | tf_op jit(solution)/shard_map/ppermute | solution.py:289
  37.1 4.9 %collective-permute-start.11 = (bf16[32,3712]{1,0:T(8,128)(2,1)S(1)}, bf16[32,3712]{1,0:T(8,128)(2,1)S(1)}, u32[]{:S(2)}, u32[]{:S(2)}) collective-permute-start(bf16[32,3712]{1,0:T(8,128)(2,1)S(1)} %get-tuple-element.109), channel_id=1, source_target_pairs={{0,1},{1,0},{2,3},{3,2},{4,5},{5,4},{6,7},{7,6},{8,9},{9,8},{10,11... | collective-permute-start | bytes 712712 | tf_op jit(solution)/shard_map/ppermute | solution.py:273
  37.2 12.6 %collective-permute-start.12 = (bf16[64,2176]{1,0:T(8,128)(2,1)S(1)}, bf16[64,2176]{1,0:T(8,128)(2,1)S(1)}, u32[]{:S(2)}, u32[]{:S(2)}) collective-permute-start(bf16[64,2176]{1,0:T(8,128)(2,1)S(1)} %get-tuple-element.83), channel_id=1, source_target_pairs={{0,4},{4,0},{8,12},{12,8},{1,5},{5,1},{9,13},{13,9},{2,6},{6,2},{1... | collective-permute-start | bytes 835592 | tf_op jit(solution)/shard_map/ppermute | solution.py:295
  39.3 3.2 %collective-permute-start.10 = (bf16[32,3712]{1,0:T(8,128)(2,1)S(1)}, bf16[32,3712]{1,0:T(8,128)(2,1)S(1)}, u32[]{:S(2)}, u32[]{:S(2)}) collective-permute-start(bf16[32,3712]{1,0:T(8,128)(2,1)S(1)} %get-tuple-element.110), channel_id=1, source_target_pairs={{0,1},{1,0},{2,3},{3,2},{4,5},{5,4},{6,7},{7,6},{8,9},{9,8},{10,11... | collective-permute-start | bytes 712712 | tf_op jit(solution)/shard_map/ppermute | solution.py:273
  39.5 9.8 %collective-permute-start.13 = (bf16[32,2176]{1,0:T(8,128)(2,1)S(1)}, bf16[32,2176]{1,0:T(8,128)(2,1)S(1)}, u32[]{:S(2)}, u32[]{:S(2)}) collective-permute-start(bf16[32,2176]{1,0:T(8,128)(2,1)S(1)} %get-tuple-element.84), channel_id=1, source_target_pairs={{0,8},{4,12},{8,0},{12,4},{1,9},{5,13},{9,1},{13,5},{2,10},{6,14},... | collective-permute-start | bytes 417800 | tf_op jit(solution)/shard_map/ppermute | solution.py:307
  42.1 10.5 %collective-permute-start.14 = (bf16[32,2176]{1,0:T(8,128)(2,1)S(1)}, bf16[32,2176]{1,0:T(8,128)(2,1)S(1)}, u32[]{:S(2)}, u32[]{:S(2)}) collective-permute-start(bf16[32,2176]{1,0:T(8,128)(2,1)S(1)} %get-tuple-element.87), channel_id=1, source_target_pairs={{0,4},{4,0},{8,12},{12,8},{1,5},{5,1},{9,13},{13,9},{2,6},{6,2},{1... | collective-permute-start | bytes 417800 | tf_op jit(solution)/shard_map/ppermute | solution.py:292
  52.6 4.5 %collective-permute-start.16 = (bf16[32,7424]{1,0:T(8,128)(2,1)S(1)}, bf16[32,7424]{1,0:T(8,128)(2,1)S(1)}, u32[]{:S(2)}, u32[]{:S(2)}) collective-permute-start(bf16[32,7424]{1,0:T(8,128)(2,1)S(1)} %collective-permute-done.9.direct_ref), channel_id=1, source_target_pairs={{0,1},{1,0},{2,3},{3,2},{4,5},{5,4},{6,7},{7,6},{8,9},{9,8},{10,11... | collective-permute-start | bytes 1425416 | tf_op jit(solution)/shard_map/ppermute | solution.py:273
  52.7 12.1 %collective-permute-start.15 = (bf16[64,2176]{1,0:T(8,128)(2,1)S(1)}, bf16[64,2176]{1,0:T(8,128)(2,1)S(1)}, u32[]{:S(2)}, u32[]{:S(2)}) collective-permute-start(bf16[64,2176]{1,0:T(8,128)(2,1)S(1)} %get-tuple-element.94), channel_id=1, source_target_pairs={{0,4},{4,0},{8,12},{12,8},{1,5},{5,1},{9,13},{13,9},{2,6},{6,2},{1... | collective-permute-start | bytes 835592 | tf_op jit(solution)/shard_map/ppermute | solution.py:295
  54.5 25.5 %copy-start = (bf16[8,64,2048]{2,1,0:T(8,128)(2,1)S(1)}, bf16[8,64,2048]{2,1,0:T(8,128)(2,1)}, u32[]{:S(2)}) copy-start(bf16[8,64,2048]{2,1,0:T(8,128)(2,1)} %param.8) | copy-start | bytes 6291460
  54.5 12.7 %collective-permute-start.18 = (bf16[32,2176]{1,0:T(8,128)(2,1)S(1)}, bf16[32,2176]{1,0:T(8,128)(2,1)S(1)}, u32[]{:S(2)}, u32[]{:S(2)}) collective-permute-start(bf16[32,2176]{1,0:T(8,128)(2,1)S(1)} %get-tuple-element.101), channel_id=1, source_target_pairs={{0,8},{4,12},{8,0},{12,4},{1,9},{5,13},{9,1},{13,5},{2,10},{6,14},... | collective-permute-start | bytes 417800 | tf_op jit(solution)/shard_map/ppermute | solution.py:307
  62.2 5.5 %collective-permute-start.17 = (bf16[32,2176]{1,0:T(8,128)(2,1)S(1)}, bf16[32,2176]{1,0:T(8,128)(2,1)S(1)}, u32[]{:S(2)}, u32[]{:S(2)}) collective-permute-start(bf16[32,2176]{1,0:T(8,128)(2,1)S(1)} %get-tuple-element.100), channel_id=1, source_target_pairs={{0,4},{4,0},{8,12},{12,8},{1,5},{5,1},{9,13},{13,9},{2,6},{6,2},{1... | collective-permute-start | bytes 417800 | tf_op jit(solution)/shard_map/ppermute | solution.py:300
  64.9 13.1 %collective-permute-start.19 = (bf16[32,2176]{1,0:T(8,128)(2,1)S(1)}, bf16[32,2176]{1,0:T(8,128)(2,1)S(1)}, u32[]{:S(2)}, u32[]{:S(2)}) collective-permute-start(bf16[32,2176]{1,0:T(8,128)(2,1)S(1)} %get-tuple-element.107), channel_id=1, source_target_pairs={{0,8},{4,12},{8,0},{12,4},{1,9},{5,13},{9,1},{13,5},{2,10},{6,14},... | collective-permute-start | bytes 417800 | tf_op jit(solution)/shard_map/ppermute | solution.py:307
  67.9 12.1 %collective-permute-start.20 = (bf16[32,2176]{1,0:T(8,128)(2,1)S(1)}, bf16[32,2176]{1,0:T(8,128)(2,1)S(1)}, u32[]{:S(2)}, u32[]{:S(2)}) collective-permute-start(bf16[32,2176]{1,0:T(8,128)(2,1)S(1)} %get-tuple-element.108), channel_id=1, source_target_pairs={{0,8},{4,12},{8,0},{12,4},{1,9},{5,13},{9,1},{13,5},{2,10},{6,14},... | collective-permute-start | bytes 417800 | tf_op jit(solution)/shard_map/ppermute | solution.py:310

commit v18 on v16

--- a/solution.py
+++ b/solution.py
@@ -10,7 +10,7 @@
 LANES = 128
 PANEL = 512
 DEPTH = 1024
-TURN = 15
+TURN = 6
 PIECES = (32, 32, 32, 32)
 CUTS = (2, 2, 2, 1)
 FULL = 128

time: 77.9 us -> 78.1 us (level)
  no operation moved by 1% of the time
where the time goes in v18:
time: 78.1 us; the launch traced here: 78 us
  Pallas kernels  38.6 us (49%)
  starting transfers between devices  23.3 us (30%)
  waiting for transfers between devices  15.8 us (20%)
    pallas_call x4, Pallas kernels, product(): pl.pallas_call(functools.partial(product_kernel, adapters, units, len(pas...  23 us
    pallas_call x1, Pallas kernels, paired(): pl.pallas_call(load_kernel, out_shape=[jax.ShapeDtypeStruct((8, LANES), j...  11.9 us
    ppermute x3, starting transfers between devices, paired(): gots.append(lax.ppermute(send, 'tensor', far_z))  8.82 us
    ppermute x4, waiting for transfers between devices, paired(): got = lax.ppermute(send, 'tensor', next_z)  6.65 us
    ppermute x3, waiting for transfers between devices, paired(): gots.append(lax.ppermute(send, 'tensor', far_z))  6.6 us
    ppermute x4, starting transfers between devices, paired(): got = lax.ppermute(send, 'tensor', next_z)  5.17 us
    ppermute x3, starting transfers between devices, paired(): direct.append(lax.ppermute(pieces[step + 1], 'req', across))  3.52 us
    ppermute x1, starting transfers between devices, paired(): direct = [lax.ppermute(pieces[0], 'req', across)]  2.56 us
  transfers between devices with their start and end apart: 20, of which 7 were waited for; matrix products, arithmetic and copies ran while one was open for 0% of the time, Pallas kernels for 45%

profile of v18, /device:TPU:0, one launch (start us, length us, event | category | flops | bytes accessed | tf_op | source)
XLA Modules:
  0.0 78.0 jit_solution(11210248284829612831)
XLA Ops:
  0.0 2.1 %turn.1 = (bf16[128,7424]{1,0:T(8,128)(2,1)S(1)}, bf16[32,7424]{1,0:T(8,128)(2,1)S(1)}, bf16[32,7424]{1,0:T(8,128)(2,1)S(1)}, bf16[32,7424]{1,0:T(8,128)(2,1)S(1)}, bf16[32,7424]{1,0:T(8,128)(2,1)S(1)}) custom-call(bf16[7392,128]{1,0:T(8,128)(2,1)} %bitcast.8, s32[1,128]{1,0:T(1,128)} %bitcast.9), custom_call_target="tpu_custom_call" | custom-call | tf_op jit(solution)/shard_map/turn/pallas_call | solution.py:197
  2.1 0.5 collective-permute-start.2
  2.6 2.6 %collective-permute-start.1 = (bf16[32,7424]{1,0:T(8,128)(2,1)S(1)}, bf16[32,7424]{1,0:T(8,128)(2,1)S(1)}, u32[]{:S(2)}, u32[]{:S(2)}) collective-permute-start(bf16[32,7424]{1,0:T(8,128)(2,1)S(1)} %get-tuple-element.55), channel_id=1, source_target_pairs={{0,2},{1,3},{2,0},{3,1},{4,6},{5,7},{6,4},{7,5},{8,10},{9,11},{10,... | collective-permute-start | bytes 1425416 | tf_op jit(solution)/shard_map/ppermute | solution.py:216
  5.3 11.9 %load.1 = (f32[8,128]{1,0:T(8,128)S(1)}, bf16[7424,512]{1,0:T(8,128)(2,1)S(1)}, bf16[7424,512]{1,0:T(8,128)(2,1)S(1)}, bf16[7424,512]{1,0:T(8,128)(2,1)S(1)}, bf...) custom-call(bf16[7392,2048]{1,0:T(8,128)(2,1)} %w_hbm.1, bf16[512,7392]{1,0:T(8,128)(2,1)} %bitcast.7), custom_call_target="tpu_custom_call" | custom-call | flops 1 | bytes 1 | tf_op jit(solution)/shard_map/load/pallas_call | solution.py:220
  17.8 1.9 %collective-permute-start = (bf16[32,7424]{1,0:T(8,128)(2,1)S(1)}, bf16[32,7424]{1,0:T(8,128)(2,1)S(1)}, u32[]{:S(2)}, u32[]{:S(2)}) collective-permute-start(bf16[32,7424]{1,0:T(8,128)(2,1)S(1)} %get-tuple-element.54), channel_id=1, source_target_pairs={{0,2},{1,3},{2,0},{3,1},{4,6},{5,7},{6,4},{7,5},{8,10},{9,11},{10,... | collective-permute-start | bytes 1425416 | tf_op jit(solution)/shard_map/ppermute | solution.py:283
  19.7 7.5 %product.4 = (bf16[96,2176]{1,0:T(8,128)(2,1)S(1)}, bf16[96,2176]{1,0:T(8,128)(2,1)S(1)}) custom-call(f32[8,128]{1,0:T(8,128)S(1)} %get-tuple-element.57._, bf16[128,7424]{1,0:T(8,128)(2,1)S(1)} %get-tuple-element.58.own_ref, bf16[128,7424]{1,0:T(8,128)(2,1)S(1)} %collective-permute-done.2.other_ref, bf16[32,7424]{1,0:T(8,128)(2,1)S(1)} %collective-permute-done.1.direct_ref, ...), custom_call_target="tpu_custom_call" | custom-call | flops 1 | bytes 1 | tf_op jit(solution)/shard_map/product/pallas_call | solution.py:240
  27.2 1.9 %collective-permute-start.8 = (bf16[96,2176]{1,0:T(8,128)(2,1)S(1)}, bf16[96,2176]{1,0:T(8,128)(2,1)S(1)}, u32[]{:S(2)}, u32[]{:S(2)}) collective-permute-start(bf16[96,2176]{1,0:T(8,128)(2,1)S(1)} %get-tuple-element.70), channel_id=1, source_target_pairs={{0,4},{4,0},{8,12},{12,8},{1,5},{5,1},{9,13},{13,9},{2,6},{6,2},{1... | collective-permute-start | bytes 1253384 | tf_op jit(solution)/shard_map/ppermute | solution.py:287
  29.7 1.5 %collective-permute-start.9 = (bf16[32,7424]{1,0:T(8,128)(2,1)S(1)}, bf16[32,7424]{1,0:T(8,128)(2,1)S(1)}, u32[]{:S(2)}, u32[]{:S(2)}) collective-permute-start(bf16[32,7424]{1,0:T(8,128)(2,1)S(1)} %get-tuple-element.76), channel_id=1, source_target_pairs={{0,2},{1,3},{2,0},{3,1},{4,6},{5,7},{6,4},{7,5},{8,10},{9,11},{10,... | collective-permute-start | bytes 1425416 | tf_op jit(solution)/shard_map/ppermute | solution.py:283
  31.2 5.3 %product.5 = (bf16[64,2176]{1,0:T(8,128)(2,1)S(1)}, bf16[64,2176]{1,0:T(8,128)(2,1)S(1)}) custom-call(f32[8,128]{1,0:T(8,128)S(1)} %get-tuple-element.57._, bf16[128,7424]{1,0:T(8,128)(2,1)S(1)} %get-tuple-element.58.own_ref, bf16[128,7424]{1,0:T(8,128)(2,1)S(1)} %collective-permute-done.2.other_ref, bf16[32,7424]{1,0:T(8,128)(2,1)S(1)} %collective-permute-done.3.direct_ref, ...), custom_call_target="tpu_custom_call" | custom-call | flops 1 | bytes 1 | tf_op jit(solution)/shard_map/product/pallas_call | solution.py:240
  36.5 0.5 collective-permute-start.12
  37.3 1.6 %collective-permute-done.8.near_b.far_b = bf16[96,2176]{1,0:T(8,128)(2,1)S(1)} collective-permute-done((bf16[96,2176]{1,0:T(8,128)(2,1)S(1)}, bf16[96,2176]{1,0:T(8,128)(2,1)S(1)}, u32[]{:S(2)}, u32[]{:S(2)}) %collective-permute-start.8) | collective-permute-done | bytes 417824 | tf_op jit(solution)/shard_map/ppermute | solution.py:287
  39.6 2.6 %collective-permute-start.13 = (bf16[32,2176]{1,0:T(8,128)(2,1)S(1)}, bf16[32,2176]{1,0:T(8,128)(2,1)S(1)}, u32[]{:S(2)}, u32[]{:S(2)}) collective-permute-start(bf16[32,2176]{1,0:T(8,128)(2,1)S(1)} %get-tuple-element.81), channel_id=1, source_target_pairs={{0,8},{4,12},{8,0},{12,4},{1,9},{5,13},{9,1},{13,5},{2,10},{6,14},... | collective-permute-start | bytes 417800 | tf_op jit(solution)/shard_map/ppermute | solution.py:297
  42.2 5.1 %product.6 = (bf16[64,2176]{1,0:T(8,128)(2,1)S(1)}, bf16[64,2176]{1,0:T(8,128)(2,1)S(1)}) custom-call(f32[8,128]{1,0:T(8,128)S(1)} %get-tuple-element.57._, bf16[128,7424]{1,0:T(8,128)(2,1)S(1)} %get-tuple-element.58.own_ref, bf16[128,7424]{1,0:T(8,128)(2,1)S(1)} %collective-permute-done.2.other_ref, bf16[32,7424]{1,0:T(8,128)(2,1)S(1)} %collective-permute-done.direct_ref, ...), custom_call_target="tpu_custom_call" | custom-call | flops 1 | bytes 1 | tf_op jit(solution)/shard_map/product/pallas_call | solution.py:240
  47.3 0.9 %collective-permute-done.12.near_b.far_b = bf16[64,2176]{1,0:T(8,128)(2,1)S(1)} collective-permute-done((bf16[64,2176]{1,0:T(8,128)(2,1)S(1)}, bf16[64,2176]{1,0:T(8,128)(2,1)S(1)}, u32[]{:S(2)}, u32[]{:S(2)}) %collective-permute-start.12) | collective-permute-done | bytes 278560 | tf_op jit(solution)/shard_map/ppermute | solution.py:287
  48.3 2.6 %collective-permute-start.14 = (bf16[64,2176]{1,0:T(8,128)(2,1)S(1)}, bf16[64,2176]{1,0:T(8,128)(2,1)S(1)}, u32[]{:S(2)}, u32[]{:S(2)}) collective-permute-start(bf16[64,2176]{1,0:T(8,128)(2,1)S(1)} %get-tuple-element.88), channel_id=1, source_target_pairs={{0,4},{4,0},{8,12},{12,8},{1,5},{5,1},{9,13},{13,9},{2,6},{6,2},{1... | collective-permute-start | bytes 835592 | tf_op jit(solution)/shard_map/ppermute | solution.py:287
  50.9 3.2 %collective-permute-start.17 = (bf16[32,2176]{1,0:T(8,128)(2,1)S(1)}, bf16[32,2176]{1,0:T(8,128)(2,1)S(1)}, u32[]{:S(2)}, u32[]{:S(2)}) collective-permute-start(bf16[32,2176]{1,0:T(8,128)(2,1)S(1)} %get-tuple-element.95), channel_id=1, source_target_pairs={{0,8},{4,12},{8,0},{12,4},{1,9},{5,13},{9,1},{13,5},{2,10},{6,14},... | collective-permute-start | bytes 417800 | tf_op jit(solution)/shard_map/ppermute | solution.py:297
  54.2 5.1 %product.7 = (bf16[32,2176]{1,0:T(8,128)(2,1)S(1)}, bf16[32,2176]{1,0:T(8,128)(2,1)S(1)}) custom-call(f32[8,128]{1,0:T(8,128)S(1)} %get-tuple-element.57._, bf16[128,7424]{1,0:T(8,128)(2,1)S(1)} %get-tuple-element.58.own_ref, bf16[128,7424]{1,0:T(8,128)(2,1)S(1)} %collective-permute-done.2.other_ref, bf16[32,7424]{1,0:T(8,128)(2,1)S(1)} %collective-permute-done.9.direct_ref, ...), custom_call_target="tpu_custom_call" | custom-call | flops 1 | bytes 1 | tf_op jit(solution)/shard_map/product/pallas_call | solution.py:240
  59.4 1.7 %collective-permute-done.14.near_b.far_b = bf16[64,2176]{1,0:T(8,128)(2,1)S(1)} collective-permute-done((bf16[64,2176]{1,0:T(8,128)(2,1)S(1)}, bf16[64,2176]{1,0:T(8,128)(2,1)S(1)}, u32[]{:S(2)}, u32[]{:S(2)}) %collective-permute-start.14) | collective-permute-done | bytes 278560 | tf_op jit(solution)/shard_map/ppermute | solution.py:287
  61.3 3.0 %collective-permute-start.18 = (bf16[32,2176]{1,0:T(8,128)(2,1)S(1)}, bf16[32,2176]{1,0:T(8,128)(2,1)S(1)}, u32[]{:S(2)}, u32[]{:S(2)}) collective-permute-start(bf16[32,2176]{1,0:T(8,128)(2,1)S(1)} %get-tuple-element.101), channel_id=1, source_target_pairs={{0,8},{4,12},{8,0},{12,4},{1,9},{5,13},{9,1},{13,5},{2,10},{6,14},... | collective-permute-start | bytes 417800 | tf_op jit(solution)/shard_map/ppermute | solution.py:297
  64.3 2.5 %collective-permute-done.16.far_b = bf16[32,2176]{1,0:T(8,128)(2,1)S(1)} collective-permute-done((bf16[32,2176]{1,0:T(8,128)(2,1)S(1)}, bf16[32,2176]{1,0:T(8,128)(2,1)S(1)}, u32[]{:S(2)}, u32[]{:S(2)}) %collective-permute-start.16) | collective-permute-done | bytes 139296 | tf_op jit(solution)/shard_map/ppermute | solution.py:290
  66.8 1.0 %collective-permute-start.19 = (bf16[32,2176]{1,0:T(8,128)(2,1)S(1)}, bf16[32,2176]{1,0:T(8,128)(2,1)S(1)}, u32[]{:S(2)}, u32[]{:S(2)}) collective-permute-start(bf16[32,2176]{1,0:T(8,128)(2,1)S(1)} %get-tuple-element.102), channel_id=1, source_target_pairs={{0,8},{4,12},{8,0},{12,4},{1,9},{5,13},{9,1},{13,5},{2,10},{6,14},... | collective-permute-start | bytes 417800 | tf_op jit(solution)/shard_map/ppermute | solution.py:300
  67.8 6.6 %collective-permute-done.18.refs_6_ = bf16[32,2176]{1,0:T(8,128)(2,1)S(1)} collective-permute-done((bf16[32,2176]{1,0:T(8,128)(2,1)S(1)}, bf16[32,2176]{1,0:T(8,128)(2,1)S(1)}, u32[]{:S(2)}, u32[]{:S(2)}) %collective-permute-start.18) | collective-permute-done | bytes 139296 | tf_op jit(solution)/shard_map/ppermute | solution.py:297
  74.4 2.3 %collective-permute-done.19.refs_7_ = bf16[32,2176]{1,0:T(8,128)(2,1)S(1)} collective-permute-done((bf16[32,2176]{1,0:T(8,128)(2,1)S(1)}, bf16[32,2176]{1,0:T(8,128)(2,1)S(1)}, u32[]{:S(2)}, u32[]{:S(2)}) %collective-permute-start.19) | collective-permute-done | bytes 139296 | tf_op jit(solution)/shard_map/ppermute | solution.py:300
  76.7 1.3 %last.1 = bf16[128,2048]{1,0:T(8,128)(2,1)} custom-call(bf16[512,2048]{1,0:T(8,128)(2,1)S(1)} %bitcast.6, bf16[32,2176]{1,0:T(8,128)(2,1)S(1)} %get-tuple-element.75.refs_0_, bf16[32,2176]{1,0:T(8,128)(2,1)S(1)} %get-tuple-element.86.refs_1_, bf16[32,2176]{1,0:T(8,128)(2,1)S(1)} %get-tuple-element.89.refs_2_, ...), custom_call_target="tpu_custom_call" | custom-call | tf_op jit(solution)/shard_map/last/pallas_call | solution.py:302
  (32 shorter events, 2.8 us)
Async XLA Ops:
  2.1 17.6 %collective-permute-start.2 = (bf16[128,7424]{1,0:T(8,128)(2,1)S(1)}, bf16[128,7424]{1,0:T(8,128)(2,1)S(1)}, u32[]{:S(2)}, u32[]{:S(2)}) collective-permute-start(bf16[128,7424]{1,0:T(8,128)(2,1)S(1)} %get-tuple-element.58.own_ref), channel_id=1, source_target_pairs={{0,1},{1,0},{2,3},{3,2},{4,5},{5,4},{6,7},{7,6},{8,9},{9,8},{10,11... | collective-permute-start | bytes 5701640 | tf_op jit(solution)/shard_map/ppermute | solution.py:217
  2.6 14.5 %collective-permute-start.1 = (bf16[32,7424]{1,0:T(8,128)(2,1)S(1)}, bf16[32,7424]{1,0:T(8,128)(2,1)S(1)}, u32[]{:S(2)}, u32[]{:S(2)}) collective-permute-start(bf16[32,7424]{1,0:T(8,128)(2,1)S(1)} %get-tuple-element.55), channel_id=1, source_target_pairs={{0,2},{1,3},{2,0},{3,1},{4,6},{5,7},{6,4},{7,5},{8,10},{9,11},{10,... | collective-permute-start | bytes 1425416 | tf_op jit(solution)/shard_map/ppermute | solution.py:216
  5.2 22.1 %collective-permute-start.3 = (bf16[32,7424]{1,0:T(8,128)(2,1)S(1)}, bf16[32,7424]{1,0:T(8,128)(2,1)S(1)}, u32[]{:S(2)}, u32[]{:S(2)}) collective-permute-start(bf16[32,7424]{1,0:T(8,128)(2,1)S(1)} %get-tuple-element.59), channel_id=1, source_target_pairs={{0,2},{1,3},{2,0},{3,1},{4,6},{5,7},{6,4},{7,5},{8,10},{9,11},{10,... | collective-permute-start | bytes 1425416 | tf_op jit(solution)/shard_map/ppermute | solution.py:283
  17.2 2.5 %collective-permute-start.5 = (bf16[32,3712]{1,0:T(8,128)(2,1)S(1)}, bf16[32,3712]{1,0:T(8,128)(2,1)S(1)}, u32[]{:S(2)}, u32[]{:S(2)}) collective-permute-start(bf16[32,3712]{1,0:T(8,128)(2,1)S(1)} %get-tuple-element.107), channel_id=1, source_target_pairs={{0,1},{1,0},{2,3},{3,2},{4,5},{5,4},{6,7},{7,6},{8,9},{9,8},{10,11... | collective-permute-start | bytes 712712 | tf_op jit(solution)/shard_map/ppermute | solution.py:267
  17.3 2.4 %collective-permute-start.4 = (bf16[32,3712]{1,0:T(8,128)(2,1)S(1)}, bf16[32,3712]{1,0:T(8,128)(2,1)S(1)}, u32[]{:S(2)}, u32[]{:S(2)}) collective-permute-start(bf16[32,3712]{1,0:T(8,128)(2,1)S(1)} %get-tuple-element.108), channel_id=1, source_target_pairs={{0,1},{1,0},{2,3},{3,2},{4,5},{5,4},{6,7},{7,6},{8,9},{9,8},{10,11... | collective-permute-start | bytes 712712 | tf_op jit(solution)/shard_map/ppermute | solution.py:267
  17.8 19.5 %collective-permute-start = (bf16[32,7424]{1,0:T(8,128)(2,1)S(1)}, bf16[32,7424]{1,0:T(8,128)(2,1)S(1)}, u32[]{:S(2)}, u32[]{:S(2)}) collective-permute-start(bf16[32,7424]{1,0:T(8,128)(2,1)S(1)} %get-tuple-element.54), channel_id=1, source_target_pairs={{0,2},{1,3},{2,0},{3,1},{4,6},{5,7},{6,4},{7,5},{8,10},{9,11},{10,... | collective-permute-start | bytes 1425416 | tf_op jit(solution)/shard_map/ppermute | solution.py:283
  27.2 11.6 %collective-permute-start.8 = (bf16[96,2176]{1,0:T(8,128)(2,1)S(1)}, bf16[96,2176]{1,0:T(8,128)(2,1)S(1)}, u32[]{:S(2)}, u32[]{:S(2)}) collective-permute-start(bf16[96,2176]{1,0:T(8,128)(2,1)S(1)} %get-tuple-element.70), channel_id=1, source_target_pairs={{0,4},{4,0},{8,12},{12,8},{1,5},{5,1},{9,13},{13,9},{2,6},{6,2},{1... | collective-permute-start | bytes 1253384 | tf_op jit(solution)/shard_map/ppermute | solution.py:287
  29.1 2.1 %collective-permute-start.7 = (bf16[32,3712]{1,0:T(8,128)(2,1)S(1)}, bf16[32,3712]{1,0:T(8,128)(2,1)S(1)}, u32[]{:S(2)}, u32[]{:S(2)}) collective-permute-start(bf16[32,3712]{1,0:T(8,128)(2,1)S(1)} %get-tuple-element.105), channel_id=1, source_target_pairs={{0,1},{1,0},{2,3},{3,2},{4,5},{5,4},{6,7},{7,6},{8,9},{9,8},{10,11... | collective-permute-start | bytes 712712 | tf_op jit(solution)/shard_map/ppermute | solution.py:267
  29.2 2.0 %collective-permute-start.6 = (bf16[32,3712]{1,0:T(8,128)(2,1)S(1)}, bf16[32,3712]{1,0:T(8,128)(2,1)S(1)}, u32[]{:S(2)}, u32[]{:S(2)}) collective-permute-start(bf16[32,3712]{1,0:T(8,128)(2,1)S(1)} %get-tuple-element.106), channel_id=1, source_target_pairs={{0,1},{1,0},{2,3},{3,2},{4,5},{5,4},{6,7},{7,6},{8,9},{9,8},{10,11... | collective-permute-start | bytes 712712 | tf_op jit(solution)/shard_map/ppermute | solution.py:267
  29.7 17.5 %collective-permute-start.9 = (bf16[32,7424]{1,0:T(8,128)(2,1)S(1)}, bf16[32,7424]{1,0:T(8,128)(2,1)S(1)}, u32[]{:S(2)}, u32[]{:S(2)}) collective-permute-start(bf16[32,7424]{1,0:T(8,128)(2,1)S(1)} %get-tuple-element.76), channel_id=1, source_target_pairs={{0,2},{1,3},{2,0},{3,1},{4,6},{5,7},{6,4},{7,5},{8,10},{9,11},{10,... | collective-permute-start | bytes 1425416 | tf_op jit(solution)/shard_map/ppermute | solution.py:283
  36.5 11.6 %collective-permute-start.12 = (bf16[64,2176]{1,0:T(8,128)(2,1)S(1)}, bf16[64,2176]{1,0:T(8,128)(2,1)S(1)}, u32[]{:S(2)}, u32[]{:S(2)}) collective-permute-start(bf16[64,2176]{1,0:T(8,128)(2,1)S(1)} %get-tuple-element.80), channel_id=1, source_target_pairs={{0,4},{4,0},{8,12},{12,8},{1,5},{5,1},{9,13},{13,9},{2,6},{6,2},{1... | collective-permute-start | bytes 835592 | tf_op jit(solution)/shard_map/ppermute | solution.py:287
  39.0 3.2 %collective-permute-start.11 = (bf16[32,3712]{1,0:T(8,128)(2,1)S(1)}, bf16[32,3712]{1,0:T(8,128)(2,1)S(1)}, u32[]{:S(2)}, u32[]{:S(2)}) collective-permute-start(bf16[32,3712]{1,0:T(8,128)(2,1)S(1)} %get-tuple-element.103), channel_id=1, source_target_pairs={{0,1},{1,0},{2,3},{3,2},{4,5},{5,4},{6,7},{7,6},{8,9},{9,8},{10,11... | collective-permute-start | bytes 712712 | tf_op jit(solution)/shard_map/ppermute | solution.py:267
  39.1 3.1 %collective-permute-start.10 = (bf16[32,3712]{1,0:T(8,128)(2,1)S(1)}, bf16[32,3712]{1,0:T(8,128)(2,1)S(1)}, u32[]{:S(2)}, u32[]{:S(2)}) collective-permute-start(bf16[32,3712]{1,0:T(8,128)(2,1)S(1)} %get-tuple-element.104), channel_id=1, source_target_pairs={{0,1},{1,0},{2,3},{3,2},{4,5},{5,4},{6,7},{7,6},{8,9},{9,8},{10,11... | collective-permute-start | bytes 712712 | tf_op jit(solution)/shard_map/ppermute | solution.py:267
  39.6 8.5 %collective-permute-start.13 = (bf16[32,2176]{1,0:T(8,128)(2,1)S(1)}, bf16[32,2176]{1,0:T(8,128)(2,1)S(1)}, u32[]{:S(2)}, u32[]{:S(2)}) collective-permute-start(bf16[32,2176]{1,0:T(8,128)(2,1)S(1)} %get-tuple-element.81), channel_id=1, source_target_pairs={{0,8},{4,12},{8,0},{12,4},{1,9},{5,13},{9,1},{13,5},{2,10},{6,14},... | collective-permute-start | bytes 417800 | tf_op jit(solution)/shard_map/ppermute | solution.py:297
  48.2 5.9 %collective-permute-start.15 = (bf16[32,7424]{1,0:T(8,128)(2,1)S(1)}, bf16[32,7424]{1,0:T(8,128)(2,1)S(1)}, u32[]{:S(2)}, u32[]{:S(2)}) collective-permute-start(bf16[32,7424]{1,0:T(8,128)(2,1)S(1)} %collective-permute-done.9.direct_ref), channel_id=1, source_target_pairs={{0,1},{1,0},{2,3},{3,2},{4,5},{5,4},{6,7},{7,6},{8,9},{9,8},{10,11... | collective-permute-start | bytes 1425416 | tf_op jit(solution)/shard_map/ppermute | solution.py:267
  48.3 12.9 %collective-permute-start.14 = (bf16[64,2176]{1,0:T(8,128)(2,1)S(1)}, bf16[64,2176]{1,0:T(8,128)(2,1)S(1)}, u32[]{:S(2)}, u32[]{:S(2)}) collective-permute-start(bf16[64,2176]{1,0:T(8,128)(2,1)S(1)} %get-tuple-element.88), channel_id=1, source_target_pairs={{0,4},{4,0},{8,12},{12,8},{1,5},{5,1},{9,13},{13,9},{2,6},{6,2},{1... | collective-permute-start | bytes 835592 | tf_op jit(solution)/shard_map/ppermute | solution.py:287
  50.9 25.7 %copy-start = (bf16[8,64,2048]{2,1,0:T(8,128)(2,1)S(1)}, bf16[8,64,2048]{2,1,0:T(8,128)(2,1)}, u32[]{:S(2)}) copy-start(bf16[8,64,2048]{2,1,0:T(8,128)(2,1)} %param.8) | copy-start | bytes 6291460
  50.9 13.3 %collective-permute-start.17 = (bf16[32,2176]{1,0:T(8,128)(2,1)S(1)}, bf16[32,2176]{1,0:T(8,128)(2,1)S(1)}, u32[]{:S(2)}, u32[]{:S(2)}) collective-permute-start(bf16[32,2176]{1,0:T(8,128)(2,1)S(1)} %get-tuple-element.95), channel_id=1, source_target_pairs={{0,8},{4,12},{8,0},{12,4},{1,9},{5,13},{9,1},{13,5},{2,10},{6,14},... | collective-permute-start | bytes 417800 | tf_op jit(solution)/shard_map/ppermute | solution.py:297
  59.3 7.4 %collective-permute-start.16 = (bf16[32,2176]{1,0:T(8,128)(2,1)S(1)}, bf16[32,2176]{1,0:T(8,128)(2,1)S(1)}, u32[]{:S(2)}, u32[]{:S(2)}) collective-permute-start(bf16[32,2176]{1,0:T(8,128)(2,1)S(1)} %get-tuple-element.94), channel_id=1, source_target_pairs={{0,4},{4,0},{8,12},{12,8},{1,5},{5,1},{9,13},{13,9},{2,6},{6,2},{1... | collective-permute-start | bytes 417800 | tf_op jit(solution)/shard_map/ppermute | solution.py:290
  61.3 13.1 %collective-permute-start.18 = (bf16[32,2176]{1,0:T(8,128)(2,1)S(1)}, bf16[32,2176]{1,0:T(8,128)(2,1)S(1)}, u32[]{:S(2)}, u32[]{:S(2)}) collective-permute-start(bf16[32,2176]{1,0:T(8,128)(2,1)S(1)} %get-tuple-element.101), channel_id=1, source_target_pairs={{0,8},{4,12},{8,0},{12,4},{1,9},{5,13},{9,1},{13,5},{2,10},{6,14},... | collective-permute-start | bytes 417800 | tf_op jit(solution)/shard_map/ppermute | solution.py:297
  66.8 9.8 %collective-permute-start.19 = (bf16[32,2176]{1,0:T(8,128)(2,1)S(1)}, bf16[32,2176]{1,0:T(8,128)(2,1)S(1)}, u32[]{:S(2)}, u32[]{:S(2)}) collective-permute-start(bf16[32,2176]{1,0:T(8,128)(2,1)S(1)} %get-tuple-element.102), channel_id=1, source_target_pairs={{0,8},{4,12},{8,0},{12,4},{1,9},{5,13},{9,1},{13,5},{2,10},{6,14},... | collective-permute-start | bytes 417800 | tf_op jit(solution)/shard_map/ppermute | solution.py:300
